TPU v7x, 32 devices: a whole 2x2x4 slice. The times are simulated.
32 devices in a mesh: groups: 2 (over x), ty: 16 (over z, y, core).
Axes of the slice: x: 2, y: 2, z: 4, core: 2. Of those that a mesh axis runs over, the one named last changes fastest.
Arguments:
- spectrum: float32 [2, 4096, 8192], P(None, ('groups', 'ty')), parts along dimension 1, may hold values from -6 to 6
- pupil: bfloat16 [1024, 1024], replicated, may hold values from 0.19921875 to 1
- measured: bfloat16 [32, 256, 1024], P(('groups', 'ty')), parts along dimension 0, may hold values from 0.29882812 to 3
- centre_rows: int32 [32], P('groups'), parts along dimension 0, may hold values from 512 to 1536
- centre_cols: int32 [32], P('groups'), parts along dimension 0, may hold values from 512 to 7680
Outputs:
- updated: float32 [2, 4096, 8192], P(None, ('groups', 'ty')), parts along dimension 1
There are 2 independent parts, one for each index of `groups`. A program takes and returns all parts, laid end to end along the dimension named above; an argument that names none is the same for every part. Nothing has to cross between parts.
Inputs may be any that keep to these rules, and one draw needn't show every extreme that they name: `centre_rows`: each pupil crop lies inside the slab's rows. `centre_cols`: each pupil crop lies inside the slab's columns.
All inputs are finite; a program needn't handle non-finite values.
Results may differ from a plain program's by a relative error of at most 0.00063.
Values may be sent and summed in bfloat16 or wider, within the bound.
No kernel may reach another device: no remote copies, remote signals or barrier semaphores. Data moves between devices by JAX's collectives and lax.ppermute only.
A program may use at most 128 MiB of HBM per device.

v0:
```python
import functools
import math

import jax
import jax.numpy as jnp
import numpy as np
from jax import lax
from jax.experimental import pallas as pl
from jax.experimental.pallas import tpu as pltpu
from jax.sharding import PartitionSpec as P

step_size = 0.5
lane = 128
row_tile = 16
vmem_bytes = 32 * 1024 * 1024


def fourier_tables(crop_width):
    counter = np.arange(crop_width, dtype=np.int64)
    angle = (counter[:, None] * counter[None, :] % crop_width) * (2.0 * math.pi / crop_width)
    factor = 1.0 / math.sqrt(crop_width)
    cos_table = (np.cos(angle) * factor).astype(np.float32).astype(jnp.bfloat16)
    sin_table = (np.sin(angle) * factor).astype(np.float32).astype(jnp.bfloat16)
    return cos_table, sin_table


def tile_weight(pupil_ref, first_row, win):
    start = win.row(first_row)
    rows = pupil_ref[pl.ds(start, win.rows), :].astype(jnp.float32)
    rows = pltpu.roll(rows, (2 * win.rows + start - first_row) % win.rows, 0)
    shape = (win.tile_rows, win.crop_width)
    row = 2 * (first_row + lax.broadcasted_iota(jnp.int32, shape, 0)) - win.crop_width + 1
    column = 2 * lax.broadcasted_iota(jnp.int32, shape, 1) - win.crop_width + 1
    inside = row * row + column * column <= win.crop_width * win.crop_width
    return jnp.where(inside, rows[: win.tile_rows], 0.0)


def tile_band(band_ref, first_row, win):
    start = win.row(first_row)
    rows = band_ref[pl.ds(start, win.rows), :].astype(jnp.float32)
    rows = pltpu.roll(rows, (2 * win.rows + start - first_row) % win.rows, 0)[: win.tile_rows]
    band = rows.shape[1] // 2
    turned = jnp.concatenate([-rows[:, band:], rows[:, :band]], axis=1)
    return jnp.concatenate([rows, turned], axis=0).astype(jnp.bfloat16)


class Windows:
    def __init__(self, tile_rows, slab_columns, crop_width):
        self.tile_rows = tile_rows
        self.crop_width = crop_width
        self.rows = tile_rows + row_tile
        self.columns = crop_width + lane
        self.last_row = crop_width - self.rows
        self.last_column = slab_columns - self.columns

    def row(self, first_row):
        start = jnp.clip(first_row, 0, self.last_row) // row_tile * row_tile
        return pl.multiple_of(start, row_tile)

    def column(self, left):
        start = jnp.minimum(left // lane * lane, self.last_column)
        return pl.multiple_of(start, lane)

    def active(self, first_row):
        return (first_row > -self.tile_rows) & (first_row < self.crop_width)


def image_band(meta_ref, slot, lows, pupil_ref, band_ref, win, store):
    halves = len(lows)
    left = meta_ref[halves, slot]
    first_rows = [meta_ref[half, slot] for half in range(halves)]
    active = functools.reduce(jnp.logical_or, [win.active(row) for row in first_rows])
    band = band_ref.shape[1] // 2
    shape = (2, band, win.crop_width)

    @pl.when(jnp.logical_not(active))
    def _():
        store(jnp.zeros(shape, jnp.bfloat16))

    @pl.when(active)
    def _():
        col_start = win.column(left)
        shift = (win.columns - (left - col_start)) % win.columns
        parts, tables = [], []
        for first_row, low_refs in zip(first_rows, lows):
            weight = tile_weight(pupil_ref, first_row, win)
            for low_ref in low_refs:
                low = low_ref[:, pl.ds(col_start, win.columns)].astype(jnp.float32)
                low = pltpu.roll(low, shift, 1)[:, : win.crop_width]
                parts.append((weight * low).astype(jnp.bfloat16))
            tables.append(tile_band(band_ref, first_row, win))
        mid = lax.dot_general(
            jnp.concatenate(tables, axis=0),
            jnp.concatenate(parts, axis=0),
            (((0,), (0,)), ((), ())),
            preferred_element_type=jnp.float32,
        )
        store(mid.astype(jnp.bfloat16).reshape(shape))


def forward_kernel(meta_ref, pupil_ref, band_ref, *refs, base, win, halves):
    low_refs, out_refs = refs[: 2 * halves], refs[2 * halves :]
    lows = [low_refs[2 * half : 2 * half + 2] for half in range(halves)]

    def image(index):
        def store(value):
            for number, out_ref in enumerate(out_refs):

                @pl.when(index == number)
                def _():
                    out_ref[...] = value

        image_band(meta_ref, base + index, lows, pupil_ref, band_ref, win, store)

    pl.loop(0, len(out_refs))(image)


def forward_grid_kernel(meta_ref, pupil_ref, band_ref, real_ref, imag_ref, out_ref, *, win):
    def store(value):
        out_ref[0] = value

    lows = [(real_ref, imag_ref)]
    image_band(meta_ref, pl.program_id(0), lows, pupil_ref, band_ref, win, store)


def subtract_image(meta_ref, slot, back_ref, pupil_ref, band_ref, out_ref, win):
    first_row, left = meta_ref[0, slot], meta_ref[meta_ref.shape[0] - 1, slot]
    tile_rows, crop_width = win.tile_rows, win.crop_width

    @pl.when(win.active(first_row))
    def _():
        col_start = win.column(left)
        weight = tile_weight(pupil_ref, first_row, win) * step_size
        table = tile_band(band_ref, first_row, win)
        back = back_ref[...].reshape(table.shape[1], crop_width)
        grad = jnp.dot(table, back, preferred_element_type=jnp.float32)
        columns = pl.ds(col_start, win.columns)
        pad = jnp.zeros((tile_rows, win.columns - crop_width), jnp.float32)
        for part in range(2):
            piece = grad[part * tile_rows : (part + 1) * tile_rows] * weight
            piece = pltpu.roll(jnp.concatenate([piece, pad], axis=1), left - col_start, 1)
            out_ref[part, :, columns] = out_ref[part, :, columns] - piece


def backward_kernel(meta_ref, pupil_ref, band_ref, spec_ref, *refs, slots, win):
    back_refs, out_ref = refs[:-1], refs[-1]
    out_ref[...] = spec_ref[...]
    for slot, back_ref in zip(slots, back_refs):
        subtract_image(meta_ref, slot, back_ref, pupil_ref, band_ref, out_ref, win)


def backward_grid_kernel(meta_ref, pupil_ref, band_ref, spec_ref, back_ref, out_ref, *, win):
    step = pl.program_id(0)

    @pl.when(step == 0)
    def _():
        out_ref[...] = spec_ref[...]

    subtract_image(meta_ref, step, back_ref, pupil_ref, band_ref, out_ref, win)


def middle_kernel(*refs, terms):
    term_refs, (image_ref, cos_ref, sin_ref, out_ref, mid_ref, resid_ref) = refs[:terms], refs[terms:]
    _, band, crop_width = term_refs[0].shape
    block = min(512, crop_width)
    total = sum(ref[...].astype(jnp.float32) for ref in term_refs)
    mid_ref[...] = total.astype(jnp.bfloat16).reshape(2 * band, crop_width)
    dot = functools.partial(jnp.dot, preferred_element_type=jnp.float32)
    for start in range(0, crop_width, block):
        columns = slice(start, start + block)
        by_cos = dot(mid_ref[...], cos_ref[:, columns])
        by_sin = dot(mid_ref[...], sin_ref[:, columns])
        field_real = by_cos[:band] - by_sin[band:]
        field_imag = by_sin[:band] + by_cos[band:]
        power = field_real * field_real + field_imag * field_imag
        measured = image_ref[0, :, columns].astype(jnp.float32)
        keeping = 1.0 - measured * lax.rsqrt(jnp.maximum(power, 1.0))
        resid_ref[:band, columns] = (field_real * keeping).astype(jnp.bfloat16)
        resid_ref[band:, columns] = (field_imag * keeping).astype(jnp.bfloat16)
    for start in range(0, crop_width, block):
        columns = slice(start, start + block)
        by_cos = dot(resid_ref[...], cos_ref[:, columns])
        by_sin = dot(resid_ref[...], sin_ref[:, columns])
        out_ref[0, :, columns] = (by_cos[:band] + by_sin[band:]).astype(jnp.bfloat16)
        out_ref[1, :, columns] = (by_cos[band:] - by_sin[:band]).astype(jnp.bfloat16)


def params():
    return pltpu.CompilerParams(vmem_limit_bytes=vmem_bytes)


def light():
    return pl.CostEstimate(flops=1024, bytes_accessed=1024, transcendentals=0)


vmem = pl.BlockSpec(memory_space=pltpu.VMEM)
smem = pl.BlockSpec(memory_space=pltpu.SMEM)


def band_type(pupil, band_table, *lead):
    shape = lead + (2, band_table.shape[1] // 2, pupil.shape[1])
    return jax.ShapeDtypeStruct(shape, jnp.bfloat16)


def forward(meta, lows, pupil, band_table, base, count):
    win = Windows(*lows[0][0].shape, pupil.shape[1])
    operands = [meta, pupil, band_table] + [part for low in lows for part in low]
    return pl.pallas_call(
        functools.partial(forward_kernel, base=base, win=win, halves=len(lows)),
        in_specs=[smem] + [vmem] * (len(operands) - 1),
        out_specs=[vmem] * count,
        out_shape=[band_type(pupil, band_table)] * count,
        compiler_params=params(),
        cost_estimate=light(),
        name="forward",
    )(*operands)


def backward(meta, spectrum, pupil, band_table, slots, backs):
    win = Windows(*spectrum.shape[1:], pupil.shape[1])
    return pl.pallas_call(
        functools.partial(backward_kernel, slots=slots, win=win),
        in_specs=[smem] + [vmem] * (3 + len(backs)),
        out_specs=vmem,
        out_shape=jax.ShapeDtypeStruct(spectrum.shape, jnp.float32),
        compiler_params=params(),
        cost_estimate=light(),
        name="backward",
    )(meta, pupil, band_table, spectrum, *backs)


def middle(terms, image, cos_table, sin_table):
    _, band, crop_width = terms[0].shape
    return pl.pallas_call(
        functools.partial(middle_kernel, terms=len(terms)),
        in_specs=[vmem] * (len(terms) + 3),
        out_specs=vmem,
        out_shape=jax.ShapeDtypeStruct((2, band, crop_width), jnp.bfloat16),
        scratch_shapes=[pltpu.VMEM((2 * band, crop_width), jnp.bfloat16)] * 2,
        compiler_params=params(),
        cost_estimate=light(),
        name="middle",
    )(*terms, image, cos_table, sin_table)


def fixed(array):
    return pl.BlockSpec(array.shape, lambda i: (0,) * array.ndim)


def forward_all(meta, low, pupil, band_table):
    win = Windows(*low[0].shape, pupil.shape[1])
    count = meta.shape[1]
    out_type = band_type(pupil, band_table, count)
    return pl.pallas_call(
        functools.partial(forward_grid_kernel, win=win),
        grid=(count,),
        in_specs=[smem] + [fixed(array) for array in (pupil, band_table, *low)],
        out_specs=pl.BlockSpec((1,) + out_type.shape[1:], lambda i: (i, 0, 0, 0)),
        out_shape=out_type,
        compiler_params=params(),
        name="forward_all",
    )(meta, pupil, band_table, *low)


def backward_all(meta, spectrum, pupil, band_table, backs):
    win = Windows(*spectrum.shape[1:], pupil.shape[1])
    return pl.pallas_call(
        functools.partial(backward_grid_kernel, win=win),
        grid=(meta.shape[1],),
        in_specs=[smem]
        + [fixed(array) for array in (pupil, band_table, spectrum)]
        + [pl.BlockSpec((1,) + backs.shape[1:], lambda i: (i, 0, 0, 0))],
        out_specs=fixed(spectrum),
        out_shape=jax.ShapeDtypeStruct(spectrum.shape, jnp.float32),
        compiler_params=params(),
        name="backward_all",
    )(meta, pupil, band_table, spectrum, backs)


def cast_kernel(spec_ref, out_ref):
    out_ref[...] = spec_ref[0].astype(jnp.bfloat16)


def low_part(spectrum, part):
    _, rows, columns = spectrum.shape
    block = columns // 4
    return pl.pallas_call(
        cast_kernel,
        grid=(4,),
        in_specs=[pl.BlockSpec((1, rows, block), lambda i: (part, 0, i))],
        out_specs=pl.BlockSpec((rows, block), lambda i: (0, i)),
        out_shape=jax.ShapeDtypeStruct((rows, columns), jnp.bfloat16),
        compiler_params=params(),
        cost_estimate=light(),
        name="low_part",
    )(spectrum)


def total(*terms):
    return sum(term.astype(jnp.float32) for term in terms).astype(jnp.bfloat16)


def per_device(spectrum, pupil, measured, centre_rows, centre_cols):
    count = lax.axis_size("ty")
    planes = count // 4
    position = lax.axis_index("ty")
    plane = position // 4
    _, tile_rows, slab_columns = spectrum.shape
    crop_width = pupil.shape[0]
    band = measured.shape[1]
    band_start = (crop_width - band) // 2
    cos_table, sin_table = fourier_tables(crop_width)
    chosen_rows = slice(band_start, band_start + band)
    band_table = jnp.asarray(
        np.concatenate([cos_table[:, chosen_rows], sin_table[:, chosen_rows]], axis=1)
    )
    cos_table, sin_table = jnp.asarray(cos_table), jnp.asarray(sin_table)

    half = crop_width // 2

    low = [low_part(spectrum, part) for part in range(2)]

    def image_meta(ids, positions):
        match = ids[:, None] == jnp.arange(count, dtype=jnp.int32)[None, :]
        tops = jnp.sum(jnp.where(match, centre_rows[None, :], 0), axis=1) - half
        lefts = jnp.sum(jnp.where(match, centre_cols[None, :], 0), axis=1) - half
        rows = [place * tile_rows - tops for place in positions]
        return jnp.stack(rows + [lefts]).astype(jnp.int32)

    if planes != 4:
        meta = image_meta(jnp.arange(count, dtype=jnp.int32), [position])
        partial = forward_all(meta, low, pupil, band_table)
        mid = lax.psum_scatter(partial, "ty", scatter_dimension=0, tiled=True)[0]
        back = lax.all_gather(middle([mid], measured, cos_table, sin_table), "ty")
        return backward_all(meta, spectrum, pupil, band_table, back)

    targets = {"far": (3, 3, 0, 0), "next": (2, 2, 1, 1), "beside": (1, 0, 3, 2), "own": (0, 1, 2, 3)}
    own_core = [("far", 2), ("far", 0), ("next", 2), ("next", 0)]
    own_core += [("beside", 2), ("beside", 0), ("own", 2), ("own", 0)]
    slots = {}
    for core in (0, 1):
        for name, y in own_core:
            slots[name, y + core] = len(slots)
    ids = [
        [targets[name][i // 4] * 4 + (i % 4 ^ flip) for (name, flip) in slots]
        for i in range(count)
    ]
    my_ids = lax.dynamic_index_in_dim(jnp.asarray(ids, jnp.int32), position, keepdims=False)
    meta = image_meta(my_ids, [position, position ^ 1])

    def sibling(value):
        return lax.ppermute(value, "ty", [(i, i ^ 1) for i in range(count)])

    def across(value):
        return lax.ppermute(value, "ty", [(i, i ^ 2) for i in range(count)])

    def along(value, plane_pairs):
        pairs = [(4 * a + i, 4 * b + i) for a, b in plane_pairs for i in range(4)]
        return lax.ppermute(value, "ty", pairs)

    inward = [(0, 1), (3, 2)]
    outward = [(1, 0), (2, 3)]
    inner = [(1, 2), (2, 1)]
    together = lax.optimization_barrier

    lows = [low, [sibling(part) for part in low]]
    (far_leaving,) = forward(meta, lows, pupil, band_table, 0, 1)
    far_other = across(far_leaving)
    (
        far_kept,
        next_leaving,
        next_kept,
        beside_leaving,
        beside_kept,
        own_leaving,
        own_kept,
    ) = forward(together((meta, far_leaving))[0], lows, pupil, band_table, 1, 7)
    far_other, far_kept, next_leaving = together((far_other, far_kept, next_leaving))

    from_end = along(total(far_kept, far_other), inward)
    next_other = across(next_leaving)
    from_end, next_other, beside_leaving = together((from_end, next_other, beside_leaving))

    far_inner = along(total(far_kept, far_other, from_end), inner)
    next_inward = along(total(next_kept, next_other), inward)
    beside_other = across(beside_leaving)
    far_inner, next_inward, beside_other, own_leaving = together(
        (far_inner, next_inward, beside_other, own_leaving)
    )

    next_inner = along(total(next_kept, next_other, next_inward), inner)
    beside = along(total(beside_kept, beside_other, far_inner), inward + outward)
    own_other = across(own_leaving)
    terms = [own_kept, own_other, next_inner, beside]
    back = middle(terms, measured, cos_table, sin_table)

    def apply(result, pieces):
        names, values = zip(*pieces)
        return backward(
            meta, result, pupil, band_table, [slots[name] for name in names], list(values)
        )

    from_beside = along(back, inward + outward)
    from_inner = along(back, inner)
    other = across(back)
    twin = sibling(back)
    from_beside, from_inner, other, twin, back = together(
        (from_beside, from_inner, other, twin, back)
    )

    far_inner = along(from_beside, inner)
    next_outward = along(from_inner, outward)
    beside_other = across(from_beside)
    beside_twin, other_twin = sibling(from_beside), sibling(other)
    result = apply(
        spectrum,
        [(("own", 0), back), (("own", 1), twin), (("beside", 0), from_beside), (("own", 2), other)],
    )
    far_inner, next_outward, beside_other, beside_twin, other_twin, result = together(
        (far_inner, next_outward, beside_other, beside_twin, other_twin, result)
    )

    at_ends = (plane == 0) | (plane == 3)
    far_outward = along(far_inner, outward)
    from_next = jnp.where(at_ends, next_outward, from_inner)
    next_other = across(from_next)
    next_twin, beside_other_twin = sibling(from_next), sibling(beside_other)
    result = apply(
        result,
        [
            (("beside", 1), beside_twin),
            (("own", 3), other_twin),
            (("next", 0), from_next),
            (("beside", 2), beside_other),
        ],
    )
    far_outward, next_other, next_twin, beside_other_twin, result = together(
        (far_outward, next_other, next_twin, beside_other_twin, result)
    )

    from_far = jnp.where(at_ends, far_outward, far_inner)
    far_other = across(from_far)
    far_twin, next_other_twin = sibling(from_far), sibling(next_other)
    result = apply(
        result,
        [
            (("next", 1), next_twin),
            (("beside", 3), beside_other_twin),
            (("far", 0), from_far),
            (("next", 2), next_other),
        ],
    )
    far_other, far_twin, next_other_twin, result = together(
        (far_other, far_twin, next_other_twin, result)
    )
    return apply(
        result,
        [
            (("far", 1), far_twin),
            (("next", 3), next_other_twin),
            (("far", 2), far_other),
            (("far", 3), sibling(far_other)),
        ],
    )


def solution(mesh):
    return jax.shard_map(
        per_device,
        mesh=mesh,
        in_specs=(
            P(None, ("groups", "ty"), None),
            P(),
            P(("groups", "ty"), None, None),
            P("groups"),
            P("groups"),
        ),
        out_specs=P(None, ("groups", "ty"), None),
        check_vma=False,
    )
```

profile of v0, /device:TPU:11, one launch (start us, length us, event | category | flops | bytes accessed | tf_op | source)
XLA Modules:
  0.0 256.5 jit_solution(15658426994175473822)
XLA Ops:
  0.0 3.4 %copy-done = f32[2,128,8192]{2,1,0:T(8,128)S(1)} copy-done((f32[2,128,8192]{2,1,0:T(8,128)S(1)}, f32[2,128,8192]{2,1,0:T(8,128)}, u32[]{:S(2)}) %copy-start) | copy-done | bytes 8388632
  3.4 2.1 low_part.3.refs_1_
  5.5 0.7 collective-permute-start.1
  6.3 2.1 low_part.2.refs_0_
  8.4 0.7 dynamic-slice_bitcast_fusion
  9.3 1.1 collective-permute-done.1.refs_3_
  10.4 3.0 %collective-permute-done.refs_2_ = bf16[128,8192]{1,0:T(8,128)(2,1)} collective-permute-done((bf16[128,8192]{1,0:T(8,128)(2,1)}, bf16[128,8192]{1,0:T(8,128)(2,1)}, u32[]{:S(2)}, u32[]{:S(2)}) %collective-permute-start) | collective-permute-done | bytes 2097184 | tf_op jit(solution)/shard_map/ppermute | solution.py:352
  13.4 5.5 %forward.2 = bf16[2,256,1024]{2,1,0:T(8,128)(2,1)S(1)} custom-call(s32[3,16]{1,0:T(4,128)S(1)} %pad_add_fusion.meta_ref, bf16[1024,1024]{1,0:T(8,128)(2,1)S(1)} %copy-done.1, bf16[1024,512]{1,0:T(8,128)(2,1)S(1)} %copy-done.2, bf16[128,8192]{1,0:T(8,128)(2,1)} %low_part.2.refs_0_, bf16[128,8192]{1,0:T(8,128)(2,1)} %low_part.3.refs_1_, ...), custom_call_target="tpu_custom_call" | custom-call | flops 1024 | bytes 1024 | tf_op jit(solution)/shard_map/forward/pallas_call | solution.py:208
  18.9 1.3 collective-permute-start.2
  20.2 14.4 %forward.3 = (bf16[2,256,1024]{2,1,0:T(8,128)(2,1)S(1)}, bf16[2,256,1024]{2,1,0:T(8,128)(2,1)S(1)}, bf16[2,256,1024]{2,1,0:T(8,128)(2,1)S(1)}, bf16[2,256,1024]{...) custom-call(s32[3,16]{1,0:T(4,128)S(1)} %pad_add_fusion.meta_ref, ...), custom_call_target="tpu_custom_call" | custom-call | flops 1024 | bytes 1024 | tf_op jit(solution)/shard_map/forward/pallas_call | solution.py:208
  34.6 9.2 %collective-permute-done.2 = bf16[2,256,1024]{2,1,0:T(8,128)(2,1)S(1)} collective-permute-done((bf16[2,256,1024]{2,1,0:T(8,128)(2,1)S(1)}, bf16[2,256,1024]{2,1,0:T(8,128)(2,1)S(1)}, u32[]{:S(2)}, u32[]{:S(2)}) %collective-permute-start.2) | collective-permute-done | bytes 1048608 | tf_op jit(solution)/shard_map/ppermute | solution.py:355
  43.9 0.4 fusion
  44.3 1.3 collective-permute-start.3
  45.6 0.7 collective-permute-start.4
  46.3 23.9 %collective-permute-done.3 = bf16[2,256,1024]{2,1,0:T(8,128)(2,1)S(1)} collective-permute-done((bf16[2,256,1024]{2,1,0:T(8,128)(2,1)S(1)}, bf16[2,256,1024]{2,1,0:T(8,128)(2,1)S(1)}, u32[]{:S(2)}, u32[]{:S(2)}) %collective-permute-start.3) | collective-permute-done | bytes 1048608 | tf_op jit(solution)/shard_map/ppermute | solution.py:359
  70.2 0.6 add_convert_fusion.2
  70.9 0.4 fusion.1
  71.3 1.3 collective-permute-start.6
  72.6 2.1 collective-permute-start.5
  74.7 1.3 collective-permute-start.7
  76.0 20.2 %collective-permute-done.6 = bf16[2,256,1024]{2,1,0:T(8,128)(2,1)S(1)} collective-permute-done((bf16[2,256,1024]{2,1,0:T(8,128)(2,1)S(1)}, bf16[2,256,1024]{2,1,0:T(8,128)(2,1)S(1)}, u32[]{:S(2)}, u32[]{:S(2)}) %collective-permute-start.6) | collective-permute-done | bytes 1048608 | tf_op jit(solution)/shard_map/ppermute | solution.py:359
  96.3 1.3 collective-permute-done.5
  97.6 0.6 add_convert_fusion.1
  98.2 3.4 %collective-permute-start.9 = (bf16[2,256,1024]{2,1,0:T(8,128)(2,1)S(1)}, bf16[2,256,1024]{2,1,0:T(8,128)(2,1)S(1)}, u32[]{:S(2)}, u32[]{:S(2)}) collective-permute-start(bf16[2,256,1024]{2,1,0:T(8,128)(2,1)S(1)} %add_convert_fusion.1), channel_id=1, source_target_pairs={{4,8},{5,9},{6,10},{7,11},{8,4},{9,5},{10,6},{11,7},{20,24},{21,25... | collective-permute-start | bytes 3145736 | tf_op jit(solution)/shard_map/ppermute | solution.py:359
  101.7 0.6 add_convert_fusion
  102.4 19.6 %collective-permute-done.9.refs_2_ = bf16[2,256,1024]{2,1,0:T(8,128)(2,1)S(1)} collective-permute-done((bf16[2,256,1024]{2,1,0:T(8,128)(2,1)S(1)}, bf16[2,256,1024]{2,1,0:T(8,128)(2,1)S(1)}, u32[]{:S(2)}, u32[]{:S(2)}) %collective-permute-start.9) | collective-permute-done | bytes 1048608 | tf_op jit(solution)/shard_map/ppermute | solution.py:359
  122.0 1.3 collective-permute-done.8.refs_1_
  123.3 0.4 collective-permute-done.10.refs_3_
  123.7 4.9 %middle.1.refs_0_ = bf16[2,256,1024]{2,1,0:T(8,128)(2,1)S(1)} custom-call(bf16[2,256,1024]{2,1,0:T(8,128)(2,1)S(1)} %get-tuple-element.44.refs_0_, bf16[2,256,1024]{2,1,0:T(8,128)(2,1)S(1)} %collective-permute-done.8.refs_1_, bf16[2,256,1024]{2,1,0:T(8,128)(2,1)S(1)} %collective-permute-done.9.refs_2_, ...), custom_call_target="tpu_custom_call" | custom-call | flops 1024 | bytes 1024 | tf_op jit(solution)/shard_map/middle/pallas_call | solution.py:234
  128.6 4.3 %collective-permute-start.14 = (bf16[2,256,1024]{2,1,0:T(8,128)(2,1)S(1)}, bf16[2,256,1024]{2,1,0:T(8,128)(2,1)S(1)}, u32[]{:S(2)}, u32[]{:S(2)}) collective-permute-start(bf16[2,256,1024]{2,1,0:T(8,128)(2,1)S(1)} %middle.1.refs_0_), channel_id=1, source_target_pairs={{0,1},{1,0},{2,3},{3,2},{4,5},{5,4},{6,7},{7,6},{8,9},{9,8},{10,11... | collective-permute-start | bytes 3145736 | tf_op jit(solution)/shard_map/ppermute | solution.py:352
  132.9 1.4 collective-permute-start.13
  134.4 2.1 collective-permute-start.12
  136.6 1.0 copy-done.5
  137.5 1.0 copy-done.9
  138.5 19.3 %collective-permute-done.13.refs_3_ = bf16[2,256,1024]{2,1,0:T(8,128)(2,1)} collective-permute-done((bf16[2,256,1024]{2,1,0:T(8,128)(2,1)S(1)}, bf16[2,256,1024]{2,1,0:T(8,128)(2,1)}, u32[]{:S(2)}, u32[]{:S(2)}) %collective-permute-start.13) | collective-permute-done | bytes 1048608 | tf_op jit(solution)/shard_map/ppermute | solution.py:355
  157.8 3.0 %collective-permute-done.12 = bf16[2,256,1024]{2,1,0:T(8,128)(2,1)} collective-permute-done((bf16[2,256,1024]{2,1,0:T(8,128)(2,1)S(1)}, bf16[2,256,1024]{2,1,0:T(8,128)(2,1)}, u32[]{:S(2)}, u32[]{:S(2)}) %collective-permute-start.12) | collective-permute-done | bytes 1048608 | tf_op jit(solution)/shard_map/ppermute | solution.py:359
  160.8 3.2 %collective-permute-start.16 = (bf16[2,256,1024]{2,1,0:T(8,128)(2,1)}, bf16[2,256,1024]{2,1,0:T(8,128)(2,1)}, u32[]{:S(2)}, u32[]{:S(2)}) collective-permute-start(bf16[2,256,1024]{2,1,0:T(8,128)(2,1)} %collective-permute-done.12), channel_id=1, source_target_pairs={{4,0},{5,1},{6,2},{7,3},{8,12},{9,13},{10,14},{11,15},{20,16},{21,... | collective-permute-start | bytes 3145736 | tf_op jit(solution)/shard_map/ppermute | solution.py:359
  164.0 1.5 collective-permute-start.19
  165.4 0.7 collective-permute-start.17
  166.2 2.5 collective-permute-start.15
  168.7 1.2 copy-done.6
  169.9 1.2 copy-done.10
  171.1 6.2 %backward.4.spec_ref = f32[2,128,8192]{2,1,0:T(8,128)S(1)} custom-call(s32[3,16]{1,0:T(4,128)S(1)} %pad_add_fusion.meta_ref, bf16[1024,1024]{1,0:T(8,128)(2,1)S(1)} %copy-done.1, bf16[1024,512]{1,0:T(8,128)(2,1)S(1)} %copy-done.2, f32[2,128,8192]{2,1,0:T(8,128)} %spec_ref.5, bf16[2,256,1024]{2,1,0:T(8,128)(2,1)S(1)} %copy-done.6, ...), custom_call_target="tpu_custom_call" | custom-call | flops 1024 | bytes 1024 | tf_op jit(solution)/shard_map/backward/pallas_call | solution.py:221
  177.3 3.4 %copy-done.3 = f32[2,128,8192]{2,1,0:T(8,128)} copy-done((f32[2,128,8192]{2,1,0:T(8,128)}, f32[2,128,8192]{2,1,0:T(8,128)S(1)}, u32[]{:S(2)}) %copy-start.3) | copy-done | bytes 8388632
  180.7 3.9 %collective-permute-done.16 = bf16[2,256,1024]{2,1,0:T(8,128)(2,1)} collective-permute-done((bf16[2,256,1024]{2,1,0:T(8,128)(2,1)}, bf16[2,256,1024]{2,1,0:T(8,128)(2,1)}, u32[]{:S(2)}, u32[]{:S(2)}) %collective-permute-start.16) | collective-permute-done | bytes 1048608 | tf_op jit(solution)/shard_map/ppermute | solution.py:359
  184.5 5.4 %collective-permute-done.17.refs_3_ = bf16[2,256,1024]{2,1,0:T(8,128)(2,1)} collective-permute-done((bf16[2,256,1024]{2,1,0:T(8,128)(2,1)}, bf16[2,256,1024]{2,1,0:T(8,128)(2,1)}, u32[]{:S(2)}, u32[]{:S(2)}) %collective-permute-start.17) | collective-permute-done | bytes 1048608 | tf_op jit(solution)/shard_map/ppermute | solution.py:355
  190.0 2.3 collective-permute-done.15
  192.3 1.3 broadcast_select_fusion.1.refs_2_
  193.6 1.7 collective-permute-start.22
  195.3 0.7 collective-permute-start.21
  196.1 1.3 collective-permute-start.20
  197.4 0.4 collective-permute-start.23
  197.8 7.5 %backward.5.spec_ref = f32[2,128,8192]{2,1,0:T(8,128)S(1)} custom-call(s32[3,16]{1,0:T(4,128)S(1)} %pad_add_fusion.meta_ref, bf16[1024,1024]{1,0:T(8,128)(2,1)S(1)} %copy-done.1, bf16[1024,512]{1,0:T(8,128)(2,1)S(1)} %copy-done.2, f32[2,128,8192]{2,1,0:T(8,128)} %copy-done.3, bf16[2,256,1024]{2,1,0:T(8,128)(2,1)} %collective-permute-done.18.refs_0_, ...), custom_call_target="tpu_custom_call" | custom-call | flops 1024 | bytes 1024 | tf_op jit(solution)/shard_map/backward/pallas_call | solution.py:221
  205.4 3.4 %copy-done.4 = f32[2,128,8192]{2,1,0:T(8,128)} copy-done((f32[2,128,8192]{2,1,0:T(8,128)}, f32[2,128,8192]{2,1,0:T(8,128)S(1)}, u32[]{:S(2)}) %copy-start.4) | copy-done | bytes 8388632
  208.7 11.3 %collective-permute-done.21.refs_3_ = bf16[2,256,1024]{2,1,0:T(8,128)(2,1)S(1)} collective-permute-done((bf16[2,256,1024]{2,1,0:T(8,128)(2,1)S(1)}, bf16[2,256,1024]{2,1,0:T(8,128)(2,1)S(1)}, u32[]{:S(2)}, u32[]{:S(2)}) %collective-permute-start.21) | collective-permute-done | bytes 1048608 | tf_op jit(solution)/shard_map/ppermute | solution.py:355
  220.2 1.3 broadcast_select_fusion.refs_2_
  221.5 0.9 collective-permute-start.25
  222.5 0.8 collective-permute-start.24
  223.2 0.3 collective-permute-start.26
  223.6 6.4 %backward.6.spec_ref = f32[2,128,8192]{2,1,0:T(8,128)S(1)} custom-call(s32[3,16]{1,0:T(4,128)S(1)} %pad_add_fusion.meta_ref, bf16[1024,1024]{1,0:T(8,128)(2,1)S(1)} %copy-done.1, bf16[1024,512]{1,0:T(8,128)(2,1)S(1)} %copy-done.2, f32[2,128,8192]{2,1,0:T(8,128)} %copy-done.4, bf16[2,256,1024]{2,1,0:T(8,128)(2,1)S(1)} %collective-permute-done.22.refs_0_, ...), custom_call_target="tpu_custom_call" | custom-call | flops 1024 | bytes 1024 | tf_op jit(solution)/shard_map/backward/pallas_call | solution.py:221
  230.0 17.2 %collective-permute-done.24.refs_2_ = bf16[2,256,1024]{2,1,0:T(8,128)(2,1)S(1)} collective-permute-done((bf16[2,256,1024]{2,1,0:T(8,128)(2,1)S(1)}, bf16[2,256,1024]{2,1,0:T(8,128)(2,1)S(1)}, u32[]{:S(2)}, u32[]{:S(2)}) %collective-permute-start.24) | collective-permute-done | bytes 1048608 | tf_op jit(solution)/shard_map/ppermute | solution.py:355
  247.2 0.9 collective-permute-start.27
  248.0 2.3 collective-permute-done.27.refs_3_
  250.3 6.2 %backward.7 = f32[2,128,8192]{2,1,0:T(8,128)} custom-call(s32[3,16]{1,0:T(4,128)S(1)} %pad_add_fusion.meta_ref, bf16[1024,1024]{1,0:T(8,128)(2,1)S(1)} %copy-done.1, bf16[1024,512]{1,0:T(8,128)(2,1)S(1)} %copy-done.2, f32[2,128,8192]{2,1,0:T(8,128)S(1)} %backward.6.spec_ref, bf16[2,256,1024]{2,1,0:T(8,128)(2,1)S(1)} %collective-permute-done.25.refs_0_, ...), custom_call_target="tpu_custom_call" | custom-call | flops 1024 | bytes 1024 | tf_op jit(solution)/shard_map/backward/pallas_call | solution.py:221
  (41 shorter events, 0.6 us)
Async XLA Ops:
  0.0 3.4 %copy-start = (f32[2,128,8192]{2,1,0:T(8,128)S(1)}, f32[2,128,8192]{2,1,0:T(8,128)}, u32[]{:S(2)}) copy-start(f32[2,128,8192]{2,1,0:T(8,128)} %spec_ref.5) | copy-start | bytes 25165828
  5.5 3.6 %copy-start.12 = (s32[16]{0:T(128)S(1)}, s32[16]{0:T(128)}, u32[]{:S(2)}) copy-start(s32[16]{0:T(128)} %param.12) | copy-start | bytes 196
  5.5 3.6 %copy-start.13 = (s32[16]{0:T(128)S(1)}, s32[16]{0:T(128)}, u32[]{:S(2)}) copy-start(s32[16]{0:T(128)} %param.13) | copy-start | bytes 196
  5.5 7.9 %copy-start.1 = (bf16[1024,1024]{1,0:T(8,128)(2,1)S(1)}, bf16[1024,1024]{1,0:T(8,128)(2,1)}, u32[]{:S(2)}) copy-start(bf16[1024,1024]{1,0:T(8,128)(2,1)} %pupil_ref.11) | copy-start | bytes 6291460
  5.5 7.9 %copy-start.2 = (bf16[1024,512]{1,0:T(8,128)(2,1)S(1)}, bf16[1024,512]{1,0:T(8,128)(2,1)}, u32[]{:S(2)}) copy-start(bf16[1024,512]{1,0:T(8,128)(2,1)} %constant.42.clone.band_ref) | copy-start | bytes 3145732
  5.5 4.9 %collective-permute-start.1 = (bf16[128,8192]{1,0:T(8,128)(2,1)}, bf16[128,8192]{1,0:T(8,128)(2,1)}, u32[]{:S(2)}, u32[]{:S(2)}) collective-permute-start(bf16[128,8192]{1,0:T(8,128)(2,1)} %low_part.3.refs_1_), channel_id=1, source_target_pairs={{0,1},{1,0},{2,3},{3,2},{4,5},{5,4},{6,7},{7,6},{8,9},{9,8},{10,11... | collective-permute-start | bytes 6291464 | tf_op jit(solution)/shard_map/ppermute | solution.py:352
  8.3 5.0 %collective-permute-start = (bf16[128,8192]{1,0:T(8,128)(2,1)}, bf16[128,8192]{1,0:T(8,128)(2,1)}, u32[]{:S(2)}, u32[]{:S(2)}) collective-permute-start(bf16[128,8192]{1,0:T(8,128)(2,1)} %low_part.2.refs_0_), channel_id=1, source_target_pairs={{0,1},{1,0},{2,3},{3,2},{4,5},{5,4},{6,7},{7,6},{8,9},{9,8},{10,11... | collective-permute-start | bytes 6291464 | tf_op jit(solution)/shard_map/ppermute | solution.py:352
  18.9 25.0 %collective-permute-start.2 = (bf16[2,256,1024]{2,1,0:T(8,128)(2,1)S(1)}, bf16[2,256,1024]{2,1,0:T(8,128)(2,1)S(1)}, u32[]{:S(2)}, u32[]{:S(2)}) collective-permute-start(bf16[2,256,1024]{2,1,0:T(8,128)(2,1)S(1)} %forward.2), channel_id=1, source_target_pairs={{0,2},{1,3},{2,0},{3,1},{4,6},{5,7},{6,4},{7,5},{8,10},{9,11},{10,... | collective-permute-start | bytes 3145736 | tf_op jit(solution)/shard_map/ppermute | solution.py:355
  44.3 25.9 %collective-permute-start.3 = (bf16[2,256,1024]{2,1,0:T(8,128)(2,1)S(1)}, bf16[2,256,1024]{2,1,0:T(8,128)(2,1)S(1)}, u32[]{:S(2)}, u32[]{:S(2)}) collective-permute-start(bf16[2,256,1024]{2,1,0:T(8,128)(2,1)S(1)} %fusion), channel_id=1, source_target_pairs={{0,4},{1,5},{2,6},{3,7},{12,8},{13,9},{14,10},{15,11},{16,20},{17,... | collective-permute-start | bytes 3145736 | tf_op jit(solution)/shard_map/ppermute | solution.py:359
  45.6 24.6 %collective-permute-start.4 = (bf16[2,256,1024]{2,1,0:T(8,128)(2,1)S(1)}, bf16[2,256,1024]{2,1,0:T(8,128)(2,1)S(1)}, u32[]{:S(2)}, u32[]{:S(2)}) collective-permute-start(bf16[2,256,1024]{2,1,0:T(8,128)(2,1)S(1)} %get-tuple-element.49), channel_id=1, source_target_pairs={{0,2},{1,3},{2,0},{3,1},{4,6},{5,7},{6,4},{7,5},{8,10},{9,11},{10,... | collective-permute-start | bytes 3145736 | tf_op jit(solution)/shard_map/ppermute | solution.py:355
  71.3 25.0 %collective-permute-start.6 = (bf16[2,256,1024]{2,1,0:T(8,128)(2,1)S(1)}, bf16[2,256,1024]{2,1,0:T(8,128)(2,1)S(1)}, u32[]{:S(2)}, u32[]{:S(2)}) collective-permute-start(bf16[2,256,1024]{2,1,0:T(8,128)(2,1)S(1)} %fusion.1), channel_id=1, source_target_pairs={{0,4},{1,5},{2,6},{3,7},{12,8},{13,9},{14,10},{15,11},{16,20},{17,... | collective-permute-start | bytes 3145736 | tf_op jit(solution)/shard_map/ppermute | solution.py:359
  72.6 25.0 %collective-permute-start.5 = (bf16[2,256,1024]{2,1,0:T(8,128)(2,1)S(1)}, bf16[2,256,1024]{2,1,0:T(8,128)(2,1)S(1)}, u32[]{:S(2)}, u32[]{:S(2)}) collective-permute-start(bf16[2,256,1024]{2,1,0:T(8,128)(2,1)S(1)} %add_convert_fusion.2), channel_id=1, source_target_pairs={{4,8},{5,9},{6,10},{7,11},{8,4},{9,5},{10,6},{11,7},{20,24},{21,25... | collective-permute-start | bytes 3145736 | tf_op jit(solution)/shard_map/ppermute | solution.py:359
  74.7 22.9 %collective-permute-start.7 = (bf16[2,256,1024]{2,1,0:T(8,128)(2,1)S(1)}, bf16[2,256,1024]{2,1,0:T(8,128)(2,1)S(1)}, u32[]{:S(2)}, u32[]{:S(2)}) collective-permute-start(bf16[2,256,1024]{2,1,0:T(8,128)(2,1)S(1)} %get-tuple-element.54), channel_id=1, source_target_pairs={{0,2},{1,3},{2,0},{3,1},{4,6},{5,7},{6,4},{7,5},{8,10},{9,11},{10,... | collective-permute-start | bytes 3145736 | tf_op jit(solution)/shard_map/ppermute | solution.py:355
  97.6 26.2 %copy-start.11 = (bf16[1,256,1024]{2,1,0:T(8,128)(2,1)S(1)}, bf16[1,256,1024]{2,1,0:T(8,128)(2,1)}, u32[]{:S(2)}) copy-start(bf16[1,256,1024]{2,1,0:T(8,128)(2,1)} %refs_4_.1) | copy-start | bytes 1572868
  98.2 23.8 %collective-permute-start.9 = (bf16[2,256,1024]{2,1,0:T(8,128)(2,1)S(1)}, bf16[2,256,1024]{2,1,0:T(8,128)(2,1)S(1)}, u32[]{:S(2)}, u32[]{:S(2)}) collective-permute-start(bf16[2,256,1024]{2,1,0:T(8,128)(2,1)S(1)} %add_convert_fusion.1), channel_id=1, source_target_pairs={{4,8},{5,9},{6,10},{7,11},{8,4},{9,5},{10,6},{11,7},{20,24},{21,25... | collective-permute-start | bytes 3145736 | tf_op jit(solution)/shard_map/ppermute | solution.py:359
  101.6 21.7 %collective-permute-start.8 = (bf16[2,256,1024]{2,1,0:T(8,128)(2,1)S(1)}, bf16[2,256,1024]{2,1,0:T(8,128)(2,1)S(1)}, u32[]{:S(2)}, u32[]{:S(2)}) collective-permute-start(bf16[2,256,1024]{2,1,0:T(8,128)(2,1)S(1)} %get-tuple-element.56), channel_id=1, source_target_pairs={{0,2},{1,3},{2,0},{3,1},{4,6},{5,7},{6,4},{7,5},{8,10},{9,11},{10,... | collective-permute-start | bytes 3145736 | tf_op jit(solution)/shard_map/ppermute | solution.py:355
  101.7 22.1 %copy-start.7 = (bf16[1024,1024]{1,0:T(8,128)(2,1)S(1)}, bf16[1024,1024]{1,0:T(8,128)(2,1)}, u32[]{:S(2)}) copy-start(bf16[1024,1024]{1,0:T(8,128)(2,1)} %constant.44.clone.refs_6_) | copy-start | bytes 6291460
  101.7 22.1 %copy-start.8 = (bf16[1024,1024]{1,0:T(8,128)(2,1)S(1)}, bf16[1024,1024]{1,0:T(8,128)(2,1)}, u32[]{:S(2)}) copy-start(bf16[1024,1024]{1,0:T(8,128)(2,1)} %constant.43.clone.refs_5_) | copy-start | bytes 6291460
  102.3 21.4 %collective-permute-start.10 = (bf16[2,256,1024]{2,1,0:T(8,128)(2,1)S(1)}, bf16[2,256,1024]{2,1,0:T(8,128)(2,1)S(1)}, u32[]{:S(2)}, u32[]{:S(2)}) collective-permute-start(bf16[2,256,1024]{2,1,0:T(8,128)(2,1)S(1)} %add_convert_fusion), channel_id=1, source_target_pairs={{0,4},{1,5},{2,6},{3,7},{12,8},{13,9},{14,10},{15,11},{4,0},{5,1},... | collective-permute-start | bytes 3145736 | tf_op jit(solution)/shard_map/ppermute | solution.py:359
  128.6 8.9 %collective-permute-start.14 = (bf16[2,256,1024]{2,1,0:T(8,128)(2,1)S(1)}, bf16[2,256,1024]{2,1,0:T(8,128)(2,1)S(1)}, u32[]{:S(2)}, u32[]{:S(2)}) collective-permute-start(bf16[2,256,1024]{2,1,0:T(8,128)(2,1)S(1)} %middle.1.refs_0_), channel_id=1, source_target_pairs={{0,1},{1,0},{2,3},{3,2},{4,5},{5,4},{6,7},{7,6},{8,9},{9,8},{10,11... | collective-permute-start | bytes 3145736 | tf_op jit(solution)/shard_map/ppermute | solution.py:352
  132.9 24.8 %collective-permute-start.13 = (bf16[2,256,1024]{2,1,0:T(8,128)(2,1)S(1)}, bf16[2,256,1024]{2,1,0:T(8,128)(2,1)}, u32[]{:S(2)}, u32[]{:S(2)}) collective-permute-start(bf16[2,256,1024]{2,1,0:T(8,128)(2,1)S(1)} %middle.1.refs_0_), channel_id=1, source_target_pairs={{0,2},{1,3},{2,0},{3,1},{4,6},{5,7},{6,4},{7,5},{8,10},{9,11},{10,... | collective-permute-start | bytes 3145736 | tf_op jit(solution)/shard_map/ppermute | solution.py:355
  134.4 26.4 %collective-permute-start.12 = (bf16[2,256,1024]{2,1,0:T(8,128)(2,1)S(1)}, bf16[2,256,1024]{2,1,0:T(8,128)(2,1)}, u32[]{:S(2)}, u32[]{:S(2)}) collective-permute-start(bf16[2,256,1024]{2,1,0:T(8,128)(2,1)S(1)} %middle.1.refs_0_), channel_id=1, source_target_pairs={{4,8},{5,9},{6,10},{7,11},{8,4},{9,5},{10,6},{11,7},{20,24},{21,25... | collective-permute-start | bytes 3145736 | tf_op jit(solution)/shard_map/ppermute | solution.py:359
  136.5 24.3 %collective-permute-start.11 = (bf16[2,256,1024]{2,1,0:T(8,128)(2,1)S(1)}, bf16[2,256,1024]{2,1,0:T(8,128)(2,1)}, u32[]{:S(2)}, u32[]{:S(2)}) collective-permute-start(bf16[2,256,1024]{2,1,0:T(8,128)(2,1)S(1)} %middle.1.refs_0_), channel_id=1, source_target_pairs={{0,4},{1,5},{2,6},{3,7},{12,8},{13,9},{14,10},{15,11},{4,0},{5,1},... | collective-permute-start | bytes 3145736 | tf_op jit(solution)/shard_map/ppermute | solution.py:359
  136.6 1.0 copy-start.5
  137.5 1.0 copy-start.9
  160.8 23.8 %collective-permute-start.16 = (bf16[2,256,1024]{2,1,0:T(8,128)(2,1)}, bf16[2,256,1024]{2,1,0:T(8,128)(2,1)}, u32[]{:S(2)}, u32[]{:S(2)}) collective-permute-start(bf16[2,256,1024]{2,1,0:T(8,128)(2,1)} %collective-permute-done.12), channel_id=1, source_target_pairs={{4,0},{5,1},{6,2},{7,3},{8,12},{9,13},{10,14},{11,15},{20,16},{21,... | collective-permute-start | bytes 3145736 | tf_op jit(solution)/shard_map/ppermute | solution.py:359
  164.0 20.6 %collective-permute-start.19 = (bf16[2,256,1024]{2,1,0:T(8,128)(2,1)}, bf16[2,256,1024]{2,1,0:T(8,128)(2,1)}, u32[]{:S(2)}, u32[]{:S(2)}) collective-permute-start(bf16[2,256,1024]{2,1,0:T(8,128)(2,1)} %collective-permute-done.13.refs_3_), channel_id=1, source_target_pairs={{0,1},{1,0},{2,3},{3,2},{4,5},{5,4},{6,7},{7,6},{8,9},{9,8},{10,11... | collective-permute-start | bytes 3145736 | tf_op jit(solution)/shard_map/ppermute | solution.py:352
  165.4 19.1 %collective-permute-start.18 = (bf16[2,256,1024]{2,1,0:T(8,128)(2,1)}, bf16[2,256,1024]{2,1,0:T(8,128)(2,1)}, u32[]{:S(2)}, u32[]{:S(2)}) collective-permute-start(bf16[2,256,1024]{2,1,0:T(8,128)(2,1)} %collective-permute-done.11.refs_2_), channel_id=1, source_target_pairs={{0,1},{1,0},{2,3},{3,2},{4,5},{5,4},{6,7},{7,6},{8,9},{9,8},{10,11... | collective-permute-start | bytes 3145736 | tf_op jit(solution)/shard_map/ppermute | solution.py:352
  165.4 24.5 %collective-permute-start.17 = (bf16[2,256,1024]{2,1,0:T(8,128)(2,1)}, bf16[2,256,1024]{2,1,0:T(8,128)(2,1)}, u32[]{:S(2)}, u32[]{:S(2)}) collective-permute-start(bf16[2,256,1024]{2,1,0:T(8,128)(2,1)} %collective-permute-done.11.refs_2_), channel_id=1, source_target_pairs={{0,2},{1,3},{2,0},{3,1},{4,6},{5,7},{6,4},{7,5},{8,10},{9,11},{10,... | collective-permute-start | bytes 3145736 | tf_op jit(solution)/shard_map/ppermute | solution.py:355
  166.2 26.1 %collective-permute-start.15 = (bf16[2,256,1024]{2,1,0:T(8,128)(2,1)}, bf16[2,256,1024]{2,1,0:T(8,128)(2,1)}, u32[]{:S(2)}, u32[]{:S(2)}) collective-permute-start(bf16[2,256,1024]{2,1,0:T(8,128)(2,1)} %collective-permute-done.11.refs_2_), channel_id=1, source_target_pairs={{4,8},{5,9},{6,10},{7,11},{8,4},{9,5},{10,6},{11,7},{20,24},{21,25... | collective-permute-start | bytes 3145736 | tf_op jit(solution)/shard_map/ppermute | solution.py:359
  168.7 1.2 copy-start.6
  169.9 1.2 copy-start.10
  177.3 3.4 %copy-start.3 = (f32[2,128,8192]{2,1,0:T(8,128)}, f32[2,128,8192]{2,1,0:T(8,128)S(1)}, u32[]{:S(2)}) copy-start(f32[2,128,8192]{2,1,0:T(8,128)S(1)} %backward.4.spec_ref) | copy-start | bytes 25165828
  193.6 15.1 %collective-permute-start.22 = (bf16[2,256,1024]{2,1,0:T(8,128)(2,1)S(1)}, bf16[2,256,1024]{2,1,0:T(8,128)(2,1)S(1)}, u32[]{:S(2)}, u32[]{:S(2)}) collective-permute-start(bf16[2,256,1024]{2,1,0:T(8,128)(2,1)S(1)} %broadcast_select_fusion.1.refs_2_), channel_id=1, source_target_pairs={{0,1},{1,0},{2,3},{3,2},{4,5},{5,4},{6,7},{7,6},{8,9},{9,8},{10,11... | collective-permute-start | bytes 3145736 | tf_op jit(solution)/shard_map/ppermute | solution.py:352
  195.3 24.7 %collective-permute-start.21 = (bf16[2,256,1024]{2,1,0:T(8,128)(2,1)S(1)}, bf16[2,256,1024]{2,1,0:T(8,128)(2,1)S(1)}, u32[]{:S(2)}, u32[]{:S(2)}) collective-permute-start(bf16[2,256,1024]{2,1,0:T(8,128)(2,1)S(1)} %broadcast_select_fusion.1.refs_2_), channel_id=1, source_target_pairs={{0,2},{1,3},{2,0},{3,1},{4,6},{5,7},{6,4},{7,5},{8,10},{9,11},{10,... | collective-permute-start | bytes 3145736 | tf_op jit(solution)/shard_map/ppermute | solution.py:355
  196.1 24.1 %collective-permute-start.20 = (bf16[2,256,1024]{2,1,0:T(8,128)(2,1)}, bf16[2,256,1024]{2,1,0:T(8,128)(2,1)S(1)}, u32[]{:S(2)}, u32[]{:S(2)}) collective-permute-start(bf16[2,256,1024]{2,1,0:T(8,128)(2,1)} %collective-permute-done.15), channel_id=1, source_target_pairs={{4,0},{5,1},{6,2},{7,3},{8,12},{9,13},{10,14},{11,15},{20,16},{21,... | collective-permute-start | bytes 3145736 | tf_op jit(solution)/shard_map/ppermute | solution.py:359
  197.4 22.8 %collective-permute-start.23 = (bf16[2,256,1024]{2,1,0:T(8,128)(2,1)}, bf16[2,256,1024]{2,1,0:T(8,128)(2,1)S(1)}, u32[]{:S(2)}, u32[]{:S(2)}) collective-permute-start(bf16[2,256,1024]{2,1,0:T(8,128)(2,1)} %collective-permute-done.17.refs_3_), channel_id=1, source_target_pairs={{0,1},{1,0},{2,3},{3,2},{4,5},{5,4},{6,7},{7,6},{8,9},{9,8},{10,11... | collective-permute-start | bytes 3145736 | tf_op jit(solution)/shard_map/ppermute | solution.py:352
  205.3 3.4 %copy-start.4 = (f32[2,128,8192]{2,1,0:T(8,128)}, f32[2,128,8192]{2,1,0:T(8,128)S(1)}, u32[]{:S(2)}) copy-start(f32[2,128,8192]{2,1,0:T(8,128)S(1)} %backward.5.spec_ref) | copy-start | bytes 25165828
  221.5 8.5 %collective-permute-start.25 = (bf16[2,256,1024]{2,1,0:T(8,128)(2,1)S(1)}, bf16[2,256,1024]{2,1,0:T(8,128)(2,1)S(1)}, u32[]{:S(2)}, u32[]{:S(2)}) collective-permute-start(bf16[2,256,1024]{2,1,0:T(8,128)(2,1)S(1)} %broadcast_select_fusion.refs_2_), channel_id=1, source_target_pairs={{0,1},{1,0},{2,3},{3,2},{4,5},{5,4},{6,7},{7,6},{8,9},{9,8},{10,11... | collective-permute-start | bytes 3145736 | tf_op jit(solution)/shard_map/ppermute | solution.py:352
  222.5 24.7 %collective-permute-start.24 = (bf16[2,256,1024]{2,1,0:T(8,128)(2,1)S(1)}, bf16[2,256,1024]{2,1,0:T(8,128)(2,1)S(1)}, u32[]{:S(2)}, u32[]{:S(2)}) collective-permute-start(bf16[2,256,1024]{2,1,0:T(8,128)(2,1)S(1)} %broadcast_select_fusion.refs_2_), channel_id=1, source_target_pairs={{0,2},{1,3},{2,0},{3,1},{4,6},{5,7},{6,4},{7,5},{8,10},{9,11},{10,... | collective-permute-start | bytes 3145736 | tf_op jit(solution)/shard_map/ppermute | solution.py:355
  223.2 24.0 %collective-permute-start.26 = (bf16[2,256,1024]{2,1,0:T(8,128)(2,1)S(1)}, bf16[2,256,1024]{2,1,0:T(8,128)(2,1)S(1)}, u32[]{:S(2)}, u32[]{:S(2)}) collective-permute-start(bf16[2,256,1024]{2,1,0:T(8,128)(2,1)S(1)} %collective-permute-done.21.refs_3_), channel_id=1, source_target_pairs={{0,1},{1,0},{2,3},{3,2},{4,5},{5,4},{6,7},{7,6},{8,9},{9,8},{10,11... | collective-permute-start | bytes 3145736 | tf_op jit(solution)/shard_map/ppermute | solution.py:352
  247.2 3.1 %collective-permute-start.27 = (bf16[2,256,1024]{2,1,0:T(8,128)(2,1)S(1)}, bf16[2,256,1024]{2,1,0:T(8,128)(2,1)S(1)}, u32[]{:S(2)}, u32[]{:S(2)}) collective-permute-start(bf16[2,256,1024]{2,1,0:T(8,128)(2,1)S(1)} %collective-permute-done.24.refs_2_), channel_id=1, source_target_pairs={{0,1},{1,0},{2,3},{3,2},{4,5},{5,4},{6,7},{7,6},{8,9},{9,8},{10,11... | collective-permute-start | bytes 3145736 | tf_op jit(solution)/shard_map/ppermute | solution.py:352
where the time goes:
time: 259 us; the launch traced here: 257 us
  waiting for transfers between devices  145 us (56%)
  Pallas kernels  55.3 us (21%)
  starting transfers between devices  35.2 us (14%)
  local copies, waits for them, and re-layouts  15.3 us (6%)
  other arithmetic  5.61 us (2%)
    ppermute x10, waiting for transfers between devices, along(): return lax.ppermute(value, 'ty', pairs)  74.7 us
    ppermute x8, waiting for transfers between devices, across(): return lax.ppermute(value, 'ty', [(i, i ^ 2) for i in range(count)])  63.7 us
    pallas_call x4, Pallas kernels, backward(): pl.pallas_call(functools.partial(backward_kernel, slots=slots, win=win),...  26.3 us
    pallas_call x2, Pallas kernels, forward(): pl.pallas_call(functools.partial(forward_kernel, base=base, win=win, halv...  19.9 us
    ppermute x10, starting transfers between devices, along(): return lax.ppermute(value, 'ty', pairs)  17.3 us
    unnamed x28, local copies, waits for them, and re-layouts  14.6 us
    ppermute x10, starting transfers between devices, sibling(): return lax.ppermute(value, 'ty', [(i, i ^ 1) for i in range(count)])  10.8 us
    ppermute x8, starting transfers between devices, across(): return lax.ppermute(value, 'ty', [(i, i ^ 2) for i in range(count)])  7.14 us
  transfers between devices with their start and end apart: 28, of which 18 were waited for; matrix products, arithmetic and copies ran while one was open for 1% of the time, Pallas kernels for 14%

commit v1 on v0

--- a/solution.py
+++ b/solution.py
@@ -35,22 +35,25 @@
     return jnp.where(inside, rows[: win.tile_rows], 0.0)
 
 
-def tile_band(band_ref, first_row, win):
+def tile_band(band_refs, first_row, win):
     start = win.row(first_row)
-    rows = band_ref[pl.ds(start, win.rows), :].astype(jnp.float32)
-    rows = pltpu.roll(rows, (2 * win.rows + start - first_row) % win.rows, 0)[: win.tile_rows]
-    band = rows.shape[1] // 2
-    turned = jnp.concatenate([-rows[:, band:], rows[:, :band]], axis=1)
-    return jnp.concatenate([rows, turned], axis=0).astype(jnp.bfloat16)
+    tables = []
+    for band_ref in band_refs:
+        rows = band_ref[pl.ds(start, win.rows), :].astype(jnp.float32)
+        rows = pltpu.roll(rows, (2 * win.rows + start - first_row) % win.rows, 0)
+        tables.append(rows[: win.tile_rows].astype(jnp.bfloat16))
+    return jnp.concatenate(tables, axis=0)
 
 
 class Windows:
-    def __init__(self, tile_rows, slab_columns, crop_width):
+    def __init__(self, tile_rows, slab_columns, crop_width, main, side):
         self.tile_rows = tile_rows
         self.crop_width = crop_width
         self.rows = tile_rows + row_tile
         self.columns = crop_width + lane
         self.last_row = crop_width - self.rows
+        self.main = main
+        self.side = side
         self.last_column = slab_columns - self.columns
 
     def row(self, first_row):
@@ -65,17 +68,19 @@
         return (first_row > -self.tile_rows) & (first_row < self.crop_width)
 
 
-def image_band(meta_ref, slot, lows, pupil_ref, band_ref, win, store):
+def image_band(meta_ref, slot, lows, pupil_ref, band_refs, win, store):
     halves = len(lows)
     left = meta_ref[halves, slot]
     first_rows = [meta_ref[half, slot] for half in range(halves)]
     active = functools.reduce(jnp.logical_or, [win.active(row) for row in first_rows])
-    band = band_ref.shape[1] // 2
-    shape = (2, band, win.crop_width)
+
+    def split(band):
+        main = band[: 2 * win.main].reshape(2, win.main, win.crop_width)
+        store(main, band[2 * win.main :].reshape(2, win.side, win.crop_width))
 
     @pl.when(jnp.logical_not(active))
     def _():
-        store(jnp.zeros(shape, jnp.bfloat16))
+        split(jnp.zeros((2 * (win.main + win.side), win.crop_width), jnp.bfloat16))
 
     @pl.when(active)
     def _():
@@ -88,52 +93,72 @@
                 low = low_ref[:, pl.ds(col_start, win.columns)].astype(jnp.float32)
                 low = pltpu.roll(low, shift, 1)[:, : win.crop_width]
                 parts.append((weight * low).astype(jnp.bfloat16))
-            tables.append(tile_band(band_ref, first_row, win))
+            tables.append(tile_band(band_refs, first_row, win))
         mid = lax.dot_general(
             jnp.concatenate(tables, axis=0),
             jnp.concatenate(parts, axis=0),
             (((0,), (0,)), ((), ())),
             preferred_element_type=jnp.float32,
         )
-        store(mid.astype(jnp.bfloat16).reshape(shape))
-
-
-def forward_kernel(meta_ref, pupil_ref, band_ref, *refs, base, win, halves):
-    low_refs, out_refs = refs[: 2 * halves], refs[2 * halves :]
+        split(mid.astype(jnp.bfloat16))
+
+
+def forward_kernel(meta_ref, pupil_ref, plain_ref, turned_ref, *refs, base, count, win, halves):
+    low_refs, out_refs = refs[: 2 * halves], refs[-count - 1 :]
     lows = [low_refs[2 * half : 2 * half + 2] for half in range(halves)]
+    main_refs, side_ref = out_refs[:-1], out_refs[-1]
+    number_row = meta_ref.shape[0] - 1
+    if base:
+        side_ref[meta_ref[number_row, 0] // 2] = refs[2 * halves][...]
 
     def image(index):
-        def store(value):
-            for number, out_ref in enumerate(out_refs):
+        def store(main, side):
+            for number, main_ref in enumerate(main_refs):
 
                 @pl.when(index == number)
                 def _():
-                    out_ref[...] = value
-
-        image_band(meta_ref, base + index, lows, pupil_ref, band_ref, win, store)
-
-    pl.loop(0, len(out_refs))(image)
-
-
-def forward_grid_kernel(meta_ref, pupil_ref, band_ref, real_ref, imag_ref, out_ref, *, win):
-    def store(value):
-        out_ref[0] = value
-
-    lows = [(real_ref, imag_ref)]
-    image_band(meta_ref, pl.program_id(0), lows, pupil_ref, band_ref, win, store)
-
-
-def subtract_image(meta_ref, slot, back_ref, pupil_ref, band_ref, out_ref, win):
-    first_row, left = meta_ref[0, slot], meta_ref[meta_ref.shape[0] - 1, slot]
+                    main_ref[...] = main
+
+            if base:
+                side_ref[meta_ref[number_row, base + index] // 2] = side
+            else:
+                side_ref[...] = side
+
+        bands = (plain_ref, turned_ref)
+        image_band(meta_ref, base + index, lows, pupil_ref, bands, win, store)
+
+    pl.loop(0, count)(image)
+
+
+def forward_grid_kernel(
+    meta_ref, pupil_ref, plain_ref, turned_ref, real_ref, imag_ref, main_ref, side_ref, *, win
+):
+    def store(main, side):
+        main_ref[0] = main
+        side_ref[0] = side
+
+    lows, bands = [(real_ref, imag_ref)], (plain_ref, turned_ref)
+    image_band(meta_ref, pl.program_id(0), lows, pupil_ref, bands, win, store)
+
+
+def subtract_image(meta_ref, slot, main_ref, side, pupil_ref, band_refs, out_ref, win):
+    first_row, left = meta_ref[0, slot], meta_ref[meta_ref.shape[0] - 2, slot]
     tile_rows, crop_width = win.tile_rows, win.crop_width
 
     @pl.when(win.active(first_row))
     def _():
         col_start = win.column(left)
         weight = tile_weight(pupil_ref, first_row, win) * step_size
-        table = tile_band(band_ref, first_row, win)
-        back = back_ref[...].reshape(table.shape[1], crop_width)
-        grad = jnp.dot(table, back, preferred_element_type=jnp.float32)
+        table = tile_band(band_refs, first_row, win)
+        dot = functools.partial(jnp.dot, preferred_element_type=jnp.float32)
+        terms = []
+        if main_ref is not None:
+            main = main_ref[...].reshape(2 * win.main, crop_width)
+            terms.append(dot(table[:, : 2 * win.main], main))
+        if side is not None:
+            side_rows = side().reshape(2 * win.side, crop_width)
+            terms.append(dot(table[:, 2 * win.main :], side_rows))
+        grad = sum(terms)
         columns = pl.ds(col_start, win.columns)
         pad = jnp.zeros((tile_rows, win.columns - crop_width), jnp.float32)
         for part in range(2):
@@ -142,29 +167,45 @@
             out_ref[part, :, columns] = out_ref[part, :, columns] - piece
 
 
-def backward_kernel(meta_ref, pupil_ref, band_ref, spec_ref, *refs, slots, win):
-    back_refs, out_ref = refs[:-1], refs[-1]
+def backward_kernel(
+    meta_ref, pupil_ref, plain_ref, turned_ref, spec_ref, *refs, slots, side_slots, win
+):
+    main_refs, out_ref = refs[: len(slots)], refs[-1]
     out_ref[...] = spec_ref[...]
-    for slot, back_ref in zip(slots, back_refs):
-        subtract_image(meta_ref, slot, back_ref, pupil_ref, band_ref, out_ref, win)
-
-
-def backward_grid_kernel(meta_ref, pupil_ref, band_ref, spec_ref, back_ref, out_ref, *, win):
+    number_row = meta_ref.shape[0] - 1
+    mains = dict(zip(slots, main_refs))
+    for slot in list(slots) + [slot for slot in side_slots if slot not in mains]:
+        side = None
+        if slot in side_slots:
+            side = functools.partial(lambda slot: refs[-2][meta_ref[number_row, slot]], slot)
+        bands = (plain_ref, turned_ref)
+        subtract_image(meta_ref, slot, mains.get(slot), side, pupil_ref, bands, out_ref, win)
+
+
+def backward_grid_kernel(
+    meta_ref, pupil_ref, plain_ref, turned_ref, spec_ref, main_ref, side_ref, out_ref, *, win
+):
     step = pl.program_id(0)
 
     @pl.when(step == 0)
     def _():
         out_ref[...] = spec_ref[...]
 
-    subtract_image(meta_ref, step, back_ref, pupil_ref, band_ref, out_ref, win)
+    bands = (plain_ref, turned_ref)
+    side = functools.partial(lambda: side_ref[0])
+    subtract_image(meta_ref, step, main_ref, side, pupil_ref, bands, out_ref, win)
 
 
 def middle_kernel(*refs, terms):
-    term_refs, (image_ref, cos_ref, sin_ref, out_ref, mid_ref, resid_ref) = refs[:terms], refs[terms:]
-    _, band, crop_width = term_refs[0].shape
+    main_refs, refs = refs[:terms], refs[terms:]
+    side_ref, image_ref, cos_ref, sin_ref, main_out, side_out, mid_ref, resid_ref = refs
+    _, main, crop_width = main_refs[0].shape
+    band = main + side_ref.shape[1]
     block = min(512, crop_width)
-    total = sum(ref[...].astype(jnp.float32) for ref in term_refs)
-    mid_ref[...] = total.astype(jnp.bfloat16).reshape(2 * band, crop_width)
+    total = sum(ref[...].astype(jnp.float32) for ref in main_refs).astype(jnp.bfloat16)
+    for part in range(2):
+        mid_ref[part * band : part * band + main] = total[part]
+        mid_ref[part * band + main : (part + 1) * band] = side_ref[part]
     dot = functools.partial(jnp.dot, preferred_element_type=jnp.float32)
     for start in range(0, crop_width, block):
         columns = slice(start, start + block)
@@ -181,8 +222,9 @@
         columns = slice(start, start + block)
         by_cos = dot(resid_ref[...], cos_ref[:, columns])
         by_sin = dot(resid_ref[...], sin_ref[:, columns])
-        out_ref[0, :, columns] = (by_cos[:band] + by_sin[band:]).astype(jnp.bfloat16)
-        out_ref[1, :, columns] = (by_cos[band:] - by_sin[:band]).astype(jnp.bfloat16)
+        for part, back in enumerate((by_cos[:band] + by_sin[band:], by_cos[band:] - by_sin[:band])):
+            main_out[part, :, columns] = back[:main].astype(jnp.bfloat16)
+            side_out[part, :, columns] = back[main:].astype(jnp.bfloat16)
 
 
 def params():
@@ -197,84 +239,105 @@
 smem = pl.BlockSpec(memory_space=pltpu.SMEM)
 
 
-def band_type(pupil, band_table, *lead):
-    shape = lead + (2, band_table.shape[1] // 2, pupil.shape[1])
-    return jax.ShapeDtypeStruct(shape, jnp.bfloat16)
-
-
-def forward(meta, lows, pupil, band_table, base, count):
-    win = Windows(*lows[0][0].shape, pupil.shape[1])
-    operands = [meta, pupil, band_table] + [part for low in lows for part in low]
+def side_rows(band):
+    return band // 4
+
+
+def band_type(rows, crop_width, *lead):
+    return jax.ShapeDtypeStruct(lead + (2, rows, crop_width), jnp.bfloat16)
+
+
+def windows(tile_shape, pupil, bands):
+    band = bands[0].shape[1] // 2
+    side = side_rows(band)
+    return Windows(*tile_shape, pupil.shape[1], band - side, side)
+
+
+def forward(meta, lows, pupil, bands, base, count, first_side=None):
+    win = windows(lows[0][0].shape, pupil, bands)
+    operands = [meta, pupil, *bands] + [part for low in lows for part in low]
+    lead = ()
+    if base:
+        operands.append(first_side)
+        lead = (base + count,)
     return pl.pallas_call(
-        functools.partial(forward_kernel, base=base, win=win, halves=len(lows)),
+        functools.partial(forward_kernel, base=base, count=count, win=win, halves=len(lows)),
         in_specs=[smem] + [vmem] * (len(operands) - 1),
-        out_specs=[vmem] * count,
-        out_shape=[band_type(pupil, band_table)] * count,
+        out_specs=[vmem] * (count + 1),
+        out_shape=[band_type(win.main, win.crop_width)] * count
+        + [band_type(win.side, win.crop_width, *lead)],
         compiler_params=params(),
         cost_estimate=light(),
         name="forward",
     )(*operands)
 
 
-def backward(meta, spectrum, pupil, band_table, slots, backs):
-    win = Windows(*spectrum.shape[1:], pupil.shape[1])
+def backward(meta, spectrum, pupil, bands, slots, backs, side_slots=(), side=None):
+    win = windows(spectrum.shape[1:], pupil, bands)
+    operands = [meta, pupil, *bands, spectrum, *backs] + [side] * (side is not None)
     return pl.pallas_call(
-        functools.partial(backward_kernel, slots=slots, win=win),
-        in_specs=[smem] + [vmem] * (3 + len(backs)),
+        functools.partial(backward_kernel, slots=slots, side_slots=side_slots, win=win),
+        in_specs=[smem] + [vmem] * (len(operands) - 1),
         out_specs=vmem,
         out_shape=jax.ShapeDtypeStruct(spectrum.shape, jnp.float32),
         compiler_params=params(),
         cost_estimate=light(),
         name="backward",
-    )(meta, pupil, band_table, spectrum, *backs)
-
-
-def middle(terms, image, cos_table, sin_table):
-    _, band, crop_width = terms[0].shape
+    )(*operands)
+
+
+def middle(terms, side, image, cos_table, sin_table):
+    _, main, crop_width = terms[0].shape
+    band = image.shape[1]
     return pl.pallas_call(
         functools.partial(middle_kernel, terms=len(terms)),
-        in_specs=[vmem] * (len(terms) + 3),
-        out_specs=vmem,
-        out_shape=jax.ShapeDtypeStruct((2, band, crop_width), jnp.bfloat16),
+        in_specs=[vmem] * (len(terms) + 4),
+        out_specs=[vmem] * 2,
+        out_shape=[band_type(main, crop_width), band_type(band - main, crop_width)],
         scratch_shapes=[pltpu.VMEM((2 * band, crop_width), jnp.bfloat16)] * 2,
         compiler_params=params(),
         cost_estimate=light(),
         name="middle",
-    )(*terms, image, cos_table, sin_table)
+    )(*terms, side, image, cos_table, sin_table)
 
 
 def fixed(array):
     return pl.BlockSpec(array.shape, lambda i: (0,) * array.ndim)
 
 
-def forward_all(meta, low, pupil, band_table):
-    win = Windows(*low[0].shape, pupil.shape[1])
+def stepped(array):
+    return pl.BlockSpec((1,) + array.shape[1:], lambda i: (i, 0, 0, 0))
+
+
+def forward_all(meta, low, pupil, bands):
+    win = windows(low[0].shape, pupil, bands)
     count = meta.shape[1]
-    out_type = band_type(pupil, band_table, count)
+    out_types = [band_type(rows, win.crop_width, count) for rows in (win.main, win.side)]
     return pl.pallas_call(
         functools.partial(forward_grid_kernel, win=win),
         grid=(count,),
-        in_specs=[smem] + [fixed(array) for array in (pupil, band_table, *low)],
-        out_specs=pl.BlockSpec((1,) + out_type.shape[1:], lambda i: (i, 0, 0, 0)),
-        out_shape=out_type,
+        in_specs=[smem] + [fixed(array) for array in (pupil, *bands, *low)],
+        out_specs=[stepped(out_type) for out_type in out_types],
+        out_shape=out_types,
         compiler_params=params(),
         name="forward_all",
-    )(meta, pupil, band_table, *low)
-
-
-def backward_all(meta, spectrum, pupil, band_table, backs):
-    win = Windows(*spectrum.shape[1:], pupil.shape[1])
+    )(meta, pupil, *bands, *low)
+
+
+def backward_all(meta, spectrum, pupil, bands, backs):
+    win = windows(spectrum.shape[1:], pupil, bands)
+    main = pl.BlockSpec((None,) + backs[0].shape[1:], lambda i: (i, 0, 0, 0))
     return pl.pallas_call(
         functools.partial(backward_grid_kernel, win=win),
         grid=(meta.shape[1],),
         in_specs=[smem]
-        + [fixed(array) for array in (pupil, band_table, spectrum)]
-        + [pl.BlockSpec((1,) + backs.shape[1:], lambda i: (i, 0, 0, 0))],
+        + [fixed(array) for array in (pupil, *bands, spectrum)]
+        + [main, stepped(backs[1])],
         out_specs=fixed(spectrum),
         out_shape=jax.ShapeDtypeStruct(spectrum.shape, jnp.float32),
         compiler_params=params(),
         name="backward_all",
-    )(meta, pupil, band_table, spectrum, backs)
+    )(meta, pupil, *bands, spectrum, *backs)
 
 
 def cast_kernel(spec_ref, out_ref):
@@ -310,10 +373,11 @@
     band = measured.shape[1]
     band_start = (crop_width - band) // 2
     cos_table, sin_table = fourier_tables(crop_width)
-    chosen_rows = slice(band_start, band_start + band)
-    band_table = jnp.asarray(
-        np.concatenate([cos_table[:, chosen_rows], sin_table[:, chosen_rows]], axis=1)
-    )
+    split = band_start + band - side_rows(band)
+    cuts = [slice(band_start, split), slice(split, band_start + band)]
+    plain = [table[:, cut] for cut in cuts for table in (cos_table, sin_table)]
+    turned = [table[:, cut] for cut in cuts for table in (-sin_table, cos_table)]
+    bands = [jnp.asarray(np.concatenate(columns, axis=1)) for columns in (plain, turned)]
     cos_table, sin_table = jnp.asarray(cos_table), jnp.asarray(sin_table)
 
     half = crop_width // 2
@@ -325,14 +389,15 @@
         tops = jnp.sum(jnp.where(match, centre_rows[None, :], 0), axis=1) - half
         lefts = jnp.sum(jnp.where(match, centre_cols[None, :], 0), axis=1) - half
         rows = [place * tile_rows - tops for place in positions]
-        return jnp.stack(rows + [lefts]).astype(jnp.int32)
+        return jnp.stack(rows + [lefts, ids]).astype(jnp.int32)
 
     if planes != 4:
         meta = image_meta(jnp.arange(count, dtype=jnp.int32), [position])
-        partial = forward_all(meta, low, pupil, band_table)
-        mid = lax.psum_scatter(partial, "ty", scatter_dimension=0, tiled=True)[0]
-        back = lax.all_gather(middle([mid], measured, cos_table, sin_table), "ty")
-        return backward_all(meta, spectrum, pupil, band_table, back)
+        parts = forward_all(meta, low, pupil, bands)
+        mid = [lax.psum_scatter(part, "ty", scatter_dimension=0, tiled=True)[0] for part in parts]
+        backs = middle(mid[:1], mid[1], measured, cos_table, sin_table)
+        backs = [lax.all_gather(back, "ty") for back in backs]
+        return backward_all(meta, spectrum, pupil, bands, backs)
 
     targets = {"far": (3, 3, 0, 0), "next": (2, 2, 1, 1), "beside": (1, 0, 3, 2), "own": (0, 1, 2, 3)}
     own_core = [("far", 2), ("far", 0), ("next", 2), ("next", 0)]
@@ -364,7 +429,7 @@
     together = lax.optimization_barrier
 
     lows = [low, [sibling(part) for part in low]]
-    (far_leaving,) = forward(meta, lows, pupil, band_table, 0, 1)
+    far_leaving, first_side = forward(meta, lows, pupil, bands, 0, 1)
     far_other = across(far_leaving)
     (
         far_kept,
@@ -374,7 +439,12 @@
         beside_kept,
         own_leaving,
         own_kept,
-    ) = forward(together((meta, far_leaving))[0], lows, pupil, band_table, 1, 7)
+        sides,
+    ) = forward(together((meta, far_leaving))[0], lows, pupil, bands, 1, 7, first_side)
+    same_core = [list(range(core, count, 2)) for core in range(2)]
+    side = lax.psum_scatter(
+        sides, "ty", scatter_dimension=0, axis_index_groups=same_core, tiled=False
+    )
     far_other, far_kept, next_leaving = together((far_other, far_kept, next_leaving))
 
     from_end = along(total(far_kept, far_other), inward)
@@ -384,21 +454,25 @@
     far_inner = along(total(far_kept, far_other, from_end), inner)
     next_inward = along(total(next_kept, next_other), inward)
     beside_other = across(beside_leaving)
-    far_inner, next_inward, beside_other, own_leaving = together(
-        (far_inner, next_inward, beside_other, own_leaving)
+    far_inner, next_inward, beside_other, own_leaving, side = together(
+        (far_inner, next_inward, beside_other, own_leaving, side)
     )
 
     next_inner = along(total(next_kept, next_other, next_inward), inner)
     beside = along(total(beside_kept, beside_other, far_inner), inward + outward)
     own_other = across(own_leaving)
     terms = [own_kept, own_other, next_inner, beside]
-    back = middle(terms, measured, cos_table, sin_table)
-
-    def apply(result, pieces):
+    back, back_side = middle(terms, side, measured, cos_table, sin_table)
+    gathered = lax.all_gather(back_side, "ty")
+    all_sides = None
+
+    def apply(result, pieces, more_sides=()):
         names, values = zip(*pieces)
-        return backward(
-            meta, result, pupil, band_table, [slots[name] for name in names], list(values)
-        )
+        own_slots = [slots[name] for name in names]
+        if all_sides is None:
+            return backward(meta, result, pupil, bands, own_slots, values)
+        side_slots = own_slots + [slots[name] for name in more_sides]
+        return backward(meta, result, pupil, bands, own_slots, values, side_slots, all_sides)
 
     from_beside = along(back, inward + outward)
     from_inner = along(back, inner)
@@ -416,8 +490,8 @@
         spectrum,
         [(("own", 0), back), (("own", 1), twin), (("beside", 0), from_beside), (("own", 2), other)],
     )
-    far_inner, next_outward, beside_other, beside_twin, other_twin, result = together(
-        (far_inner, next_outward, beside_other, beside_twin, other_twin, result)
+    far_inner, next_outward, beside_other, beside_twin, other_twin, result, all_sides = together(
+        (far_inner, next_outward, beside_other, beside_twin, other_twin, result, gathered)
     )
 
     at_ends = (plane == 0) | (plane == 3)
@@ -433,6 +507,7 @@
             (("next", 0), from_next),
             (("beside", 2), beside_other),
         ],
+        [("own", 0), ("own", 1), ("beside", 0), ("own", 2)],
     )
     far_outward, next_other, next_twin, beside_other_twin, result = together(
         (far_outward, next_other, next_twin, beside_other_twin, result)

time: 259 us -> 305 us (1.18)
  local copies, waits for them, and re-layouts: 15.3 us -> 36.6 us
  between operations: 0.3 us -> 13.8 us
  starting transfers between devices: 35.2 us -> 42 us
  other arithmetic: 5.61 us -> 9.04 us
    unnamed x28 -> x76, local copies, waits for them, and re-layouts: 14.6 us -> 35.9 us
    ppermute x10, waiting for transfers between devices: 74.7 us -> 87.9 us  [along(): return lax.ppermute(value, 'ty', pairs)]
    ppermute x8, waiting for transfers between devices: 63.7 us -> 50.7 us  [across(): return lax.ppermute(value, 'ty', [(i, i ^ 2) for i in range(count)])]
    ppermute x8, starting transfers between devices: 7.14 us -> 15.9 us  [across(): return lax.ppermute(value, 'ty', [(i, i ^ 2) for i in range(count)])]
    convert_element_type x5, other arithmetic: 2.73 us -> 6.31 us  [total(): sum((term.astype(jnp.float32) for term in terms)).astype(jnp.bfloat16)]
    ppermute x10, starting transfers between devices: 10.8 us -> 7.41 us  [sibling(): return lax.ppermute(value, 'ty', [(i, i ^ 1) for i in range(count)])]
  transfers between devices with their start and end apart: 28 -> 30, of which waited for: 18 -> 17; matrix products, arithmetic and copies ran while one was open for 1% -> 2% of each run, Pallas kernels for 14% -> 7%
where the time goes in v1:
time: 305 us; the launch traced here: 303 us
  waiting for transfers between devices  145 us (48%)
  Pallas kernels  57.3 us (19%)
  starting transfers between devices  42 us (14%)
  local copies, waits for them, and re-layouts  36.6 us (12%)
  between operations  13.8 us (5%)
  other arithmetic  9.04 us (3%)
    ppermute x10, waiting for transfers between devices, along(): return lax.ppermute(value, 'ty', pairs)  87.9 us
    ppermute x8, waiting for transfers between devices, across(): return lax.ppermute(value, 'ty', [(i, i ^ 2) for i in range(count)])  50.7 us
    unnamed x76, local copies, waits for them, and re-layouts  35.9 us
    pallas_call x4, Pallas kernels, backward(): pl.pallas_call(functools.partial(backward_kernel, slots=slots, side_slots...  28.5 us
    pallas_call x2, Pallas kernels, forward(): pl.pallas_call(functools.partial(forward_kernel, base=base, count=count,...  19 us
    ppermute x10, starting transfers between devices, along(): return lax.ppermute(value, 'ty', pairs)  18.6 us
    ppermute x8, starting transfers between devices, across(): return lax.ppermute(value, 'ty', [(i, i ^ 2) for i in range(count)])  15.9 us
    ppermute x10, starting transfers between devices, sibling(): return lax.ppermute(value, 'ty', [(i, i ^ 1) for i in range(count)])  7.41 us
  transfers between devices with their start and end apart: 30, of which 17 were waited for; matrix products, arithmetic and copies ran while one was open for 2% of the time, Pallas kernels for 7%

profile of v1, /device:TPU:11, one launch (start us, length us, event | category | flops | bytes accessed | tf_op | source)
XLA Modules:
  0.0 303.5 jit_solution(15632547383527688140)
XLA Ops:
  6.5 3.4 %copy-done.1 = f32[2,128,8192]{2,1,0:T(8,128)S(1)} copy-done((f32[2,128,8192]{2,1,0:T(8,128)S(1)}, f32[2,128,8192]{2,1,0:T(8,128)}, u32[]{:S(2)}) %copy-start.1) | copy-done | bytes 8388632
  9.9 2.1 low_part.3.refs_1_
  12.8 2.1 low_part.2.refs_0_
  15.8 1.1 collective-permute-done.1.refs_3_
  16.9 3.0 collective-permute-done.refs_2_
  19.9 1.2 copy-done.3
  21.2 5.7 %forward.2 = (bf16[2,192,1024]{2,1,0:T(8,128)(2,1)S(1)}, bf16[2,64,1024]{2,1,0:T(8,128)(2,1)S(1)}) custom-call(s32[4,16]{1,0:T(4,128)S(1)} %pad_add_fusion.meta_ref, bf16[1024,1024]{1,0:T(8,128)(2,1)S(1)} %copy-done, bf16[1024,512]{1,0:T(8,128)(2,1)S(1)} %copy-done.3, bf16[1024,512]{1,0:T(8,128)(2,1)S(1)} %copy-done.2, bf16[128,8192]{1,0:T(8,128)(2,1)} %low_part.2.refs_0_, ...), custom_call_target="tpu_custom_call" | custom-call | flops 1024 | bytes 1024 | tf_op jit(solution)/shard_map/forward/pallas_call | solution.py:263
  26.9 0.9 copy-done.34
  27.8 13.3 %forward.3 = (bf16[2,192,1024]{2,1,0:T(8,128)(2,1)S(1)}, bf16[2,192,1024]{2,1,0:T(8,128)(2,1)S(1)}, bf16[2,192,1024]{2,1,0:T(8,128)(2,1)S(1)}, bf16[2,192,1024]{...) custom-call(s32[4,16]{1,0:T(4,128)S(1)} %pad_add_fusion.meta_ref, ...), custom_call_target="tpu_custom_call" | custom-call | flops 1024 | bytes 1024 | tf_op jit(solution)/shard_map/forward/pallas_call | solution.py:263
  42.0 0.9 copy-done.14
  42.9 1.3 copy-done.16
  44.2 0.9 copy-done.23
  45.1 0.9 copy-done.25
  46.9 0.9 copy-done.30
  47.8 0.9 copy-done.32
  48.7 8.0 %collective-permute-start.2 = (bf16[2,192,1024]{2,1,0:T(8,128)(2,1)}, bf16[2,192,1024]{2,1,0:T(8,128)(2,1)S(1)}, u32[]{:S(2)}, u32[]{:S(2)}) collective-permute-start(bf16[2,192,1024]{2,1,0:T(8,128)(2,1)} %copy-done.34), channel_id=1, source_target_pairs={{0,2},{1,3},{2,0},{3,1},{4,6},{5,7},{6,4},{7,5},{8,10},{9,11},{10,... | collective-permute-start | bytes 2359304 | tf_op jit(solution)/shard_map/ppermute | solution.py:420
  56.7 21.6 %collective-permute-done.2 = bf16[2,192,1024]{2,1,0:T(8,128)(2,1)S(1)} collective-permute-done((bf16[2,192,1024]{2,1,0:T(8,128)(2,1)}, bf16[2,192,1024]{2,1,0:T(8,128)(2,1)S(1)}, u32[]{:S(2)}, u32[]{:S(2)}) %collective-permute-start.2) | collective-permute-done | bytes 786464 | tf_op jit(solution)/shard_map/ppermute | solution.py:420
  78.2 1.4 fusion
  79.7 1.4 collective-permute-start.3
  81.1 2.2 collective-permute-start.4
  83.4 19.3 %collective-permute-done.3 = bf16[2,192,1024]{2,1,0:T(8,128)(2,1)S(1)} collective-permute-done((bf16[2,192,1024]{2,1,0:T(8,128)(2,1)S(1)}, bf16[2,192,1024]{2,1,0:T(8,128)(2,1)S(1)}, u32[]{:S(2)}, u32[]{:S(2)}) %collective-permute-start.3) | collective-permute-done | bytes 786464 | tf_op jit(solution)/shard_map/ppermute | solution.py:424
  103.6 0.9 copy-done.35
  104.8 1.4 collective-permute-start.6
  106.7 1.9 collective-permute-start.5
  108.6 1.8 collective-permute-start.7
  110.4 23.2 %collective-permute-done.6 = bf16[2,192,1024]{2,1,0:T(8,128)(2,1)} collective-permute-done((bf16[2,192,1024]{2,1,0:T(8,128)(2,1)S(1)}, bf16[2,192,1024]{2,1,0:T(8,128)(2,1)}, u32[]{:S(2)}, u32[]{:S(2)}) %collective-permute-start.6) | collective-permute-done | bytes 786464 | tf_op jit(solution)/shard_map/ppermute | solution.py:424
  133.7 1.5 collective-permute-done.5
  135.1 2.2 add_convert_fusion.1
  137.3 3.3 %collective-permute-start.9 = (bf16[2,192,1024]{2,1,0:T(8,128)(2,1)S(1)}, bf16[2,192,1024]{2,1,0:T(8,128)(2,1)S(1)}, u32[]{:S(2)}, u32[]{:S(2)}) collective-permute-start(bf16[2,192,1024]{2,1,0:T(8,128)(2,1)S(1)} %add_convert_fusion.1), channel_id=1, source_target_pairs={{4,8},{5,9},{6,10},{7,11},{8,4},{9,5},{10,6},{11,7},{20,24},{21,25... | collective-permute-start | bytes 2359304 | tf_op jit(solution)/shard_map/ppermute | solution.py:424
  141.3 1.9 add_convert_fusion
  143.4 14.8 %collective-permute-done.9.refs_2_ = bf16[2,192,1024]{2,1,0:T(8,128)(2,1)S(1)} collective-permute-done((bf16[2,192,1024]{2,1,0:T(8,128)(2,1)S(1)}, bf16[2,192,1024]{2,1,0:T(8,128)(2,1)S(1)}, u32[]{:S(2)}, u32[]{:S(2)}) %collective-permute-start.9) | collective-permute-done | bytes 786464 | tf_op jit(solution)/shard_map/ppermute | solution.py:424
  158.9 3.1 %collective-permute-done.10.refs_3_ = bf16[2,192,1024]{2,1,0:T(8,128)(2,1)S(1)} collective-permute-done((bf16[2,192,1024]{2,1,0:T(8,128)(2,1)S(1)}, bf16[2,192,1024]{2,1,0:T(8,128)(2,1)S(1)}, u32[]{:S(2)}, u32[]{:S(2)}) %collective-permute-start.10) | collective-permute-done | bytes 786464 | tf_op jit(solution)/shard_map/ppermute | solution.py:424
  162.1 0.9 copy-done.28
  163.0 5.5 %middle.1 = (bf16[2,192,1024]{2,1,0:T(8,128)(2,1)S(1)}, bf16[2,64,1024]{2,1,0:T(8,128)(2,1)}) custom-call(bf16[2,192,1024]{2,1,0:T(8,128)(2,1)S(1)} %copy-done.26, bf16[2,192,1024]{2,1,0:T(8,128)(2,1)S(1)} %collective-permute-done.8.refs_1_, bf16[2,192,1024]{2,1,0:T(8,128)(2,1)S(1)} %collective-permute-done.9.refs_2_, ...), custom_call_target="tpu_custom_call" | custom-call | flops 1024 | bytes 1024 | tf_op jit(solution)/shard_map/middle/pallas_call | solution.py:292
  169.4 1.4 collective-permute-start.14
  171.6 2.2 collective-permute-start.12
  174.8 18.3 %collective-permute-done.13.refs_3_ = bf16[2,192,1024]{2,1,0:T(8,128)(2,1)} collective-permute-done((bf16[2,192,1024]{2,1,0:T(8,128)(2,1)}, bf16[2,192,1024]{2,1,0:T(8,128)(2,1)}, u32[]{:S(2)}, u32[]{:S(2)}) %collective-permute-start.13) | collective-permute-done | bytes 786464 | tf_op jit(solution)/shard_map/ppermute | solution.py:420
  193.0 8.0 %collective-permute-done.12 = bf16[2,192,1024]{2,1,0:T(8,128)(2,1)} collective-permute-done((bf16[2,192,1024]{2,1,0:T(8,128)(2,1)}, bf16[2,192,1024]{2,1,0:T(8,128)(2,1)}, u32[]{:S(2)}, u32[]{:S(2)}) %collective-permute-start.12) | collective-permute-done | bytes 786464 | tf_op jit(solution)/shard_map/ppermute | solution.py:424
  201.1 3.2 %collective-permute-start.16 = (bf16[2,192,1024]{2,1,0:T(8,128)(2,1)}, bf16[2,192,1024]{2,1,0:T(8,128)(2,1)}, u32[]{:S(2)}, u32[]{:S(2)}) collective-permute-start(bf16[2,192,1024]{2,1,0:T(8,128)(2,1)} %collective-permute-done.12), channel_id=1, source_target_pairs={{4,0},{5,1},{6,2},{7,3},{8,12},{9,13},{10,14},{11,15},{20,16},{21,... | collective-permute-start | bytes 2359304 | tf_op jit(solution)/shard_map/ppermute | solution.py:424
  204.2 1.5 collective-permute-start.19
  205.7 0.9 collective-permute-start.17
  206.6 2.8 collective-permute-start.15
  209.5 1.2 copy-done.4
  210.7 1.1 copy-done.20
  211.8 1.2 copy-done.22
  213.0 5.2 %backward.4.spec_ref = f32[2,128,8192]{2,1,0:T(8,128)S(1)} custom-call(s32[4,16]{1,0:T(4,128)S(1)} %pad_add_fusion.meta_ref, bf16[1024,1024]{1,0:T(8,128)(2,1)S(1)} %copy-done, bf16[1024,512]{1,0:T(8,128)(2,1)S(1)} %copy-done.4, bf16[1024,512]{1,0:T(8,128)(2,1)S(1)} %copy-done.2, f32[2,128,8192]{2,1,0:T(8,128)} %spec_ref.5, ...), custom_call_target="tpu_custom_call" | custom-call | flops 1024 | bytes 1024 | tf_op jit(solution)/shard_map/backward/pallas_call | solution.py:278
  218.2 3.4 %copy-done.8 = f32[2,128,8192]{2,1,0:T(8,128)} copy-done((f32[2,128,8192]{2,1,0:T(8,128)}, f32[2,128,8192]{2,1,0:T(8,128)S(1)}, u32[]{:S(2)}) %copy-start.8) | copy-done | bytes 8388632
  221.6 14.8 %collective-permute-done.16 = bf16[2,192,1024]{2,1,0:T(8,128)(2,1)} collective-permute-done((bf16[2,192,1024]{2,1,0:T(8,128)(2,1)}, bf16[2,192,1024]{2,1,0:T(8,128)(2,1)}, u32[]{:S(2)}, u32[]{:S(2)}) %collective-permute-start.16) | collective-permute-done | bytes 786464 | tf_op jit(solution)/shard_map/ppermute | solution.py:424
  236.4 2.0 collective-permute-done.15
  238.4 1.3 broadcast_select_fusion.1.refs_2_
  240.4 1.2 collective-permute-start.21
  241.6 2.3 collective-permute-start.20
  244.6 2.2 copy-done.6
  246.7 9.4 %backward.5.spec_ref = f32[2,128,8192]{2,1,0:T(8,128)S(1)} custom-call(s32[4,16]{1,0:T(4,128)S(1)} %pad_add_fusion.meta_ref, bf16[1024,1024]{1,0:T(8,128)(2,1)S(1)} %copy-done, bf16[1024,512]{1,0:T(8,128)(2,1)S(1)} %copy-done.5, bf16[1024,512]{1,0:T(8,128)(2,1)S(1)} %copy-done.2, f32[2,128,8192]{2,1,0:T(8,128)} %copy-done.8, ...), custom_call_target="tpu_custom_call" | custom-call | flops 1024 | bytes 1024 | tf_op jit(solution)/shard_map/backward/pallas_call | solution.py:278
  256.1 3.4 %copy-done.9 = f32[2,128,8192]{2,1,0:T(8,128)} copy-done((f32[2,128,8192]{2,1,0:T(8,128)}, f32[2,128,8192]{2,1,0:T(8,128)S(1)}, u32[]{:S(2)}) %copy-start.9) | copy-done | bytes 8388632
  259.5 1.2 collective-permute-done.20
  260.7 1.2 broadcast_select_fusion.refs_2_
  261.9 1.2 collective-permute-start.25
  263.8 5.8 %backward.6.spec_ref = f32[2,128,8192]{2,1,0:T(8,128)S(1)} custom-call(s32[4,16]{1,0:T(4,128)S(1)} %pad_add_fusion.meta_ref, bf16[1024,1024]{1,0:T(8,128)(2,1)S(1)} %copy-done, bf16[1024,512]{1,0:T(8,128)(2,1)S(1)} %copy-done.5, bf16[1024,512]{1,0:T(8,128)(2,1)S(1)} %copy-done.2, f32[2,128,8192]{2,1,0:T(8,128)} %copy-done.9, ...), custom_call_target="tpu_custom_call" | custom-call | flops 1024 | bytes 1024 | tf_op jit(solution)/shard_map/backward/pallas_call | solution.py:278
  269.6 3.4 %copy-done.10 = f32[2,128,8192]{2,1,0:T(8,128)} copy-done((f32[2,128,8192]{2,1,0:T(8,128)}, f32[2,128,8192]{2,1,0:T(8,128)S(1)}, u32[]{:S(2)}) %copy-start.10) | copy-done | bytes 8388632
  273.0 9.3 %collective-permute-done.24.refs_2_ = bf16[2,192,1024]{2,1,0:T(8,128)(2,1)S(1)} collective-permute-done((bf16[2,192,1024]{2,1,0:T(8,128)(2,1)S(1)}, bf16[2,192,1024]{2,1,0:T(8,128)(2,1)S(1)}, u32[]{:S(2)}, u32[]{:S(2)}) %collective-permute-start.24) | collective-permute-done | bytes 786464 | tf_op jit(solution)/shard_map/ppermute | solution.py:420
  283.1 1.9 collective-permute-done.27.refs_3_
  285.0 3.4 %copy-done.11 = f32[2,128,8192]{2,1,0:T(8,128)S(1)} copy-done((f32[2,128,8192]{2,1,0:T(8,128)S(1)}, f32[2,128,8192]{2,1,0:T(8,128)}, u32[]{:S(2)}) %copy-start.11) | copy-done | bytes 8388632
  288.4 8.2 %backward.7 = f32[2,128,8192]{2,1,0:T(8,128)} custom-call(s32[4,16]{1,0:T(4,128)S(1)} %pad_add_fusion.meta_ref, bf16[1024,1024]{1,0:T(8,128)(2,1)S(1)} %copy-done, bf16[1024,512]{1,0:T(8,128)(2,1)S(1)} %copy-done.5, bf16[1024,512]{1,0:T(8,128)(2,1)S(1)} %copy-done.2, f32[2,128,8192]{2,1,0:T(8,128)S(1)} %copy-done.11, ...), custom_call_target="tpu_custom_call" | custom-call | flops 1024 | bytes 1024 | tf_op jit(solution)/shard_map/backward/pallas_call | solution.py:278
  (95 shorter events, 12.3 us)
Async XLA Ops:
  6.5 128.6 %reduce-scatter.2.cloned.1.call-start = ((), (), s32[]{:S(2)}) async-start(), calls=%async_computation.1 | async-start | bytes 2359296 | tf_op jit(solution)/shard_map/reduce_scatter | solution.py:445
  6.5 3.4 %copy-start.1 = (f32[2,128,8192]{2,1,0:T(8,128)S(1)}, f32[2,128,8192]{2,1,0:T(8,128)}, u32[]{:S(2)}) copy-start(f32[2,128,8192]{2,1,0:T(8,128)} %spec_ref.5) | copy-start | bytes 25165828
  12.1 3.6 %copy-start.36 = (s32[16]{0:T(128)S(1)}, s32[16]{0:T(128)}, u32[]{:S(2)}) copy-start(s32[16]{0:T(128)} %param.13) | copy-start | bytes 196
  12.1 3.6 %copy-start.37 = (s32[16]{0:T(128)S(1)}, s32[16]{0:T(128)}, u32[]{:S(2)}) copy-start(s32[16]{0:T(128)} %param.14) | copy-start | bytes 196
  12.1 7.9 %copy-start = (bf16[1024,1024]{1,0:T(8,128)(2,1)S(1)}, bf16[1024,1024]{1,0:T(8,128)(2,1)}, u32[]{:S(2)}) copy-start(bf16[1024,1024]{1,0:T(8,128)(2,1)} %pupil_ref.11) | copy-start | bytes 6291460
  12.1 7.9 %copy-start.2 = (bf16[1024,512]{1,0:T(8,128)(2,1)S(1)}, bf16[1024,512]{1,0:T(8,128)(2,1)}, u32[]{:S(2)}) copy-start(bf16[1024,512]{1,0:T(8,128)(2,1)} %constant.45.clone.turned_ref) | copy-start | bytes 3145732
  12.1 4.9 %collective-permute-start.1 = (bf16[128,8192]{1,0:T(8,128)(2,1)}, bf16[128,8192]{1,0:T(8,128)(2,1)}, u32[]{:S(2)}, u32[]{:S(2)}) collective-permute-start(bf16[128,8192]{1,0:T(8,128)(2,1)} %low_part.3.refs_1_), channel_id=1, source_target_pairs={{0,1},{1,0},{2,3},{3,2},{4,5},{5,4},{6,7},{7,6},{8,9},{9,8},{10,11... | collective-permute-start | bytes 6291464 | tf_op jit(solution)/shard_map/ppermute | solution.py:417
  14.9 5.0 %collective-permute-start = (bf16[128,8192]{1,0:T(8,128)(2,1)}, bf16[128,8192]{1,0:T(8,128)(2,1)}, u32[]{:S(2)}, u32[]{:S(2)}) collective-permute-start(bf16[128,8192]{1,0:T(8,128)(2,1)} %low_part.2.refs_0_), channel_id=1, source_target_pairs={{0,1},{1,0},{2,3},{3,2},{4,5},{5,4},{6,7},{7,6},{8,9},{9,8},{10,11... | collective-permute-start | bytes 6291464 | tf_op jit(solution)/shard_map/ppermute | solution.py:417
  19.9 1.2 copy-start.3
  26.9 0.9 copy-start.34
  41.1 0.9 copy-start.12
  42.0 0.9 copy-start.14
  42.9 1.3 copy-start.16
  45.1 0.9 copy-start.25
  46.9 0.9 copy-start.30
  47.8 0.9 copy-start.32
  48.7 189.7 %all-gather.3.cloned.1.call-start = ((), (), s32[]{:S(2)}) async-start(), calls=%async_computation.2 | async-start | bytes 4456448 | tf_op jit(solution)/shard_map/all_gather | solution.py:466
  48.7 32.4 %copy-start.33 = (bf16[2,192,1024]{2,1,0:T(8,128)(2,1)S(1)}, bf16[2,192,1024]{2,1,0:T(8,128)(2,1)}, u32[]{:S(2)}) copy-start(bf16[2,192,1024]{2,1,0:T(8,128)(2,1)} %copy-done.32) | copy-start | bytes 2359300
  48.7 55.7 %copy-start.13 = (bf16[2,192,1024]{2,1,0:T(8,128)(2,1)S(1)}, bf16[2,192,1024]{2,1,0:T(8,128)(2,1)}, u32[]{:S(2)}) copy-start(bf16[2,192,1024]{2,1,0:T(8,128)(2,1)} %copy-done.12) | copy-start | bytes 2359300
  48.7 29.5 %collective-permute-start.2 = (bf16[2,192,1024]{2,1,0:T(8,128)(2,1)}, bf16[2,192,1024]{2,1,0:T(8,128)(2,1)S(1)}, u32[]{:S(2)}, u32[]{:S(2)}) collective-permute-start(bf16[2,192,1024]{2,1,0:T(8,128)(2,1)} %copy-done.34), channel_id=1, source_target_pairs={{0,2},{1,3},{2,0},{3,1},{4,6},{5,7},{6,4},{7,5},{8,10},{9,11},{10,... | collective-permute-start | bytes 2359304 | tf_op jit(solution)/shard_map/ppermute | solution.py:420
  79.7 26.5 %copy-start.15 = (bf16[2,192,1024]{2,1,0:T(8,128)(2,1)S(1)}, bf16[2,192,1024]{2,1,0:T(8,128)(2,1)}, u32[]{:S(2)}) copy-start(bf16[2,192,1024]{2,1,0:T(8,128)(2,1)} %copy-done.14) | copy-start | bytes 2359300
  79.7 23.0 %collective-permute-start.3 = (bf16[2,192,1024]{2,1,0:T(8,128)(2,1)S(1)}, bf16[2,192,1024]{2,1,0:T(8,128)(2,1)S(1)}, u32[]{:S(2)}, u32[]{:S(2)}) collective-permute-start(bf16[2,192,1024]{2,1,0:T(8,128)(2,1)S(1)} %fusion), channel_id=1, source_target_pairs={{0,4},{1,5},{2,6},{3,7},{12,8},{13,9},{14,10},{15,11},{16,20},{17,... | collective-permute-start | bytes 2359304 | tf_op jit(solution)/shard_map/ppermute | solution.py:424
  81.1 22.4 %collective-permute-start.4 = (bf16[2,192,1024]{2,1,0:T(8,128)(2,1)S(1)}, bf16[2,192,1024]{2,1,0:T(8,128)(2,1)S(1)}, u32[]{:S(2)}, u32[]{:S(2)}) collective-permute-start(bf16[2,192,1024]{2,1,0:T(8,128)(2,1)S(1)} %copy-done.33), channel_id=1, source_target_pairs={{0,2},{1,3},{2,0},{3,1},{4,6},{5,7},{6,4},{7,5},{8,10},{9,11},{10,... | collective-permute-start | bytes 2359304 | tf_op jit(solution)/shard_map/ppermute | solution.py:420
  103.6 0.9 copy-start.35
  104.8 3.8 %copy-start.31 = (bf16[2,192,1024]{2,1,0:T(8,128)(2,1)S(1)}, bf16[2,192,1024]{2,1,0:T(8,128)(2,1)}, u32[]{:S(2)}) copy-start(bf16[2,192,1024]{2,1,0:T(8,128)(2,1)} %copy-done.30) | copy-start | bytes 2359300
  104.8 28.9 %collective-permute-start.6 = (bf16[2,192,1024]{2,1,0:T(8,128)(2,1)S(1)}, bf16[2,192,1024]{2,1,0:T(8,128)(2,1)}, u32[]{:S(2)}, u32[]{:S(2)}) collective-permute-start(bf16[2,192,1024]{2,1,0:T(8,128)(2,1)S(1)} %fusion.1), channel_id=1, source_target_pairs={{0,4},{1,5},{2,6},{3,7},{12,8},{13,9},{14,10},{15,11},{16,20},{17,... | collective-permute-start | bytes 2359304 | tf_op jit(solution)/shard_map/ppermute | solution.py:424
  106.7 28.4 %collective-permute-start.5 = (bf16[2,192,1024]{2,1,0:T(8,128)(2,1)S(1)}, bf16[2,192,1024]{2,1,0:T(8,128)(2,1)}, u32[]{:S(2)}, u32[]{:S(2)}) collective-permute-start(bf16[2,192,1024]{2,1,0:T(8,128)(2,1)S(1)} %add_convert_fusion.2), channel_id=1, source_target_pairs={{4,8},{5,9},{6,10},{7,11},{8,4},{9,5},{10,6},{11,7},{20,24},{21,25... | collective-permute-start | bytes 2359304 | tf_op jit(solution)/shard_map/ppermute | solution.py:424
  108.6 26.5 %collective-permute-start.7 = (bf16[2,192,1024]{2,1,0:T(8,128)(2,1)S(1)}, bf16[2,192,1024]{2,1,0:T(8,128)(2,1)}, u32[]{:S(2)}, u32[]{:S(2)}) collective-permute-start(bf16[2,192,1024]{2,1,0:T(8,128)(2,1)S(1)} %copy-done.31), channel_id=1, source_target_pairs={{0,2},{1,3},{2,0},{3,1},{4,6},{5,7},{6,4},{7,5},{8,10},{9,11},{10,... | collective-permute-start | bytes 2359304 | tf_op jit(solution)/shard_map/ppermute | solution.py:420
  135.1 6.2 %copy-start.24 = (bf16[2,192,1024]{2,1,0:T(8,128)(2,1)S(1)}, bf16[2,192,1024]{2,1,0:T(8,128)(2,1)}, u32[]{:S(2)}) copy-start(bf16[2,192,1024]{2,1,0:T(8,128)(2,1)} %copy-done.23) | copy-start | bytes 2359300
  135.1 26.9 %copy-start.18 = (bf16[1024,1024]{1,0:T(8,128)(2,1)S(1)}, bf16[1024,1024]{1,0:T(8,128)(2,1)}, u32[]{:S(2)}) copy-start(bf16[1024,1024]{1,0:T(8,128)(2,1)} %constant.46.clone.refs_6_) | copy-start | bytes 6291460
  135.1 26.9 %copy-start.27 = (bf16[1,256,1024]{2,1,0:T(8,128)(2,1)S(1)}, bf16[1,256,1024]{2,1,0:T(8,128)(2,1)}, u32[]{:S(2)}) copy-start(bf16[1,256,1024]{2,1,0:T(8,128)(2,1)} %refs_5_.1) | copy-start | bytes 1572868
  137.3 20.8 %collective-permute-start.9 = (bf16[2,192,1024]{2,1,0:T(8,128)(2,1)S(1)}, bf16[2,192,1024]{2,1,0:T(8,128)(2,1)S(1)}, u32[]{:S(2)}, u32[]{:S(2)}) collective-permute-start(bf16[2,192,1024]{2,1,0:T(8,128)(2,1)S(1)} %add_convert_fusion.1), channel_id=1, source_target_pairs={{4,8},{5,9},{6,10},{7,11},{8,4},{9,5},{10,6},{11,7},{20,24},{21,25... | collective-permute-start | bytes 2359304 | tf_op jit(solution)/shard_map/ppermute | solution.py:424
  140.6 18.3 %collective-permute-start.8 = (bf16[2,192,1024]{2,1,0:T(8,128)(2,1)}, bf16[2,192,1024]{2,1,0:T(8,128)(2,1)S(1)}, u32[]{:S(2)}, u32[]{:S(2)}) collective-permute-start(bf16[2,192,1024]{2,1,0:T(8,128)(2,1)} %copy-done.29), channel_id=1, source_target_pairs={{0,2},{1,3},{2,0},{3,1},{4,6},{5,7},{6,4},{7,5},{8,10},{9,11},{10,... | collective-permute-start | bytes 2359304 | tf_op jit(solution)/shard_map/ppermute | solution.py:420
  141.3 20.7 %copy-start.17 = (bf16[1024,1024]{1,0:T(8,128)(2,1)S(1)}, bf16[1024,1024]{1,0:T(8,128)(2,1)}, u32[]{:S(2)}) copy-start(bf16[1024,1024]{1,0:T(8,128)(2,1)} %constant.47.clone.refs_7_) | copy-start | bytes 6291460
  141.3 20.7 %copy-start.26 = (bf16[2,192,1024]{2,1,0:T(8,128)(2,1)S(1)}, bf16[2,192,1024]{2,1,0:T(8,128)(2,1)}, u32[]{:S(2)}) copy-start(bf16[2,192,1024]{2,1,0:T(8,128)(2,1)} %copy-done.25) | copy-start | bytes 2359300
  143.3 18.7 %collective-permute-start.10 = (bf16[2,192,1024]{2,1,0:T(8,128)(2,1)S(1)}, bf16[2,192,1024]{2,1,0:T(8,128)(2,1)S(1)}, u32[]{:S(2)}, u32[]{:S(2)}) collective-permute-start(bf16[2,192,1024]{2,1,0:T(8,128)(2,1)S(1)} %add_convert_fusion), channel_id=1, source_target_pairs={{0,4},{1,5},{2,6},{3,7},{12,8},{13,9},{14,10},{15,11},{4,0},{5,1},... | collective-permute-start | bytes 2359304 | tf_op jit(solution)/shard_map/ppermute | solution.py:424
  162.1 1.0 copy-start.28
  169.4 4.5 %collective-permute-start.14 = (bf16[2,192,1024]{2,1,0:T(8,128)(2,1)}, bf16[2,192,1024]{2,1,0:T(8,128)(2,1)S(1)}, u32[]{:S(2)}, u32[]{:S(2)}) collective-permute-start(bf16[2,192,1024]{2,1,0:T(8,128)(2,1)} %copy-done.19), channel_id=1, source_target_pairs={{0,1},{1,0},{2,3},{3,2},{4,5},{5,4},{6,7},{7,6},{8,9},{9,8},{10,11... | collective-permute-start | bytes 2359304 | tf_op jit(solution)/shard_map/ppermute | solution.py:417
  170.8 22.2 %collective-permute-start.13 = (bf16[2,192,1024]{2,1,0:T(8,128)(2,1)}, bf16[2,192,1024]{2,1,0:T(8,128)(2,1)}, u32[]{:S(2)}, u32[]{:S(2)}) collective-permute-start(bf16[2,192,1024]{2,1,0:T(8,128)(2,1)} %copy-done.19), channel_id=1, source_target_pairs={{0,2},{1,3},{2,0},{3,1},{4,6},{5,7},{6,4},{7,5},{8,10},{9,11},{10,... | collective-permute-start | bytes 2359304 | tf_op jit(solution)/shard_map/ppermute | solution.py:420
  171.6 29.4 %collective-permute-start.12 = (bf16[2,192,1024]{2,1,0:T(8,128)(2,1)}, bf16[2,192,1024]{2,1,0:T(8,128)(2,1)}, u32[]{:S(2)}, u32[]{:S(2)}) collective-permute-start(bf16[2,192,1024]{2,1,0:T(8,128)(2,1)} %copy-done.19), channel_id=1, source_target_pairs={{4,8},{5,9},{6,10},{7,11},{8,4},{9,5},{10,6},{11,7},{20,24},{21,25... | collective-permute-start | bytes 2359304 | tf_op jit(solution)/shard_map/ppermute | solution.py:424
  173.8 27.3 %collective-permute-start.11 = (bf16[2,192,1024]{2,1,0:T(8,128)(2,1)}, bf16[2,192,1024]{2,1,0:T(8,128)(2,1)}, u32[]{:S(2)}, u32[]{:S(2)}) collective-permute-start(bf16[2,192,1024]{2,1,0:T(8,128)(2,1)} %copy-done.19), channel_id=1, source_target_pairs={{0,4},{1,5},{2,6},{3,7},{12,8},{13,9},{14,10},{15,11},{4,0},{5,1},... | collective-permute-start | bytes 2359304 | tf_op jit(solution)/shard_map/ppermute | solution.py:424
  201.1 35.3 %collective-permute-start.16 = (bf16[2,192,1024]{2,1,0:T(8,128)(2,1)}, bf16[2,192,1024]{2,1,0:T(8,128)(2,1)}, u32[]{:S(2)}, u32[]{:S(2)}) collective-permute-start(bf16[2,192,1024]{2,1,0:T(8,128)(2,1)} %collective-permute-done.12), channel_id=1, source_target_pairs={{4,0},{5,1},{6,2},{7,3},{8,12},{9,13},{10,14},{11,15},{20,16},{21,... | collective-permute-start | bytes 2359304 | tf_op jit(solution)/shard_map/ppermute | solution.py:424
  204.2 32.1 %collective-permute-start.19 = (bf16[2,192,1024]{2,1,0:T(8,128)(2,1)}, bf16[2,192,1024]{2,1,0:T(8,128)(2,1)}, u32[]{:S(2)}, u32[]{:S(2)}) collective-permute-start(bf16[2,192,1024]{2,1,0:T(8,128)(2,1)} %collective-permute-done.13.refs_3_), channel_id=1, source_target_pairs={{0,1},{1,0},{2,3},{3,2},{4,5},{5,4},{6,7},{7,6},{8,9},{9,8},{10,11... | collective-permute-start | bytes 2359304 | tf_op jit(solution)/shard_map/ppermute | solution.py:417
  205.7 30.7 %collective-permute-start.18 = (bf16[2,192,1024]{2,1,0:T(8,128)(2,1)}, bf16[2,192,1024]{2,1,0:T(8,128)(2,1)}, u32[]{:S(2)}, u32[]{:S(2)}) collective-permute-start(bf16[2,192,1024]{2,1,0:T(8,128)(2,1)} %collective-permute-done.11.refs_2_), channel_id=1, source_target_pairs={{0,1},{1,0},{2,3},{3,2},{4,5},{5,4},{6,7},{7,6},{8,9},{9,8},{10,11... | collective-permute-start | bytes 2359304 | tf_op jit(solution)/shard_map/ppermute | solution.py:417
  205.7 30.7 %collective-permute-start.17 = (bf16[2,192,1024]{2,1,0:T(8,128)(2,1)}, bf16[2,192,1024]{2,1,0:T(8,128)(2,1)}, u32[]{:S(2)}, u32[]{:S(2)}) collective-permute-start(bf16[2,192,1024]{2,1,0:T(8,128)(2,1)} %collective-permute-done.11.refs_2_), channel_id=1, source_target_pairs={{0,2},{1,3},{2,0},{3,1},{4,6},{5,7},{6,4},{7,5},{8,10},{9,11},{10,... | collective-permute-start | bytes 2359304 | tf_op jit(solution)/shard_map/ppermute | solution.py:420
  206.6 31.8 %collective-permute-start.15 = (bf16[2,192,1024]{2,1,0:T(8,128)(2,1)}, bf16[2,192,1024]{2,1,0:T(8,128)(2,1)}, u32[]{:S(2)}, u32[]{:S(2)}) collective-permute-start(bf16[2,192,1024]{2,1,0:T(8,128)(2,1)} %collective-permute-done.11.refs_2_), channel_id=1, source_target_pairs={{4,8},{5,9},{6,10},{7,11},{8,4},{9,5},{10,6},{11,7},{20,24},{21,25... | collective-permute-start | bytes 2359304 | tf_op jit(solution)/shard_map/ppermute | solution.py:424
  209.4 1.2 copy-start.4
  210.7 1.1 copy-start.20
  211.8 1.2 copy-start.22
  218.2 3.4 %copy-start.8 = (f32[2,128,8192]{2,1,0:T(8,128)}, f32[2,128,8192]{2,1,0:T(8,128)S(1)}, u32[]{:S(2)}) copy-start(f32[2,128,8192]{2,1,0:T(8,128)S(1)} %backward.4.spec_ref) | copy-start | bytes 25165828
  238.4 6.2 %copy-start.5 = (bf16[1024,512]{1,0:T(8,128)(2,1)S(1)}, bf16[1024,512]{1,0:T(8,128)(2,1)}, u32[]{:S(2)}) copy-start(bf16[1024,512]{1,0:T(8,128)(2,1)} %constant.44.clone.plain_ref) | copy-start | bytes 3145732
  239.7 19.8 %collective-permute-start.22 = (bf16[2,192,1024]{2,1,0:T(8,128)(2,1)S(1)}, bf16[2,192,1024]{2,1,0:T(8,128)(2,1)S(1)}, u32[]{:S(2)}, u32[]{:S(2)}) collective-permute-start(bf16[2,192,1024]{2,1,0:T(8,128)(2,1)S(1)} %broadcast_select_fusion.1.refs_2_), channel_id=1, source_target_pairs={{0,1},{1,0},{2,3},{3,2},{4,5},{5,4},{6,7},{7,6},{8,9},{9,8},{10,11... | collective-permute-start | bytes 2359304 | tf_op jit(solution)/shard_map/ppermute | solution.py:417
  240.4 19.1 %collective-permute-start.21 = (bf16[2,192,1024]{2,1,0:T(8,128)(2,1)S(1)}, bf16[2,192,1024]{2,1,0:T(8,128)(2,1)S(1)}, u32[]{:S(2)}, u32[]{:S(2)}) collective-permute-start(bf16[2,192,1024]{2,1,0:T(8,128)(2,1)S(1)} %broadcast_select_fusion.1.refs_2_), channel_id=1, source_target_pairs={{0,2},{1,3},{2,0},{3,1},{4,6},{5,7},{6,4},{7,5},{8,10},{9,11},{10,... | collective-permute-start | bytes 2359304 | tf_op jit(solution)/shard_map/ppermute | solution.py:420
  241.6 19.1 %collective-permute-start.20 = (bf16[2,192,1024]{2,1,0:T(8,128)(2,1)}, bf16[2,192,1024]{2,1,0:T(8,128)(2,1)S(1)}, u32[]{:S(2)}, u32[]{:S(2)}) collective-permute-start(bf16[2,192,1024]{2,1,0:T(8,128)(2,1)} %collective-permute-done.15), channel_id=1, source_target_pairs={{4,0},{5,1},{6,2},{7,3},{8,12},{9,13},{10,14},{11,15},{20,16},{21,... | collective-permute-start | bytes 2359304 | tf_op jit(solution)/shard_map/ppermute | solution.py:424
  243.9 16.8 %collective-permute-start.23 = (bf16[2,192,1024]{2,1,0:T(8,128)(2,1)}, bf16[2,192,1024]{2,1,0:T(8,128)(2,1)S(1)}, u32[]{:S(2)}, u32[]{:S(2)}) collective-permute-start(bf16[2,192,1024]{2,1,0:T(8,128)(2,1)} %collective-permute-done.17.refs_3_), channel_id=1, source_target_pairs={{0,1},{1,0},{2,3},{3,2},{4,5},{5,4},{6,7},{7,6},{8,9},{9,8},{10,11... | collective-permute-start | bytes 2359304 | tf_op jit(solution)/shard_map/ppermute | solution.py:417
  244.6 2.2 copy-start.6
  246.7 17.0 %copy-start.7 = (bf16[32,64,1024]{2,1,0:T(8,128)(2,1)S(1)}, bf16[32,64,1024]{2,1,0:T(8,128)(2,1)}, u32[]{:S(2)}) copy-start(bf16[32,64,1024]{2,1,0:T(8,128)(2,1)} %all-gather.3.cloned.1.call-done) | copy-start | bytes 12582916
  256.1 3.4 %copy-start.9 = (f32[2,128,8192]{2,1,0:T(8,128)}, f32[2,128,8192]{2,1,0:T(8,128)S(1)}, u32[]{:S(2)}) copy-start(f32[2,128,8192]{2,1,0:T(8,128)S(1)} %backward.5.spec_ref) | copy-start | bytes 25165828
  261.9 11.1 %collective-permute-start.25 = (bf16[2,192,1024]{2,1,0:T(8,128)(2,1)S(1)}, bf16[2,192,1024]{2,1,0:T(8,128)(2,1)S(1)}, u32[]{:S(2)}, u32[]{:S(2)}) collective-permute-start(bf16[2,192,1024]{2,1,0:T(8,128)(2,1)S(1)} %broadcast_select_fusion.refs_2_), channel_id=1, source_target_pairs={{0,1},{1,0},{2,3},{3,2},{4,5},{5,4},{6,7},{7,6},{8,9},{9,8},{10,11... | collective-permute-start | bytes 2359304 | tf_op jit(solution)/shard_map/ppermute | solution.py:417
  263.2 19.1 %collective-permute-start.24 = (bf16[2,192,1024]{2,1,0:T(8,128)(2,1)S(1)}, bf16[2,192,1024]{2,1,0:T(8,128)(2,1)S(1)}, u32[]{:S(2)}, u32[]{:S(2)}) collective-permute-start(bf16[2,192,1024]{2,1,0:T(8,128)(2,1)S(1)} %broadcast_select_fusion.refs_2_), channel_id=1, source_target_pairs={{0,2},{1,3},{2,0},{3,1},{4,6},{5,7},{6,4},{7,5},{8,10},{9,11},{10,... | collective-permute-start | bytes 2359304 | tf_op jit(solution)/shard_map/ppermute | solution.py:420
  263.4 18.8 %collective-permute-start.26 = (bf16[2,192,1024]{2,1,0:T(8,128)(2,1)S(1)}, bf16[2,192,1024]{2,1,0:T(8,128)(2,1)S(1)}, u32[]{:S(2)}, u32[]{:S(2)}) collective-permute-start(bf16[2,192,1024]{2,1,0:T(8,128)(2,1)S(1)} %collective-permute-done.21.refs_3_), channel_id=1, source_target_pairs={{0,1},{1,0},{2,3},{3,2},{4,5},{5,4},{6,7},{7,6},{8,9},{9,8},{10,11... | collective-permute-start | bytes 2359304 | tf_op jit(solution)/shard_map/ppermute | solution.py:417
  269.6 3.4 %copy-start.10 = (f32[2,128,8192]{2,1,0:T(8,128)}, f32[2,128,8192]{2,1,0:T(8,128)S(1)}, u32[]{:S(2)}) copy-start(f32[2,128,8192]{2,1,0:T(8,128)S(1)} %backward.6.spec_ref) | copy-start | bytes 25165828
  282.3 2.8 collective-permute-start.27
  285.0 3.4 %copy-start.11 = (f32[2,128,8192]{2,1,0:T(8,128)S(1)}, f32[2,128,8192]{2,1,0:T(8,128)}, u32[]{:S(2)}) copy-start(f32[2,128,8192]{2,1,0:T(8,128)} %copy-done.10) | copy-start | bytes 25165828
  (4 other events, 3.5 us)
Sparse Core Ops, SparseCore 0:
  48.8 82.5 reduce-scatter.1
  169.6 67.2 all-gather.2

commit v2 on v0

--- a/solution.py
+++ b/solution.py
@@ -65,17 +65,16 @@
         return (first_row > -self.tile_rows) & (first_row < self.crop_width)
 
 
-def image_band(meta_ref, slot, lows, pupil_ref, band_ref, win, store):
-    halves = len(lows)
-    left = meta_ref[halves, slot]
-    first_rows = [meta_ref[half, slot] for half in range(halves)]
+def image_band(meta_ref, slot, lows, tiles, pupil_ref, band_ref, win, store, came=None):
+    left = meta_ref[meta_ref.shape[0] - 1, slot]
+    first_rows = [meta_ref[tile, slot] for tile in tiles]
     active = functools.reduce(jnp.logical_or, [win.active(row) for row in first_rows])
     band = band_ref.shape[1] // 2
     shape = (2, band, win.crop_width)
 
     @pl.when(jnp.logical_not(active))
     def _():
-        store(jnp.zeros(shape, jnp.bfloat16))
+        store(jnp.zeros(shape, jnp.bfloat16) if came is None else came[...])
 
     @pl.when(active)
     def _():
@@ -95,12 +94,15 @@
             (((0,), (0,)), ((), ())),
             preferred_element_type=jnp.float32,
         )
+        if came is not None:
+            mid = mid + came[...].reshape(mid.shape).astype(jnp.float32)
         store(mid.astype(jnp.bfloat16).reshape(shape))
 
 
-def forward_kernel(meta_ref, pupil_ref, band_ref, *refs, base, win, halves):
-    low_refs, out_refs = refs[: 2 * halves], refs[2 * halves :]
-    lows = [low_refs[2 * half : 2 * half + 2] for half in range(halves)]
+def forward_kernel(meta_ref, pupil_ref, band_ref, *refs, base, count, win, tiles):
+    out_refs = refs[-count:]
+    lows = [refs[2 * half : 2 * half + 2] for half in range(len(tiles))]
+    came = refs[2 * len(tiles)] if len(refs) > 2 * len(tiles) + count else None
 
     def image(index):
         def store(value):
@@ -110,7 +112,7 @@
                 def _():
                     out_ref[...] = value
 
-        image_band(meta_ref, base + index, lows, pupil_ref, band_ref, win, store)
+        image_band(meta_ref, base + index, lows, tiles, pupil_ref, band_ref, win, store, came)
 
     pl.loop(0, len(out_refs))(image)
 
@@ -120,7 +122,7 @@
         out_ref[0] = value
 
     lows = [(real_ref, imag_ref)]
-    image_band(meta_ref, pl.program_id(0), lows, pupil_ref, band_ref, win, store)
+    image_band(meta_ref, pl.program_id(0), lows, (0,), pupil_ref, band_ref, win, store)
 
 
 def subtract_image(meta_ref, slot, back_ref, pupil_ref, band_ref, out_ref, win):
@@ -202,11 +204,12 @@
     return jax.ShapeDtypeStruct(shape, jnp.bfloat16)
 
 
-def forward(meta, lows, pupil, band_table, base, count):
+def forward(meta, lows, pupil, band_table, base, count, tiles=(0, 1), came=None):
     win = Windows(*lows[0][0].shape, pupil.shape[1])
     operands = [meta, pupil, band_table] + [part for low in lows for part in low]
-    return pl.pallas_call(
-        functools.partial(forward_kernel, base=base, win=win, halves=len(lows)),
+    operands += [came] * (came is not None)
+    return pl.pallas_call(
+        functools.partial(forward_kernel, base=base, count=count, win=win, tiles=tiles),
         in_specs=[smem] + [vmem] * (len(operands) - 1),
         out_specs=[vmem] * count,
         out_shape=[band_type(pupil, band_table)] * count,
@@ -277,19 +280,31 @@
     )(meta, pupil, band_table, spectrum, backs)
 
 
-def cast_kernel(spec_ref, out_ref):
-    out_ref[...] = spec_ref[0].astype(jnp.bfloat16)
+def cast_kernel(spec_ref, out_ref, held, sems, *, part):
+    blocks, _, width = held.shape
+    columns = [pl.ds(block * width, width) for block in range(blocks)]
+    copies = [
+        pltpu.make_async_copy(spec_ref.at[part, :, columns[i]], held.at[i], sems.at[i])
+        for i in range(blocks)
+    ]
+    for copy in copies:
+        copy.start()
+    for i, copy in enumerate(copies):
+        copy.wait()
+        out_ref[:, columns[i]] = held[i].astype(jnp.bfloat16)
 
 
 def low_part(spectrum, part):
     _, rows, columns = spectrum.shape
-    block = columns // 4
-    return pl.pallas_call(
-        cast_kernel,
-        grid=(4,),
-        in_specs=[pl.BlockSpec((1, rows, block), lambda i: (part, 0, i))],
-        out_specs=pl.BlockSpec((rows, block), lambda i: (0, i)),
+    return pl.pallas_call(
+        functools.partial(cast_kernel, part=part),
+        in_specs=[pl.BlockSpec(memory_space=pltpu.HBM)],
+        out_specs=vmem,
         out_shape=jax.ShapeDtypeStruct((rows, columns), jnp.bfloat16),
+        scratch_shapes=[
+            pltpu.VMEM((4, rows, columns // 4), jnp.float32),
+            pltpu.SemaphoreType.DMA((4,)),
+        ],
         compiler_params=params(),
         cost_estimate=light(),
         name="low_part",
@@ -364,7 +379,8 @@
     together = lax.optimization_barrier
 
     lows = [low, [sibling(part) for part in low]]
-    (far_leaving,) = forward(meta, lows, pupil, band_table, 0, 1)
+    (far_leaving,) = forward(meta, lows[:1], pupil, band_table, 0, 1, (0,))
+    (far_leaving,) = forward(meta, lows[1:], pupil, band_table, 0, 1, (1,), far_leaving)
     far_other = across(far_leaving)
     (
         far_kept,
@@ -400,68 +416,63 @@
             meta, result, pupil, band_table, [slots[name] for name in names], list(values)
         )
 
+    other = across(back)
+    from_inner = along(back, inner)
     from_beside = along(back, inward + outward)
-    from_inner = along(back, inner)
-    other = across(back)
-    twin = sibling(back)
-    from_beside, from_inner, other, twin, back = together(
-        (from_beside, from_inner, other, twin, back)
-    )
-
+    other, from_inner, from_beside, back = together((other, from_inner, from_beside, back))
+
+    twin, beside_twin = sibling(back), sibling(from_beside)
+    beside_other = across(from_beside)
     far_inner = along(from_beside, inner)
     next_outward = along(from_inner, outward)
-    beside_other = across(from_beside)
-    beside_twin, other_twin = sibling(from_beside), sibling(other)
     result = apply(
-        spectrum,
-        [(("own", 0), back), (("own", 1), twin), (("beside", 0), from_beside), (("own", 2), other)],
-    )
-    far_inner, next_outward, beside_other, beside_twin, other_twin, result = together(
-        (far_inner, next_outward, beside_other, beside_twin, other_twin, result)
+        spectrum, [(("own", 0), back), (("beside", 0), from_beside), (("own", 2), other)]
+    )
+    twin, beside_twin, beside_other, far_inner, next_outward, other, result = together(
+        (twin, beside_twin, beside_other, far_inner, next_outward, other, result)
     )
 
     at_ends = (plane == 0) | (plane == 3)
+    from_next = jnp.where(at_ends, next_outward, from_inner)
+    other_twin, next_twin = sibling(other), sibling(from_next)
+    next_other = across(from_next)
     far_outward = along(far_inner, outward)
-    from_next = jnp.where(at_ends, next_outward, from_inner)
-    next_other = across(from_next)
-    next_twin, beside_other_twin = sibling(from_next), sibling(beside_other)
     result = apply(
         result,
         [
+            (("own", 1), twin),
             (("beside", 1), beside_twin),
-            (("own", 3), other_twin),
             (("next", 0), from_next),
             (("beside", 2), beside_other),
         ],
     )
-    far_outward, next_other, next_twin, beside_other_twin, result = together(
-        (far_outward, next_other, next_twin, beside_other_twin, result)
+    other_twin, next_twin, next_other, far_outward, beside_other, result = together(
+        (other_twin, next_twin, next_other, far_outward, beside_other, result)
     )
 
     from_far = jnp.where(at_ends, far_outward, far_inner)
+    beside_other_twin, far_twin = sibling(beside_other), sibling(from_far)
+    next_other_twin = sibling(next_other)
     far_other = across(from_far)
-    far_twin, next_other_twin = sibling(from_far), sibling(next_other)
     result = apply(
         result,
         [
+            (("own", 3), other_twin),
             (("next", 1), next_twin),
-            (("beside", 3), beside_other_twin),
             (("far", 0), from_far),
             (("next", 2), next_other),
         ],
     )
-    far_other, far_twin, next_other_twin, result = together(
-        (far_other, far_twin, next_other_twin, result)
-    )
-    return apply(
+    result = apply(
         result,
         [
+            (("beside", 3), beside_other_twin),
             (("far", 1), far_twin),
             (("next", 3), next_other_twin),
-            (("far", 2), far_other),
-            (("far", 3), sibling(far_other)),
         ],
     )
+    far_other, result = together((far_other, result))
+    return apply(result, [(("far", 2), far_other), (("far", 3), sibling(far_other))])
 
 
 def solution(mesh):

time: 259 us -> 254 us (0.981)
  waiting for transfers between devices: 145 us -> 128 us
  Pallas kernels: 55.3 us -> 63.6 us
    ppermute x8, waiting for transfers between devices: 63.7 us -> 27.9 us  [across(): return lax.ppermute(value, 'ty', [(i, i ^ 2) for i in range(count)])]
    ppermute x10, waiting for transfers between devices: 74.7 us -> 96.9 us  [along(): return lax.ppermute(value, 'ty', pairs)]
    pallas_call x4 -> x5, Pallas kernels: 26.3 us -> 31 us  [backward(): pl.pallas_call(functools.partial(backward_kernel, slots=slots, win=win),...]
    ppermute x10, waiting for transfers between devices: 6.41 us -> 3.21 us  [sibling(): return lax.ppermute(value, 'ty', [(i, i ^ 1) for i in range(count)])]
    pallas_call x4 -> x5, Pallas kernels: 24.1 us -> 26.7 us  [the longest x3 23 us: forward(): pl.pallas_call(functools.partial(forward_kernel, base=base, count=count,...]
    unnamed x28 -> x26, local copies, waits for them, and re-layouts: 14.6 us -> 15.8 us
  transfers between devices with their start and end apart: 28 -> 28, of which waited for: 18 -> 19; matrix products, arithmetic and copies ran while one was open for 1% -> 1% of each run, Pallas kernels for 14% -> 18%
where the time goes in v2:
time: 254 us; the launch traced here: 251 us
  waiting for transfers between devices  128 us (50%)
  Pallas kernels  63.6 us (25%)
  starting transfers between devices  36.9 us (15%)
  local copies, waits for them, and re-layouts  16.5 us (6%)
  other arithmetic  5.58 us (2%)
    ppermute x10, waiting for transfers between devices, along(): return lax.ppermute(value, 'ty', pairs)  96.9 us
    pallas_call x5, Pallas kernels, backward(): pl.pallas_call(functools.partial(backward_kernel, slots=slots, win=win),...  31 us
    ppermute x8, waiting for transfers between devices, across(): return lax.ppermute(value, 'ty', [(i, i ^ 2) for i in range(count)])  27.9 us
    pallas_call x3, Pallas kernels, forward(): pl.pallas_call(functools.partial(forward_kernel, base=base, count=count,...  23 us
    ppermute x10, starting transfers between devices, along(): return lax.ppermute(value, 'ty', pairs)  17.9 us
    unnamed x26, local copies, waits for them, and re-layouts  15.8 us
    ppermute x10, starting transfers between devices, sibling(): return lax.ppermute(value, 'ty', [(i, i ^ 1) for i in range(count)])  11.5 us
    ppermute x8, starting transfers between devices, across(): return lax.ppermute(value, 'ty', [(i, i ^ 2) for i in range(count)])  7.48 us
  transfers between devices with their start and end apart: 28, of which 19 were waited for; matrix products, arithmetic and copies ran while one was open for 1% of the time, Pallas kernels for 18%

profile of v2, /device:TPU:11, one launch (start us, length us, event | category | flops | bytes accessed | tf_op | source)
XLA Modules:
  0.0 250.9 jit_solution(13266144367736883029)
XLA Ops:
  0.0 3.4 %copy-done.1 = f32[2,128,8192]{2,1,0:T(8,128)S(1)} copy-done((f32[2,128,8192]{2,1,0:T(8,128)S(1)}, f32[2,128,8192]{2,1,0:T(8,128)}, u32[]{:S(2)}) %copy-start.1) | copy-done | bytes 8388632
  3.4 1.9 low_part.3.refs_1_
  5.3 0.7 collective-permute-start.1
  6.1 1.8 low_part.2.refs_0_
  8.0 0.7 dynamic-slice_bitcast_fusion
  9.0 3.3 %forward.3.refs_2_ = bf16[2,256,1024]{2,1,0:T(8,128)(2,1)S(1)} custom-call(s32[3,16]{1,0:T(4,128)S(1)} %pad_add_fusion.meta_ref, bf16[1024,1024]{1,0:T(8,128)(2,1)S(1)} %copy-done, bf16[1024,512]{1,0:T(8,128)(2,1)S(1)} %copy-done.2, bf16[128,8192]{1,0:T(8,128)(2,1)} %low_part.2.refs_0_, bf16[128,8192]{1,0:T(8,128)(2,1)} %low_part.3.refs_1_), custom_call_target="tpu_custom_call" | custom-call | flops 1024 | bytes 1024 | tf_op jit(solution)/shard_map/forward/pallas_call | solution.py:211
  12.3 0.9 collective-permute-done.refs_0_.refs_2_
  13.2 3.3 %forward.4 = bf16[2,256,1024]{2,1,0:T(8,128)(2,1)S(1)} custom-call(s32[3,16]{1,0:T(4,128)S(1)} %pad_add_fusion.meta_ref, bf16[1024,1024]{1,0:T(8,128)(2,1)S(1)} %copy-done, bf16[1024,512]{1,0:T(8,128)(2,1)S(1)} %copy-done.2, bf16[128,8192]{1,0:T(8,128)(2,1)} %collective-permute-done.refs_0_.refs_2_, ...), custom_call_target="tpu_custom_call" | custom-call | flops 1024 | bytes 1024 | tf_op jit(solution)/shard_map/forward/pallas_call | solution.py:211
  16.5 1.3 collective-permute-start.2
  17.8 16.4 %forward.5 = (bf16[2,256,1024]{2,1,0:T(8,128)(2,1)S(1)}, bf16[2,256,1024]{2,1,0:T(8,128)(2,1)S(1)}, bf16[2,256,1024]{2,1,0:T(8,128)(2,1)S(1)}, bf16[2,256,1024]{...) custom-call(s32[3,16]{1,0:T(4,128)S(1)} %pad_add_fusion.meta_ref, ...), custom_call_target="tpu_custom_call" | custom-call | flops 1024 | bytes 1024 | tf_op jit(solution)/shard_map/forward/pallas_call | solution.py:211
  34.2 6.7 %collective-permute-done.2 = bf16[2,256,1024]{2,1,0:T(8,128)(2,1)S(1)} collective-permute-done((bf16[2,256,1024]{2,1,0:T(8,128)(2,1)S(1)}, bf16[2,256,1024]{2,1,0:T(8,128)(2,1)S(1)}, u32[]{:S(2)}, u32[]{:S(2)}) %collective-permute-start.2) | collective-permute-done | bytes 1048608 | tf_op jit(solution)/shard_map/ppermute | solution.py:370
  41.0 0.4 fusion
  41.4 1.3 collective-permute-start.3
  42.7 1.3 collective-permute-start.4
  44.0 22.7 %collective-permute-done.3 = bf16[2,256,1024]{2,1,0:T(8,128)(2,1)S(1)} collective-permute-done((bf16[2,256,1024]{2,1,0:T(8,128)(2,1)S(1)}, bf16[2,256,1024]{2,1,0:T(8,128)(2,1)S(1)}, u32[]{:S(2)}, u32[]{:S(2)}) %collective-permute-start.3) | collective-permute-done | bytes 1048608 | tf_op jit(solution)/shard_map/ppermute | solution.py:374
  66.7 0.6 add_convert_fusion.2
  67.3 0.4 fusion.1
  67.7 1.3 collective-permute-start.6
  69.0 3.2 %collective-permute-start.5 = (bf16[2,256,1024]{2,1,0:T(8,128)(2,1)S(1)}, bf16[2,256,1024]{2,1,0:T(8,128)(2,1)S(1)}, u32[]{:S(2)}, u32[]{:S(2)}) collective-permute-start(bf16[2,256,1024]{2,1,0:T(8,128)(2,1)S(1)} %add_convert_fusion.2), channel_id=1, source_target_pairs={{4,8},{5,9},{6,10},{7,11},{8,4},{9,5},{10,6},{11,7},{20,24},{21,25... | collective-permute-start | bytes 3145736 | tf_op jit(solution)/shard_map/ppermute | solution.py:374
  72.4 19.8 %collective-permute-done.6 = bf16[2,256,1024]{2,1,0:T(8,128)(2,1)S(1)} collective-permute-done((bf16[2,256,1024]{2,1,0:T(8,128)(2,1)S(1)}, bf16[2,256,1024]{2,1,0:T(8,128)(2,1)S(1)}, u32[]{:S(2)}, u32[]{:S(2)}) %collective-permute-start.6) | collective-permute-done | bytes 1048608 | tf_op jit(solution)/shard_map/ppermute | solution.py:374
  92.2 1.3 collective-permute-done.5
  93.5 1.1 collective-permute-done.7
  94.6 0.6 add_convert_fusion.1
  95.2 2.3 collective-permute-start.9
  97.5 1.3 collective-permute-start.8
  98.8 0.6 add_convert_fusion
  99.5 18.9 %collective-permute-done.9.refs_2_ = bf16[2,256,1024]{2,1,0:T(8,128)(2,1)S(1)} collective-permute-done((bf16[2,256,1024]{2,1,0:T(8,128)(2,1)S(1)}, bf16[2,256,1024]{2,1,0:T(8,128)(2,1)S(1)}, u32[]{:S(2)}, u32[]{:S(2)}) %collective-permute-start.9) | collective-permute-done | bytes 1048608 | tf_op jit(solution)/shard_map/ppermute | solution.py:374
  118.7 1.6 collective-permute-done.10.refs_3_
  120.3 5.9 %middle.1.refs_0_ = bf16[2,256,1024]{2,1,0:T(8,128)(2,1)} custom-call(bf16[2,256,1024]{2,1,0:T(8,128)(2,1)S(1)} %get-tuple-element.43.refs_0_, bf16[2,256,1024]{2,1,0:T(8,128)(2,1)S(1)} %collective-permute-done.8.refs_1_, bf16[2,256,1024]{2,1,0:T(8,128)(2,1)S(1)} %collective-permute-done.9.refs_2_, ...), custom_call_target="tpu_custom_call" | custom-call | flops 1024 | bytes 1024 | tf_op jit(solution)/shard_map/middle/pallas_call | solution.py:237
  126.5 2.5 collective-permute-start.12
  129.0 1.0 collective-permute-start.11
  129.9 16.4 %collective-permute-done.13.refs_1_ = bf16[2,256,1024]{2,1,0:T(8,128)(2,1)} collective-permute-done((bf16[2,256,1024]{2,1,0:T(8,128)(2,1)}, bf16[2,256,1024]{2,1,0:T(8,128)(2,1)}, u32[]{:S(2)}, u32[]{:S(2)}) %collective-permute-start.13) | collective-permute-done | bytes 1048608 | tf_op jit(solution)/shard_map/ppermute | solution.py:374
  146.3 2.2 collective-permute-done.12
  148.5 0.7 collective-permute-done.11.refs_2_
  149.2 1.0 copy-done.8
  150.2 5.6 %collective-permute-start.14 = (bf16[2,256,1024]{2,1,0:T(8,128)(2,1)}, bf16[2,256,1024]{2,1,0:T(8,128)(2,1)}, u32[]{:S(2)}, u32[]{:S(2)}) collective-permute-start(bf16[2,256,1024]{2,1,0:T(8,128)(2,1)} %middle.1.refs_0_), channel_id=1, source_target_pairs={{0,1},{1,0},{2,3},{3,2},{4,5},{5,4},{6,7},{7,6},{8,9},{9,8},{10,11... | collective-permute-start | bytes 3145736 | tf_op jit(solution)/shard_map/ppermute | solution.py:367
  155.8 3.1 %collective-permute-start.18 = (bf16[2,256,1024]{2,1,0:T(8,128)(2,1)}, bf16[2,256,1024]{2,1,0:T(8,128)(2,1)}, u32[]{:S(2)}, u32[]{:S(2)}) collective-permute-start(bf16[2,256,1024]{2,1,0:T(8,128)(2,1)} %collective-permute-done.12), channel_id=1, source_target_pairs={{4,0},{5,1},{6,2},{7,3},{8,12},{9,13},{10,14},{11,15},{20,16},{21,... | collective-permute-start | bytes 3145736 | tf_op jit(solution)/shard_map/ppermute | solution.py:374
  158.9 2.5 collective-permute-start.17
  161.4 1.0 collective-permute-start.16
  162.4 0.8 collective-permute-start.15
  163.2 1.2 copy-done.9
  164.5 6.9 %backward.5.spec_ref = f32[2,128,8192]{2,1,0:T(8,128)S(1)} custom-call(s32[3,16]{1,0:T(4,128)S(1)} %pad_add_fusion.meta_ref, bf16[1024,1024]{1,0:T(8,128)(2,1)S(1)} %copy-done, bf16[1024,512]{1,0:T(8,128)(2,1)S(1)} %copy-done.2, f32[2,128,8192]{2,1,0:T(8,128)} %spec_ref.5, bf16[2,256,1024]{2,1,0:T(8,128)(2,1)} %middle.1.refs_0_, ...), custom_call_target="tpu_custom_call" | custom-call | flops 1024 | bytes 1024 | tf_op jit(solution)/shard_map/backward/pallas_call | solution.py:224
  171.4 3.4 %copy-done.4 = f32[2,128,8192]{2,1,0:T(8,128)} copy-done((f32[2,128,8192]{2,1,0:T(8,128)}, f32[2,128,8192]{2,1,0:T(8,128)S(1)}, u32[]{:S(2)}) %copy-start.4) | copy-done | bytes 8388632
  174.8 6.0 %collective-permute-done.18 = bf16[2,256,1024]{2,1,0:T(8,128)(2,1)} collective-permute-done((bf16[2,256,1024]{2,1,0:T(8,128)(2,1)}, bf16[2,256,1024]{2,1,0:T(8,128)(2,1)}, u32[]{:S(2)}, u32[]{:S(2)}) %collective-permute-start.18) | collective-permute-done | bytes 1048608 | tf_op jit(solution)/shard_map/ppermute | solution.py:374
  180.8 4.7 %collective-permute-done.17 = bf16[2,256,1024]{2,1,0:T(8,128)(2,1)} collective-permute-done((bf16[2,256,1024]{2,1,0:T(8,128)(2,1)}, bf16[2,256,1024]{2,1,0:T(8,128)(2,1)}, u32[]{:S(2)}, u32[]{:S(2)}) %collective-permute-start.17) | collective-permute-done | bytes 1048608 | tf_op jit(solution)/shard_map/ppermute | solution.py:374
  186.0 1.3 broadcast_select_fusion.1.refs_2_
  187.3 1.0 collective-permute-start.21
  188.3 1.7 collective-permute-start.20
  190.0 1.3 collective-permute-start.22
  191.3 7.5 %backward.6.spec_ref = f32[2,128,8192]{2,1,0:T(8,128)S(1)} custom-call(s32[3,16]{1,0:T(4,128)S(1)} %pad_add_fusion.meta_ref, bf16[1024,1024]{1,0:T(8,128)(2,1)S(1)} %copy-done, bf16[1024,512]{1,0:T(8,128)(2,1)S(1)} %copy-done.2, f32[2,128,8192]{2,1,0:T(8,128)} %copy-done.4, bf16[2,256,1024]{2,1,0:T(8,128)(2,1)} %collective-permute-done.14.refs_0_, ...), custom_call_target="tpu_custom_call" | custom-call | flops 1024 | bytes 1024 | tf_op jit(solution)/shard_map/backward/pallas_call | solution.py:224
  198.9 3.4 %copy-done.3 = f32[2,128,8192]{2,1,0:T(8,128)} copy-done((f32[2,128,8192]{2,1,0:T(8,128)}, f32[2,128,8192]{2,1,0:T(8,128)S(1)}, u32[]{:S(2)}) %copy-start.3) | copy-done | bytes 8388632
  202.2 8.4 %collective-permute-done.21.refs_3_ = bf16[2,256,1024]{2,1,0:T(8,128)(2,1)S(1)} collective-permute-done((bf16[2,256,1024]{2,1,0:T(8,128)(2,1)S(1)}, bf16[2,256,1024]{2,1,0:T(8,128)(2,1)S(1)}, u32[]{:S(2)}, u32[]{:S(2)}) %collective-permute-start.21) | collective-permute-done | bytes 1048608 | tf_op jit(solution)/shard_map/ppermute | solution.py:370
  210.6 3.3 %collective-permute-done.22 = bf16[2,256,1024]{2,1,0:T(8,128)(2,1)S(1)} collective-permute-done((bf16[2,256,1024]{2,1,0:T(8,128)(2,1)}, bf16[2,256,1024]{2,1,0:T(8,128)(2,1)S(1)}, u32[]{:S(2)}, u32[]{:S(2)}) %collective-permute-start.22) | collective-permute-done | bytes 1048608 | tf_op jit(solution)/shard_map/ppermute | solution.py:374
  213.9 1.3 broadcast_select_fusion.refs_2_
  215.2 1.1 collective-permute-start.25
  216.4 0.4 collective-permute-start.26
  216.9 0.6 collective-permute-start.23
  217.4 5.6 %backward.7.spec_ref = f32[2,128,8192]{2,1,0:T(8,128)S(1)} custom-call(s32[3,16]{1,0:T(4,128)S(1)} %pad_add_fusion.meta_ref, bf16[1024,1024]{1,0:T(8,128)(2,1)S(1)} %copy-done, bf16[1024,512]{1,0:T(8,128)(2,1)S(1)} %copy-done.2, f32[2,128,8192]{2,1,0:T(8,128)} %copy-done.3, bf16[2,256,1024]{2,1,0:T(8,128)(2,1)S(1)} %collective-permute-done.19.refs_0_, ...), custom_call_target="tpu_custom_call" | custom-call | flops 1024 | bytes 1024 | tf_op jit(solution)/shard_map/backward/pallas_call | solution.py:224
  223.1 3.4 %copy-done.5 = f32[2,128,8192]{2,1,0:T(8,128)} copy-done((f32[2,128,8192]{2,1,0:T(8,128)}, f32[2,128,8192]{2,1,0:T(8,128)S(1)}, u32[]{:S(2)}) %copy-start.5) | copy-done | bytes 8388632
  226.5 4.8 %backward.8.spec_ref = f32[2,128,8192]{2,1,0:T(8,128)S(1)} custom-call(s32[3,16]{1,0:T(4,128)S(1)} %pad_add_fusion.meta_ref, bf16[1024,1024]{1,0:T(8,128)(2,1)S(1)} %copy-done, bf16[1024,512]{1,0:T(8,128)(2,1)S(1)} %copy-done.2, f32[2,128,8192]{2,1,0:T(8,128)} %copy-done.5, bf16[2,256,1024]{2,1,0:T(8,128)(2,1)S(1)} %collective-permute-done.24.refs_0_, ...), custom_call_target="tpu_custom_call" | custom-call | flops 1024 | bytes 1024 | tf_op jit(solution)/shard_map/backward/pallas_call | solution.py:224
  231.3 10.3 %collective-permute-done.23.refs_0_ = bf16[2,256,1024]{2,1,0:T(8,128)(2,1)S(1)} collective-permute-done((bf16[2,256,1024]{2,1,0:T(8,128)(2,1)S(1)}, bf16[2,256,1024]{2,1,0:T(8,128)(2,1)S(1)}, u32[]{:S(2)}, u32[]{:S(2)}) %collective-permute-start.23) | collective-permute-done | bytes 1048608 | tf_op jit(solution)/shard_map/ppermute | solution.py:370
  241.6 0.8 collective-permute-start.27
  242.4 2.3 collective-permute-done.27.refs_1_
  244.7 6.2 %backward.9 = f32[2,128,8192]{2,1,0:T(8,128)} custom-call(s32[3,16]{1,0:T(4,128)S(1)} %pad_add_fusion.meta_ref, bf16[1024,1024]{1,0:T(8,128)(2,1)S(1)} %copy-done, bf16[1024,512]{1,0:T(8,128)(2,1)S(1)} %copy-done.2, f32[2,128,8192]{2,1,0:T(8,128)S(1)} %backward.8.spec_ref, bf16[2,256,1024]{2,1,0:T(8,128)(2,1)S(1)} %collective-permute-done.23.refs_0_, ...), custom_call_target="tpu_custom_call" | custom-call | flops 1024 | bytes 1024 | tf_op jit(solution)/shard_map/backward/pallas_call | solution.py:224
  (41 shorter events, 1.5 us)
Async XLA Ops:
  0.0 3.4 %copy-start.1 = (f32[2,128,8192]{2,1,0:T(8,128)S(1)}, f32[2,128,8192]{2,1,0:T(8,128)}, u32[]{:S(2)}) copy-start(f32[2,128,8192]{2,1,0:T(8,128)} %spec_ref.5) | copy-start | bytes 25165828
  5.3 3.4 %copy-start.11 = (s32[16]{0:T(128)S(1)}, s32[16]{0:T(128)}, u32[]{:S(2)}) copy-start(s32[16]{0:T(128)} %param.12) | copy-start | bytes 196
  5.3 3.4 %copy-start.12 = (s32[16]{0:T(128)S(1)}, s32[16]{0:T(128)}, u32[]{:S(2)}) copy-start(s32[16]{0:T(128)} %param.13) | copy-start | bytes 196
  5.3 3.6 %copy-start = (bf16[1024,1024]{1,0:T(8,128)(2,1)S(1)}, bf16[1024,1024]{1,0:T(8,128)(2,1)}, u32[]{:S(2)}) copy-start(bf16[1024,1024]{1,0:T(8,128)(2,1)} %pupil_ref.15) | copy-start | bytes 6291460
  5.3 3.6 %copy-start.2 = (bf16[1024,512]{1,0:T(8,128)(2,1)S(1)}, bf16[1024,512]{1,0:T(8,128)(2,1)}, u32[]{:S(2)}) copy-start(bf16[1024,512]{1,0:T(8,128)(2,1)} %constant.42.clone.band_ref) | copy-start | bytes 3145732
  5.3 7.0 %collective-permute-start.1 = (bf16[128,8192]{1,0:T(8,128)(2,1)}, bf16[128,8192]{1,0:T(8,128)(2,1)}, u32[]{:S(2)}, u32[]{:S(2)}) collective-permute-start(bf16[128,8192]{1,0:T(8,128)(2,1)} %low_part.3.refs_1_), channel_id=1, source_target_pairs={{0,1},{1,0},{2,3},{3,2},{4,5},{5,4},{6,7},{7,6},{8,9},{9,8},{10,11... | collective-permute-start | bytes 6291464 | tf_op jit(solution)/shard_map/ppermute | solution.py:367
  7.9 5.3 %collective-permute-start = (bf16[128,8192]{1,0:T(8,128)(2,1)}, bf16[128,8192]{1,0:T(8,128)(2,1)}, u32[]{:S(2)}, u32[]{:S(2)}) collective-permute-start(bf16[128,8192]{1,0:T(8,128)(2,1)} %low_part.2.refs_0_), channel_id=1, source_target_pairs={{0,1},{1,0},{2,3},{3,2},{4,5},{5,4},{6,7},{7,6},{8,9},{9,8},{10,11... | collective-permute-start | bytes 6291464 | tf_op jit(solution)/shard_map/ppermute | solution.py:367
  16.5 24.4 %collective-permute-start.2 = (bf16[2,256,1024]{2,1,0:T(8,128)(2,1)S(1)}, bf16[2,256,1024]{2,1,0:T(8,128)(2,1)S(1)}, u32[]{:S(2)}, u32[]{:S(2)}) collective-permute-start(bf16[2,256,1024]{2,1,0:T(8,128)(2,1)S(1)} %forward.4), channel_id=1, source_target_pairs={{0,2},{1,3},{2,0},{3,1},{4,6},{5,7},{6,4},{7,5},{8,10},{9,11},{10,... | collective-permute-start | bytes 3145736 | tf_op jit(solution)/shard_map/ppermute | solution.py:370
  41.4 25.3 %collective-permute-start.3 = (bf16[2,256,1024]{2,1,0:T(8,128)(2,1)S(1)}, bf16[2,256,1024]{2,1,0:T(8,128)(2,1)S(1)}, u32[]{:S(2)}, u32[]{:S(2)}) collective-permute-start(bf16[2,256,1024]{2,1,0:T(8,128)(2,1)S(1)} %fusion), channel_id=1, source_target_pairs={{0,4},{1,5},{2,6},{3,7},{12,8},{13,9},{14,10},{15,11},{16,20},{17,... | collective-permute-start | bytes 3145736 | tf_op jit(solution)/shard_map/ppermute | solution.py:374
  42.7 24.0 %collective-permute-start.4 = (bf16[2,256,1024]{2,1,0:T(8,128)(2,1)S(1)}, bf16[2,256,1024]{2,1,0:T(8,128)(2,1)S(1)}, u32[]{:S(2)}, u32[]{:S(2)}) collective-permute-start(bf16[2,256,1024]{2,1,0:T(8,128)(2,1)S(1)} %get-tuple-element.48), channel_id=1, source_target_pairs={{0,2},{1,3},{2,0},{3,1},{4,6},{5,7},{6,4},{7,5},{8,10},{9,11},{10,... | collective-permute-start | bytes 3145736 | tf_op jit(solution)/shard_map/ppermute | solution.py:370
  67.7 24.4 %collective-permute-start.6 = (bf16[2,256,1024]{2,1,0:T(8,128)(2,1)S(1)}, bf16[2,256,1024]{2,1,0:T(8,128)(2,1)S(1)}, u32[]{:S(2)}, u32[]{:S(2)}) collective-permute-start(bf16[2,256,1024]{2,1,0:T(8,128)(2,1)S(1)} %fusion.1), channel_id=1, source_target_pairs={{0,4},{1,5},{2,6},{3,7},{12,8},{13,9},{14,10},{15,11},{16,20},{17,... | collective-permute-start | bytes 3145736 | tf_op jit(solution)/shard_map/ppermute | solution.py:374
  69.0 24.4 %collective-permute-start.5 = (bf16[2,256,1024]{2,1,0:T(8,128)(2,1)S(1)}, bf16[2,256,1024]{2,1,0:T(8,128)(2,1)S(1)}, u32[]{:S(2)}, u32[]{:S(2)}) collective-permute-start(bf16[2,256,1024]{2,1,0:T(8,128)(2,1)S(1)} %add_convert_fusion.2), channel_id=1, source_target_pairs={{4,8},{5,9},{6,10},{7,11},{8,4},{9,5},{10,6},{11,7},{20,24},{21,25... | collective-permute-start | bytes 3145736 | tf_op jit(solution)/shard_map/ppermute | solution.py:374
  72.3 22.3 %collective-permute-start.7 = (bf16[2,256,1024]{2,1,0:T(8,128)(2,1)S(1)}, bf16[2,256,1024]{2,1,0:T(8,128)(2,1)S(1)}, u32[]{:S(2)}, u32[]{:S(2)}) collective-permute-start(bf16[2,256,1024]{2,1,0:T(8,128)(2,1)S(1)} %get-tuple-element.53), channel_id=1, source_target_pairs={{0,2},{1,3},{2,0},{3,1},{4,6},{5,7},{6,4},{7,5},{8,10},{9,11},{10,... | collective-permute-start | bytes 3145736 | tf_op jit(solution)/shard_map/ppermute | solution.py:370
  94.6 25.7 %copy-start.10 = (bf16[1,256,1024]{2,1,0:T(8,128)(2,1)S(1)}, bf16[1,256,1024]{2,1,0:T(8,128)(2,1)}, u32[]{:S(2)}) copy-start(bf16[1,256,1024]{2,1,0:T(8,128)(2,1)} %refs_4_.1) | copy-start | bytes 1572868
  95.2 23.2 %collective-permute-start.9 = (bf16[2,256,1024]{2,1,0:T(8,128)(2,1)S(1)}, bf16[2,256,1024]{2,1,0:T(8,128)(2,1)S(1)}, u32[]{:S(2)}, u32[]{:S(2)}) collective-permute-start(bf16[2,256,1024]{2,1,0:T(8,128)(2,1)S(1)} %add_convert_fusion.1), channel_id=1, source_target_pairs={{4,8},{5,9},{6,10},{7,11},{8,4},{9,5},{10,6},{11,7},{20,24},{21,25... | collective-permute-start | bytes 3145736 | tf_op jit(solution)/shard_map/ppermute | solution.py:374
  97.5 21.2 %collective-permute-start.8 = (bf16[2,256,1024]{2,1,0:T(8,128)(2,1)S(1)}, bf16[2,256,1024]{2,1,0:T(8,128)(2,1)S(1)}, u32[]{:S(2)}, u32[]{:S(2)}) collective-permute-start(bf16[2,256,1024]{2,1,0:T(8,128)(2,1)S(1)} %get-tuple-element.55), channel_id=1, source_target_pairs={{0,2},{1,3},{2,0},{3,1},{4,6},{5,7},{6,4},{7,5},{8,10},{9,11},{10,... | collective-permute-start | bytes 3145736 | tf_op jit(solution)/shard_map/ppermute | solution.py:370
  98.8 21.5 %copy-start.6 = (bf16[1024,1024]{1,0:T(8,128)(2,1)S(1)}, bf16[1024,1024]{1,0:T(8,128)(2,1)}, u32[]{:S(2)}) copy-start(bf16[1024,1024]{1,0:T(8,128)(2,1)} %constant.44.clone.refs_6_) | copy-start | bytes 6291460
  98.8 21.5 %copy-start.7 = (bf16[1024,1024]{1,0:T(8,128)(2,1)S(1)}, bf16[1024,1024]{1,0:T(8,128)(2,1)}, u32[]{:S(2)}) copy-start(bf16[1024,1024]{1,0:T(8,128)(2,1)} %constant.43.clone.refs_5_) | copy-start | bytes 6291460
  99.5 20.8 %collective-permute-start.10 = (bf16[2,256,1024]{2,1,0:T(8,128)(2,1)S(1)}, bf16[2,256,1024]{2,1,0:T(8,128)(2,1)S(1)}, u32[]{:S(2)}, u32[]{:S(2)}) collective-permute-start(bf16[2,256,1024]{2,1,0:T(8,128)(2,1)S(1)} %add_convert_fusion), channel_id=1, source_target_pairs={{0,4},{1,5},{2,6},{3,7},{12,8},{13,9},{14,10},{15,11},{4,0},{5,1},... | collective-permute-start | bytes 3145736 | tf_op jit(solution)/shard_map/ppermute | solution.py:374
  126.2 20.2 %collective-permute-start.13 = (bf16[2,256,1024]{2,1,0:T(8,128)(2,1)}, bf16[2,256,1024]{2,1,0:T(8,128)(2,1)}, u32[]{:S(2)}, u32[]{:S(2)}) collective-permute-start(bf16[2,256,1024]{2,1,0:T(8,128)(2,1)} %middle.1.refs_0_), channel_id=1, source_target_pairs={{0,4},{1,5},{2,6},{3,7},{12,8},{13,9},{14,10},{15,11},{4,0},{5,1},... | collective-permute-start | bytes 3145736 | tf_op jit(solution)/shard_map/ppermute | solution.py:374
  126.5 22.0 %collective-permute-start.12 = (bf16[2,256,1024]{2,1,0:T(8,128)(2,1)}, bf16[2,256,1024]{2,1,0:T(8,128)(2,1)}, u32[]{:S(2)}, u32[]{:S(2)}) collective-permute-start(bf16[2,256,1024]{2,1,0:T(8,128)(2,1)} %middle.1.refs_0_), channel_id=1, source_target_pairs={{4,8},{5,9},{6,10},{7,11},{8,4},{9,5},{10,6},{11,7},{20,24},{21,25... | collective-permute-start | bytes 3145736 | tf_op jit(solution)/shard_map/ppermute | solution.py:374
  129.0 20.2 %collective-permute-start.11 = (bf16[2,256,1024]{2,1,0:T(8,128)(2,1)}, bf16[2,256,1024]{2,1,0:T(8,128)(2,1)S(1)}, u32[]{:S(2)}, u32[]{:S(2)}) collective-permute-start(bf16[2,256,1024]{2,1,0:T(8,128)(2,1)} %middle.1.refs_0_), channel_id=1, source_target_pairs={{0,2},{1,3},{2,0},{3,1},{4,6},{5,7},{6,4},{7,5},{8,10},{9,11},{10,... | collective-permute-start | bytes 3145736 | tf_op jit(solution)/shard_map/ppermute | solution.py:370
  149.2 1.0 copy-start.8
  150.2 24.6 %collective-permute-start.14 = (bf16[2,256,1024]{2,1,0:T(8,128)(2,1)}, bf16[2,256,1024]{2,1,0:T(8,128)(2,1)}, u32[]{:S(2)}, u32[]{:S(2)}) collective-permute-start(bf16[2,256,1024]{2,1,0:T(8,128)(2,1)} %middle.1.refs_0_), channel_id=1, source_target_pairs={{0,1},{1,0},{2,3},{3,2},{4,5},{5,4},{6,7},{7,6},{8,9},{9,8},{10,11... | collective-permute-start | bytes 3145736 | tf_op jit(solution)/shard_map/ppermute | solution.py:367
  155.8 25.0 %collective-permute-start.18 = (bf16[2,256,1024]{2,1,0:T(8,128)(2,1)}, bf16[2,256,1024]{2,1,0:T(8,128)(2,1)}, u32[]{:S(2)}, u32[]{:S(2)}) collective-permute-start(bf16[2,256,1024]{2,1,0:T(8,128)(2,1)} %collective-permute-done.12), channel_id=1, source_target_pairs={{4,0},{5,1},{6,2},{7,3},{8,12},{9,13},{10,14},{11,15},{20,16},{21,... | collective-permute-start | bytes 3145736 | tf_op jit(solution)/shard_map/ppermute | solution.py:374
  158.9 26.7 %collective-permute-start.17 = (bf16[2,256,1024]{2,1,0:T(8,128)(2,1)}, bf16[2,256,1024]{2,1,0:T(8,128)(2,1)}, u32[]{:S(2)}, u32[]{:S(2)}) collective-permute-start(bf16[2,256,1024]{2,1,0:T(8,128)(2,1)} %collective-permute-done.13.refs_1_), channel_id=1, source_target_pairs={{4,8},{5,9},{6,10},{7,11},{8,4},{9,5},{10,6},{11,7},{20,24},{21,25... | collective-permute-start | bytes 3145736 | tf_op jit(solution)/shard_map/ppermute | solution.py:374
  161.4 24.5 %collective-permute-start.16 = (bf16[2,256,1024]{2,1,0:T(8,128)(2,1)}, bf16[2,256,1024]{2,1,0:T(8,128)(2,1)}, u32[]{:S(2)}, u32[]{:S(2)}) collective-permute-start(bf16[2,256,1024]{2,1,0:T(8,128)(2,1)} %collective-permute-done.13.refs_1_), channel_id=1, source_target_pairs={{0,2},{1,3},{2,0},{3,1},{4,6},{5,7},{6,4},{7,5},{8,10},{9,11},{10,... | collective-permute-start | bytes 3145736 | tf_op jit(solution)/shard_map/ppermute | solution.py:370
  162.4 23.6 %collective-permute-start.15 = (bf16[2,256,1024]{2,1,0:T(8,128)(2,1)}, bf16[2,256,1024]{2,1,0:T(8,128)(2,1)}, u32[]{:S(2)}, u32[]{:S(2)}) collective-permute-start(bf16[2,256,1024]{2,1,0:T(8,128)(2,1)} %collective-permute-done.13.refs_1_), channel_id=1, source_target_pairs={{0,1},{1,0},{2,3},{3,2},{4,5},{5,4},{6,7},{7,6},{8,9},{9,8},{10,11... | collective-permute-start | bytes 3145736 | tf_op jit(solution)/shard_map/ppermute | solution.py:367
  163.2 1.2 copy-start.9
  171.4 3.4 %copy-start.4 = (f32[2,128,8192]{2,1,0:T(8,128)}, f32[2,128,8192]{2,1,0:T(8,128)S(1)}, u32[]{:S(2)}) copy-start(f32[2,128,8192]{2,1,0:T(8,128)S(1)} %backward.5.spec_ref) | copy-start | bytes 25165828
  187.3 23.3 %collective-permute-start.21 = (bf16[2,256,1024]{2,1,0:T(8,128)(2,1)S(1)}, bf16[2,256,1024]{2,1,0:T(8,128)(2,1)S(1)}, u32[]{:S(2)}, u32[]{:S(2)}) collective-permute-start(bf16[2,256,1024]{2,1,0:T(8,128)(2,1)S(1)} %broadcast_select_fusion.1.refs_2_), channel_id=1, source_target_pairs={{0,2},{1,3},{2,0},{3,1},{4,6},{5,7},{6,4},{7,5},{8,10},{9,11},{10,... | collective-permute-start | bytes 3145736 | tf_op jit(solution)/shard_map/ppermute | solution.py:370
  188.3 22.3 %collective-permute-start.20 = (bf16[2,256,1024]{2,1,0:T(8,128)(2,1)S(1)}, bf16[2,256,1024]{2,1,0:T(8,128)(2,1)S(1)}, u32[]{:S(2)}, u32[]{:S(2)}) collective-permute-start(bf16[2,256,1024]{2,1,0:T(8,128)(2,1)S(1)} %broadcast_select_fusion.1.refs_2_), channel_id=1, source_target_pairs={{0,1},{1,0},{2,3},{3,2},{4,5},{5,4},{6,7},{7,6},{8,9},{9,8},{10,11... | collective-permute-start | bytes 3145736 | tf_op jit(solution)/shard_map/ppermute | solution.py:367
  190.0 20.6 %collective-permute-start.19 = (bf16[2,256,1024]{2,1,0:T(8,128)(2,1)S(1)}, bf16[2,256,1024]{2,1,0:T(8,128)(2,1)S(1)}, u32[]{:S(2)}, u32[]{:S(2)}) collective-permute-start(bf16[2,256,1024]{2,1,0:T(8,128)(2,1)S(1)} %copy-done.9), channel_id=1, source_target_pairs={{0,1},{1,0},{2,3},{3,2},{4,5},{5,4},{6,7},{7,6},{8,9},{9,8},{10,11... | collective-permute-start | bytes 3145736 | tf_op jit(solution)/shard_map/ppermute | solution.py:367
  190.0 23.9 %collective-permute-start.22 = (bf16[2,256,1024]{2,1,0:T(8,128)(2,1)}, bf16[2,256,1024]{2,1,0:T(8,128)(2,1)S(1)}, u32[]{:S(2)}, u32[]{:S(2)}) collective-permute-start(bf16[2,256,1024]{2,1,0:T(8,128)(2,1)} %collective-permute-done.17), channel_id=1, source_target_pairs={{4,0},{5,1},{6,2},{7,3},{8,12},{9,13},{10,14},{11,15},{20,16},{21,... | collective-permute-start | bytes 3145736 | tf_op jit(solution)/shard_map/ppermute | solution.py:374
  198.8 3.4 %copy-start.3 = (f32[2,128,8192]{2,1,0:T(8,128)}, f32[2,128,8192]{2,1,0:T(8,128)S(1)}, u32[]{:S(2)}) copy-start(f32[2,128,8192]{2,1,0:T(8,128)S(1)} %backward.6.spec_ref) | copy-start | bytes 25165828
  215.2 11.2 %collective-permute-start.25 = (bf16[2,256,1024]{2,1,0:T(8,128)(2,1)S(1)}, bf16[2,256,1024]{2,1,0:T(8,128)(2,1)S(1)}, u32[]{:S(2)}, u32[]{:S(2)}) collective-permute-start(bf16[2,256,1024]{2,1,0:T(8,128)(2,1)S(1)} %broadcast_select_fusion.refs_2_), channel_id=1, source_target_pairs={{0,1},{1,0},{2,3},{3,2},{4,5},{5,4},{6,7},{7,6},{8,9},{9,8},{10,11... | collective-permute-start | bytes 3145736 | tf_op jit(solution)/shard_map/ppermute | solution.py:367
  216.3 10.1 %collective-permute-start.24 = (bf16[2,256,1024]{2,1,0:T(8,128)(2,1)}, bf16[2,256,1024]{2,1,0:T(8,128)(2,1)S(1)}, u32[]{:S(2)}, u32[]{:S(2)}) collective-permute-start(bf16[2,256,1024]{2,1,0:T(8,128)(2,1)} %collective-permute-done.16.refs_3_), channel_id=1, source_target_pairs={{0,1},{1,0},{2,3},{3,2},{4,5},{5,4},{6,7},{7,6},{8,9},{9,8},{10,11... | collective-permute-start | bytes 3145736 | tf_op jit(solution)/shard_map/ppermute | solution.py:367
  216.4 10.1 %collective-permute-start.26 = (bf16[2,256,1024]{2,1,0:T(8,128)(2,1)S(1)}, bf16[2,256,1024]{2,1,0:T(8,128)(2,1)S(1)}, u32[]{:S(2)}, u32[]{:S(2)}) collective-permute-start(bf16[2,256,1024]{2,1,0:T(8,128)(2,1)S(1)} %collective-permute-done.21.refs_3_), channel_id=1, source_target_pairs={{0,1},{1,0},{2,3},{3,2},{4,5},{5,4},{6,7},{7,6},{8,9},{9,8},{10,11... | collective-permute-start | bytes 3145736 | tf_op jit(solution)/shard_map/ppermute | solution.py:367
  216.9 24.7 %collective-permute-start.23 = (bf16[2,256,1024]{2,1,0:T(8,128)(2,1)S(1)}, bf16[2,256,1024]{2,1,0:T(8,128)(2,1)S(1)}, u32[]{:S(2)}, u32[]{:S(2)}) collective-permute-start(bf16[2,256,1024]{2,1,0:T(8,128)(2,1)S(1)} %broadcast_select_fusion.refs_2_), channel_id=1, source_target_pairs={{0,2},{1,3},{2,0},{3,1},{4,6},{5,7},{6,4},{7,5},{8,10},{9,11},{10,... | collective-permute-start | bytes 3145736 | tf_op jit(solution)/shard_map/ppermute | solution.py:370
  223.1 3.4 %copy-start.5 = (f32[2,128,8192]{2,1,0:T(8,128)}, f32[2,128,8192]{2,1,0:T(8,128)S(1)}, u32[]{:S(2)}) copy-start(f32[2,128,8192]{2,1,0:T(8,128)S(1)} %backward.7.spec_ref) | copy-start | bytes 25165828
  241.6 3.1 %collective-permute-start.27 = (bf16[2,256,1024]{2,1,0:T(8,128)(2,1)S(1)}, bf16[2,256,1024]{2,1,0:T(8,128)(2,1)S(1)}, u32[]{:S(2)}, u32[]{:S(2)}) collective-permute-start(bf16[2,256,1024]{2,1,0:T(8,128)(2,1)S(1)} %collective-permute-done.23.refs_0_), channel_id=1, source_target_pairs={{0,1},{1,0},{2,3},{3,2},{4,5},{5,4},{6,7},{7,6},{8,9},{9,8},{10,11... | collective-permute-start | bytes 3145736 | tf_op jit(solution)/shard_map/ppermute | solution.py:367

commit v3 on v2

--- a/solution.py
+++ b/solution.py
@@ -99,22 +99,26 @@
         store(mid.astype(jnp.bfloat16).reshape(shape))
 
 
-def forward_kernel(meta_ref, pupil_ref, band_ref, *refs, base, count, win, tiles):
+def forward_kernel(meta_ref, pupil_ref, band_ref, *refs, base, images, count, win, tiles):
     out_refs = refs[-count:]
     lows = [refs[2 * half : 2 * half + 2] for half in range(len(tiles))]
     came = refs[2 * len(tiles)] if len(refs) > 2 * len(tiles) + count else None
+    streams = count // images
 
     def image(index):
         def store(value):
-            for number, out_ref in enumerate(out_refs):
+            for number in range(images):
 
                 @pl.when(index == number)
                 def _():
-                    out_ref[...] = value
+                    for stream in range(streams):
+                        out_ref = out_refs[number * streams + stream]
+                        rows = out_ref.shape[1]
+                        out_ref[...] = value[:, stream * rows : (stream + 1) * rows]
 
         image_band(meta_ref, base + index, lows, tiles, pupil_ref, band_ref, win, store, came)
 
-    pl.loop(0, len(out_refs))(image)
+    pl.loop(0, images)(image)
 
 
 def forward_grid_kernel(meta_ref, pupil_ref, band_ref, real_ref, imag_ref, out_ref, *, win):
@@ -161,12 +165,18 @@
     subtract_image(meta_ref, step, back_ref, pupil_ref, band_ref, out_ref, win)
 
 
-def middle_kernel(*refs, terms):
-    term_refs, (image_ref, cos_ref, sin_ref, out_ref, mid_ref, resid_ref) = refs[:terms], refs[terms:]
-    _, band, crop_width = term_refs[0].shape
+def middle_kernel(*refs, terms, streams):
+    term_refs, refs = refs[: terms * streams], refs[terms * streams :]
+    image_ref, cos_ref, sin_ref, out_ref, mid_ref, resid_ref = refs
+    _, rows, crop_width = term_refs[0].shape
+    band = rows * streams
     block = min(512, crop_width)
-    total = sum(ref[...].astype(jnp.float32) for ref in term_refs)
-    mid_ref[...] = total.astype(jnp.bfloat16).reshape(2 * band, crop_width)
+    for stream in range(streams):
+        of_stream = term_refs[stream * terms : (stream + 1) * terms]
+        total = sum(ref[...].astype(jnp.float32) for ref in of_stream).astype(jnp.bfloat16)
+        for part in range(2):
+            start = part * band + stream * rows
+            mid_ref[start : start + rows] = total[part]
     dot = functools.partial(jnp.dot, preferred_element_type=jnp.float32)
     for start in range(0, crop_width, block):
         columns = slice(start, start + block)
@@ -204,15 +214,19 @@
     return jax.ShapeDtypeStruct(shape, jnp.bfloat16)
 
 
-def forward(meta, lows, pupil, band_table, base, count, tiles=(0, 1), came=None):
+def forward(meta, lows, pupil, band_table, base, images, tiles=(0, 1), came=None, streams=1):
     win = Windows(*lows[0][0].shape, pupil.shape[1])
     operands = [meta, pupil, band_table] + [part for low in lows for part in low]
     operands += [came] * (came is not None)
+    count = images * streams
+    _, rows, columns = band_type(pupil, band_table).shape
     return pl.pallas_call(
-        functools.partial(forward_kernel, base=base, count=count, win=win, tiles=tiles),
+        functools.partial(
+            forward_kernel, base=base, images=images, count=count, win=win, tiles=tiles
+        ),
         in_specs=[smem] + [vmem] * (len(operands) - 1),
         out_specs=[vmem] * count,
-        out_shape=[band_type(pupil, band_table)] * count,
+        out_shape=[jax.ShapeDtypeStruct((2, rows // streams, columns), jnp.bfloat16)] * count,
         compiler_params=params(),
         cost_estimate=light(),
         name="forward",
@@ -232,10 +246,14 @@
     )(meta, pupil, band_table, spectrum, *backs)
 
 
-def middle(terms, image, cos_table, sin_table):
-    _, band, crop_width = terms[0].shape
+def middle(streams, image, cos_table, sin_table):
+    _, rows, crop_width = streams[0][0].shape
+    band = rows * len(streams)
+    terms = [term for stream in streams for term in stream]
     return pl.pallas_call(
-        functools.partial(middle_kernel, terms=len(terms)),
+        functools.partial(
+            middle_kernel, terms=len(streams[0]), streams=len(streams)
+        ),
         in_specs=[vmem] * (len(terms) + 3),
         out_specs=vmem,
         out_shape=jax.ShapeDtypeStruct((2, band, crop_width), jnp.bfloat16),
@@ -346,7 +364,7 @@
         meta = image_meta(jnp.arange(count, dtype=jnp.int32), [position])
         partial = forward_all(meta, low, pupil, band_table)
         mid = lax.psum_scatter(partial, "ty", scatter_dimension=0, tiled=True)[0]
-        back = lax.all_gather(middle([mid], measured, cos_table, sin_table), "ty")
+        back = lax.all_gather(middle([[mid]], measured, cos_table, sin_table), "ty")
         return backward_all(meta, spectrum, pupil, band_table, back)
 
     targets = {"far": (3, 3, 0, 0), "next": (2, 2, 1, 1), "beside": (1, 0, 3, 2), "own": (0, 1, 2, 3)}
@@ -379,36 +397,51 @@
     together = lax.optimization_barrier
 
     lows = [low, [sibling(part) for part in low]]
-    (far_leaving,) = forward(meta, lows[:1], pupil, band_table, 0, 1, (0,))
-    (far_leaving,) = forward(meta, lows[1:], pupil, band_table, 0, 1, (1,), far_leaving)
-    far_other = across(far_leaving)
-    (
-        far_kept,
-        next_leaving,
-        next_kept,
-        beside_leaving,
-        beside_kept,
-        own_leaving,
-        own_kept,
-    ) = forward(together((meta, far_leaving))[0], lows, pupil, band_table, 1, 7)
-    far_other, far_kept, next_leaving = together((far_other, far_kept, next_leaving))
-
-    from_end = along(total(far_kept, far_other), inward)
-    next_other = across(next_leaving)
-    from_end, next_other, beside_leaving = together((from_end, next_other, beside_leaving))
-
-    far_inner = along(total(far_kept, far_other, from_end), inner)
-    next_inward = along(total(next_kept, next_other), inward)
-    beside_other = across(beside_leaving)
-    far_inner, next_inward, beside_other, own_leaving = together(
-        (far_inner, next_inward, beside_other, own_leaving)
-    )
-
-    next_inner = along(total(next_kept, next_other, next_inward), inner)
-    beside = along(total(beside_kept, beside_other, far_inner), inward + outward)
-    own_other = across(own_leaving)
-    terms = [own_kept, own_other, next_inner, beside]
-    back = middle(terms, measured, cos_table, sin_table)
+    streams = 2
+    (own_rows,) = forward(meta, lows[:1], pupil, band_table, 0, 1, (0,))
+    far_leaving = forward(
+        meta, lows[1:], pupil, band_table, 0, 1, (1,), own_rows, streams=streams
+    )
+    far_other = [across(value) for value in far_leaving]
+    made = forward(
+        together((meta, far_leaving[0]))[0], lows, pupil, band_table, 1, 7, streams=streams
+    )
+    summed, held = [], None
+    for stream in reversed(range(streams)):
+        (
+            far_kept,
+            next_leaving,
+            next_kept,
+            beside_leaving,
+            beside_kept,
+            own_leaving,
+            own_kept,
+        ) = made[stream::streams]
+        far, far_kept, next_leaving = together((far_other[stream], far_kept, next_leaving))
+
+        next_other = across(next_leaving)
+        from_end = along(total(far_kept, far), inward)
+        from_end, next_other, beside_leaving = together((from_end, next_other, beside_leaving))
+
+        beside_other = across(beside_leaving)
+        next_inward = along(total(next_kept, next_other), inward)
+        far_inner = along(total(far_kept, far, from_end), inner)
+        far_inner, next_inward, beside_other, own_leaving = together(
+            (far_inner, next_inward, beside_other, own_leaving)
+        )
+
+        own_other = across(own_leaving)
+        next_inner = along(total(next_kept, next_other, next_inward), inner)
+        beside = along(total(beside_kept, beside_other, far_inner), inward + outward)
+        terms = [own_kept, own_other, next_inner, beside]
+        if stream > 0:
+            terms = [total(*terms)]
+            held = terms[0]
+        else:
+            terms[0] = together((terms[0], held))[0]
+            terms = [total(*terms)]
+        summed.insert(0, terms)
+    back = middle(summed, measured, cos_table, sin_table)
 
     def apply(result, pieces):
         names, values = zip(*pieces)
@@ -421,33 +454,33 @@
     from_beside = along(back, inward + outward)
     other, from_inner, from_beside, back = together((other, from_inner, from_beside, back))
 
-    twin, beside_twin = sibling(back), sibling(from_beside)
+    beside_twin, other_twin = sibling(from_beside), sibling(other)
     beside_other = across(from_beside)
     far_inner = along(from_beside, inner)
     next_outward = along(from_inner, outward)
     result = apply(
         spectrum, [(("own", 0), back), (("beside", 0), from_beside), (("own", 2), other)]
     )
-    twin, beside_twin, beside_other, far_inner, next_outward, other, result = together(
-        (twin, beside_twin, beside_other, far_inner, next_outward, other, result)
+    beside_twin, other_twin, beside_other, far_inner, next_outward, back, result = together(
+        (beside_twin, other_twin, beside_other, far_inner, next_outward, back, result)
     )
 
     at_ends = (plane == 0) | (plane == 3)
     from_next = jnp.where(at_ends, next_outward, from_inner)
-    other_twin, next_twin = sibling(other), sibling(from_next)
+    twin, next_twin = sibling(back), sibling(from_next)
     next_other = across(from_next)
     far_outward = along(far_inner, outward)
     result = apply(
         result,
         [
-            (("own", 1), twin),
+            (("own", 3), other_twin),
             (("beside", 1), beside_twin),
             (("next", 0), from_next),
             (("beside", 2), beside_other),
         ],
     )
-    other_twin, next_twin, next_other, far_outward, beside_other, result = together(
-        (other_twin, next_twin, next_other, far_outward, beside_other, result)
+    twin, next_twin, next_other, far_outward, beside_other, result = together(
+        (twin, next_twin, next_other, far_outward, beside_other, result)
     )
 
     from_far = jnp.where(at_ends, far_outward, far_inner)
@@ -457,7 +490,7 @@
     result = apply(
         result,
         [
-            (("own", 3), other_twin),
+            (("own", 1), twin),
             (("next", 1), next_twin),
             (("far", 0), from_far),
             (("next", 2), next_other),

time: 254 us -> 241 us (0.949)
  waiting for transfers between devices: 128 us -> 94.1 us
  starting transfers between devices: 36.9 us -> 64.3 us
  Pallas kernels: 63.6 us -> 58.6 us
    ppermute x10 -> x15, waiting for transfers between devices: 96.9 us -> 44.8 us  [along(): return lax.ppermute(value, 'ty', pairs)]
    ppermute x10 -> x15, starting transfers between devices: 17.9 us -> 40.7 us  [along(): return lax.ppermute(value, 'ty', pairs)]
    ppermute x8 -> x12, waiting for transfers between devices: 27.9 us -> 46.1 us  [across(): return lax.ppermute(value, 'ty', [(i, i ^ 2) for i in range(count)])]
    ppermute x8 -> x12, starting transfers between devices: 7.48 us -> 16.3 us  [across(): return lax.ppermute(value, 'ty', [(i, i ^ 2) for i in range(count)])]
    pallas_call x4, Pallas kernels: 28.9 us -> 23.9 us  [the longest x3 19.1 us: forward(): pl.pallas_call(functools.partial(forward_kernel, base=base, images=images...]
    ppermute x10, starting transfers between devices: 11.5 us -> 7.37 us  [sibling(): return lax.ppermute(value, 'ty', [(i, i ^ 1) for i in range(count)])]
    unnamed x26 -> x28, local copies, waits for them, and re-layouts: 15.8 us -> 15.8 us
  transfers between devices with their start and end apart: 28 -> 37, of which waited for: 19 -> 20; matrix products, arithmetic and copies ran while one was open for 1% -> 2% of each run, Pallas kernels for 18% -> 18%
where the time goes in v3:
time: 241 us; the launch traced here: 240 us
  waiting for transfers between devices  94.1 us (39%)
  starting transfers between devices  64.3 us (27%)
  Pallas kernels  58.6 us (24%)
  local copies, waits for them, and re-layouts  16.5 us (7%)
  other arithmetic  5.98 us (2%)
    ppermute x12, waiting for transfers between devices, across(): return lax.ppermute(value, 'ty', [(i, i ^ 2) for i in range(count)])  46.1 us
    ppermute x15, waiting for transfers between devices, along(): return lax.ppermute(value, 'ty', pairs)  44.8 us
    ppermute x15, starting transfers between devices, along(): return lax.ppermute(value, 'ty', pairs)  40.7 us
    pallas_call x5, Pallas kernels, backward(): pl.pallas_call(functools.partial(backward_kernel, slots=slots, win=win),...  31 us
    pallas_call x3, Pallas kernels, forward(): pl.pallas_call(functools.partial(forward_kernel, base=base, images=images...  19.1 us
    ppermute x12, starting transfers between devices, across(): return lax.ppermute(value, 'ty', [(i, i ^ 2) for i in range(count)])  16.3 us
    unnamed x28, local copies, waits for them, and re-layouts  15.8 us
    ppermute x10, starting transfers between devices, sibling(): return lax.ppermute(value, 'ty', [(i, i ^ 1) for i in range(count)])  7.37 us
  transfers between devices with their start and end apart: 37, of which 20 were waited for; matrix products, arithmetic and copies ran while one was open for 2% of the time, Pallas kernels for 18%

profile of v3, /device:TPU:11, one launch (start us, length us, event | category | flops | bytes accessed | tf_op | source)
XLA Modules:
  0.0 240.0 jit_solution(10063315709911162531)
XLA Ops:
  0.0 3.4 %copy-done.1 = f32[2,128,8192]{2,1,0:T(8,128)S(1)} copy-done((f32[2,128,8192]{2,1,0:T(8,128)S(1)}, f32[2,128,8192]{2,1,0:T(8,128)}, u32[]{:S(2)}) %copy-start.1) | copy-done | bytes 8388632
  3.4 1.9 low_part.3.refs_1_
  5.3 0.7 collective-permute-start.1
  6.0 1.8 low_part.2.refs_0_
  8.0 0.7 dynamic-slice_bitcast_fusion
  8.9 3.3 %forward.3.refs_2_ = bf16[2,256,1024]{2,1,0:T(8,128)(2,1)S(1)} custom-call(s32[3,16]{1,0:T(4,128)S(1)} %pad_add_fusion.meta_ref, bf16[1024,1024]{1,0:T(8,128)(2,1)S(1)} %copy-done, bf16[1024,512]{1,0:T(8,128)(2,1)S(1)} %copy-done.2, bf16[128,8192]{1,0:T(8,128)(2,1)} %low_part.2.refs_0_, bf16[128,8192]{1,0:T(8,128)(2,1)} %low_part.3.refs_1_), custom_call_target="tpu_custom_call" | custom-call | flops 1024 | bytes 1024 | tf_op jit(solution)/shard_map/forward/pallas_call | solution.py:223
  12.3 0.9 collective-permute-done.refs_0_.refs_2_
  13.2 3.3 %forward.4 = (bf16[2,128,1024]{2,1,0:T(8,128)(2,1)S(1)}, bf16[2,128,1024]{2,1,0:T(8,128)(2,1)S(1)}) custom-call(s32[3,16]{1,0:T(4,128)S(1)} %pad_add_fusion.meta_ref, bf16[1024,1024]{1,0:T(8,128)(2,1)S(1)} %copy-done, bf16[1024,512]{1,0:T(8,128)(2,1)S(1)} %copy-done.2, bf16[128,8192]{1,0:T(8,128)(2,1)} %collective-permute-done.refs_0_.refs_2_, ...), custom_call_target="tpu_custom_call" | custom-call | flops 1024 | bytes 1024 | tf_op jit(solution)/shard_map/forward/pallas_call | solution.py:223
  16.8 1.2 collective-permute-start.11
  18.0 12.4 %forward.5 = (bf16[2,128,1024]{2,1,0:T(8,128)(2,1)S(1)}, bf16[2,128,1024]{2,1,0:T(8,128)(2,1)S(1)}, bf16[2,128,1024]{2,1,0:T(8,128)(2,1)S(1)}, bf16[2,128,1024]{...) custom-call(s32[3,16]{1,0:T(4,128)S(1)} %pad_add_fusion.meta_ref, ...), custom_call_target="tpu_custom_call" | custom-call | flops 1024 | bytes 1024 | tf_op jit(solution)/shard_map/forward/pallas_call | solution.py:223
  30.7 1.3 collective-permute-start.3
  32.0 6.3 %collective-permute-start.4 = (bf16[2,128,1024]{2,1,0:T(8,128)(2,1)S(1)}, bf16[2,128,1024]{2,1,0:T(8,128)(2,1)S(1)}, u32[]{:S(2)}, u32[]{:S(2)}) collective-permute-start(bf16[2,128,1024]{2,1,0:T(8,128)(2,1)S(1)} %get-tuple-element.71), channel_id=1, source_target_pairs={{0,2},{1,3},{2,0},{3,1},{4,6},{5,7},{6,4},{7,5},{8,10},{9,11},{10,... | collective-permute-start | bytes 1572872 | tf_op jit(solution)/shard_map/ppermute | solution.py:388
  38.3 2.6 %collective-permute-done.11 = bf16[2,128,1024]{2,1,0:T(8,128)(2,1)S(1)} collective-permute-done((bf16[2,128,1024]{2,1,0:T(8,128)(2,1)S(1)}, bf16[2,128,1024]{2,1,0:T(8,128)(2,1)S(1)}, u32[]{:S(2)}, u32[]{:S(2)}) %collective-permute-start.11) | collective-permute-done | bytes 524320 | tf_op jit(solution)/shard_map/ppermute | solution.py:388
  41.1 1.3 collective-permute-start.12
  42.5 0.5 collective-permute-done.3
  43.0 9.2 %collective-permute-done.4 = bf16[2,128,1024]{2,1,0:T(8,128)(2,1)S(1)} collective-permute-done((bf16[2,128,1024]{2,1,0:T(8,128)(2,1)S(1)}, bf16[2,128,1024]{2,1,0:T(8,128)(2,1)S(1)}, u32[]{:S(2)}, u32[]{:S(2)}) %collective-permute-start.4) | collective-permute-done | bytes 524320 | tf_op jit(solution)/shard_map/ppermute | solution.py:388
  52.4 1.3 collective-permute-start.6
  53.9 3.5 %collective-permute-start.5 = (bf16[2,128,1024]{2,1,0:T(8,128)(2,1)S(1)}, bf16[2,128,1024]{2,1,0:T(8,128)(2,1)S(1)}, u32[]{:S(2)}, u32[]{:S(2)}) collective-permute-start(bf16[2,128,1024]{2,1,0:T(8,128)(2,1)S(1)} %add_convert_fusion.7), channel_id=1, source_target_pairs={{4,8},{5,9},{6,10},{7,11},{8,4},{9,5},{10,6},{11,7},{20,24},{21,25... | collective-permute-start | bytes 1572872 | tf_op jit(solution)/shard_map/ppermute | solution.py:392
  57.4 1.0 collective-permute-start.7
  58.5 4.9 %collective-permute-done.13 = bf16[2,128,1024]{2,1,0:T(8,128)(2,1)S(1)} collective-permute-done((bf16[2,128,1024]{2,1,0:T(8,128)(2,1)S(1)}, bf16[2,128,1024]{2,1,0:T(8,128)(2,1)S(1)}, u32[]{:S(2)}, u32[]{:S(2)}) %collective-permute-start.13) | collective-permute-done | bytes 524320 | tf_op jit(solution)/shard_map/ppermute | solution.py:388
  63.6 1.3 collective-permute-start.15
  65.2 3.5 %collective-permute-start.14 = (bf16[2,128,1024]{2,1,0:T(8,128)(2,1)S(1)}, bf16[2,128,1024]{2,1,0:T(8,128)(2,1)S(1)}, u32[]{:S(2)}, u32[]{:S(2)}) collective-permute-start(bf16[2,128,1024]{2,1,0:T(8,128)(2,1)S(1)} %add_convert_fusion.3), channel_id=1, source_target_pairs={{4,8},{5,9},{6,10},{7,11},{8,4},{9,5},{10,6},{11,7},{20,24},{21,25... | collective-permute-start | bytes 1572872 | tf_op jit(solution)/shard_map/ppermute | solution.py:392
  68.7 4.0 %collective-permute-start.16 = (bf16[2,128,1024]{2,1,0:T(8,128)(2,1)S(1)}, bf16[2,128,1024]{2,1,0:T(8,128)(2,1)S(1)}, u32[]{:S(2)}, u32[]{:S(2)}) collective-permute-start(bf16[2,128,1024]{2,1,0:T(8,128)(2,1)S(1)} %get-tuple-element.93), channel_id=1, source_target_pairs={{0,2},{1,3},{2,0},{3,1},{4,6},{5,7},{6,4},{7,5},{8,10},{9,11},{10,... | collective-permute-start | bytes 1572872 | tf_op jit(solution)/shard_map/ppermute | solution.py:388
  72.7 1.9 collective-permute-done.7
  74.9 3.5 %collective-permute-start.9 = (bf16[2,128,1024]{2,1,0:T(8,128)(2,1)S(1)}, bf16[2,128,1024]{2,1,0:T(8,128)(2,1)S(1)}, u32[]{:S(2)}, u32[]{:S(2)}) collective-permute-start(bf16[2,128,1024]{2,1,0:T(8,128)(2,1)S(1)} %add_convert_fusion.6), channel_id=1, source_target_pairs={{4,8},{5,9},{6,10},{7,11},{8,4},{9,5},{10,6},{11,7},{20,24},{21,25... | collective-permute-start | bytes 1572872 | tf_op jit(solution)/shard_map/ppermute | solution.py:392
  78.4 1.5 collective-permute-start.8
  80.3 2.2 collective-permute-done.16
  82.7 9.8 %collective-permute-start.18 = (bf16[2,128,1024]{2,1,0:T(8,128)(2,1)S(1)}, bf16[2,128,1024]{2,1,0:T(8,128)(2,1)S(1)}, u32[]{:S(2)}, u32[]{:S(2)}) collective-permute-start(bf16[2,128,1024]{2,1,0:T(8,128)(2,1)S(1)} %add_convert_fusion.2), channel_id=1, source_target_pairs={{4,8},{5,9},{6,10},{7,11},{8,4},{9,5},{10,6},{11,7},{20,24},{21,25... | collective-permute-start | bytes 1572872 | tf_op jit(solution)/shard_map/ppermute | solution.py:392
  93.0 0.8 collective-permute-done.8
  94.1 8.6 %collective-permute-done.18 = bf16[2,128,1024]{2,1,0:T(8,128)(2,1)S(1)} collective-permute-done((bf16[2,128,1024]{2,1,0:T(8,128)(2,1)S(1)}, bf16[2,128,1024]{2,1,0:T(8,128)(2,1)S(1)}, u32[]{:S(2)}, u32[]{:S(2)}) %collective-permute-start.18) | collective-permute-done | bytes 524320 | tf_op jit(solution)/shard_map/ppermute | solution.py:392
  102.6 3.9 %collective-permute-done.17 = bf16[2,128,1024]{2,1,0:T(8,128)(2,1)S(1)} collective-permute-done((bf16[2,128,1024]{2,1,0:T(8,128)(2,1)S(1)}, bf16[2,128,1024]{2,1,0:T(8,128)(2,1)S(1)}, u32[]{:S(2)}, u32[]{:S(2)}) %collective-permute-start.17) | collective-permute-done | bytes 524320 | tf_op jit(solution)/shard_map/ppermute | solution.py:388
  107.0 4.8 %middle.1.refs_0_ = bf16[2,256,1024]{2,1,0:T(8,128)(2,1)S(1)} custom-call(bf16[2,128,1024]{2,1,0:T(8,128)(2,1)S(1)} %add_convert_fusion.refs_0_, bf16[2,128,1024]{2,1,0:T(8,128)(2,1)S(1)} %add_convert_fusion.4.refs_1_, bf16[1,256,1024]{2,1,0:T(8,128)(2,1)S(1)} %copy-done.11, bf16[1024,1024]{1,0:T(8,128)(2,1)S(1)} %copy-done.10, bf16[1024,1024]{1,0:T(8,128)(2,1)S(1)} %copy-done.9), custom_call_target="tpu_custom_call" | custom-call | flops 1024 | bytes 1024 | tf_op jit(solution)/shard_map/middle/pallas_call | solution.py:253
  111.9 7.9 %collective-permute-start.21 = (bf16[2,256,1024]{2,1,0:T(8,128)(2,1)S(1)}, bf16[2,256,1024]{2,1,0:T(8,128)(2,1)}, u32[]{:S(2)}, u32[]{:S(2)}) collective-permute-start(bf16[2,256,1024]{2,1,0:T(8,128)(2,1)S(1)} %middle.1.refs_0_), channel_id=1, source_target_pairs={{4,8},{5,9},{6,10},{7,11},{8,4},{9,5},{10,6},{11,7},{20,24},{21,25... | collective-permute-start | bytes 3145736 | tf_op jit(solution)/shard_map/ppermute | solution.py:392
  119.9 1.0 copy-done.6
  120.9 12.8 %collective-permute-done.22.refs_1_ = bf16[2,256,1024]{2,1,0:T(8,128)(2,1)} collective-permute-done((bf16[2,256,1024]{2,1,0:T(8,128)(2,1)S(1)}, bf16[2,256,1024]{2,1,0:T(8,128)(2,1)}, u32[]{:S(2)}, u32[]{:S(2)}) %collective-permute-start.22) | collective-permute-done | bytes 1048608 | tf_op jit(solution)/shard_map/ppermute | solution.py:392
  133.7 9.4 %collective-permute-done.21 = bf16[2,256,1024]{2,1,0:T(8,128)(2,1)} collective-permute-done((bf16[2,256,1024]{2,1,0:T(8,128)(2,1)S(1)}, bf16[2,256,1024]{2,1,0:T(8,128)(2,1)}, u32[]{:S(2)}, u32[]{:S(2)}) %collective-permute-start.21) | collective-permute-done | bytes 1048608 | tf_op jit(solution)/shard_map/ppermute | solution.py:392
  143.1 0.9 collective-permute-done.20.refs_2_
  144.0 1.6 collective-permute-start.24
  145.5 2.3 collective-permute-start.27
  147.8 3.6 %collective-permute-start.26 = (bf16[2,256,1024]{2,1,0:T(8,128)(2,1)}, bf16[2,256,1024]{2,1,0:T(8,128)(2,1)}, u32[]{:S(2)}, u32[]{:S(2)}) collective-permute-start(bf16[2,256,1024]{2,1,0:T(8,128)(2,1)} %collective-permute-done.22.refs_1_), channel_id=1, source_target_pairs={{4,8},{5,9},{6,10},{7,11},{8,4},{9,5},{10,6},{11,7},{20,24},{21,25... | collective-permute-start | bytes 3145736 | tf_op jit(solution)/shard_map/ppermute | solution.py:392
  151.5 0.8 collective-permute-start.23
  152.3 1.2 copy-done.7
  153.5 7.0 %backward.5.spec_ref = f32[2,128,8192]{2,1,0:T(8,128)S(1)} custom-call(s32[3,16]{1,0:T(4,128)S(1)} %pad_add_fusion.meta_ref, bf16[1024,1024]{1,0:T(8,128)(2,1)S(1)} %copy-done, bf16[1024,512]{1,0:T(8,128)(2,1)S(1)} %copy-done.2, f32[2,128,8192]{2,1,0:T(8,128)} %spec_ref.5, bf16[2,256,1024]{2,1,0:T(8,128)(2,1)S(1)} %copy-done.7, ...), custom_call_target="tpu_custom_call" | custom-call | flops 1024 | bytes 1024 | tf_op jit(solution)/shard_map/backward/pallas_call | solution.py:238
  160.5 3.4 %copy-done.4 = f32[2,128,8192]{2,1,0:T(8,128)} copy-done((f32[2,128,8192]{2,1,0:T(8,128)}, f32[2,128,8192]{2,1,0:T(8,128)S(1)}, u32[]{:S(2)}) %copy-start.4) | copy-done | bytes 8388632
  163.9 6.0 %collective-permute-done.27 = bf16[2,256,1024]{2,1,0:T(8,128)(2,1)} collective-permute-done((bf16[2,256,1024]{2,1,0:T(8,128)(2,1)}, bf16[2,256,1024]{2,1,0:T(8,128)(2,1)}, u32[]{:S(2)}, u32[]{:S(2)}) %collective-permute-start.27) | collective-permute-done | bytes 1048608 | tf_op jit(solution)/shard_map/ppermute | solution.py:392
  169.9 5.1 %collective-permute-done.26 = bf16[2,256,1024]{2,1,0:T(8,128)(2,1)} collective-permute-done((bf16[2,256,1024]{2,1,0:T(8,128)(2,1)}, bf16[2,256,1024]{2,1,0:T(8,128)(2,1)}, u32[]{:S(2)}, u32[]{:S(2)}) %collective-permute-start.26) | collective-permute-done | bytes 1048608 | tf_op jit(solution)/shard_map/ppermute | solution.py:392
  175.0 0.9 collective-permute-done.25.refs_3_
  175.9 1.3 broadcast_select_fusion.1.refs_2_
  177.4 1.7 collective-permute-start.29
  179.1 1.3 collective-permute-start.31
  180.4 6.6 %backward.6.spec_ref = f32[2,128,8192]{2,1,0:T(8,128)S(1)} custom-call(s32[3,16]{1,0:T(4,128)S(1)} %pad_add_fusion.meta_ref, bf16[1024,1024]{1,0:T(8,128)(2,1)S(1)} %copy-done, bf16[1024,512]{1,0:T(8,128)(2,1)S(1)} %copy-done.2, f32[2,128,8192]{2,1,0:T(8,128)} %copy-done.4, bf16[2,256,1024]{2,1,0:T(8,128)(2,1)} %collective-permute-done.24.refs_0_, ...), custom_call_target="tpu_custom_call" | custom-call | flops 1024 | bytes 1024 | tf_op jit(solution)/shard_map/backward/pallas_call | solution.py:238
  187.1 3.4 %copy-done.3 = f32[2,128,8192]{2,1,0:T(8,128)} copy-done((f32[2,128,8192]{2,1,0:T(8,128)}, f32[2,128,8192]{2,1,0:T(8,128)S(1)}, u32[]{:S(2)}) %copy-start.3) | copy-done | bytes 8388632
  190.4 10.1 %collective-permute-done.30.refs_3_ = bf16[2,256,1024]{2,1,0:T(8,128)(2,1)S(1)} collective-permute-done((bf16[2,256,1024]{2,1,0:T(8,128)(2,1)S(1)}, bf16[2,256,1024]{2,1,0:T(8,128)(2,1)S(1)}, u32[]{:S(2)}, u32[]{:S(2)}) %collective-permute-start.30) | collective-permute-done | bytes 1048608 | tf_op jit(solution)/shard_map/ppermute | solution.py:388
  200.6 2.4 collective-permute-done.31
  203.0 1.3 broadcast_select_fusion.refs_2_
  204.3 1.1 collective-permute-start.34
  205.9 1.5 collective-permute-start.32
  207.4 4.8 %backward.7.spec_ref = f32[2,128,8192]{2,1,0:T(8,128)S(1)} custom-call(s32[3,16]{1,0:T(4,128)S(1)} %pad_add_fusion.meta_ref, bf16[1024,1024]{1,0:T(8,128)(2,1)S(1)} %copy-done, bf16[1024,512]{1,0:T(8,128)(2,1)S(1)} %copy-done.2, f32[2,128,8192]{2,1,0:T(8,128)} %copy-done.3, bf16[2,256,1024]{2,1,0:T(8,128)(2,1)S(1)} %collective-permute-done.28.refs_0_, ...), custom_call_target="tpu_custom_call" | custom-call | flops 1024 | bytes 1024 | tf_op jit(solution)/shard_map/backward/pallas_call | solution.py:238
  212.2 3.4 %copy-done.5 = f32[2,128,8192]{2,1,0:T(8,128)} copy-done((f32[2,128,8192]{2,1,0:T(8,128)}, f32[2,128,8192]{2,1,0:T(8,128)S(1)}, u32[]{:S(2)}) %copy-start.5) | copy-done | bytes 8388632
  215.6 6.4 %backward.8.spec_ref = f32[2,128,8192]{2,1,0:T(8,128)S(1)} custom-call(s32[3,16]{1,0:T(4,128)S(1)} %pad_add_fusion.meta_ref, bf16[1024,1024]{1,0:T(8,128)(2,1)S(1)} %copy-done, bf16[1024,512]{1,0:T(8,128)(2,1)S(1)} %copy-done.2, f32[2,128,8192]{2,1,0:T(8,128)} %copy-done.5, bf16[2,256,1024]{2,1,0:T(8,128)(2,1)S(1)} %collective-permute-done.33.refs_0_, ...), custom_call_target="tpu_custom_call" | custom-call | flops 1024 | bytes 1024 | tf_op jit(solution)/shard_map/backward/pallas_call | solution.py:238
  222.1 8.6 %collective-permute-done.32.refs_0_ = bf16[2,256,1024]{2,1,0:T(8,128)(2,1)S(1)} collective-permute-done((bf16[2,256,1024]{2,1,0:T(8,128)(2,1)S(1)}, bf16[2,256,1024]{2,1,0:T(8,128)(2,1)S(1)}, u32[]{:S(2)}, u32[]{:S(2)}) %collective-permute-start.32) | collective-permute-done | bytes 1048608 | tf_op jit(solution)/shard_map/ppermute | solution.py:388
  230.7 0.8 collective-permute-start.36
  231.5 2.3 collective-permute-done.36.refs_1_
  233.8 6.2 %backward.9 = f32[2,128,8192]{2,1,0:T(8,128)} custom-call(s32[3,16]{1,0:T(4,128)S(1)} %pad_add_fusion.meta_ref, bf16[1024,1024]{1,0:T(8,128)(2,1)S(1)} %copy-done, bf16[1024,512]{1,0:T(8,128)(2,1)S(1)} %copy-done.2, f32[2,128,8192]{2,1,0:T(8,128)S(1)} %backward.8.spec_ref, bf16[2,256,1024]{2,1,0:T(8,128)(2,1)S(1)} %collective-permute-done.32.refs_0_, ...), custom_call_target="tpu_custom_call" | custom-call | flops 1024 | bytes 1024 | tf_op jit(solution)/shard_map/backward/pallas_call | solution.py:238
  (68 shorter events, 4.9 us)
Async XLA Ops:
  0.0 3.4 %copy-start.1 = (f32[2,128,8192]{2,1,0:T(8,128)S(1)}, f32[2,128,8192]{2,1,0:T(8,128)}, u32[]{:S(2)}) copy-start(f32[2,128,8192]{2,1,0:T(8,128)} %spec_ref.5) | copy-start | bytes 25165828
  5.3 3.4 %copy-start.12 = (s32[16]{0:T(128)S(1)}, s32[16]{0:T(128)}, u32[]{:S(2)}) copy-start(s32[16]{0:T(128)} %param.12) | copy-start | bytes 196
  5.3 3.4 %copy-start.13 = (s32[16]{0:T(128)S(1)}, s32[16]{0:T(128)}, u32[]{:S(2)}) copy-start(s32[16]{0:T(128)} %param.13) | copy-start | bytes 196
  5.3 3.6 %copy-start = (bf16[1024,1024]{1,0:T(8,128)(2,1)S(1)}, bf16[1024,1024]{1,0:T(8,128)(2,1)}, u32[]{:S(2)}) copy-start(bf16[1024,1024]{1,0:T(8,128)(2,1)} %pupil_ref.15) | copy-start | bytes 6291460
  5.3 3.6 %copy-start.2 = (bf16[1024,512]{1,0:T(8,128)(2,1)S(1)}, bf16[1024,512]{1,0:T(8,128)(2,1)}, u32[]{:S(2)}) copy-start(bf16[1024,512]{1,0:T(8,128)(2,1)} %constant.42.clone.band_ref) | copy-start | bytes 3145732
  5.3 7.0 %collective-permute-start.1 = (bf16[128,8192]{1,0:T(8,128)(2,1)}, bf16[128,8192]{1,0:T(8,128)(2,1)}, u32[]{:S(2)}, u32[]{:S(2)}) collective-permute-start(bf16[128,8192]{1,0:T(8,128)(2,1)} %low_part.3.refs_1_), channel_id=1, source_target_pairs={{0,1},{1,0},{2,3},{3,2},{4,5},{5,4},{6,7},{7,6},{8,9},{9,8},{10,11... | collective-permute-start | bytes 6291464 | tf_op jit(solution)/shard_map/ppermute | solution.py:385
  7.9 5.3 %collective-permute-start = (bf16[128,8192]{1,0:T(8,128)(2,1)}, bf16[128,8192]{1,0:T(8,128)(2,1)}, u32[]{:S(2)}, u32[]{:S(2)}) collective-permute-start(bf16[128,8192]{1,0:T(8,128)(2,1)} %low_part.2.refs_0_), channel_id=1, source_target_pairs={{0,1},{1,0},{2,3},{3,2},{4,5},{5,4},{6,7},{7,6},{8,9},{9,8},{10,11... | collective-permute-start | bytes 6291464 | tf_op jit(solution)/shard_map/ppermute | solution.py:385
  16.5 13.9 %collective-permute-start.2 = (bf16[2,128,1024]{2,1,0:T(8,128)(2,1)S(1)}, bf16[2,128,1024]{2,1,0:T(8,128)(2,1)S(1)}, u32[]{:S(2)}, u32[]{:S(2)}) collective-permute-start(bf16[2,128,1024]{2,1,0:T(8,128)(2,1)S(1)} %get-tuple-element.66), channel_id=1, source_target_pairs={{0,2},{1,3},{2,0},{3,1},{4,6},{5,7},{6,4},{7,5},{8,10},{9,11},{10,... | collective-permute-start | bytes 1572872 | tf_op jit(solution)/shard_map/ppermute | solution.py:388
  16.8 24.1 %collective-permute-start.11 = (bf16[2,128,1024]{2,1,0:T(8,128)(2,1)S(1)}, bf16[2,128,1024]{2,1,0:T(8,128)(2,1)S(1)}, u32[]{:S(2)}, u32[]{:S(2)}) collective-permute-start(bf16[2,128,1024]{2,1,0:T(8,128)(2,1)S(1)} %get-tuple-element.62), channel_id=1, source_target_pairs={{0,2},{1,3},{2,0},{3,1},{4,6},{5,7},{6,4},{7,5},{8,10},{9,11},{10,... | collective-permute-start | bytes 1572872 | tf_op jit(solution)/shard_map/ppermute | solution.py:388
  30.7 12.3 %collective-permute-start.3 = (bf16[2,128,1024]{2,1,0:T(8,128)(2,1)S(1)}, bf16[2,128,1024]{2,1,0:T(8,128)(2,1)S(1)}, u32[]{:S(2)}, u32[]{:S(2)}) collective-permute-start(bf16[2,128,1024]{2,1,0:T(8,128)(2,1)S(1)} %fusion), channel_id=1, source_target_pairs={{0,4},{1,5},{2,6},{3,7},{12,8},{13,9},{14,10},{15,11},{16,20},{17,... | collective-permute-start | bytes 1572872 | tf_op jit(solution)/shard_map/ppermute | solution.py:392
  32.0 20.2 %collective-permute-start.4 = (bf16[2,128,1024]{2,1,0:T(8,128)(2,1)S(1)}, bf16[2,128,1024]{2,1,0:T(8,128)(2,1)S(1)}, u32[]{:S(2)}, u32[]{:S(2)}) collective-permute-start(bf16[2,128,1024]{2,1,0:T(8,128)(2,1)S(1)} %get-tuple-element.71), channel_id=1, source_target_pairs={{0,2},{1,3},{2,0},{3,1},{4,6},{5,7},{6,4},{7,5},{8,10},{9,11},{10,... | collective-permute-start | bytes 1572872 | tf_op jit(solution)/shard_map/ppermute | solution.py:388
  41.1 17.3 %collective-permute-start.12 = (bf16[2,128,1024]{2,1,0:T(8,128)(2,1)S(1)}, bf16[2,128,1024]{2,1,0:T(8,128)(2,1)S(1)}, u32[]{:S(2)}, u32[]{:S(2)}) collective-permute-start(bf16[2,128,1024]{2,1,0:T(8,128)(2,1)S(1)} %fusion.2), channel_id=1, source_target_pairs={{0,4},{1,5},{2,6},{3,7},{12,8},{13,9},{14,10},{15,11},{16,20},{17,... | collective-permute-start | bytes 1572872 | tf_op jit(solution)/shard_map/ppermute | solution.py:392
  42.4 21.0 %collective-permute-start.13 = (bf16[2,128,1024]{2,1,0:T(8,128)(2,1)S(1)}, bf16[2,128,1024]{2,1,0:T(8,128)(2,1)S(1)}, u32[]{:S(2)}, u32[]{:S(2)}) collective-permute-start(bf16[2,128,1024]{2,1,0:T(8,128)(2,1)S(1)} %get-tuple-element.88), channel_id=1, source_target_pairs={{0,2},{1,3},{2,0},{3,1},{4,6},{5,7},{6,4},{7,5},{8,10},{9,11},{10,... | collective-permute-start | bytes 1572872 | tf_op jit(solution)/shard_map/ppermute | solution.py:388
  52.4 16.3 %collective-permute-start.6 = (bf16[2,128,1024]{2,1,0:T(8,128)(2,1)S(1)}, bf16[2,128,1024]{2,1,0:T(8,128)(2,1)S(1)}, u32[]{:S(2)}, u32[]{:S(2)}) collective-permute-start(bf16[2,128,1024]{2,1,0:T(8,128)(2,1)S(1)} %fusion.1), channel_id=1, source_target_pairs={{0,4},{1,5},{2,6},{3,7},{12,8},{13,9},{14,10},{15,11},{16,20},{17,... | collective-permute-start | bytes 1572872 | tf_op jit(solution)/shard_map/ppermute | solution.py:392
  53.9 18.7 %collective-permute-start.5 = (bf16[2,128,1024]{2,1,0:T(8,128)(2,1)S(1)}, bf16[2,128,1024]{2,1,0:T(8,128)(2,1)S(1)}, u32[]{:S(2)}, u32[]{:S(2)}) collective-permute-start(bf16[2,128,1024]{2,1,0:T(8,128)(2,1)S(1)} %add_convert_fusion.7), channel_id=1, source_target_pairs={{4,8},{5,9},{6,10},{7,11},{8,4},{9,5},{10,6},{11,7},{20,24},{21,25... | collective-permute-start | bytes 1572872 | tf_op jit(solution)/shard_map/ppermute | solution.py:392
  57.4 17.2 %collective-permute-start.7 = (bf16[2,128,1024]{2,1,0:T(8,128)(2,1)S(1)}, bf16[2,128,1024]{2,1,0:T(8,128)(2,1)S(1)}, u32[]{:S(2)}, u32[]{:S(2)}) collective-permute-start(bf16[2,128,1024]{2,1,0:T(8,128)(2,1)S(1)} %get-tuple-element.76), channel_id=1, source_target_pairs={{0,2},{1,3},{2,0},{3,1},{4,6},{5,7},{6,4},{7,5},{8,10},{9,11},{10,... | collective-permute-start | bytes 1572872 | tf_op jit(solution)/shard_map/ppermute | solution.py:388
  63.6 16.6 %collective-permute-start.15 = (bf16[2,128,1024]{2,1,0:T(8,128)(2,1)S(1)}, bf16[2,128,1024]{2,1,0:T(8,128)(2,1)S(1)}, u32[]{:S(2)}, u32[]{:S(2)}) collective-permute-start(bf16[2,128,1024]{2,1,0:T(8,128)(2,1)S(1)} %fusion.3), channel_id=1, source_target_pairs={{0,4},{1,5},{2,6},{3,7},{12,8},{13,9},{14,10},{15,11},{16,20},{17,... | collective-permute-start | bytes 1572872 | tf_op jit(solution)/shard_map/ppermute | solution.py:392
  65.2 15.1 %collective-permute-start.14 = (bf16[2,128,1024]{2,1,0:T(8,128)(2,1)S(1)}, bf16[2,128,1024]{2,1,0:T(8,128)(2,1)S(1)}, u32[]{:S(2)}, u32[]{:S(2)}) collective-permute-start(bf16[2,128,1024]{2,1,0:T(8,128)(2,1)S(1)} %add_convert_fusion.3), channel_id=1, source_target_pairs={{4,8},{5,9},{6,10},{7,11},{8,4},{9,5},{10,6},{11,7},{20,24},{21,25... | collective-permute-start | bytes 1572872 | tf_op jit(solution)/shard_map/ppermute | solution.py:392
  68.7 13.8 %collective-permute-start.16 = (bf16[2,128,1024]{2,1,0:T(8,128)(2,1)S(1)}, bf16[2,128,1024]{2,1,0:T(8,128)(2,1)S(1)}, u32[]{:S(2)}, u32[]{:S(2)}) collective-permute-start(bf16[2,128,1024]{2,1,0:T(8,128)(2,1)S(1)} %get-tuple-element.93), channel_id=1, source_target_pairs={{0,2},{1,3},{2,0},{3,1},{4,6},{5,7},{6,4},{7,5},{8,10},{9,11},{10,... | collective-permute-start | bytes 1572872 | tf_op jit(solution)/shard_map/ppermute | solution.py:388
  74.9 18.0 %collective-permute-start.9 = (bf16[2,128,1024]{2,1,0:T(8,128)(2,1)S(1)}, bf16[2,128,1024]{2,1,0:T(8,128)(2,1)S(1)}, u32[]{:S(2)}, u32[]{:S(2)}) collective-permute-start(bf16[2,128,1024]{2,1,0:T(8,128)(2,1)S(1)} %add_convert_fusion.6), channel_id=1, source_target_pairs={{4,8},{5,9},{6,10},{7,11},{8,4},{9,5},{10,6},{11,7},{20,24},{21,25... | collective-permute-start | bytes 1572872 | tf_op jit(solution)/shard_map/ppermute | solution.py:392
  78.4 15.3 %collective-permute-start.8 = (bf16[2,128,1024]{2,1,0:T(8,128)(2,1)S(1)}, bf16[2,128,1024]{2,1,0:T(8,128)(2,1)S(1)}, u32[]{:S(2)}, u32[]{:S(2)}) collective-permute-start(bf16[2,128,1024]{2,1,0:T(8,128)(2,1)S(1)} %get-tuple-element.78), channel_id=1, source_target_pairs={{0,2},{1,3},{2,0},{3,1},{4,6},{5,7},{6,4},{7,5},{8,10},{9,11},{10,... | collective-permute-start | bytes 1572872 | tf_op jit(solution)/shard_map/ppermute | solution.py:388
  80.2 13.5 %collective-permute-start.10 = (bf16[2,128,1024]{2,1,0:T(8,128)(2,1)S(1)}, bf16[2,128,1024]{2,1,0:T(8,128)(2,1)S(1)}, u32[]{:S(2)}, u32[]{:S(2)}) collective-permute-start(bf16[2,128,1024]{2,1,0:T(8,128)(2,1)S(1)} %add_convert_fusion.5), channel_id=1, source_target_pairs={{0,4},{1,5},{2,6},{3,7},{12,8},{13,9},{14,10},{15,11},{4,0},{5,1},... | collective-permute-start | bytes 1572872 | tf_op jit(solution)/shard_map/ppermute | solution.py:392
  82.7 19.9 %collective-permute-start.18 = (bf16[2,128,1024]{2,1,0:T(8,128)(2,1)S(1)}, bf16[2,128,1024]{2,1,0:T(8,128)(2,1)S(1)}, u32[]{:S(2)}, u32[]{:S(2)}) collective-permute-start(bf16[2,128,1024]{2,1,0:T(8,128)(2,1)S(1)} %add_convert_fusion.2), channel_id=1, source_target_pairs={{4,8},{5,9},{6,10},{7,11},{8,4},{9,5},{10,6},{11,7},{20,24},{21,25... | collective-permute-start | bytes 1572872 | tf_op jit(solution)/shard_map/ppermute | solution.py:392
  92.5 14.1 %collective-permute-start.17 = (bf16[2,128,1024]{2,1,0:T(8,128)(2,1)S(1)}, bf16[2,128,1024]{2,1,0:T(8,128)(2,1)S(1)}, u32[]{:S(2)}, u32[]{:S(2)}) collective-permute-start(bf16[2,128,1024]{2,1,0:T(8,128)(2,1)S(1)} %get-tuple-element.95), channel_id=1, source_target_pairs={{0,2},{1,3},{2,0},{3,1},{4,6},{5,7},{6,4},{7,5},{8,10},{9,11},{10,... | collective-permute-start | bytes 1572872 | tf_op jit(solution)/shard_map/ppermute | solution.py:388
  92.9 13.7 %collective-permute-start.19 = (bf16[2,128,1024]{2,1,0:T(8,128)(2,1)S(1)}, bf16[2,128,1024]{2,1,0:T(8,128)(2,1)S(1)}, u32[]{:S(2)}, u32[]{:S(2)}) collective-permute-start(bf16[2,128,1024]{2,1,0:T(8,128)(2,1)S(1)} %add_convert_fusion.1), channel_id=1, source_target_pairs={{0,4},{1,5},{2,6},{3,7},{12,8},{13,9},{14,10},{15,11},{4,0},{5,1},... | collective-permute-start | bytes 1572872 | tf_op jit(solution)/shard_map/ppermute | solution.py:392
  93.7 13.2 %copy-start.9 = (bf16[1024,1024]{1,0:T(8,128)(2,1)S(1)}, bf16[1024,1024]{1,0:T(8,128)(2,1)}, u32[]{:S(2)}) copy-start(bf16[1024,1024]{1,0:T(8,128)(2,1)} %constant.44.clone.refs_4_) | copy-start | bytes 6291460
  93.7 13.3 %copy-start.10 = (bf16[1024,1024]{1,0:T(8,128)(2,1)S(1)}, bf16[1024,1024]{1,0:T(8,128)(2,1)}, u32[]{:S(2)}) copy-start(bf16[1024,1024]{1,0:T(8,128)(2,1)} %constant.43.clone.refs_3_) | copy-start | bytes 6291460
  93.7 13.3 %copy-start.11 = (bf16[1,256,1024]{2,1,0:T(8,128)(2,1)S(1)}, bf16[1,256,1024]{2,1,0:T(8,128)(2,1)}, u32[]{:S(2)}) copy-start(bf16[1,256,1024]{2,1,0:T(8,128)(2,1)} %refs_2_.1) | copy-start | bytes 1572868
  111.8 21.9 %collective-permute-start.22 = (bf16[2,256,1024]{2,1,0:T(8,128)(2,1)S(1)}, bf16[2,256,1024]{2,1,0:T(8,128)(2,1)}, u32[]{:S(2)}, u32[]{:S(2)}) collective-permute-start(bf16[2,256,1024]{2,1,0:T(8,128)(2,1)S(1)} %middle.1.refs_0_), channel_id=1, source_target_pairs={{0,4},{1,5},{2,6},{3,7},{12,8},{13,9},{14,10},{15,11},{4,0},{5,1},... | collective-permute-start | bytes 3145736 | tf_op jit(solution)/shard_map/ppermute | solution.py:392
  111.9 31.2 %collective-permute-start.21 = (bf16[2,256,1024]{2,1,0:T(8,128)(2,1)S(1)}, bf16[2,256,1024]{2,1,0:T(8,128)(2,1)}, u32[]{:S(2)}, u32[]{:S(2)}) collective-permute-start(bf16[2,256,1024]{2,1,0:T(8,128)(2,1)S(1)} %middle.1.refs_0_), channel_id=1, source_target_pairs={{4,8},{5,9},{6,10},{7,11},{8,4},{9,5},{10,6},{11,7},{20,24},{21,25... | collective-permute-start | bytes 3145736 | tf_op jit(solution)/shard_map/ppermute | solution.py:392
  119.8 24.2 %collective-permute-start.20 = (bf16[2,256,1024]{2,1,0:T(8,128)(2,1)S(1)}, bf16[2,256,1024]{2,1,0:T(8,128)(2,1)}, u32[]{:S(2)}, u32[]{:S(2)}) collective-permute-start(bf16[2,256,1024]{2,1,0:T(8,128)(2,1)S(1)} %middle.1.refs_0_), channel_id=1, source_target_pairs={{0,2},{1,3},{2,0},{3,1},{4,6},{5,7},{6,4},{7,5},{8,10},{9,11},{10,... | collective-permute-start | bytes 3145736 | tf_op jit(solution)/shard_map/ppermute | solution.py:388
  119.9 1.0 copy-start.6
  144.0 19.9 %collective-permute-start.24 = (bf16[2,256,1024]{2,1,0:T(8,128)(2,1)}, bf16[2,256,1024]{2,1,0:T(8,128)(2,1)}, u32[]{:S(2)}, u32[]{:S(2)}) collective-permute-start(bf16[2,256,1024]{2,1,0:T(8,128)(2,1)} %collective-permute-done.20.refs_2_), channel_id=1, source_target_pairs={{0,1},{1,0},{2,3},{3,2},{4,5},{5,4},{6,7},{7,6},{8,9},{9,8},{10,11... | collective-permute-start | bytes 3145736 | tf_op jit(solution)/shard_map/ppermute | solution.py:385
  145.5 24.4 %collective-permute-start.27 = (bf16[2,256,1024]{2,1,0:T(8,128)(2,1)}, bf16[2,256,1024]{2,1,0:T(8,128)(2,1)}, u32[]{:S(2)}, u32[]{:S(2)}) collective-permute-start(bf16[2,256,1024]{2,1,0:T(8,128)(2,1)} %collective-permute-done.21), channel_id=1, source_target_pairs={{4,0},{5,1},{6,2},{7,3},{8,12},{9,13},{10,14},{11,15},{20,16},{21,... | collective-permute-start | bytes 3145736 | tf_op jit(solution)/shard_map/ppermute | solution.py:392
  147.8 27.2 %collective-permute-start.26 = (bf16[2,256,1024]{2,1,0:T(8,128)(2,1)}, bf16[2,256,1024]{2,1,0:T(8,128)(2,1)}, u32[]{:S(2)}, u32[]{:S(2)}) collective-permute-start(bf16[2,256,1024]{2,1,0:T(8,128)(2,1)} %collective-permute-done.22.refs_1_), channel_id=1, source_target_pairs={{4,8},{5,9},{6,10},{7,11},{8,4},{9,5},{10,6},{11,7},{20,24},{21,25... | collective-permute-start | bytes 3145736 | tf_op jit(solution)/shard_map/ppermute | solution.py:392
  151.4 24.5 %collective-permute-start.25 = (bf16[2,256,1024]{2,1,0:T(8,128)(2,1)}, bf16[2,256,1024]{2,1,0:T(8,128)(2,1)}, u32[]{:S(2)}, u32[]{:S(2)}) collective-permute-start(bf16[2,256,1024]{2,1,0:T(8,128)(2,1)} %collective-permute-done.22.refs_1_), channel_id=1, source_target_pairs={{0,2},{1,3},{2,0},{3,1},{4,6},{5,7},{6,4},{7,5},{8,10},{9,11},{10,... | collective-permute-start | bytes 3145736 | tf_op jit(solution)/shard_map/ppermute | solution.py:388
  151.5 24.5 %collective-permute-start.23 = (bf16[2,256,1024]{2,1,0:T(8,128)(2,1)}, bf16[2,256,1024]{2,1,0:T(8,128)(2,1)}, u32[]{:S(2)}, u32[]{:S(2)}) collective-permute-start(bf16[2,256,1024]{2,1,0:T(8,128)(2,1)} %collective-permute-done.22.refs_1_), channel_id=1, source_target_pairs={{0,1},{1,0},{2,3},{3,2},{4,5},{5,4},{6,7},{7,6},{8,9},{9,8},{10,11... | collective-permute-start | bytes 3145736 | tf_op jit(solution)/shard_map/ppermute | solution.py:385
  152.3 1.2 copy-start.7
  160.5 3.4 %copy-start.4 = (f32[2,128,8192]{2,1,0:T(8,128)}, f32[2,128,8192]{2,1,0:T(8,128)S(1)}, u32[]{:S(2)}) copy-start(f32[2,128,8192]{2,1,0:T(8,128)S(1)} %backward.5.spec_ref) | copy-start | bytes 25165828
  163.9 15.1 %copy-start.8 = (bf16[2,256,1024]{2,1,0:T(8,128)(2,1)S(1)}, bf16[2,256,1024]{2,1,0:T(8,128)(2,1)}, u32[]{:S(2)}) copy-start(bf16[2,256,1024]{2,1,0:T(8,128)(2,1)} %copy-done.6) | copy-start | bytes 3145732
  177.3 23.3 %collective-permute-start.30 = (bf16[2,256,1024]{2,1,0:T(8,128)(2,1)S(1)}, bf16[2,256,1024]{2,1,0:T(8,128)(2,1)S(1)}, u32[]{:S(2)}, u32[]{:S(2)}) collective-permute-start(bf16[2,256,1024]{2,1,0:T(8,128)(2,1)S(1)} %broadcast_select_fusion.1.refs_2_), channel_id=1, source_target_pairs={{0,2},{1,3},{2,0},{3,1},{4,6},{5,7},{6,4},{7,5},{8,10},{9,11},{10,... | collective-permute-start | bytes 3145736 | tf_op jit(solution)/shard_map/ppermute | solution.py:388
  177.4 23.2 %collective-permute-start.29 = (bf16[2,256,1024]{2,1,0:T(8,128)(2,1)S(1)}, bf16[2,256,1024]{2,1,0:T(8,128)(2,1)S(1)}, u32[]{:S(2)}, u32[]{:S(2)}) collective-permute-start(bf16[2,256,1024]{2,1,0:T(8,128)(2,1)S(1)} %broadcast_select_fusion.1.refs_2_), channel_id=1, source_target_pairs={{0,1},{1,0},{2,3},{3,2},{4,5},{5,4},{6,7},{7,6},{8,9},{9,8},{10,11... | collective-permute-start | bytes 3145736 | tf_op jit(solution)/shard_map/ppermute | solution.py:385
  179.1 21.5 %collective-permute-start.28 = (bf16[2,256,1024]{2,1,0:T(8,128)(2,1)S(1)}, bf16[2,256,1024]{2,1,0:T(8,128)(2,1)S(1)}, u32[]{:S(2)}, u32[]{:S(2)}) collective-permute-start(bf16[2,256,1024]{2,1,0:T(8,128)(2,1)S(1)} %copy-done.8), channel_id=1, source_target_pairs={{0,1},{1,0},{2,3},{3,2},{4,5},{5,4},{6,7},{7,6},{8,9},{9,8},{10,11... | collective-permute-start | bytes 3145736 | tf_op jit(solution)/shard_map/ppermute | solution.py:385
  179.1 23.9 %collective-permute-start.31 = (bf16[2,256,1024]{2,1,0:T(8,128)(2,1)}, bf16[2,256,1024]{2,1,0:T(8,128)(2,1)S(1)}, u32[]{:S(2)}, u32[]{:S(2)}) collective-permute-start(bf16[2,256,1024]{2,1,0:T(8,128)(2,1)} %collective-permute-done.26), channel_id=1, source_target_pairs={{4,0},{5,1},{6,2},{7,3},{8,12},{9,13},{10,14},{11,15},{20,16},{21,... | collective-permute-start | bytes 3145736 | tf_op jit(solution)/shard_map/ppermute | solution.py:392
  187.0 3.4 %copy-start.3 = (f32[2,128,8192]{2,1,0:T(8,128)}, f32[2,128,8192]{2,1,0:T(8,128)S(1)}, u32[]{:S(2)}) copy-start(f32[2,128,8192]{2,1,0:T(8,128)S(1)} %backward.6.spec_ref) | copy-start | bytes 25165828
  204.3 11.3 %collective-permute-start.34 = (bf16[2,256,1024]{2,1,0:T(8,128)(2,1)S(1)}, bf16[2,256,1024]{2,1,0:T(8,128)(2,1)S(1)}, u32[]{:S(2)}, u32[]{:S(2)}) collective-permute-start(bf16[2,256,1024]{2,1,0:T(8,128)(2,1)S(1)} %broadcast_select_fusion.refs_2_), channel_id=1, source_target_pairs={{0,1},{1,0},{2,3},{3,2},{4,5},{5,4},{6,7},{7,6},{8,9},{9,8},{10,11... | collective-permute-start | bytes 3145736 | tf_op jit(solution)/shard_map/ppermute | solution.py:385
  205.4 10.2 %collective-permute-start.33 = (bf16[2,256,1024]{2,1,0:T(8,128)(2,1)}, bf16[2,256,1024]{2,1,0:T(8,128)(2,1)S(1)}, u32[]{:S(2)}, u32[]{:S(2)}) collective-permute-start(bf16[2,256,1024]{2,1,0:T(8,128)(2,1)} %collective-permute-done.25.refs_3_), channel_id=1, source_target_pairs={{0,1},{1,0},{2,3},{3,2},{4,5},{5,4},{6,7},{7,6},{8,9},{9,8},{10,11... | collective-permute-start | bytes 3145736 | tf_op jit(solution)/shard_map/ppermute | solution.py:385
  205.5 10.1 %collective-permute-start.35 = (bf16[2,256,1024]{2,1,0:T(8,128)(2,1)S(1)}, bf16[2,256,1024]{2,1,0:T(8,128)(2,1)S(1)}, u32[]{:S(2)}, u32[]{:S(2)}) collective-permute-start(bf16[2,256,1024]{2,1,0:T(8,128)(2,1)S(1)} %collective-permute-done.30.refs_3_), channel_id=1, source_target_pairs={{0,1},{1,0},{2,3},{3,2},{4,5},{5,4},{6,7},{7,6},{8,9},{9,8},{10,11... | collective-permute-start | bytes 3145736 | tf_op jit(solution)/shard_map/ppermute | solution.py:385
  205.9 24.7 %collective-permute-start.32 = (bf16[2,256,1024]{2,1,0:T(8,128)(2,1)S(1)}, bf16[2,256,1024]{2,1,0:T(8,128)(2,1)S(1)}, u32[]{:S(2)}, u32[]{:S(2)}) collective-permute-start(bf16[2,256,1024]{2,1,0:T(8,128)(2,1)S(1)} %broadcast_select_fusion.refs_2_), channel_id=1, source_target_pairs={{0,2},{1,3},{2,0},{3,1},{4,6},{5,7},{6,4},{7,5},{8,10},{9,11},{10,... | collective-permute-start | bytes 3145736 | tf_op jit(solution)/shard_map/ppermute | solution.py:388
  212.2 3.4 %copy-start.5 = (f32[2,128,8192]{2,1,0:T(8,128)}, f32[2,128,8192]{2,1,0:T(8,128)S(1)}, u32[]{:S(2)}) copy-start(f32[2,128,8192]{2,1,0:T(8,128)S(1)} %backward.7.spec_ref) | copy-start | bytes 25165828
  230.7 3.1 %collective-permute-start.36 = (bf16[2,256,1024]{2,1,0:T(8,128)(2,1)S(1)}, bf16[2,256,1024]{2,1,0:T(8,128)(2,1)S(1)}, u32[]{:S(2)}, u32[]{:S(2)}) collective-permute-start(bf16[2,256,1024]{2,1,0:T(8,128)(2,1)S(1)} %collective-permute-done.32.refs_0_), channel_id=1, source_target_pairs={{0,1},{1,0},{2,3},{3,2},{4,5},{5,4},{6,7},{7,6},{8,9},{9,8},{10,11... | collective-permute-start | bytes 3145736 | tf_op jit(solution)/shard_map/ppermute | solution.py:385

commit v4 on v3

--- a/solution.py
+++ b/solution.py
@@ -13,6 +13,7 @@
 lane = 128
 row_tile = 16
 vmem_bytes = 32 * 1024 * 1024
+backward_bytes = 40 * 1024 * 1024
 
 
 def fourier_tables(crop_width):
@@ -129,8 +130,8 @@
     image_band(meta_ref, pl.program_id(0), lows, (0,), pupil_ref, band_ref, win, store)
 
 
-def subtract_image(meta_ref, slot, back_ref, pupil_ref, band_ref, out_ref, win):
-    first_row, left = meta_ref[0, slot], meta_ref[meta_ref.shape[0] - 1, slot]
+def subtract_image(meta_ref, slot, back_refs, pupil_ref, band_ref, out_ref, win, tile=0):
+    first_row, left = meta_ref[tile, slot], meta_ref[meta_ref.shape[0] - 1, slot]
     tile_rows, crop_width = win.tile_rows, win.crop_width
 
     @pl.when(win.active(first_row))
@@ -138,7 +139,14 @@
         col_start = win.column(left)
         weight = tile_weight(pupil_ref, first_row, win) * step_size
         table = tile_band(band_ref, first_row, win)
-        back = back_ref[...].reshape(table.shape[1], crop_width)
+        band = table.shape[1] // 2
+        rows = band // len(back_refs)
+        held = [number for number, ref in enumerate(back_refs) if ref is not None]
+        if len(held) < len(back_refs):
+            starts = [part * band + number * rows for part in range(2) for number in held]
+            table = jnp.concatenate([table[:, start : start + rows] for start in starts], axis=1)
+        back = [back_refs[number][part] for part in range(2) for number in held]
+        back = jnp.concatenate(back, axis=0)
         grad = jnp.dot(table, back, preferred_element_type=jnp.float32)
         columns = pl.ds(col_start, win.columns)
         pad = jnp.zeros((tile_rows, win.columns - crop_width), jnp.float32)
@@ -148,11 +156,34 @@
             out_ref[part, :, columns] = out_ref[part, :, columns] - piece
 
 
-def backward_kernel(meta_ref, pupil_ref, band_ref, spec_ref, *refs, slots, win):
-    back_refs, out_ref = refs[:-1], refs[-1]
-    out_ref[...] = spec_ref[...]
-    for slot, back_ref in zip(slots, back_refs):
-        subtract_image(meta_ref, slot, back_ref, pupil_ref, band_ref, out_ref, win)
+def backward_kernel(meta_ref, pupil_ref, band_ref, *refs, slots, held, parts, win):
+    part_refs, back_refs, out_ref = refs[:parts], iter(refs[parts:-1]), refs[-1]
+    for number in range(parts - 1):
+        chunk = part_refs[number + 1][...].astype(jnp.float32)
+        width = chunk.shape[2]
+        columns = slice(number * width, (number + 1) * width)
+        out_ref[:, :, columns] = part_refs[0][:, :, columns] + chunk
+    if parts == 1:
+        out_ref[...] = part_refs[0][...]
+    for slot, groups in zip(slots, held):
+        of_image = [next(back_refs) if there else None for there in groups]
+        subtract_image(meta_ref, slot, of_image, pupil_ref, band_ref, out_ref, win)
+
+
+def sibling_kernel(meta_ref, pupil_ref, band_ref, *refs, slots, held, parts, win):
+    backs = sum(map(sum, held))
+    part_refs, back_refs, total_ref = refs[:parts], iter(refs[parts : parts + backs]), refs[-1]
+    out_refs = refs[parts + backs : -1]
+    if parts:
+        total_ref[...] = part_refs[0][...].astype(jnp.float32)
+    else:
+        total_ref[...] = jnp.zeros_like(total_ref)
+    for slot, groups in zip(slots, held):
+        of_image = [next(back_refs) if there else None for there in groups]
+        subtract_image(meta_ref, slot, of_image, pupil_ref, band_ref, total_ref, win, 1)
+    width = out_refs[0].shape[2]
+    for number, out_ref in enumerate(out_refs):
+        out_ref[...] = total_ref[:, :, number * width : (number + 1) * width].astype(jnp.bfloat16)
 
 
 def backward_grid_kernel(meta_ref, pupil_ref, band_ref, spec_ref, back_ref, out_ref, *, win):
@@ -162,12 +193,13 @@
     def _():
         out_ref[...] = spec_ref[...]
 
-    subtract_image(meta_ref, step, back_ref, pupil_ref, band_ref, out_ref, win)
+    subtract_image(meta_ref, step, [back_ref.at[0]], pupil_ref, band_ref, out_ref, win)
 
 
 def middle_kernel(*refs, terms, streams):
     term_refs, refs = refs[: terms * streams], refs[terms * streams :]
-    image_ref, cos_ref, sin_ref, out_ref, mid_ref, resid_ref = refs
+    (image_ref, cos_ref, sin_ref), refs = refs[:3], refs[3:]
+    out_refs, (mid_ref, resid_ref) = refs[:streams], refs[streams:]
     _, rows, crop_width = term_refs[0].shape
     band = rows * streams
     block = min(512, crop_width)
@@ -193,8 +225,10 @@
         columns = slice(start, start + block)
         by_cos = dot(resid_ref[...], cos_ref[:, columns])
         by_sin = dot(resid_ref[...], sin_ref[:, columns])
-        out_ref[0, :, columns] = (by_cos[:band] + by_sin[band:]).astype(jnp.bfloat16)
-        out_ref[1, :, columns] = (by_cos[band:] - by_sin[:band]).astype(jnp.bfloat16)
+        for part, back in enumerate((by_cos[:band] + by_sin[band:], by_cos[band:] - by_sin[:band])):
+            for stream, out_ref in enumerate(out_refs):
+                of_stream = back[stream * rows : (stream + 1) * rows]
+                out_ref[part, :, columns] = of_stream.astype(jnp.bfloat16)
 
 
 def params():
@@ -233,17 +267,25 @@
     )(*operands)
 
 
-def backward(meta, spectrum, pupil, band_table, slots, backs):
-    win = Windows(*spectrum.shape[1:], pupil.shape[1])
+def backward(meta, shape, pupil, band_table, parts, slots, backs, chunks=0):
+    win = Windows(*shape[1:], pupil.shape[1])
+    held = [[back is not None for back in groups] for groups in backs]
+    operands = list(parts) + [back for groups in backs for back in groups if back is not None]
+    kernel = sibling_kernel if chunks else backward_kernel
+    out_shape = jax.ShapeDtypeStruct(shape, jnp.float32)
+    if chunks:
+        chunk = shape[:2] + (shape[2] // chunks,)
+        out_shape = [jax.ShapeDtypeStruct(chunk, jnp.bfloat16)] * chunks
     return pl.pallas_call(
-        functools.partial(backward_kernel, slots=slots, win=win),
-        in_specs=[smem] + [vmem] * (3 + len(backs)),
-        out_specs=vmem,
-        out_shape=jax.ShapeDtypeStruct(spectrum.shape, jnp.float32),
-        compiler_params=params(),
+        functools.partial(kernel, slots=slots, held=held, parts=len(parts), win=win),
+        in_specs=[smem] + [vmem] * (2 + len(operands)),
+        out_specs=[vmem] * chunks if chunks else vmem,
+        out_shape=out_shape,
+        scratch_shapes=[pltpu.VMEM(shape, jnp.float32)] * (chunks > 0),
+        compiler_params=pltpu.CompilerParams(vmem_limit_bytes=backward_bytes),
         cost_estimate=light(),
         name="backward",
-    )(meta, pupil, band_table, spectrum, *backs)
+    )(meta, pupil, band_table, *operands)
 
 
 def middle(streams, image, cos_table, sin_table):
@@ -255,8 +297,8 @@
             middle_kernel, terms=len(streams[0]), streams=len(streams)
         ),
         in_specs=[vmem] * (len(terms) + 3),
-        out_specs=vmem,
-        out_shape=jax.ShapeDtypeStruct((2, band, crop_width), jnp.bfloat16),
+        out_specs=[vmem] * len(streams),
+        out_shape=[jax.ShapeDtypeStruct((2, rows, crop_width), jnp.bfloat16)] * len(streams),
         scratch_shapes=[pltpu.VMEM((2 * band, crop_width), jnp.bfloat16)] * 2,
         compiler_params=params(),
         cost_estimate=light(),
@@ -364,7 +406,7 @@
         meta = image_meta(jnp.arange(count, dtype=jnp.int32), [position])
         partial = forward_all(meta, low, pupil, band_table)
         mid = lax.psum_scatter(partial, "ty", scatter_dimension=0, tiled=True)[0]
-        back = lax.all_gather(middle([[mid]], measured, cos_table, sin_table), "ty")
+        back = lax.all_gather(middle([[mid]], measured, cos_table, sin_table)[0], "ty")
         return backward_all(meta, spectrum, pupil, band_table, back)
 
     targets = {"far": (3, 3, 0, 0), "next": (2, 2, 1, 1), "beside": (1, 0, 3, 2), "own": (0, 1, 2, 3)}
@@ -441,71 +483,68 @@
             terms[0] = together((terms[0], held))[0]
             terms = [total(*terms)]
         summed.insert(0, terms)
-    back = middle(summed, measured, cos_table, sin_table)
-
-    def apply(result, pieces):
-        names, values = zip(*pieces)
-        return backward(
-            meta, result, pupil, band_table, [slots[name] for name in names], list(values)
-        )
-
-    other = across(back)
-    from_inner = along(back, inner)
-    from_beside = along(back, inward + outward)
-    other, from_inner, from_beside, back = together((other, from_inner, from_beside, back))
-
-    beside_twin, other_twin = sibling(from_beside), sibling(other)
-    beside_other = across(from_beside)
-    far_inner = along(from_beside, inner)
-    next_outward = along(from_inner, outward)
-    result = apply(
-        spectrum, [(("own", 0), back), (("beside", 0), from_beside), (("own", 2), other)]
+    backs = middle(summed, measured, cos_table, sin_table)
+
+    at_ends = (plane == 0) | (plane == 3)
+    lead, last = streams - 1, 0
+    pieces = {}
+
+    def apply(parts, names, chunks=0):
+        taken = [[pieces.get((name, stream)) for stream in range(streams)] for name in names]
+        own_slots = [slots[name] for name in names]
+        shape = spectrum.shape
+        return backward(meta, shape, pupil, band_table, parts, own_slots, taken, chunks)
+
+    def close(stream, *names):
+        closed = together(tuple(pieces[name, stream] for name in names))
+        for name, value in zip(names, closed):
+            pieces[name, stream] = value
+
+    for stream in (lead, last):
+        back = pieces[("own", 0), stream] = backs[stream]
+        pieces[("own", 2), stream] = across(back)
+        pieces["inner", stream] = along(back, inner)
+        pieces[("beside", 0), stream] = along(back, inward + outward)
+        close(stream, ("own", 2), "inner", ("beside", 0))
+    early, later, late = (
+        [("own", 0), ("beside", 0), ("own", 2)],
+        [("next", 0), ("beside", 2)],
+        [("far", 0), ("next", 2)],
     )
-    beside_twin, other_twin, beside_other, far_inner, next_outward, back, result = together(
-        (beside_twin, other_twin, beside_other, far_inner, next_outward, back, result)
-    )
-
-    at_ends = (plane == 0) | (plane == 3)
-    from_next = jnp.where(at_ends, next_outward, from_inner)
-    twin, next_twin = sibling(back), sibling(from_next)
-    next_other = across(from_next)
-    far_outward = along(far_inner, outward)
-    result = apply(
-        result,
-        [
-            (("own", 3), other_twin),
-            (("beside", 1), beside_twin),
-            (("next", 0), from_next),
-            (("beside", 2), beside_other),
-        ],
-    )
-    twin, next_twin, next_other, far_outward, beside_other, result = together(
-        (twin, next_twin, next_other, far_outward, beside_other, result)
-    )
-
-    from_far = jnp.where(at_ends, far_outward, far_inner)
-    beside_other_twin, far_twin = sibling(beside_other), sibling(from_far)
-    next_other_twin = sibling(next_other)
-    far_other = across(from_far)
-    result = apply(
-        result,
-        [
-            (("own", 1), twin),
-            (("next", 1), next_twin),
-            (("far", 0), from_far),
-            (("next", 2), next_other),
-        ],
-    )
-    result = apply(
-        result,
-        [
-            (("beside", 3), beside_other_twin),
-            (("far", 1), far_twin),
-            (("next", 3), next_other_twin),
-        ],
-    )
-    far_other, result = together((far_other, result))
-    return apply(result, [(("far", 2), far_other), (("far", 3), sibling(far_other))])
+    for stream in (lead, last):
+        pieces[("beside", 2), stream] = across(pieces[("beside", 0), stream])
+        pieces["far inner", stream] = along(pieces[("beside", 0), stream], inner)
+        pieces["outward", stream] = along(pieces["inner", stream], outward)
+        if stream == last:
+            pieces["result", stream] = apply([spectrum], early)
+            close(stream, ("beside", 2), "far inner", "outward", "result")
+        else:
+            close(stream, ("beside", 2), "far inner", "outward")
+    for stream in (lead, last):
+        from_next = jnp.where(at_ends, pieces["outward", stream], pieces["inner", stream])
+        pieces[("next", 0), stream] = from_next
+        pieces[("next", 2), stream] = across(from_next)
+        pieces["far outward", stream] = along(pieces["far inner", stream], outward)
+        if stream == lead:
+            pieces["slab", stream] = apply([], early, 1)[0]
+        else:
+            pieces["slab", stream] = apply([pieces["slab", lead]], later, 1)[0]
+        close(stream, ("next", 2), "far outward", "slab")
+    for stream in (lead, last):
+        from_far = jnp.where(at_ends, pieces["far outward", stream], pieces["far inner", stream])
+        pieces[("far", 0), stream] = from_far
+        pieces[("far", 2), stream] = across(from_far)
+    slab, pieces[("far", 2), lead] = together((pieces["slab", last], pieces[("far", 2), lead]))
+    slab = [sibling(chunk) for chunk in apply([slab], late, 2)]
+    result = apply([pieces["result", last]], later + late)
+    for stream in (lead, last):
+        if stream == last:
+            arriving, result, twin = together(
+                (pieces[("far", 2), stream], result, pieces[("far", 3), lead])
+            )
+            pieces[("far", 2), stream], pieces[("far", 3), lead] = arriving, twin
+        pieces[("far", 3), stream] = sibling(pieces[("far", 2), stream])
+    return apply([result] + slab, [("far", 2), ("far", 3)])
 
 
 def solution(mesh):

time: 241 us -> 232 us (0.963)
  waiting for transfers between devices: 94.1 us -> 75.4 us
  Pallas kernels: 58.6 us -> 69.6 us
  local copies, waits for them, and re-layouts: 16.5 us -> 7.79 us
  starting transfers between devices: 64.3 us -> 70.9 us
    ppermute x15 -> x20, waiting for transfers between devices: 44.8 us -> 33.5 us  [along(): return lax.ppermute(value, 'ty', pairs)]
    unnamed x28 -> x24, local copies, waits for them, and re-layouts: 15.8 us -> 7.09 us
    pallas_call x5 -> x6, Pallas kernels: 31 us -> 39.2 us  [backward(): pl.pallas_call(functools.partial(kernel, slots=slots, held=held, parts=le...]
    ppermute x15 -> x20, starting transfers between devices: 40.7 us -> 48.5 us  [along(): return lax.ppermute(value, 'ty', pairs)]
    ppermute x12 -> x16, waiting for transfers between devices: 46.1 us -> 39.4 us  [across(): return lax.ppermute(value, 'ty', [(i, i ^ 2) for i in range(count)])]
    ppermute x10 -> x6, starting transfers between devices: 7.37 us -> 5 us  [sibling(): return lax.ppermute(value, 'ty', [(i, i ^ 1) for i in range(count)])]
    ppermute x12 -> x16, starting transfers between devices: 16.3 us -> 17.4 us  [across(): return lax.ppermute(value, 'ty', [(i, i ^ 2) for i in range(count)])]
  transfers between devices with their start and end apart: 37 -> 42, of which waited for: 20 -> 25; matrix products, arithmetic and copies ran while one was open for 2% -> 3% of each run, Pallas kernels for 18% -> 20%
where the time goes in v4:
time: 232 us; the launch traced here: 231 us
  waiting for transfers between devices  75.4 us (33%)
  starting transfers between devices  70.9 us (31%)
  Pallas kernels  69.6 us (30%)
  local copies, waits for them, and re-layouts  7.79 us (3%)
  other arithmetic  6.67 us (3%)
    ppermute x20, starting transfers between devices, along(): return lax.ppermute(value, 'ty', pairs)  48.5 us
    ppermute x16, waiting for transfers between devices, across(): return lax.ppermute(value, 'ty', [(i, i ^ 2) for i in range(count)])  39.4 us
    pallas_call x6, Pallas kernels, backward(): pl.pallas_call(functools.partial(kernel, slots=slots, held=held, parts=le...  39.2 us
    ppermute x20, waiting for transfers between devices, along(): return lax.ppermute(value, 'ty', pairs)  33.5 us
    pallas_call x3, Pallas kernels, forward(): pl.pallas_call(functools.partial(forward_kernel, base=base, images=images...  21.1 us
    ppermute x16, starting transfers between devices, across(): return lax.ppermute(value, 'ty', [(i, i ^ 2) for i in range(count)])  17.4 us
    unnamed x24, local copies, waits for them, and re-layouts  7.09 us
    pallas_call x1, Pallas kernels, middle(): pl.pallas_call(functools.partial(middle_kernel, terms=len(streams[0]), st...  5.6 us
  transfers between devices with their start and end apart: 42, of which 25 were waited for; matrix products, arithmetic and copies ran while one was open for 3% of the time, Pallas kernels for 20%

profile of v4, /device:TPU:11, one launch (start us, length us, event | category | flops | bytes accessed | tf_op | source)
XLA Modules:
  0.0 230.8 jit_solution(9720353390995184997)
XLA Ops:
  0.0 3.4 %copy-done.2 = f32[2,128,8192]{2,1,0:T(8,128)S(1)} copy-done((f32[2,128,8192]{2,1,0:T(8,128)S(1)}, f32[2,128,8192]{2,1,0:T(8,128)}, u32[]{:S(2)}) %copy-start.2) | copy-done | bytes 8388632
  3.4 1.9 low_part.3.refs_1_
  6.1 1.8 low_part.2.refs_0_
  9.0 3.3 %forward.3.refs_2_ = bf16[2,256,1024]{2,1,0:T(8,128)(2,1)S(1)} custom-call(s32[3,16]{1,0:T(4,128)S(1)} %pad_add_fusion.meta_ref, bf16[1024,1024]{1,0:T(8,128)(2,1)S(1)} %copy-done, bf16[1024,512]{1,0:T(8,128)(2,1)S(1)} %copy-done.1, bf16[128,8192]{1,0:T(8,128)(2,1)} %low_part.2.refs_0_, bf16[128,8192]{1,0:T(8,128)(2,1)} %low_part.3.refs_1_), custom_call_target="tpu_custom_call" | custom-call | flops 1024 | bytes 1024 | tf_op jit(solution)/shard_map/forward/pallas_call | solution.py:257
  13.2 3.3 %forward.4 = (bf16[2,128,1024]{2,1,0:T(8,128)(2,1)S(1)}, bf16[2,128,1024]{2,1,0:T(8,128)(2,1)S(1)}) custom-call(s32[3,16]{1,0:T(4,128)S(1)} %pad_add_fusion.meta_ref, bf16[1024,1024]{1,0:T(8,128)(2,1)S(1)} %copy-done, bf16[1024,512]{1,0:T(8,128)(2,1)S(1)} %copy-done.1, bf16[128,8192]{1,0:T(8,128)(2,1)} %collective-permute-done.refs_0_.refs_2_, ...), custom_call_target="tpu_custom_call" | custom-call | flops 1024 | bytes 1024 | tf_op jit(solution)/shard_map/forward/pallas_call | solution.py:257
  16.5 1.3 collective-permute-start.2
  18.1 14.4 %forward.5 = (bf16[2,128,1024]{2,1,0:T(8,128)(2,1)S(1)}, bf16[2,128,1024]{2,1,0:T(8,128)(2,1)S(1)}, bf16[2,128,1024]{2,1,0:T(8,128)(2,1)S(1)}, bf16[2,128,1024]{...) custom-call(s32[3,16]{1,0:T(4,128)S(1)} %pad_add_fusion.meta_ref, ...), custom_call_target="tpu_custom_call" | custom-call | flops 1024 | bytes 1024 | tf_op jit(solution)/shard_map/forward/pallas_call | solution.py:257
  32.7 1.3 collective-permute-start.3
  34.0 3.3 %collective-permute-start.4 = (bf16[2,128,1024]{2,1,0:T(8,128)(2,1)S(1)}, bf16[2,128,1024]{2,1,0:T(8,128)(2,1)S(1)}, u32[]{:S(2)}, u32[]{:S(2)}) collective-permute-start(bf16[2,128,1024]{2,1,0:T(8,128)(2,1)S(1)} %get-tuple-element.80), channel_id=1, source_target_pairs={{0,2},{1,3},{2,0},{3,1},{4,6},{5,7},{6,4},{7,5},{8,10},{9,11},{10,... | collective-permute-start | bytes 1572872 | tf_op jit(solution)/shard_map/ppermute | solution.py:430
  37.3 3.7 %collective-permute-done.11 = bf16[2,128,1024]{2,1,0:T(8,128)(2,1)S(1)} collective-permute-done((bf16[2,128,1024]{2,1,0:T(8,128)(2,1)S(1)}, bf16[2,128,1024]{2,1,0:T(8,128)(2,1)S(1)}, u32[]{:S(2)}, u32[]{:S(2)}) %collective-permute-start.11) | collective-permute-done | bytes 524320 | tf_op jit(solution)/shard_map/ppermute | solution.py:430
  41.2 1.3 collective-permute-start.12
  42.5 1.3 collective-permute-start.13
  43.8 4.5 %collective-permute-done.3 = bf16[2,128,1024]{2,1,0:T(8,128)(2,1)S(1)} collective-permute-done((bf16[2,128,1024]{2,1,0:T(8,128)(2,1)S(1)}, bf16[2,128,1024]{2,1,0:T(8,128)(2,1)S(1)}, u32[]{:S(2)}, u32[]{:S(2)}) %collective-permute-start.3) | collective-permute-done | bytes 524320 | tf_op jit(solution)/shard_map/ppermute | solution.py:434
  48.2 4.0 %collective-permute-done.4 = bf16[2,128,1024]{2,1,0:T(8,128)(2,1)S(1)} collective-permute-done((bf16[2,128,1024]{2,1,0:T(8,128)(2,1)S(1)}, bf16[2,128,1024]{2,1,0:T(8,128)(2,1)S(1)}, u32[]{:S(2)}, u32[]{:S(2)}) %collective-permute-start.4) | collective-permute-done | bytes 524320 | tf_op jit(solution)/shard_map/ppermute | solution.py:430
  52.4 1.3 collective-permute-start.6
  54.0 3.6 %collective-permute-start.5 = (bf16[2,128,1024]{2,1,0:T(8,128)(2,1)S(1)}, bf16[2,128,1024]{2,1,0:T(8,128)(2,1)S(1)}, u32[]{:S(2)}, u32[]{:S(2)}) collective-permute-start(bf16[2,128,1024]{2,1,0:T(8,128)(2,1)S(1)} %add_convert_fusion.7), channel_id=1, source_target_pairs={{4,8},{5,9},{6,10},{7,11},{8,4},{9,5},{10,6},{11,7},{20,24},{21,25... | collective-permute-start | bytes 1572872 | tf_op jit(solution)/shard_map/ppermute | solution.py:434
  57.6 0.9 collective-permute-start.7
  58.5 0.9 collective-permute-done.12
  59.4 4.0 %collective-permute-done.13 = bf16[2,128,1024]{2,1,0:T(8,128)(2,1)S(1)} collective-permute-done((bf16[2,128,1024]{2,1,0:T(8,128)(2,1)S(1)}, bf16[2,128,1024]{2,1,0:T(8,128)(2,1)S(1)}, u32[]{:S(2)}, u32[]{:S(2)}) %collective-permute-start.13) | collective-permute-done | bytes 524320 | tf_op jit(solution)/shard_map/ppermute | solution.py:430
  63.6 1.3 collective-permute-start.15
  65.2 3.6 %collective-permute-start.14 = (bf16[2,128,1024]{2,1,0:T(8,128)(2,1)S(1)}, bf16[2,128,1024]{2,1,0:T(8,128)(2,1)S(1)}, u32[]{:S(2)}, u32[]{:S(2)}) collective-permute-start(bf16[2,128,1024]{2,1,0:T(8,128)(2,1)S(1)} %add_convert_fusion.3), channel_id=1, source_target_pairs={{4,8},{5,9},{6,10},{7,11},{8,4},{9,5},{10,6},{11,7},{20,24},{21,25... | collective-permute-start | bytes 1572872 | tf_op jit(solution)/shard_map/ppermute | solution.py:434
  68.8 1.9 collective-permute-done.6
  70.8 3.9 %collective-permute-done.7 = bf16[2,128,1024]{2,1,0:T(8,128)(2,1)S(1)} collective-permute-done((bf16[2,128,1024]{2,1,0:T(8,128)(2,1)S(1)}, bf16[2,128,1024]{2,1,0:T(8,128)(2,1)S(1)}, u32[]{:S(2)}, u32[]{:S(2)}) %collective-permute-start.7) | collective-permute-done | bytes 524320 | tf_op jit(solution)/shard_map/ppermute | solution.py:430
  75.0 3.6 %collective-permute-start.9 = (bf16[2,128,1024]{2,1,0:T(8,128)(2,1)S(1)}, bf16[2,128,1024]{2,1,0:T(8,128)(2,1)S(1)}, u32[]{:S(2)}, u32[]{:S(2)}) collective-permute-start(bf16[2,128,1024]{2,1,0:T(8,128)(2,1)S(1)} %add_convert_fusion.6), channel_id=1, source_target_pairs={{4,8},{5,9},{6,10},{7,11},{8,4},{9,5},{10,6},{11,7},{20,24},{21,25... | collective-permute-start | bytes 1572872 | tf_op jit(solution)/shard_map/ppermute | solution.py:434
  78.5 1.5 collective-permute-start.8
  80.3 1.5 collective-permute-done.15
  82.9 9.7 %collective-permute-start.18 = (bf16[2,128,1024]{2,1,0:T(8,128)(2,1)S(1)}, bf16[2,128,1024]{2,1,0:T(8,128)(2,1)S(1)}, u32[]{:S(2)}, u32[]{:S(2)}) collective-permute-start(bf16[2,128,1024]{2,1,0:T(8,128)(2,1)S(1)} %add_convert_fusion.2), channel_id=1, source_target_pairs={{4,8},{5,9},{6,10},{7,11},{8,4},{9,5},{10,6},{11,7},{20,24},{21,25... | collective-permute-start | bytes 1572872 | tf_op jit(solution)/shard_map/ppermute | solution.py:434
  93.8 1.1 collective-permute-done.10
  95.3 7.5 %collective-permute-done.18 = bf16[2,128,1024]{2,1,0:T(8,128)(2,1)S(1)} collective-permute-done((bf16[2,128,1024]{2,1,0:T(8,128)(2,1)S(1)}, bf16[2,128,1024]{2,1,0:T(8,128)(2,1)S(1)}, u32[]{:S(2)}, u32[]{:S(2)}) %collective-permute-start.18) | collective-permute-done | bytes 524320 | tf_op jit(solution)/shard_map/ppermute | solution.py:434
  102.8 3.8 %collective-permute-done.17 = bf16[2,128,1024]{2,1,0:T(8,128)(2,1)S(1)} collective-permute-done((bf16[2,128,1024]{2,1,0:T(8,128)(2,1)S(1)}, bf16[2,128,1024]{2,1,0:T(8,128)(2,1)S(1)}, u32[]{:S(2)}, u32[]{:S(2)}) %collective-permute-start.17) | collective-permute-done | bytes 524320 | tf_op jit(solution)/shard_map/ppermute | solution.py:430
  107.0 5.6 %middle.1 = (bf16[2,128,1024]{2,1,0:T(8,128)(2,1)}, bf16[2,128,1024]{2,1,0:T(8,128)(2,1)S(1)}) custom-call(bf16[2,128,1024]{2,1,0:T(8,128)(2,1)S(1)} %add_convert_fusion.refs_0_, bf16[2,128,1024]{2,1,0:T(8,128)(2,1)S(1)} %add_convert_fusion.4.refs_1_, bf16[1,256,1024]{2,1,0:T(8,128)(2,1)S(1)} %copy-done.9, bf16[1024,1024]{1,0:T(8,128)(2,1)S(1)} %copy-done.8, ...), custom_call_target="tpu_custom_call" | custom-call | flops 1024 | bytes 1024 | tf_op jit(solution)/shard_map/middle/pallas_call | solution.py:295
  112.6 7.4 %collective-permute-start.27 = (bf16[2,128,1024]{2,1,0:T(8,128)(2,1)S(1)}, bf16[2,128,1024]{2,1,0:T(8,128)(2,1)}, u32[]{:S(2)}, u32[]{:S(2)}) collective-permute-start(bf16[2,128,1024]{2,1,0:T(8,128)(2,1)S(1)} %get-tuple-element.112.refs_2_.refs_1_), channel_id=1, source_target_pairs={{4,8},{5,9},{6,10},{7,11},{8,4},{9,5},{10,6},{11,7},{20,24},{21,25... | collective-permute-start | bytes 1572872 | tf_op jit(solution)/shard_map/ppermute | solution.py:434
  121.0 2.7 %collective-permute-start.21 = (bf16[2,128,1024]{2,1,0:T(8,128)(2,1)}, bf16[2,128,1024]{2,1,0:T(8,128)(2,1)}, u32[]{:S(2)}, u32[]{:S(2)}) collective-permute-start(bf16[2,128,1024]{2,1,0:T(8,128)(2,1)} %get-tuple-element.109.refs_1_.refs_0_), channel_id=1, source_target_pairs={{4,8},{5,9},{6,10},{7,11},{8,4},{9,5},{10,6},{11,7},{20,24},{21,25... | collective-permute-start | bytes 1572872 | tf_op jit(solution)/shard_map/ppermute | solution.py:434
  123.7 1.5 collective-permute-start.20
  125.3 6.6 %collective-permute-done.27 = bf16[2,128,1024]{2,1,0:T(8,128)(2,1)} collective-permute-done((bf16[2,128,1024]{2,1,0:T(8,128)(2,1)S(1)}, bf16[2,128,1024]{2,1,0:T(8,128)(2,1)}, u32[]{:S(2)}, u32[]{:S(2)}) %collective-permute-start.27) | collective-permute-done | bytes 524320 | tf_op jit(solution)/shard_map/ppermute | solution.py:434
  131.9 0.9 collective-permute-done.26.refs_6_.refs_5_
  133.6 2.1 collective-permute-start.33
  135.7 3.7 %collective-permute-start.32 = (bf16[2,128,1024]{2,1,0:T(8,128)(2,1)}, bf16[2,128,1024]{2,1,0:T(8,128)(2,1)}, u32[]{:S(2)}, u32[]{:S(2)}) collective-permute-start(bf16[2,128,1024]{2,1,0:T(8,128)(2,1)} %collective-permute-done.28.refs_4_.refs_3_), channel_id=1, source_target_pairs={{4,8},{5,9},{6,10},{7,11},{8,4},{9,5},{10,6},{11,7},{20,24},{21,25... | collective-permute-start | bytes 1572872 | tf_op jit(solution)/shard_map/ppermute | solution.py:434
  139.7 3.4 %collective-permute-done.21 = bf16[2,128,1024]{2,1,0:T(8,128)(2,1)} collective-permute-done((bf16[2,128,1024]{2,1,0:T(8,128)(2,1)}, bf16[2,128,1024]{2,1,0:T(8,128)(2,1)}, u32[]{:S(2)}, u32[]{:S(2)}) %collective-permute-start.21) | collective-permute-done | bytes 524320 | tf_op jit(solution)/shard_map/ppermute | solution.py:434
  143.1 0.9 collective-permute-done.20.refs_5_.refs_4_
  144.0 1.3 collective-permute-start.25
  145.3 3.1 %collective-permute-start.24 = (bf16[2,128,1024]{2,1,0:T(8,128)(2,1)}, bf16[2,128,1024]{2,1,0:T(8,128)(2,1)S(1)}, u32[]{:S(2)}, u32[]{:S(2)}) collective-permute-start(bf16[2,128,1024]{2,1,0:T(8,128)(2,1)} %collective-permute-done.22.refs_3_.refs_2_), channel_id=1, source_target_pairs={{4,8},{5,9},{6,10},{7,11},{8,4},{9,5},{10,6},{11,7},{20,24},{21,25... | collective-permute-start | bytes 1572872 | tf_op jit(solution)/shard_map/ppermute | solution.py:434
  148.5 5.8 %collective-permute-done.32 = bf16[2,128,1024]{2,1,0:T(8,128)(2,1)} collective-permute-done((bf16[2,128,1024]{2,1,0:T(8,128)(2,1)}, bf16[2,128,1024]{2,1,0:T(8,128)(2,1)}, u32[]{:S(2)}, u32[]{:S(2)}) %collective-permute-start.32) | collective-permute-done | bytes 524320 | tf_op jit(solution)/shard_map/ppermute | solution.py:434
  155.2 1.1 broadcast_select_fusion.2.refs_2_
  156.4 1.3 collective-permute-start.35
  157.8 1.0 copy-done.4
  158.8 1.0 copy-done.6
  159.8 4.1 %backward.7.refs_0_ = bf16[2,128,8192]{2,1,0:T(8,128)(2,1)S(1)} custom-call(s32[3,16]{1,0:T(4,128)S(1)} %pad_add_fusion.meta_ref, bf16[1024,1024]{1,0:T(8,128)(2,1)S(1)} %copy-done, bf16[1024,512]{1,0:T(8,128)(2,1)S(1)} %copy-done.1, bf16[2,128,1024]{2,1,0:T(8,128)(2,1)} %get-tuple-element.109.refs_1_.refs_0_, bf16[2,128,1024]{2,1,0:T(8,128)(2,1)S(1)} %copy-done.4, ...), custom_call_target="tpu_custom_call" | custom-call | flops 1024 | bytes 1024 | tf_op jit(solution)/shard_map/backward/pallas_call | solution.py:279
  164.0 9.7 %backward.6.refs_0_ = f32[2,128,8192]{2,1,0:T(8,128)} custom-call(s32[3,16]{1,0:T(4,128)S(1)} %pad_add_fusion.meta_ref, bf16[1024,1024]{1,0:T(8,128)(2,1)S(1)} %copy-done, bf16[1024,512]{1,0:T(8,128)(2,1)S(1)} %copy-done.1, f32[2,128,8192]{2,1,0:T(8,128)} %refs_0_.1, bf16[2,128,1024]{2,1,0:T(8,128)(2,1)} %get-tuple-element.109.refs_1_.refs_0_, ...), custom_call_target="tpu_custom_call" | custom-call | flops 1024 | bytes 1024 | tf_op jit(solution)/shard_map/backward/pallas_call | solution.py:279
  173.8 1.1 broadcast_select_fusion.3.refs_1_
  174.9 3.1 %collective-permute-start.29 = (bf16[2,128,1024]{2,1,0:T(8,128)(2,1)S(1)}, bf16[2,128,1024]{2,1,0:T(8,128)(2,1)S(1)}, u32[]{:S(2)}, u32[]{:S(2)}) collective-permute-start(bf16[2,128,1024]{2,1,0:T(8,128)(2,1)S(1)} %broadcast_select_fusion.3.refs_1_), channel_id=1, source_target_pairs={{0,2},{1,3},{2,0},{3,1},{4,6},{5,7},{6,4},{7,5},{8,10},{9,11},{10,... | collective-permute-start | bytes 1572872 | tf_op jit(solution)/shard_map/ppermute | solution.py:430
  178.0 1.3 collective-permute-start.30
  179.3 1.1 broadcast_select_fusion.refs_6_.refs_2_
  180.5 2.8 %backward.8.refs_0_ = bf16[2,128,8192]{2,1,0:T(8,128)(2,1)S(1)} custom-call(s32[3,16]{1,0:T(4,128)S(1)} %pad_add_fusion.meta_ref, bf16[1024,1024]{1,0:T(8,128)(2,1)S(1)} %copy-done, bf16[1024,512]{1,0:T(8,128)(2,1)S(1)} %copy-done.1, bf16[2,128,8192]{2,1,0:T(8,128)(2,1)S(1)} %backward.7.refs_0_, bf16[2,128,1024]{2,1,0:T(8,128)(2,1)S(1)} %broadcast_select_fusion.3.refs_1_, ...), custom_call_target="tpu_custom_call" | custom-call | flops 1024 | bytes 1024 | tf_op jit(solution)/shard_map/backward/pallas_call | solution.py:279
  183.3 3.5 %collective-permute-done.29.refs_7_.refs_3_ = bf16[2,128,1024]{2,1,0:T(8,128)(2,1)S(1)} collective-permute-done((bf16[2,128,1024]{2,1,0:T(8,128)(2,1)S(1)}, bf16[2,128,1024]{2,1,0:T(8,128)(2,1)S(1)}, u32[]{:S(2)}, u32[]{:S(2)}) %collective-permute-start.29) | collective-permute-done | bytes 524320 | tf_op jit(solution)/shard_map/ppermute | solution.py:430
  187.1 10.9 %collective-permute-done.37.refs_4_ = bf16[2,128,1024]{2,1,0:T(8,128)(2,1)S(1)} collective-permute-done((bf16[2,128,1024]{2,1,0:T(8,128)(2,1)S(1)}, bf16[2,128,1024]{2,1,0:T(8,128)(2,1)S(1)}, u32[]{:S(2)}, u32[]{:S(2)}) %collective-permute-start.37) | collective-permute-done | bytes 524320 | tf_op jit(solution)/shard_map/ppermute | solution.py:430
  198.0 3.2 %backward.10 = (bf16[2,128,4096]{2,1,0:T(8,128)(2,1)S(1)}, bf16[2,128,4096]{2,1,0:T(8,128)(2,1)S(1)}) custom-call(s32[3,16]{1,0:T(4,128)S(1)} %pad_add_fusion.meta_ref, bf16[1024,1024]{1,0:T(8,128)(2,1)S(1)} %copy-done, bf16[1024,512]{1,0:T(8,128)(2,1)S(1)} %copy-done.1, bf16[2,128,8192]{2,1,0:T(8,128)(2,1)S(1)} %backward.8.refs_0_, ...), custom_call_target="tpu_custom_call" | custom-call | flops 1024 | bytes 1024 | tf_op jit(solution)/shard_map/backward/pallas_call | solution.py:279
  201.2 2.4 %collective-permute-start.39 = (bf16[2,128,4096]{2,1,0:T(8,128)(2,1)S(1)}, bf16[2,128,4096]{2,1,0:T(8,128)(2,1)S(1)}, u32[]{:S(2)}, u32[]{:S(2)}) collective-permute-start(bf16[2,128,4096]{2,1,0:T(8,128)(2,1)S(1)} %get-tuple-element.133), channel_id=1, source_target_pairs={{0,1},{1,0},{2,3},{3,2},{4,5},{5,4},{6,7},{7,6},{8,9},{9,8},{10,11... | collective-permute-start | bytes 6291464 | tf_op jit(solution)/shard_map/ppermute | solution.py:427
  203.8 3.1 %collective-permute-start.36 = (bf16[2,128,1024]{2,1,0:T(8,128)(2,1)S(1)}, bf16[2,128,1024]{2,1,0:T(8,128)(2,1)S(1)}, u32[]{:S(2)}, u32[]{:S(2)}) collective-permute-start(bf16[2,128,1024]{2,1,0:T(8,128)(2,1)S(1)} %broadcast_select_fusion.1.refs_5_.refs_1_), channel_id=1, source_target_pairs={{0,2},{1,3},{2,0},{3,1},{4,6},{5,7},{6,4},{7,5},{8,10},{9,11},{10,... | collective-permute-start | bytes 1572872 | tf_op jit(solution)/shard_map/ppermute | solution.py:430
  207.6 9.8 %backward.9.refs_0_ = f32[2,128,8192]{2,1,0:T(8,128)} custom-call(s32[3,16]{1,0:T(4,128)S(1)} %pad_add_fusion.meta_ref, bf16[1024,1024]{1,0:T(8,128)(2,1)S(1)} %copy-done, bf16[1024,512]{1,0:T(8,128)(2,1)S(1)} %copy-done.1, f32[2,128,8192]{2,1,0:T(8,128)} %backward.6.refs_0_, bf16[2,128,1024]{2,1,0:T(8,128)(2,1)S(1)} %broadcast_select_fusion.3.refs_1_, ...), custom_call_target="tpu_custom_call" | custom-call | flops 1024 | bytes 1024 | tf_op jit(solution)/shard_map/backward/pallas_call | solution.py:279
  217.4 1.4 collective-permute-done.36.refs_3_
  218.8 1.0 collective-permute-start.41
  219.7 1.5 collective-permute-done.41.refs_5_
  221.3 9.5 %backward.11 = f32[2,128,8192]{2,1,0:T(8,128)} custom-call(s32[3,16]{1,0:T(4,128)S(1)} %pad_add_fusion.meta_ref, bf16[1024,1024]{1,0:T(8,128)(2,1)S(1)} %copy-done, bf16[1024,512]{1,0:T(8,128)(2,1)S(1)} %copy-done.1, f32[2,128,8192]{2,1,0:T(8,128)} %backward.9.refs_0_, bf16[2,128,4096]{2,1,0:T(8,128)(2,1)S(1)} %collective-permute-done.39.refs_1_, ...), custom_call_target="tpu_custom_call" | custom-call | flops 1024 | bytes 1024 | tf_op jit(solution)/shard_map/backward/pallas_call | solution.py:279
  (77 shorter events, 12.3 us)
Async XLA Ops:
  0.0 3.4 %copy-start.2 = (f32[2,128,8192]{2,1,0:T(8,128)S(1)}, f32[2,128,8192]{2,1,0:T(8,128)}, u32[]{:S(2)}) copy-start(f32[2,128,8192]{2,1,0:T(8,128)} %refs_0_.1) | copy-start | bytes 25165828
  5.3 3.4 %copy-start.10 = (s32[16]{0:T(128)S(1)}, s32[16]{0:T(128)}, u32[]{:S(2)}) copy-start(s32[16]{0:T(128)} %param.12) | copy-start | bytes 196
  5.3 3.4 %copy-start.11 = (s32[16]{0:T(128)S(1)}, s32[16]{0:T(128)}, u32[]{:S(2)}) copy-start(s32[16]{0:T(128)} %param.13) | copy-start | bytes 196
  5.3 3.6 %copy-start = (bf16[1024,1024]{1,0:T(8,128)(2,1)S(1)}, bf16[1024,1024]{1,0:T(8,128)(2,1)}, u32[]{:S(2)}) copy-start(bf16[1024,1024]{1,0:T(8,128)(2,1)} %pupil_ref.17) | copy-start | bytes 6291460
  5.3 3.6 %copy-start.1 = (bf16[1024,512]{1,0:T(8,128)(2,1)S(1)}, bf16[1024,512]{1,0:T(8,128)(2,1)}, u32[]{:S(2)}) copy-start(bf16[1024,512]{1,0:T(8,128)(2,1)} %constant.42.clone.band_ref) | copy-start | bytes 3145732
  5.3 7.0 %collective-permute-start.1 = (bf16[128,8192]{1,0:T(8,128)(2,1)}, bf16[128,8192]{1,0:T(8,128)(2,1)}, u32[]{:S(2)}, u32[]{:S(2)}) collective-permute-start(bf16[128,8192]{1,0:T(8,128)(2,1)} %low_part.3.refs_1_), channel_id=1, source_target_pairs={{0,1},{1,0},{2,3},{3,2},{4,5},{5,4},{6,7},{7,6},{8,9},{9,8},{10,11... | collective-permute-start | bytes 6291464 | tf_op jit(solution)/shard_map/ppermute | solution.py:427
  7.9 5.3 %collective-permute-start = (bf16[128,8192]{1,0:T(8,128)(2,1)}, bf16[128,8192]{1,0:T(8,128)(2,1)}, u32[]{:S(2)}, u32[]{:S(2)}) collective-permute-start(bf16[128,8192]{1,0:T(8,128)(2,1)} %low_part.2.refs_0_), channel_id=1, source_target_pairs={{0,1},{1,0},{2,3},{3,2},{4,5},{5,4},{6,7},{7,6},{8,9},{9,8},{10,11... | collective-permute-start | bytes 6291464 | tf_op jit(solution)/shard_map/ppermute | solution.py:427
  16.5 16.0 %collective-permute-start.2 = (bf16[2,128,1024]{2,1,0:T(8,128)(2,1)S(1)}, bf16[2,128,1024]{2,1,0:T(8,128)(2,1)S(1)}, u32[]{:S(2)}, u32[]{:S(2)}) collective-permute-start(bf16[2,128,1024]{2,1,0:T(8,128)(2,1)S(1)} %get-tuple-element.75), channel_id=1, source_target_pairs={{0,2},{1,3},{2,0},{3,1},{4,6},{5,7},{6,4},{7,5},{8,10},{9,11},{10,... | collective-permute-start | bytes 1572872 | tf_op jit(solution)/shard_map/ppermute | solution.py:430
  17.8 23.1 %collective-permute-start.11 = (bf16[2,128,1024]{2,1,0:T(8,128)(2,1)S(1)}, bf16[2,128,1024]{2,1,0:T(8,128)(2,1)S(1)}, u32[]{:S(2)}, u32[]{:S(2)}) collective-permute-start(bf16[2,128,1024]{2,1,0:T(8,128)(2,1)S(1)} %get-tuple-element.71), channel_id=1, source_target_pairs={{0,2},{1,3},{2,0},{3,1},{4,6},{5,7},{6,4},{7,5},{8,10},{9,11},{10,... | collective-permute-start | bytes 1572872 | tf_op jit(solution)/shard_map/ppermute | solution.py:430
  32.7 15.5 %collective-permute-start.3 = (bf16[2,128,1024]{2,1,0:T(8,128)(2,1)S(1)}, bf16[2,128,1024]{2,1,0:T(8,128)(2,1)S(1)}, u32[]{:S(2)}, u32[]{:S(2)}) collective-permute-start(bf16[2,128,1024]{2,1,0:T(8,128)(2,1)S(1)} %fusion), channel_id=1, source_target_pairs={{0,4},{1,5},{2,6},{3,7},{12,8},{13,9},{14,10},{15,11},{16,20},{17,... | collective-permute-start | bytes 1572872 | tf_op jit(solution)/shard_map/ppermute | solution.py:434
  34.0 18.2 %collective-permute-start.4 = (bf16[2,128,1024]{2,1,0:T(8,128)(2,1)S(1)}, bf16[2,128,1024]{2,1,0:T(8,128)(2,1)S(1)}, u32[]{:S(2)}, u32[]{:S(2)}) collective-permute-start(bf16[2,128,1024]{2,1,0:T(8,128)(2,1)S(1)} %get-tuple-element.80), channel_id=1, source_target_pairs={{0,2},{1,3},{2,0},{3,1},{4,6},{5,7},{6,4},{7,5},{8,10},{9,11},{10,... | collective-permute-start | bytes 1572872 | tf_op jit(solution)/shard_map/ppermute | solution.py:430
  41.2 18.2 %collective-permute-start.12 = (bf16[2,128,1024]{2,1,0:T(8,128)(2,1)S(1)}, bf16[2,128,1024]{2,1,0:T(8,128)(2,1)S(1)}, u32[]{:S(2)}, u32[]{:S(2)}) collective-permute-start(bf16[2,128,1024]{2,1,0:T(8,128)(2,1)S(1)} %fusion.2), channel_id=1, source_target_pairs={{0,4},{1,5},{2,6},{3,7},{12,8},{13,9},{14,10},{15,11},{16,20},{17,... | collective-permute-start | bytes 1572872 | tf_op jit(solution)/shard_map/ppermute | solution.py:434
  42.5 21.0 %collective-permute-start.13 = (bf16[2,128,1024]{2,1,0:T(8,128)(2,1)S(1)}, bf16[2,128,1024]{2,1,0:T(8,128)(2,1)S(1)}, u32[]{:S(2)}, u32[]{:S(2)}) collective-permute-start(bf16[2,128,1024]{2,1,0:T(8,128)(2,1)S(1)} %get-tuple-element.97), channel_id=1, source_target_pairs={{0,2},{1,3},{2,0},{3,1},{4,6},{5,7},{6,4},{7,5},{8,10},{9,11},{10,... | collective-permute-start | bytes 1572872 | tf_op jit(solution)/shard_map/ppermute | solution.py:430
  52.4 18.2 %collective-permute-start.6 = (bf16[2,128,1024]{2,1,0:T(8,128)(2,1)S(1)}, bf16[2,128,1024]{2,1,0:T(8,128)(2,1)S(1)}, u32[]{:S(2)}, u32[]{:S(2)}) collective-permute-start(bf16[2,128,1024]{2,1,0:T(8,128)(2,1)S(1)} %fusion.1), channel_id=1, source_target_pairs={{0,4},{1,5},{2,6},{3,7},{12,8},{13,9},{14,10},{15,11},{16,20},{17,... | collective-permute-start | bytes 1572872 | tf_op jit(solution)/shard_map/ppermute | solution.py:434
  54.0 16.8 %collective-permute-start.5 = (bf16[2,128,1024]{2,1,0:T(8,128)(2,1)S(1)}, bf16[2,128,1024]{2,1,0:T(8,128)(2,1)S(1)}, u32[]{:S(2)}, u32[]{:S(2)}) collective-permute-start(bf16[2,128,1024]{2,1,0:T(8,128)(2,1)S(1)} %add_convert_fusion.7), channel_id=1, source_target_pairs={{4,8},{5,9},{6,10},{7,11},{8,4},{9,5},{10,6},{11,7},{20,24},{21,25... | collective-permute-start | bytes 1572872 | tf_op jit(solution)/shard_map/ppermute | solution.py:434
  57.6 17.1 %collective-permute-start.7 = (bf16[2,128,1024]{2,1,0:T(8,128)(2,1)S(1)}, bf16[2,128,1024]{2,1,0:T(8,128)(2,1)S(1)}, u32[]{:S(2)}, u32[]{:S(2)}) collective-permute-start(bf16[2,128,1024]{2,1,0:T(8,128)(2,1)S(1)} %get-tuple-element.85), channel_id=1, source_target_pairs={{0,2},{1,3},{2,0},{3,1},{4,6},{5,7},{6,4},{7,5},{8,10},{9,11},{10,... | collective-permute-start | bytes 1572872 | tf_op jit(solution)/shard_map/ppermute | solution.py:430
  63.6 18.2 %collective-permute-start.15 = (bf16[2,128,1024]{2,1,0:T(8,128)(2,1)S(1)}, bf16[2,128,1024]{2,1,0:T(8,128)(2,1)S(1)}, u32[]{:S(2)}, u32[]{:S(2)}) collective-permute-start(bf16[2,128,1024]{2,1,0:T(8,128)(2,1)S(1)} %fusion.3), channel_id=1, source_target_pairs={{0,4},{1,5},{2,6},{3,7},{12,8},{13,9},{14,10},{15,11},{16,20},{17,... | collective-permute-start | bytes 1572872 | tf_op jit(solution)/shard_map/ppermute | solution.py:434
  65.2 16.7 %collective-permute-start.14 = (bf16[2,128,1024]{2,1,0:T(8,128)(2,1)S(1)}, bf16[2,128,1024]{2,1,0:T(8,128)(2,1)S(1)}, u32[]{:S(2)}, u32[]{:S(2)}) collective-permute-start(bf16[2,128,1024]{2,1,0:T(8,128)(2,1)S(1)} %add_convert_fusion.3), channel_id=1, source_target_pairs={{4,8},{5,9},{6,10},{7,11},{8,4},{9,5},{10,6},{11,7},{20,24},{21,25... | collective-permute-start | bytes 1572872 | tf_op jit(solution)/shard_map/ppermute | solution.py:434
  70.6 11.9 %collective-permute-start.16 = (bf16[2,128,1024]{2,1,0:T(8,128)(2,1)S(1)}, bf16[2,128,1024]{2,1,0:T(8,128)(2,1)S(1)}, u32[]{:S(2)}, u32[]{:S(2)}) collective-permute-start(bf16[2,128,1024]{2,1,0:T(8,128)(2,1)S(1)} %get-tuple-element.102), channel_id=1, source_target_pairs={{0,2},{1,3},{2,0},{3,1},{4,6},{5,7},{6,4},{7,5},{8,10},{9,11},{10,... | collective-permute-start | bytes 1572872 | tf_op jit(solution)/shard_map/ppermute | solution.py:430
  75.0 18.0 %collective-permute-start.9 = (bf16[2,128,1024]{2,1,0:T(8,128)(2,1)S(1)}, bf16[2,128,1024]{2,1,0:T(8,128)(2,1)S(1)}, u32[]{:S(2)}, u32[]{:S(2)}) collective-permute-start(bf16[2,128,1024]{2,1,0:T(8,128)(2,1)S(1)} %add_convert_fusion.6), channel_id=1, source_target_pairs={{4,8},{5,9},{6,10},{7,11},{8,4},{9,5},{10,6},{11,7},{20,24},{21,25... | collective-permute-start | bytes 1572872 | tf_op jit(solution)/shard_map/ppermute | solution.py:434
  78.5 15.3 %collective-permute-start.8 = (bf16[2,128,1024]{2,1,0:T(8,128)(2,1)S(1)}, bf16[2,128,1024]{2,1,0:T(8,128)(2,1)S(1)}, u32[]{:S(2)}, u32[]{:S(2)}) collective-permute-start(bf16[2,128,1024]{2,1,0:T(8,128)(2,1)S(1)} %get-tuple-element.87), channel_id=1, source_target_pairs={{0,2},{1,3},{2,0},{3,1},{4,6},{5,7},{6,4},{7,5},{8,10},{9,11},{10,... | collective-permute-start | bytes 1572872 | tf_op jit(solution)/shard_map/ppermute | solution.py:430
  81.9 13.0 %collective-permute-start.10 = (bf16[2,128,1024]{2,1,0:T(8,128)(2,1)S(1)}, bf16[2,128,1024]{2,1,0:T(8,128)(2,1)S(1)}, u32[]{:S(2)}, u32[]{:S(2)}) collective-permute-start(bf16[2,128,1024]{2,1,0:T(8,128)(2,1)S(1)} %add_convert_fusion.5), channel_id=1, source_target_pairs={{0,4},{1,5},{2,6},{3,7},{12,8},{13,9},{14,10},{15,11},{4,0},{5,1},... | collective-permute-start | bytes 1572872 | tf_op jit(solution)/shard_map/ppermute | solution.py:434
  82.9 20.0 %collective-permute-start.18 = (bf16[2,128,1024]{2,1,0:T(8,128)(2,1)S(1)}, bf16[2,128,1024]{2,1,0:T(8,128)(2,1)S(1)}, u32[]{:S(2)}, u32[]{:S(2)}) collective-permute-start(bf16[2,128,1024]{2,1,0:T(8,128)(2,1)S(1)} %add_convert_fusion.2), channel_id=1, source_target_pairs={{4,8},{5,9},{6,10},{7,11},{8,4},{9,5},{10,6},{11,7},{20,24},{21,25... | collective-permute-start | bytes 1572872 | tf_op jit(solution)/shard_map/ppermute | solution.py:434
  92.6 14.1 %collective-permute-start.17 = (bf16[2,128,1024]{2,1,0:T(8,128)(2,1)S(1)}, bf16[2,128,1024]{2,1,0:T(8,128)(2,1)S(1)}, u32[]{:S(2)}, u32[]{:S(2)}) collective-permute-start(bf16[2,128,1024]{2,1,0:T(8,128)(2,1)S(1)} %get-tuple-element.104), channel_id=1, source_target_pairs={{0,2},{1,3},{2,0},{3,1},{4,6},{5,7},{6,4},{7,5},{8,10},{9,11},{10,... | collective-permute-start | bytes 1572872 | tf_op jit(solution)/shard_map/ppermute | solution.py:430
  93.0 13.7 %collective-permute-start.19 = (bf16[2,128,1024]{2,1,0:T(8,128)(2,1)S(1)}, bf16[2,128,1024]{2,1,0:T(8,128)(2,1)S(1)}, u32[]{:S(2)}, u32[]{:S(2)}) collective-permute-start(bf16[2,128,1024]{2,1,0:T(8,128)(2,1)S(1)} %add_convert_fusion.1), channel_id=1, source_target_pairs={{0,4},{1,5},{2,6},{3,7},{12,8},{13,9},{14,10},{15,11},{4,0},{5,1},... | collective-permute-start | bytes 1572872 | tf_op jit(solution)/shard_map/ppermute | solution.py:434
  94.9 12.1 %copy-start.7 = (bf16[1024,1024]{1,0:T(8,128)(2,1)S(1)}, bf16[1024,1024]{1,0:T(8,128)(2,1)}, u32[]{:S(2)}) copy-start(bf16[1024,1024]{1,0:T(8,128)(2,1)} %constant.44.clone.refs_4_) | copy-start | bytes 6291460
  94.9 12.1 %copy-start.8 = (bf16[1024,1024]{1,0:T(8,128)(2,1)S(1)}, bf16[1024,1024]{1,0:T(8,128)(2,1)}, u32[]{:S(2)}) copy-start(bf16[1024,1024]{1,0:T(8,128)(2,1)} %constant.43.clone.refs_3_) | copy-start | bytes 6291460
  94.9 12.1 %copy-start.9 = (bf16[1,256,1024]{2,1,0:T(8,128)(2,1)S(1)}, bf16[1,256,1024]{2,1,0:T(8,128)(2,1)}, u32[]{:S(2)}) copy-start(bf16[1,256,1024]{2,1,0:T(8,128)(2,1)} %refs_2_.1) | copy-start | bytes 1572868
  112.6 11.1 %collective-permute-start.28 = (bf16[2,128,1024]{2,1,0:T(8,128)(2,1)S(1)}, bf16[2,128,1024]{2,1,0:T(8,128)(2,1)}, u32[]{:S(2)}, u32[]{:S(2)}) collective-permute-start(bf16[2,128,1024]{2,1,0:T(8,128)(2,1)S(1)} %get-tuple-element.112.refs_2_.refs_1_), channel_id=1, source_target_pairs={{0,4},{1,5},{2,6},{3,7},{12,8},{13,9},{14,10},{15,11},{4,0},{5,1},... | collective-permute-start | bytes 1572872 | tf_op jit(solution)/shard_map/ppermute | solution.py:434
  112.6 19.2 %collective-permute-start.27 = (bf16[2,128,1024]{2,1,0:T(8,128)(2,1)S(1)}, bf16[2,128,1024]{2,1,0:T(8,128)(2,1)}, u32[]{:S(2)}, u32[]{:S(2)}) collective-permute-start(bf16[2,128,1024]{2,1,0:T(8,128)(2,1)S(1)} %get-tuple-element.112.refs_2_.refs_1_), channel_id=1, source_target_pairs={{4,8},{5,9},{6,10},{7,11},{8,4},{9,5},{10,6},{11,7},{20,24},{21,25... | collective-permute-start | bytes 1572872 | tf_op jit(solution)/shard_map/ppermute | solution.py:434
  120.0 12.8 %collective-permute-start.26 = (bf16[2,128,1024]{2,1,0:T(8,128)(2,1)S(1)}, bf16[2,128,1024]{2,1,0:T(8,128)(2,1)S(1)}, u32[]{:S(2)}, u32[]{:S(2)}) collective-permute-start(bf16[2,128,1024]{2,1,0:T(8,128)(2,1)S(1)} %get-tuple-element.112.refs_2_.refs_1_), channel_id=1, source_target_pairs={{0,2},{1,3},{2,0},{3,1},{4,6},{5,7},{6,4},{7,5},{8,10},{9,11},{10,... | collective-permute-start | bytes 1572872 | tf_op jit(solution)/shard_map/ppermute | solution.py:430
  120.2 0.8 copy-start.3
  121.0 18.3 %collective-permute-start.22 = (bf16[2,128,1024]{2,1,0:T(8,128)(2,1)}, bf16[2,128,1024]{2,1,0:T(8,128)(2,1)}, u32[]{:S(2)}, u32[]{:S(2)}) collective-permute-start(bf16[2,128,1024]{2,1,0:T(8,128)(2,1)} %get-tuple-element.109.refs_1_.refs_0_), channel_id=1, source_target_pairs={{0,4},{1,5},{2,6},{3,7},{12,8},{13,9},{14,10},{15,11},{4,0},{5,1},... | collective-permute-start | bytes 1572872 | tf_op jit(solution)/shard_map/ppermute | solution.py:434
  121.0 22.1 %collective-permute-start.21 = (bf16[2,128,1024]{2,1,0:T(8,128)(2,1)}, bf16[2,128,1024]{2,1,0:T(8,128)(2,1)}, u32[]{:S(2)}, u32[]{:S(2)}) collective-permute-start(bf16[2,128,1024]{2,1,0:T(8,128)(2,1)} %get-tuple-element.109.refs_1_.refs_0_), channel_id=1, source_target_pairs={{4,8},{5,9},{6,10},{7,11},{8,4},{9,5},{10,6},{11,7},{20,24},{21,25... | collective-permute-start | bytes 1572872 | tf_op jit(solution)/shard_map/ppermute | solution.py:434
  123.7 20.3 %collective-permute-start.20 = (bf16[2,128,1024]{2,1,0:T(8,128)(2,1)}, bf16[2,128,1024]{2,1,0:T(8,128)(2,1)}, u32[]{:S(2)}, u32[]{:S(2)}) collective-permute-start(bf16[2,128,1024]{2,1,0:T(8,128)(2,1)} %get-tuple-element.109.refs_1_.refs_0_), channel_id=1, source_target_pairs={{0,2},{1,3},{2,0},{3,1},{4,6},{5,7},{6,4},{7,5},{8,10},{9,11},{10,... | collective-permute-start | bytes 1572872 | tf_op jit(solution)/shard_map/ppermute | solution.py:430
  132.8 0.8 copy-start.5
  133.6 14.8 %collective-permute-start.33 = (bf16[2,128,1024]{2,1,0:T(8,128)(2,1)}, bf16[2,128,1024]{2,1,0:T(8,128)(2,1)}, u32[]{:S(2)}, u32[]{:S(2)}) collective-permute-start(bf16[2,128,1024]{2,1,0:T(8,128)(2,1)} %collective-permute-done.27), channel_id=1, source_target_pairs={{4,0},{5,1},{6,2},{7,3},{8,12},{9,13},{10,14},{11,15},{20,16},{21,... | collective-permute-start | bytes 1572872 | tf_op jit(solution)/shard_map/ppermute | solution.py:434
  135.7 18.7 %collective-permute-start.32 = (bf16[2,128,1024]{2,1,0:T(8,128)(2,1)}, bf16[2,128,1024]{2,1,0:T(8,128)(2,1)}, u32[]{:S(2)}, u32[]{:S(2)}) collective-permute-start(bf16[2,128,1024]{2,1,0:T(8,128)(2,1)} %collective-permute-done.28.refs_4_.refs_3_), channel_id=1, source_target_pairs={{4,8},{5,9},{6,10},{7,11},{8,4},{9,5},{10,6},{11,7},{20,24},{21,25... | collective-permute-start | bytes 1572872 | tf_op jit(solution)/shard_map/ppermute | solution.py:434
  139.3 15.9 %collective-permute-start.31 = (bf16[2,128,1024]{2,1,0:T(8,128)(2,1)}, bf16[2,128,1024]{2,1,0:T(8,128)(2,1)}, u32[]{:S(2)}, u32[]{:S(2)}) collective-permute-start(bf16[2,128,1024]{2,1,0:T(8,128)(2,1)} %collective-permute-done.28.refs_4_.refs_3_), channel_id=1, source_target_pairs={{0,2},{1,3},{2,0},{3,1},{4,6},{5,7},{6,4},{7,5},{8,10},{9,11},{10,... | collective-permute-start | bytes 1572872 | tf_op jit(solution)/shard_map/ppermute | solution.py:430
  144.0 29.7 %collective-permute-start.25 = (bf16[2,128,1024]{2,1,0:T(8,128)(2,1)}, bf16[2,128,1024]{2,1,0:T(8,128)(2,1)S(1)}, u32[]{:S(2)}, u32[]{:S(2)}) collective-permute-start(bf16[2,128,1024]{2,1,0:T(8,128)(2,1)} %collective-permute-done.21), channel_id=1, source_target_pairs={{4,0},{5,1},{6,2},{7,3},{8,12},{9,13},{10,14},{11,15},{20,16},{21,... | collective-permute-start | bytes 1572872 | tf_op jit(solution)/shard_map/ppermute | solution.py:434
  145.3 28.4 %collective-permute-start.24 = (bf16[2,128,1024]{2,1,0:T(8,128)(2,1)}, bf16[2,128,1024]{2,1,0:T(8,128)(2,1)S(1)}, u32[]{:S(2)}, u32[]{:S(2)}) collective-permute-start(bf16[2,128,1024]{2,1,0:T(8,128)(2,1)} %collective-permute-done.22.refs_3_.refs_2_), channel_id=1, source_target_pairs={{4,8},{5,9},{6,10},{7,11},{8,4},{9,5},{10,6},{11,7},{20,24},{21,25... | collective-permute-start | bytes 1572872 | tf_op jit(solution)/shard_map/ppermute | solution.py:434
  148.4 25.3 %collective-permute-start.23 = (bf16[2,128,1024]{2,1,0:T(8,128)(2,1)}, bf16[2,128,1024]{2,1,0:T(8,128)(2,1)S(1)}, u32[]{:S(2)}, u32[]{:S(2)}) collective-permute-start(bf16[2,128,1024]{2,1,0:T(8,128)(2,1)} %collective-permute-done.22.refs_3_.refs_2_), channel_id=1, source_target_pairs={{0,2},{1,3},{2,0},{3,1},{4,6},{5,7},{6,4},{7,5},{8,10},{9,11},{10,... | collective-permute-start | bytes 1572872 | tf_op jit(solution)/shard_map/ppermute | solution.py:430
  156.3 22.9 %collective-permute-start.34 = (bf16[2,128,1024]{2,1,0:T(8,128)(2,1)S(1)}, bf16[2,128,1024]{2,1,0:T(8,128)(2,1)S(1)}, u32[]{:S(2)}, u32[]{:S(2)}) collective-permute-start(bf16[2,128,1024]{2,1,0:T(8,128)(2,1)S(1)} %broadcast_select_fusion.2.refs_2_), channel_id=1, source_target_pairs={{0,2},{1,3},{2,0},{3,1},{4,6},{5,7},{6,4},{7,5},{8,10},{9,11},{10,... | collective-permute-start | bytes 1572872 | tf_op jit(solution)/shard_map/ppermute | solution.py:430
  156.4 22.9 %collective-permute-start.35 = (bf16[2,128,1024]{2,1,0:T(8,128)(2,1)}, bf16[2,128,1024]{2,1,0:T(8,128)(2,1)S(1)}, u32[]{:S(2)}, u32[]{:S(2)}) collective-permute-start(bf16[2,128,1024]{2,1,0:T(8,128)(2,1)} %collective-permute-done.32), channel_id=1, source_target_pairs={{4,0},{5,1},{6,2},{7,3},{8,12},{9,13},{10,14},{11,15},{20,16},{21,... | collective-permute-start | bytes 1572872 | tf_op jit(solution)/shard_map/ppermute | solution.py:434
  157.8 1.0 copy-start.4
  158.8 1.0 copy-start.6
  174.9 11.9 %collective-permute-start.29 = (bf16[2,128,1024]{2,1,0:T(8,128)(2,1)S(1)}, bf16[2,128,1024]{2,1,0:T(8,128)(2,1)S(1)}, u32[]{:S(2)}, u32[]{:S(2)}) collective-permute-start(bf16[2,128,1024]{2,1,0:T(8,128)(2,1)S(1)} %broadcast_select_fusion.3.refs_1_), channel_id=1, source_target_pairs={{0,2},{1,3},{2,0},{3,1},{4,6},{5,7},{6,4},{7,5},{8,10},{9,11},{10,... | collective-permute-start | bytes 1572872 | tf_op jit(solution)/shard_map/ppermute | solution.py:430
  178.0 9.1 %collective-permute-start.30 = (bf16[2,128,1024]{2,1,0:T(8,128)(2,1)S(1)}, bf16[2,128,1024]{2,1,0:T(8,128)(2,1)S(1)}, u32[]{:S(2)}, u32[]{:S(2)}) collective-permute-start(bf16[2,128,1024]{2,1,0:T(8,128)(2,1)S(1)} %collective-permute-done.24), channel_id=1, source_target_pairs={{4,0},{5,1},{6,2},{7,3},{8,12},{9,13},{10,14},{11,15},{20,16},{21,... | collective-permute-start | bytes 1572872 | tf_op jit(solution)/shard_map/ppermute | solution.py:434
  180.4 17.6 %collective-permute-start.37 = (bf16[2,128,1024]{2,1,0:T(8,128)(2,1)S(1)}, bf16[2,128,1024]{2,1,0:T(8,128)(2,1)S(1)}, u32[]{:S(2)}, u32[]{:S(2)}) collective-permute-start(bf16[2,128,1024]{2,1,0:T(8,128)(2,1)S(1)} %broadcast_select_fusion.refs_6_.refs_2_), channel_id=1, source_target_pairs={{0,2},{1,3},{2,0},{3,1},{4,6},{5,7},{6,4},{7,5},{8,10},{9,11},{10,... | collective-permute-start | bytes 1572872 | tf_op jit(solution)/shard_map/ppermute | solution.py:430
  201.2 20.0 %collective-permute-start.39 = (bf16[2,128,4096]{2,1,0:T(8,128)(2,1)S(1)}, bf16[2,128,4096]{2,1,0:T(8,128)(2,1)S(1)}, u32[]{:S(2)}, u32[]{:S(2)}) collective-permute-start(bf16[2,128,4096]{2,1,0:T(8,128)(2,1)S(1)} %get-tuple-element.133), channel_id=1, source_target_pairs={{0,1},{1,0},{2,3},{3,2},{4,5},{5,4},{6,7},{7,6},{8,9},{9,8},{10,11... | collective-permute-start | bytes 6291464 | tf_op jit(solution)/shard_map/ppermute | solution.py:427
  203.7 17.6 %collective-permute-start.40 = (bf16[2,128,4096]{2,1,0:T(8,128)(2,1)S(1)}, bf16[2,128,4096]{2,1,0:T(8,128)(2,1)S(1)}, u32[]{:S(2)}, u32[]{:S(2)}) collective-permute-start(bf16[2,128,4096]{2,1,0:T(8,128)(2,1)S(1)} %get-tuple-element.134), channel_id=1, source_target_pairs={{0,1},{1,0},{2,3},{3,2},{4,5},{5,4},{6,7},{7,6},{8,9},{9,8},{10,11... | collective-permute-start | bytes 6291464 | tf_op jit(solution)/shard_map/ppermute | solution.py:427
  203.8 15.0 %collective-permute-start.36 = (bf16[2,128,1024]{2,1,0:T(8,128)(2,1)S(1)}, bf16[2,128,1024]{2,1,0:T(8,128)(2,1)S(1)}, u32[]{:S(2)}, u32[]{:S(2)}) collective-permute-start(bf16[2,128,1024]{2,1,0:T(8,128)(2,1)S(1)} %broadcast_select_fusion.1.refs_5_.refs_1_), channel_id=1, source_target_pairs={{0,2},{1,3},{2,0},{3,1},{4,6},{5,7},{6,4},{7,5},{8,10},{9,11},{10,... | collective-permute-start | bytes 1572872 | tf_op jit(solution)/shard_map/ppermute | solution.py:430
  206.9 11.9 %collective-permute-start.38 = (bf16[2,128,1024]{2,1,0:T(8,128)(2,1)S(1)}, bf16[2,128,1024]{2,1,0:T(8,128)(2,1)S(1)}, u32[]{:S(2)}, u32[]{:S(2)}) collective-permute-start(bf16[2,128,1024]{2,1,0:T(8,128)(2,1)S(1)} %collective-permute-done.37.refs_4_), channel_id=1, source_target_pairs={{0,1},{1,0},{2,3},{3,2},{4,5},{5,4},{6,7},{7,6},{8,9},{9,8},{10,11... | collective-permute-start | bytes 1572872 | tf_op jit(solution)/shard_map/ppermute | solution.py:427
  218.8 2.5 %collective-permute-start.41 = (bf16[2,128,1024]{2,1,0:T(8,128)(2,1)S(1)}, bf16[2,128,1024]{2,1,0:T(8,128)(2,1)S(1)}, u32[]{:S(2)}, u32[]{:S(2)}) collective-permute-start(bf16[2,128,1024]{2,1,0:T(8,128)(2,1)S(1)} %collective-permute-done.36.refs_3_), channel_id=1, source_target_pairs={{0,1},{1,0},{2,3},{3,2},{4,5},{5,4},{6,7},{7,6},{8,9},{9,8},{10,11... | collective-permute-start | bytes 1572872 | tf_op jit(solution)/shard_map/ppermute | solution.py:427

commit v5 on v4

--- a/solution.py
+++ b/solution.py
@@ -12,8 +12,8 @@
 step_size = 0.5
 lane = 128
 row_tile = 16
-vmem_bytes = 32 * 1024 * 1024
-backward_bytes = 40 * 1024 * 1024
+vmem_bytes = 20 * 1024 * 1024
+backward_bytes = 20 * 1024 * 1024
 
 
 def fourier_tables(crop_width):

time: 232 us -> 228 us (0.983)
  Pallas kernels: 69.6 us -> 50.3 us
  waiting for transfers between devices: 75.4 us -> 84.1 us
  local copies, waits for them, and re-layouts: 7.79 us -> 11.2 us
  starting transfers between devices: 70.9 us -> 73.8 us
    pallas_call x6, Pallas kernels: 39.2 us -> 22 us  [backward(): pl.pallas_call(functools.partial(kernel, slots=slots, held=held, parts=le...]
    ppermute x16, waiting for transfers between devices: 39.4 us -> 52.1 us  [across(): return lax.ppermute(value, 'ty', [(i, i ^ 2) for i in range(count)])]
    ppermute x20, waiting for transfers between devices: 33.5 us -> 28.5 us  [along(): return lax.ppermute(value, 'ty', pairs)]
    unnamed x24 -> x28, local copies, waits for them, and re-layouts: 7.09 us -> 10.5 us
  transfers between devices with their start and end apart: 42 -> 42, of which waited for: 25 -> 22; matrix products, arithmetic and copies ran while one was open for 3% -> 3% of each run, Pallas kernels for 20% -> 14%
where the time goes in v5:
time: 228 us; the launch traced here: 227 us
  waiting for transfers between devices  84.1 us (37%)
  starting transfers between devices  73.8 us (32%)
  Pallas kernels  50.3 us (22%)
  local copies, waits for them, and re-layouts  11.2 us (5%)
  other arithmetic  6.72 us (3%)
    ppermute x16, waiting for transfers between devices, across(): return lax.ppermute(value, 'ty', [(i, i ^ 2) for i in range(count)])  52.1 us
    ppermute x20, starting transfers between devices, along(): return lax.ppermute(value, 'ty', pairs)  50.8 us
    ppermute x20, waiting for transfers between devices, along(): return lax.ppermute(value, 'ty', pairs)  28.5 us
    pallas_call x6, Pallas kernels, backward(): pl.pallas_call(functools.partial(kernel, slots=slots, held=held, parts=le...  22 us
    pallas_call x3, Pallas kernels, forward(): pl.pallas_call(functools.partial(forward_kernel, base=base, images=images...  19 us
    ppermute x16, starting transfers between devices, across(): return lax.ppermute(value, 'ty', [(i, i ^ 2) for i in range(count)])  17.7 us
    unnamed x28, local copies, waits for them, and re-layouts  10.5 us
    pallas_call x1, Pallas kernels, middle(): pl.pallas_call(functools.partial(middle_kernel, terms=len(streams[0]), st...  5.59 us
  transfers between devices with their start and end apart: 42, of which 22 were waited for; matrix products, arithmetic and copies ran while one was open for 3% of the time, Pallas kernels for 14%

profile of v5, /device:TPU:11, one launch (start us, length us, event | category | flops | bytes accessed | tf_op | source)
XLA Modules:
  0.0 226.8 jit_solution(15680745407586651705)
XLA Ops:
  0.0 3.4 %copy-done.2 = f32[2,128,8192]{2,1,0:T(8,128)S(1)} copy-done((f32[2,128,8192]{2,1,0:T(8,128)S(1)}, f32[2,128,8192]{2,1,0:T(8,128)}, u32[]{:S(2)}) %copy-start.2) | copy-done | bytes 8388632
  3.4 1.9 low_part.3.refs_1_
  6.1 1.8 low_part.2.refs_0_
  8.9 2.3 %forward.3.refs_2_ = bf16[2,256,1024]{2,1,0:T(8,128)(2,1)S(1)} custom-call(s32[3,16]{1,0:T(4,128)S(1)} %pad_add_fusion.meta_ref, bf16[1024,1024]{1,0:T(8,128)(2,1)S(1)} %copy-done, bf16[1024,512]{1,0:T(8,128)(2,1)S(1)} %copy-done.1, bf16[128,8192]{1,0:T(8,128)(2,1)} %low_part.2.refs_0_, bf16[128,8192]{1,0:T(8,128)(2,1)} %low_part.3.refs_1_), custom_call_target="tpu_custom_call" | custom-call | flops 1024 | bytes 1024 | tf_op jit(solution)/shard_map/forward/pallas_call | solution.py:257
  11.3 1.9 collective-permute-done.refs_0_.refs_2_
  13.2 2.3 %forward.4 = (bf16[2,128,1024]{2,1,0:T(8,128)(2,1)S(1)}, bf16[2,128,1024]{2,1,0:T(8,128)(2,1)S(1)}) custom-call(s32[3,16]{1,0:T(4,128)S(1)} %pad_add_fusion.meta_ref, bf16[1024,1024]{1,0:T(8,128)(2,1)S(1)} %copy-done, bf16[1024,512]{1,0:T(8,128)(2,1)S(1)} %copy-done.1, bf16[128,8192]{1,0:T(8,128)(2,1)} %collective-permute-done.refs_0_.refs_2_, ...), custom_call_target="tpu_custom_call" | custom-call | flops 1024 | bytes 1024 | tf_op jit(solution)/shard_map/forward/pallas_call | solution.py:257
  15.5 2.3 %collective-permute-start.2 = (bf16[2,128,1024]{2,1,0:T(8,128)(2,1)S(1)}, bf16[2,128,1024]{2,1,0:T(8,128)(2,1)S(1)}, u32[]{:S(2)}, u32[]{:S(2)}) collective-permute-start(bf16[2,128,1024]{2,1,0:T(8,128)(2,1)S(1)} %get-tuple-element.75), channel_id=1, source_target_pairs={{0,2},{1,3},{2,0},{3,1},{4,6},{5,7},{6,4},{7,5},{8,10},{9,11},{10,... | collective-permute-start | bytes 1572872 | tf_op jit(solution)/shard_map/ppermute | solution.py:430
  17.9 14.4 %forward.5 = (bf16[2,128,1024]{2,1,0:T(8,128)(2,1)S(1)}, bf16[2,128,1024]{2,1,0:T(8,128)(2,1)S(1)}, bf16[2,128,1024]{2,1,0:T(8,128)(2,1)S(1)}, bf16[2,128,1024]{...) custom-call(s32[3,16]{1,0:T(4,128)S(1)} %pad_add_fusion.meta_ref, ...), custom_call_target="tpu_custom_call" | custom-call | flops 1024 | bytes 1024 | tf_op jit(solution)/shard_map/forward/pallas_call | solution.py:257
  32.5 1.3 collective-permute-start.3
  33.8 3.4 %collective-permute-start.4 = (bf16[2,128,1024]{2,1,0:T(8,128)(2,1)S(1)}, bf16[2,128,1024]{2,1,0:T(8,128)(2,1)S(1)}, u32[]{:S(2)}, u32[]{:S(2)}) collective-permute-start(bf16[2,128,1024]{2,1,0:T(8,128)(2,1)S(1)} %get-tuple-element.80), channel_id=1, source_target_pairs={{0,2},{1,3},{2,0},{3,1},{4,6},{5,7},{6,4},{7,5},{8,10},{9,11},{10,... | collective-permute-start | bytes 1572872 | tf_op jit(solution)/shard_map/ppermute | solution.py:430
  37.3 3.2 %collective-permute-done.11 = bf16[2,128,1024]{2,1,0:T(8,128)(2,1)S(1)} collective-permute-done((bf16[2,128,1024]{2,1,0:T(8,128)(2,1)S(1)}, bf16[2,128,1024]{2,1,0:T(8,128)(2,1)S(1)}, u32[]{:S(2)}, u32[]{:S(2)}) %collective-permute-start.11) | collective-permute-done | bytes 524320 | tf_op jit(solution)/shard_map/ppermute | solution.py:430
  40.7 1.3 collective-permute-start.12
  42.0 1.8 collective-permute-start.13
  43.8 3.0 %collective-permute-done.3 = bf16[2,128,1024]{2,1,0:T(8,128)(2,1)S(1)} collective-permute-done((bf16[2,128,1024]{2,1,0:T(8,128)(2,1)S(1)}, bf16[2,128,1024]{2,1,0:T(8,128)(2,1)S(1)}, u32[]{:S(2)}, u32[]{:S(2)}) %collective-permute-start.3) | collective-permute-done | bytes 524320 | tf_op jit(solution)/shard_map/ppermute | solution.py:434
  46.7 5.0 %collective-permute-done.4 = bf16[2,128,1024]{2,1,0:T(8,128)(2,1)S(1)} collective-permute-done((bf16[2,128,1024]{2,1,0:T(8,128)(2,1)S(1)}, bf16[2,128,1024]{2,1,0:T(8,128)(2,1)S(1)}, u32[]{:S(2)}, u32[]{:S(2)}) %collective-permute-start.4) | collective-permute-done | bytes 524320 | tf_op jit(solution)/shard_map/ppermute | solution.py:430
  51.9 1.3 collective-permute-start.6
  53.5 4.0 %collective-permute-start.5 = (bf16[2,128,1024]{2,1,0:T(8,128)(2,1)S(1)}, bf16[2,128,1024]{2,1,0:T(8,128)(2,1)S(1)}, u32[]{:S(2)}, u32[]{:S(2)}) collective-permute-start(bf16[2,128,1024]{2,1,0:T(8,128)(2,1)S(1)} %add_convert_fusion.7), channel_id=1, source_target_pairs={{4,8},{5,9},{6,10},{7,11},{8,4},{9,5},{10,6},{11,7},{20,24},{21,25... | collective-permute-start | bytes 1572872 | tf_op jit(solution)/shard_map/ppermute | solution.py:434
  57.5 1.0 collective-permute-start.7
  58.5 4.5 %collective-permute-done.13 = bf16[2,128,1024]{2,1,0:T(8,128)(2,1)S(1)} collective-permute-done((bf16[2,128,1024]{2,1,0:T(8,128)(2,1)S(1)}, bf16[2,128,1024]{2,1,0:T(8,128)(2,1)S(1)}, u32[]{:S(2)}, u32[]{:S(2)}) %collective-permute-start.13) | collective-permute-done | bytes 524320 | tf_op jit(solution)/shard_map/ppermute | solution.py:430
  63.2 1.3 collective-permute-start.15
  64.7 4.0 %collective-permute-start.14 = (bf16[2,128,1024]{2,1,0:T(8,128)(2,1)S(1)}, bf16[2,128,1024]{2,1,0:T(8,128)(2,1)S(1)}, u32[]{:S(2)}, u32[]{:S(2)}) collective-permute-start(bf16[2,128,1024]{2,1,0:T(8,128)(2,1)S(1)} %add_convert_fusion.3), channel_id=1, source_target_pairs={{4,8},{5,9},{6,10},{7,11},{8,4},{9,5},{10,6},{11,7},{20,24},{21,25... | collective-permute-start | bytes 1572872 | tf_op jit(solution)/shard_map/ppermute | solution.py:434
  69.2 1.5 collective-permute-start.16
  70.7 3.5 %collective-permute-done.7 = bf16[2,128,1024]{2,1,0:T(8,128)(2,1)S(1)} collective-permute-done((bf16[2,128,1024]{2,1,0:T(8,128)(2,1)S(1)}, bf16[2,128,1024]{2,1,0:T(8,128)(2,1)S(1)}, u32[]{:S(2)}, u32[]{:S(2)}) %collective-permute-start.7) | collective-permute-done | bytes 524320 | tf_op jit(solution)/shard_map/ppermute | solution.py:430
  74.5 4.3 %collective-permute-start.9 = (bf16[2,128,1024]{2,1,0:T(8,128)(2,1)S(1)}, bf16[2,128,1024]{2,1,0:T(8,128)(2,1)S(1)}, u32[]{:S(2)}, u32[]{:S(2)}) collective-permute-start(bf16[2,128,1024]{2,1,0:T(8,128)(2,1)S(1)} %add_convert_fusion.6), channel_id=1, source_target_pairs={{4,8},{5,9},{6,10},{7,11},{8,4},{9,5},{10,6},{11,7},{20,24},{21,25... | collective-permute-start | bytes 1572872 | tf_op jit(solution)/shard_map/ppermute | solution.py:434
  78.8 1.2 collective-permute-start.8
  80.5 1.6 collective-permute-done.16
  82.4 10.2 %collective-permute-start.18 = (bf16[2,128,1024]{2,1,0:T(8,128)(2,1)S(1)}, bf16[2,128,1024]{2,1,0:T(8,128)(2,1)S(1)}, u32[]{:S(2)}, u32[]{:S(2)}) collective-permute-start(bf16[2,128,1024]{2,1,0:T(8,128)(2,1)S(1)} %add_convert_fusion.2), channel_id=1, source_target_pairs={{4,8},{5,9},{6,10},{7,11},{8,4},{9,5},{10,6},{11,7},{20,24},{21,25... | collective-permute-start | bytes 1572872 | tf_op jit(solution)/shard_map/ppermute | solution.py:434
  93.7 9.0 %collective-permute-done.18 = bf16[2,128,1024]{2,1,0:T(8,128)(2,1)S(1)} collective-permute-done((bf16[2,128,1024]{2,1,0:T(8,128)(2,1)S(1)}, bf16[2,128,1024]{2,1,0:T(8,128)(2,1)S(1)}, u32[]{:S(2)}, u32[]{:S(2)}) %collective-permute-start.18) | collective-permute-done | bytes 524320 | tf_op jit(solution)/shard_map/ppermute | solution.py:434
  102.8 3.9 %collective-permute-done.17 = bf16[2,128,1024]{2,1,0:T(8,128)(2,1)S(1)} collective-permute-done((bf16[2,128,1024]{2,1,0:T(8,128)(2,1)S(1)}, bf16[2,128,1024]{2,1,0:T(8,128)(2,1)S(1)}, u32[]{:S(2)}, u32[]{:S(2)}) %collective-permute-start.17) | collective-permute-done | bytes 524320 | tf_op jit(solution)/shard_map/ppermute | solution.py:430
  107.0 5.6 %middle.1 = (bf16[2,128,1024]{2,1,0:T(8,128)(2,1)}, bf16[2,128,1024]{2,1,0:T(8,128)(2,1)S(1)}) custom-call(bf16[2,128,1024]{2,1,0:T(8,128)(2,1)S(1)} %add_convert_fusion.refs_0_, bf16[2,128,1024]{2,1,0:T(8,128)(2,1)S(1)} %add_convert_fusion.4.refs_1_, bf16[1,256,1024]{2,1,0:T(8,128)(2,1)S(1)} %copy-done.11, bf16[1024,1024]{1,0:T(8,128)(2,1)S(1)} %copy-done.10, ...), custom_call_target="tpu_custom_call" | custom-call | flops 1024 | bytes 1024 | tf_op jit(solution)/shard_map/middle/pallas_call | solution.py:295
  112.6 7.7 %collective-permute-start.27 = (bf16[2,128,1024]{2,1,0:T(8,128)(2,1)S(1)}, bf16[2,128,1024]{2,1,0:T(8,128)(2,1)}, u32[]{:S(2)}, u32[]{:S(2)}) collective-permute-start(bf16[2,128,1024]{2,1,0:T(8,128)(2,1)S(1)} %get-tuple-element.112.refs_2_.refs_1_), channel_id=1, source_target_pairs={{4,8},{5,9},{6,10},{7,11},{8,4},{9,5},{10,6},{11,7},{20,24},{21,25... | collective-permute-start | bytes 1572872 | tf_op jit(solution)/shard_map/ppermute | solution.py:434
  121.2 2.8 %collective-permute-start.21 = (bf16[2,128,1024]{2,1,0:T(8,128)(2,1)}, bf16[2,128,1024]{2,1,0:T(8,128)(2,1)}, u32[]{:S(2)}, u32[]{:S(2)}) collective-permute-start(bf16[2,128,1024]{2,1,0:T(8,128)(2,1)} %get-tuple-element.109.refs_1_.refs_0_), channel_id=1, source_target_pairs={{4,8},{5,9},{6,10},{7,11},{8,4},{9,5},{10,6},{11,7},{20,24},{21,25... | collective-permute-start | bytes 1572872 | tf_op jit(solution)/shard_map/ppermute | solution.py:434
  124.0 1.5 collective-permute-start.20
  125.5 6.7 %collective-permute-done.27 = bf16[2,128,1024]{2,1,0:T(8,128)(2,1)} collective-permute-done((bf16[2,128,1024]{2,1,0:T(8,128)(2,1)S(1)}, bf16[2,128,1024]{2,1,0:T(8,128)(2,1)}, u32[]{:S(2)}, u32[]{:S(2)}) %collective-permute-start.27) | collective-permute-done | bytes 524320 | tf_op jit(solution)/shard_map/ppermute | solution.py:434
  134.0 2.1 collective-permute-start.33
  136.1 3.5 %collective-permute-start.32 = (bf16[2,128,1024]{2,1,0:T(8,128)(2,1)}, bf16[2,128,1024]{2,1,0:T(8,128)(2,1)}, u32[]{:S(2)}, u32[]{:S(2)}) collective-permute-start(bf16[2,128,1024]{2,1,0:T(8,128)(2,1)} %collective-permute-done.28.refs_4_.refs_3_), channel_id=1, source_target_pairs={{4,8},{5,9},{6,10},{7,11},{8,4},{9,5},{10,6},{11,7},{20,24},{21,25... | collective-permute-start | bytes 1572872 | tf_op jit(solution)/shard_map/ppermute | solution.py:434
  140.0 3.5 %collective-permute-done.21 = bf16[2,128,1024]{2,1,0:T(8,128)(2,1)} collective-permute-done((bf16[2,128,1024]{2,1,0:T(8,128)(2,1)}, bf16[2,128,1024]{2,1,0:T(8,128)(2,1)}, u32[]{:S(2)}, u32[]{:S(2)}) %collective-permute-start.21) | collective-permute-done | bytes 524320 | tf_op jit(solution)/shard_map/ppermute | solution.py:434
  143.5 0.9 collective-permute-done.20.refs_5_.refs_4_
  144.4 1.3 collective-permute-start.25
  145.7 3.1 %collective-permute-start.24 = (bf16[2,128,1024]{2,1,0:T(8,128)(2,1)}, bf16[2,128,1024]{2,1,0:T(8,128)(2,1)S(1)}, u32[]{:S(2)}, u32[]{:S(2)}) collective-permute-start(bf16[2,128,1024]{2,1,0:T(8,128)(2,1)} %collective-permute-done.22.refs_3_.refs_2_), channel_id=1, source_target_pairs={{4,8},{5,9},{6,10},{7,11},{8,4},{9,5},{10,6},{11,7},{20,24},{21,25... | collective-permute-start | bytes 1572872 | tf_op jit(solution)/shard_map/ppermute | solution.py:434
  149.2 5.6 %collective-permute-done.32 = bf16[2,128,1024]{2,1,0:T(8,128)(2,1)} collective-permute-done((bf16[2,128,1024]{2,1,0:T(8,128)(2,1)}, bf16[2,128,1024]{2,1,0:T(8,128)(2,1)}, u32[]{:S(2)}, u32[]{:S(2)}) %collective-permute-start.32) | collective-permute-done | bytes 524320 | tf_op jit(solution)/shard_map/ppermute | solution.py:434
  154.7 0.9 collective-permute-done.31.refs_4_
  155.6 1.2 broadcast_select_fusion.2.refs_2_
  157.2 1.3 collective-permute-start.35
  158.5 1.0 copy-done.5
  159.6 1.0 copy-done.8
  160.6 3.3 %backward.7.refs_0_ = bf16[2,128,8192]{2,1,0:T(8,128)(2,1)S(1)} custom-call(s32[3,16]{1,0:T(4,128)S(1)} %pad_add_fusion.meta_ref, bf16[1024,1024]{1,0:T(8,128)(2,1)S(1)} %copy-done, bf16[1024,512]{1,0:T(8,128)(2,1)S(1)} %copy-done.1, bf16[2,128,1024]{2,1,0:T(8,128)(2,1)} %get-tuple-element.109.refs_1_.refs_0_, bf16[2,128,1024]{2,1,0:T(8,128)(2,1)S(1)} %copy-done.5, ...), custom_call_target="tpu_custom_call" | custom-call | flops 1024 | bytes 1024 | tf_op jit(solution)/shard_map/backward/pallas_call | solution.py:279
  163.9 3.4 %copy-done.3 = f32[2,128,8192]{2,1,0:T(8,128)S(1)} copy-done((f32[2,128,8192]{2,1,0:T(8,128)S(1)}, f32[2,128,8192]{2,1,0:T(8,128)}, u32[]{:S(2)}) %copy-start.3) | copy-done | bytes 8388632
  167.3 3.9 %backward.6.refs_0_ = f32[2,128,8192]{2,1,0:T(8,128)S(1)} custom-call(s32[3,16]{1,0:T(4,128)S(1)} %pad_add_fusion.meta_ref, bf16[1024,1024]{1,0:T(8,128)(2,1)S(1)} %copy-done, bf16[1024,512]{1,0:T(8,128)(2,1)S(1)} %copy-done.1, f32[2,128,8192]{2,1,0:T(8,128)S(1)} %copy-done.3, bf16[2,128,1024]{2,1,0:T(8,128)(2,1)} %get-tuple-element.109.refs_1_.refs_0_, ...), custom_call_target="tpu_custom_call" | custom-call | flops 1024 | bytes 1024 | tf_op jit(solution)/shard_map/backward/pallas_call | solution.py:279
  171.3 1.1 broadcast_select_fusion.3.refs_1_
  172.4 2.9 %collective-permute-start.29 = (bf16[2,128,1024]{2,1,0:T(8,128)(2,1)S(1)}, bf16[2,128,1024]{2,1,0:T(8,128)(2,1)S(1)}, u32[]{:S(2)}, u32[]{:S(2)}) collective-permute-start(bf16[2,128,1024]{2,1,0:T(8,128)(2,1)S(1)} %broadcast_select_fusion.3.refs_1_), channel_id=1, source_target_pairs={{0,2},{1,3},{2,0},{3,1},{4,6},{5,7},{6,4},{7,5},{8,10},{9,11},{10,... | collective-permute-start | bytes 1572872 | tf_op jit(solution)/shard_map/ppermute | solution.py:430
  175.3 1.3 collective-permute-start.30
  176.6 1.4 collective-permute-done.34.refs_8_.refs_4_
  178.0 1.1 broadcast_select_fusion.refs_6_.refs_2_
  179.5 2.8 %backward.8.refs_0_ = bf16[2,128,8192]{2,1,0:T(8,128)(2,1)S(1)} custom-call(s32[3,16]{1,0:T(4,128)S(1)} %pad_add_fusion.meta_ref, bf16[1024,1024]{1,0:T(8,128)(2,1)S(1)} %copy-done, bf16[1024,512]{1,0:T(8,128)(2,1)S(1)} %copy-done.1, bf16[2,128,8192]{2,1,0:T(8,128)(2,1)S(1)} %backward.7.refs_0_, bf16[2,128,1024]{2,1,0:T(8,128)(2,1)S(1)} %broadcast_select_fusion.3.refs_1_, ...), custom_call_target="tpu_custom_call" | custom-call | flops 1024 | bytes 1024 | tf_op jit(solution)/shard_map/backward/pallas_call | solution.py:279
  182.3 6.9 %collective-permute-done.29.refs_7_.refs_3_ = bf16[2,128,1024]{2,1,0:T(8,128)(2,1)S(1)} collective-permute-done((bf16[2,128,1024]{2,1,0:T(8,128)(2,1)S(1)}, bf16[2,128,1024]{2,1,0:T(8,128)(2,1)S(1)}, u32[]{:S(2)}, u32[]{:S(2)}) %collective-permute-start.29) | collective-permute-done | bytes 524320 | tf_op jit(solution)/shard_map/ppermute | solution.py:430
  189.3 11.2 %collective-permute-done.37.refs_4_ = bf16[2,128,1024]{2,1,0:T(8,128)(2,1)S(1)} collective-permute-done((bf16[2,128,1024]{2,1,0:T(8,128)(2,1)S(1)}, bf16[2,128,1024]{2,1,0:T(8,128)(2,1)S(1)}, u32[]{:S(2)}, u32[]{:S(2)}) %collective-permute-start.37) | collective-permute-done | bytes 524320 | tf_op jit(solution)/shard_map/ppermute | solution.py:430
  200.5 2.4 %backward.10 = (bf16[2,128,4096]{2,1,0:T(8,128)(2,1)S(1)}, bf16[2,128,4096]{2,1,0:T(8,128)(2,1)S(1)}) custom-call(s32[3,16]{1,0:T(4,128)S(1)} %pad_add_fusion.meta_ref, bf16[1024,1024]{1,0:T(8,128)(2,1)S(1)} %copy-done, bf16[1024,512]{1,0:T(8,128)(2,1)S(1)} %copy-done.1, bf16[2,128,8192]{2,1,0:T(8,128)(2,1)S(1)} %backward.8.refs_0_, ...), custom_call_target="tpu_custom_call" | custom-call | flops 1024 | bytes 1024 | tf_op jit(solution)/shard_map/backward/pallas_call | solution.py:279
  202.8 2.5 %collective-permute-start.39 = (bf16[2,128,4096]{2,1,0:T(8,128)(2,1)S(1)}, bf16[2,128,4096]{2,1,0:T(8,128)(2,1)S(1)}, u32[]{:S(2)}, u32[]{:S(2)}) collective-permute-start(bf16[2,128,4096]{2,1,0:T(8,128)(2,1)S(1)} %get-tuple-element.133), channel_id=1, source_target_pairs={{0,1},{1,0},{2,3},{3,2},{4,5},{5,4},{6,7},{7,6},{8,9},{9,8},{10,11... | collective-permute-start | bytes 6291464 | tf_op jit(solution)/shard_map/ppermute | solution.py:427
  206.1 4.1 %backward.9.refs_0_ = f32[2,128,8192]{2,1,0:T(8,128)S(1)} custom-call(s32[3,16]{1,0:T(4,128)S(1)} %pad_add_fusion.meta_ref, bf16[1024,1024]{1,0:T(8,128)(2,1)S(1)} %copy-done, bf16[1024,512]{1,0:T(8,128)(2,1)S(1)} %copy-done.1, f32[2,128,8192]{2,1,0:T(8,128)S(1)} %backward.6.refs_0_, bf16[2,128,1024]{2,1,0:T(8,128)(2,1)S(1)} %broadcast_select_fusion.3.refs_1_, ...), custom_call_target="tpu_custom_call" | custom-call | flops 1024 | bytes 1024 | tf_op jit(solution)/shard_map/backward/pallas_call | solution.py:279
  210.2 8.3 %collective-permute-done.36.refs_3_ = bf16[2,128,1024]{2,1,0:T(8,128)(2,1)S(1)} collective-permute-done((bf16[2,128,1024]{2,1,0:T(8,128)(2,1)S(1)}, bf16[2,128,1024]{2,1,0:T(8,128)(2,1)S(1)}, u32[]{:S(2)}, u32[]{:S(2)}) %collective-permute-start.36) | collective-permute-done | bytes 524320 | tf_op jit(solution)/shard_map/ppermute | solution.py:430
  218.5 1.3 collective-permute-start.41
  219.8 1.5 collective-permute-done.41.refs_5_
  221.3 5.5 %backward.11 = f32[2,128,8192]{2,1,0:T(8,128)} custom-call(s32[3,16]{1,0:T(4,128)S(1)} %pad_add_fusion.meta_ref, bf16[1024,1024]{1,0:T(8,128)(2,1)S(1)} %copy-done, bf16[1024,512]{1,0:T(8,128)(2,1)S(1)} %copy-done.1, f32[2,128,8192]{2,1,0:T(8,128)S(1)} %backward.9.refs_0_, bf16[2,128,4096]{2,1,0:T(8,128)(2,1)S(1)} %collective-permute-done.39.refs_1_, ...), custom_call_target="tpu_custom_call" | custom-call | flops 1024 | bytes 1024 | tf_op jit(solution)/shard_map/backward/pallas_call | solution.py:279
  (81 shorter events, 11.2 us)
Async XLA Ops:
  0.0 3.4 %copy-start.2 = (f32[2,128,8192]{2,1,0:T(8,128)S(1)}, f32[2,128,8192]{2,1,0:T(8,128)}, u32[]{:S(2)}) copy-start(f32[2,128,8192]{2,1,0:T(8,128)} %refs_0_.1) | copy-start | bytes 25165828
  5.3 3.4 %copy-start.12 = (s32[16]{0:T(128)S(1)}, s32[16]{0:T(128)}, u32[]{:S(2)}) copy-start(s32[16]{0:T(128)} %param.12) | copy-start | bytes 196
  5.3 3.4 %copy-start.13 = (s32[16]{0:T(128)S(1)}, s32[16]{0:T(128)}, u32[]{:S(2)}) copy-start(s32[16]{0:T(128)} %param.13) | copy-start | bytes 196
  5.3 3.6 %copy-start = (bf16[1024,1024]{1,0:T(8,128)(2,1)S(1)}, bf16[1024,1024]{1,0:T(8,128)(2,1)}, u32[]{:S(2)}) copy-start(bf16[1024,1024]{1,0:T(8,128)(2,1)} %pupil_ref.17) | copy-start | bytes 6291460
  5.3 3.6 %copy-start.1 = (bf16[1024,512]{1,0:T(8,128)(2,1)S(1)}, bf16[1024,512]{1,0:T(8,128)(2,1)}, u32[]{:S(2)}) copy-start(bf16[1024,512]{1,0:T(8,128)(2,1)} %constant.42.clone.band_ref) | copy-start | bytes 3145732
  5.3 5.9 %collective-permute-start.1 = (bf16[128,8192]{1,0:T(8,128)(2,1)}, bf16[128,8192]{1,0:T(8,128)(2,1)}, u32[]{:S(2)}, u32[]{:S(2)}) collective-permute-start(bf16[128,8192]{1,0:T(8,128)(2,1)} %low_part.3.refs_1_), channel_id=1, source_target_pairs={{0,1},{1,0},{2,3},{3,2},{4,5},{5,4},{6,7},{7,6},{8,9},{9,8},{10,11... | collective-permute-start | bytes 6291464 | tf_op jit(solution)/shard_map/ppermute | solution.py:427
  7.9 5.3 %collective-permute-start = (bf16[128,8192]{1,0:T(8,128)(2,1)}, bf16[128,8192]{1,0:T(8,128)(2,1)}, u32[]{:S(2)}, u32[]{:S(2)}) collective-permute-start(bf16[128,8192]{1,0:T(8,128)(2,1)} %low_part.2.refs_0_), channel_id=1, source_target_pairs={{0,1},{1,0},{2,3},{3,2},{4,5},{5,4},{6,7},{7,6},{8,9},{9,8},{10,11... | collective-permute-start | bytes 6291464 | tf_op jit(solution)/shard_map/ppermute | solution.py:427
  15.5 16.8 %collective-permute-start.2 = (bf16[2,128,1024]{2,1,0:T(8,128)(2,1)S(1)}, bf16[2,128,1024]{2,1,0:T(8,128)(2,1)S(1)}, u32[]{:S(2)}, u32[]{:S(2)}) collective-permute-start(bf16[2,128,1024]{2,1,0:T(8,128)(2,1)S(1)} %get-tuple-element.75), channel_id=1, source_target_pairs={{0,2},{1,3},{2,0},{3,1},{4,6},{5,7},{6,4},{7,5},{8,10},{9,11},{10,... | collective-permute-start | bytes 1572872 | tf_op jit(solution)/shard_map/ppermute | solution.py:430
  17.8 22.7 %collective-permute-start.11 = (bf16[2,128,1024]{2,1,0:T(8,128)(2,1)S(1)}, bf16[2,128,1024]{2,1,0:T(8,128)(2,1)S(1)}, u32[]{:S(2)}, u32[]{:S(2)}) collective-permute-start(bf16[2,128,1024]{2,1,0:T(8,128)(2,1)S(1)} %get-tuple-element.71), channel_id=1, source_target_pairs={{0,2},{1,3},{2,0},{3,1},{4,6},{5,7},{6,4},{7,5},{8,10},{9,11},{10,... | collective-permute-start | bytes 1572872 | tf_op jit(solution)/shard_map/ppermute | solution.py:430
  32.5 14.2 %collective-permute-start.3 = (bf16[2,128,1024]{2,1,0:T(8,128)(2,1)S(1)}, bf16[2,128,1024]{2,1,0:T(8,128)(2,1)S(1)}, u32[]{:S(2)}, u32[]{:S(2)}) collective-permute-start(bf16[2,128,1024]{2,1,0:T(8,128)(2,1)S(1)} %fusion), channel_id=1, source_target_pairs={{0,4},{1,5},{2,6},{3,7},{12,8},{13,9},{14,10},{15,11},{16,20},{17,... | collective-permute-start | bytes 1572872 | tf_op jit(solution)/shard_map/ppermute | solution.py:434
  33.8 17.9 %collective-permute-start.4 = (bf16[2,128,1024]{2,1,0:T(8,128)(2,1)S(1)}, bf16[2,128,1024]{2,1,0:T(8,128)(2,1)S(1)}, u32[]{:S(2)}, u32[]{:S(2)}) collective-permute-start(bf16[2,128,1024]{2,1,0:T(8,128)(2,1)S(1)} %get-tuple-element.80), channel_id=1, source_target_pairs={{0,2},{1,3},{2,0},{3,1},{4,6},{5,7},{6,4},{7,5},{8,10},{9,11},{10,... | collective-permute-start | bytes 1572872 | tf_op jit(solution)/shard_map/ppermute | solution.py:430
  40.7 17.8 %collective-permute-start.12 = (bf16[2,128,1024]{2,1,0:T(8,128)(2,1)S(1)}, bf16[2,128,1024]{2,1,0:T(8,128)(2,1)S(1)}, u32[]{:S(2)}, u32[]{:S(2)}) collective-permute-start(bf16[2,128,1024]{2,1,0:T(8,128)(2,1)S(1)} %fusion.2), channel_id=1, source_target_pairs={{0,4},{1,5},{2,6},{3,7},{12,8},{13,9},{14,10},{15,11},{16,20},{17,... | collective-permute-start | bytes 1572872 | tf_op jit(solution)/shard_map/ppermute | solution.py:434
  42.0 21.0 %collective-permute-start.13 = (bf16[2,128,1024]{2,1,0:T(8,128)(2,1)S(1)}, bf16[2,128,1024]{2,1,0:T(8,128)(2,1)S(1)}, u32[]{:S(2)}, u32[]{:S(2)}) collective-permute-start(bf16[2,128,1024]{2,1,0:T(8,128)(2,1)S(1)} %get-tuple-element.97), channel_id=1, source_target_pairs={{0,2},{1,3},{2,0},{3,1},{4,6},{5,7},{6,4},{7,5},{8,10},{9,11},{10,... | collective-permute-start | bytes 1572872 | tf_op jit(solution)/shard_map/ppermute | solution.py:430
  51.9 17.3 %collective-permute-start.6 = (bf16[2,128,1024]{2,1,0:T(8,128)(2,1)S(1)}, bf16[2,128,1024]{2,1,0:T(8,128)(2,1)S(1)}, u32[]{:S(2)}, u32[]{:S(2)}) collective-permute-start(bf16[2,128,1024]{2,1,0:T(8,128)(2,1)S(1)} %fusion.1), channel_id=1, source_target_pairs={{0,4},{1,5},{2,6},{3,7},{12,8},{13,9},{14,10},{15,11},{16,20},{17,... | collective-permute-start | bytes 1572872 | tf_op jit(solution)/shard_map/ppermute | solution.py:434
  53.5 17.2 %collective-permute-start.5 = (bf16[2,128,1024]{2,1,0:T(8,128)(2,1)S(1)}, bf16[2,128,1024]{2,1,0:T(8,128)(2,1)S(1)}, u32[]{:S(2)}, u32[]{:S(2)}) collective-permute-start(bf16[2,128,1024]{2,1,0:T(8,128)(2,1)S(1)} %add_convert_fusion.7), channel_id=1, source_target_pairs={{4,8},{5,9},{6,10},{7,11},{8,4},{9,5},{10,6},{11,7},{20,24},{21,25... | collective-permute-start | bytes 1572872 | tf_op jit(solution)/shard_map/ppermute | solution.py:434
  57.5 16.7 %collective-permute-start.7 = (bf16[2,128,1024]{2,1,0:T(8,128)(2,1)S(1)}, bf16[2,128,1024]{2,1,0:T(8,128)(2,1)S(1)}, u32[]{:S(2)}, u32[]{:S(2)}) collective-permute-start(bf16[2,128,1024]{2,1,0:T(8,128)(2,1)S(1)} %get-tuple-element.85), channel_id=1, source_target_pairs={{0,2},{1,3},{2,0},{3,1},{4,6},{5,7},{6,4},{7,5},{8,10},{9,11},{10,... | collective-permute-start | bytes 1572872 | tf_op jit(solution)/shard_map/ppermute | solution.py:430
  63.2 17.3 %collective-permute-start.15 = (bf16[2,128,1024]{2,1,0:T(8,128)(2,1)S(1)}, bf16[2,128,1024]{2,1,0:T(8,128)(2,1)S(1)}, u32[]{:S(2)}, u32[]{:S(2)}) collective-permute-start(bf16[2,128,1024]{2,1,0:T(8,128)(2,1)S(1)} %fusion.3), channel_id=1, source_target_pairs={{0,4},{1,5},{2,6},{3,7},{12,8},{13,9},{14,10},{15,11},{16,20},{17,... | collective-permute-start | bytes 1572872 | tf_op jit(solution)/shard_map/ppermute | solution.py:434
  64.7 15.7 %collective-permute-start.14 = (bf16[2,128,1024]{2,1,0:T(8,128)(2,1)S(1)}, bf16[2,128,1024]{2,1,0:T(8,128)(2,1)S(1)}, u32[]{:S(2)}, u32[]{:S(2)}) collective-permute-start(bf16[2,128,1024]{2,1,0:T(8,128)(2,1)S(1)} %add_convert_fusion.3), channel_id=1, source_target_pairs={{4,8},{5,9},{6,10},{7,11},{8,4},{9,5},{10,6},{11,7},{20,24},{21,25... | collective-permute-start | bytes 1572872 | tf_op jit(solution)/shard_map/ppermute | solution.py:434
  69.2 12.9 %collective-permute-start.16 = (bf16[2,128,1024]{2,1,0:T(8,128)(2,1)S(1)}, bf16[2,128,1024]{2,1,0:T(8,128)(2,1)S(1)}, u32[]{:S(2)}, u32[]{:S(2)}) collective-permute-start(bf16[2,128,1024]{2,1,0:T(8,128)(2,1)S(1)} %get-tuple-element.102), channel_id=1, source_target_pairs={{0,2},{1,3},{2,0},{3,1},{4,6},{5,7},{6,4},{7,5},{8,10},{9,11},{10,... | collective-permute-start | bytes 1572872 | tf_op jit(solution)/shard_map/ppermute | solution.py:430
  74.5 18.8 %collective-permute-start.9 = (bf16[2,128,1024]{2,1,0:T(8,128)(2,1)S(1)}, bf16[2,128,1024]{2,1,0:T(8,128)(2,1)S(1)}, u32[]{:S(2)}, u32[]{:S(2)}) collective-permute-start(bf16[2,128,1024]{2,1,0:T(8,128)(2,1)S(1)} %add_convert_fusion.6), channel_id=1, source_target_pairs={{4,8},{5,9},{6,10},{7,11},{8,4},{9,5},{10,6},{11,7},{20,24},{21,25... | collective-permute-start | bytes 1572872 | tf_op jit(solution)/shard_map/ppermute | solution.py:434
  78.8 14.5 %collective-permute-start.8 = (bf16[2,128,1024]{2,1,0:T(8,128)(2,1)S(1)}, bf16[2,128,1024]{2,1,0:T(8,128)(2,1)S(1)}, u32[]{:S(2)}, u32[]{:S(2)}) collective-permute-start(bf16[2,128,1024]{2,1,0:T(8,128)(2,1)S(1)} %get-tuple-element.87), channel_id=1, source_target_pairs={{0,2},{1,3},{2,0},{3,1},{4,6},{5,7},{6,4},{7,5},{8,10},{9,11},{10,... | collective-permute-start | bytes 1572872 | tf_op jit(solution)/shard_map/ppermute | solution.py:430
  80.4 12.9 %collective-permute-start.10 = (bf16[2,128,1024]{2,1,0:T(8,128)(2,1)S(1)}, bf16[2,128,1024]{2,1,0:T(8,128)(2,1)S(1)}, u32[]{:S(2)}, u32[]{:S(2)}) collective-permute-start(bf16[2,128,1024]{2,1,0:T(8,128)(2,1)S(1)} %add_convert_fusion.5), channel_id=1, source_target_pairs={{0,4},{1,5},{2,6},{3,7},{12,8},{13,9},{14,10},{15,11},{4,0},{5,1},... | collective-permute-start | bytes 1572872 | tf_op jit(solution)/shard_map/ppermute | solution.py:434
  82.4 20.4 %collective-permute-start.18 = (bf16[2,128,1024]{2,1,0:T(8,128)(2,1)S(1)}, bf16[2,128,1024]{2,1,0:T(8,128)(2,1)S(1)}, u32[]{:S(2)}, u32[]{:S(2)}) collective-permute-start(bf16[2,128,1024]{2,1,0:T(8,128)(2,1)S(1)} %add_convert_fusion.2), channel_id=1, source_target_pairs={{4,8},{5,9},{6,10},{7,11},{8,4},{9,5},{10,6},{11,7},{20,24},{21,25... | collective-permute-start | bytes 1572872 | tf_op jit(solution)/shard_map/ppermute | solution.py:434
  92.5 14.1 %collective-permute-start.17 = (bf16[2,128,1024]{2,1,0:T(8,128)(2,1)S(1)}, bf16[2,128,1024]{2,1,0:T(8,128)(2,1)S(1)}, u32[]{:S(2)}, u32[]{:S(2)}) collective-permute-start(bf16[2,128,1024]{2,1,0:T(8,128)(2,1)S(1)} %get-tuple-element.104), channel_id=1, source_target_pairs={{0,2},{1,3},{2,0},{3,1},{4,6},{5,7},{6,4},{7,5},{8,10},{9,11},{10,... | collective-permute-start | bytes 1572872 | tf_op jit(solution)/shard_map/ppermute | solution.py:430
  93.2 13.4 %collective-permute-start.19 = (bf16[2,128,1024]{2,1,0:T(8,128)(2,1)S(1)}, bf16[2,128,1024]{2,1,0:T(8,128)(2,1)S(1)}, u32[]{:S(2)}, u32[]{:S(2)}) collective-permute-start(bf16[2,128,1024]{2,1,0:T(8,128)(2,1)S(1)} %add_convert_fusion.1), channel_id=1, source_target_pairs={{0,4},{1,5},{2,6},{3,7},{12,8},{13,9},{14,10},{15,11},{4,0},{5,1},... | collective-permute-start | bytes 1572872 | tf_op jit(solution)/shard_map/ppermute | solution.py:434
  93.3 13.7 %copy-start.9 = (bf16[1024,1024]{1,0:T(8,128)(2,1)S(1)}, bf16[1024,1024]{1,0:T(8,128)(2,1)}, u32[]{:S(2)}) copy-start(bf16[1024,1024]{1,0:T(8,128)(2,1)} %constant.44.clone.refs_4_) | copy-start | bytes 6291460
  93.3 13.7 %copy-start.10 = (bf16[1024,1024]{1,0:T(8,128)(2,1)S(1)}, bf16[1024,1024]{1,0:T(8,128)(2,1)}, u32[]{:S(2)}) copy-start(bf16[1024,1024]{1,0:T(8,128)(2,1)} %constant.43.clone.refs_3_) | copy-start | bytes 6291460
  93.4 13.7 %copy-start.11 = (bf16[1,256,1024]{2,1,0:T(8,128)(2,1)S(1)}, bf16[1,256,1024]{2,1,0:T(8,128)(2,1)}, u32[]{:S(2)}) copy-start(bf16[1,256,1024]{2,1,0:T(8,128)(2,1)} %refs_2_.1) | copy-start | bytes 1572868
  112.6 11.4 %collective-permute-start.28 = (bf16[2,128,1024]{2,1,0:T(8,128)(2,1)S(1)}, bf16[2,128,1024]{2,1,0:T(8,128)(2,1)}, u32[]{:S(2)}, u32[]{:S(2)}) collective-permute-start(bf16[2,128,1024]{2,1,0:T(8,128)(2,1)S(1)} %get-tuple-element.112.refs_2_.refs_1_), channel_id=1, source_target_pairs={{0,4},{1,5},{2,6},{3,7},{12,8},{13,9},{14,10},{15,11},{4,0},{5,1},... | collective-permute-start | bytes 1572872 | tf_op jit(solution)/shard_map/ppermute | solution.py:434
  112.6 19.6 %collective-permute-start.27 = (bf16[2,128,1024]{2,1,0:T(8,128)(2,1)S(1)}, bf16[2,128,1024]{2,1,0:T(8,128)(2,1)}, u32[]{:S(2)}, u32[]{:S(2)}) collective-permute-start(bf16[2,128,1024]{2,1,0:T(8,128)(2,1)S(1)} %get-tuple-element.112.refs_2_.refs_1_), channel_id=1, source_target_pairs={{4,8},{5,9},{6,10},{7,11},{8,4},{9,5},{10,6},{11,7},{20,24},{21,25... | collective-permute-start | bytes 1572872 | tf_op jit(solution)/shard_map/ppermute | solution.py:434
  120.3 12.9 %collective-permute-start.26 = (bf16[2,128,1024]{2,1,0:T(8,128)(2,1)S(1)}, bf16[2,128,1024]{2,1,0:T(8,128)(2,1)S(1)}, u32[]{:S(2)}, u32[]{:S(2)}) collective-permute-start(bf16[2,128,1024]{2,1,0:T(8,128)(2,1)S(1)} %get-tuple-element.112.refs_2_.refs_1_), channel_id=1, source_target_pairs={{0,2},{1,3},{2,0},{3,1},{4,6},{5,7},{6,4},{7,5},{8,10},{9,11},{10,... | collective-permute-start | bytes 1572872 | tf_op jit(solution)/shard_map/ppermute | solution.py:430
  120.4 0.8 copy-start.4
  121.2 18.5 %collective-permute-start.22 = (bf16[2,128,1024]{2,1,0:T(8,128)(2,1)}, bf16[2,128,1024]{2,1,0:T(8,128)(2,1)}, u32[]{:S(2)}, u32[]{:S(2)}) collective-permute-start(bf16[2,128,1024]{2,1,0:T(8,128)(2,1)} %get-tuple-element.109.refs_1_.refs_0_), channel_id=1, source_target_pairs={{0,4},{1,5},{2,6},{3,7},{12,8},{13,9},{14,10},{15,11},{4,0},{5,1},... | collective-permute-start | bytes 1572872 | tf_op jit(solution)/shard_map/ppermute | solution.py:434
  121.2 22.3 %collective-permute-start.21 = (bf16[2,128,1024]{2,1,0:T(8,128)(2,1)}, bf16[2,128,1024]{2,1,0:T(8,128)(2,1)}, u32[]{:S(2)}, u32[]{:S(2)}) collective-permute-start(bf16[2,128,1024]{2,1,0:T(8,128)(2,1)} %get-tuple-element.109.refs_1_.refs_0_), channel_id=1, source_target_pairs={{4,8},{5,9},{6,10},{7,11},{8,4},{9,5},{10,6},{11,7},{20,24},{21,25... | collective-permute-start | bytes 1572872 | tf_op jit(solution)/shard_map/ppermute | solution.py:434
  124.0 20.4 %collective-permute-start.20 = (bf16[2,128,1024]{2,1,0:T(8,128)(2,1)}, bf16[2,128,1024]{2,1,0:T(8,128)(2,1)}, u32[]{:S(2)}, u32[]{:S(2)}) collective-permute-start(bf16[2,128,1024]{2,1,0:T(8,128)(2,1)} %get-tuple-element.109.refs_1_.refs_0_), channel_id=1, source_target_pairs={{0,2},{1,3},{2,0},{3,1},{4,6},{5,7},{6,4},{7,5},{8,10},{9,11},{10,... | collective-permute-start | bytes 1572872 | tf_op jit(solution)/shard_map/ppermute | solution.py:430
  133.2 0.8 copy-start.7
  134.0 14.8 %collective-permute-start.33 = (bf16[2,128,1024]{2,1,0:T(8,128)(2,1)}, bf16[2,128,1024]{2,1,0:T(8,128)(2,1)}, u32[]{:S(2)}, u32[]{:S(2)}) collective-permute-start(bf16[2,128,1024]{2,1,0:T(8,128)(2,1)} %collective-permute-done.27), channel_id=1, source_target_pairs={{4,0},{5,1},{6,2},{7,3},{8,12},{9,13},{10,14},{11,15},{20,16},{21,... | collective-permute-start | bytes 1572872 | tf_op jit(solution)/shard_map/ppermute | solution.py:434
  136.1 18.7 %collective-permute-start.32 = (bf16[2,128,1024]{2,1,0:T(8,128)(2,1)}, bf16[2,128,1024]{2,1,0:T(8,128)(2,1)}, u32[]{:S(2)}, u32[]{:S(2)}) collective-permute-start(bf16[2,128,1024]{2,1,0:T(8,128)(2,1)} %collective-permute-done.28.refs_4_.refs_3_), channel_id=1, source_target_pairs={{4,8},{5,9},{6,10},{7,11},{8,4},{9,5},{10,6},{11,7},{20,24},{21,25... | collective-permute-start | bytes 1572872 | tf_op jit(solution)/shard_map/ppermute | solution.py:434
  139.6 16.0 %collective-permute-start.31 = (bf16[2,128,1024]{2,1,0:T(8,128)(2,1)}, bf16[2,128,1024]{2,1,0:T(8,128)(2,1)}, u32[]{:S(2)}, u32[]{:S(2)}) collective-permute-start(bf16[2,128,1024]{2,1,0:T(8,128)(2,1)} %collective-permute-done.28.refs_4_.refs_3_), channel_id=1, source_target_pairs={{0,2},{1,3},{2,0},{3,1},{4,6},{5,7},{6,4},{7,5},{8,10},{9,11},{10,... | collective-permute-start | bytes 1572872 | tf_op jit(solution)/shard_map/ppermute | solution.py:430
  144.4 26.8 %collective-permute-start.25 = (bf16[2,128,1024]{2,1,0:T(8,128)(2,1)}, bf16[2,128,1024]{2,1,0:T(8,128)(2,1)S(1)}, u32[]{:S(2)}, u32[]{:S(2)}) collective-permute-start(bf16[2,128,1024]{2,1,0:T(8,128)(2,1)} %collective-permute-done.21), channel_id=1, source_target_pairs={{4,0},{5,1},{6,2},{7,3},{8,12},{9,13},{10,14},{11,15},{20,16},{21,... | collective-permute-start | bytes 1572872 | tf_op jit(solution)/shard_map/ppermute | solution.py:434
  145.7 25.5 %collective-permute-start.24 = (bf16[2,128,1024]{2,1,0:T(8,128)(2,1)}, bf16[2,128,1024]{2,1,0:T(8,128)(2,1)S(1)}, u32[]{:S(2)}, u32[]{:S(2)}) collective-permute-start(bf16[2,128,1024]{2,1,0:T(8,128)(2,1)} %collective-permute-done.22.refs_3_.refs_2_), channel_id=1, source_target_pairs={{4,8},{5,9},{6,10},{7,11},{8,4},{9,5},{10,6},{11,7},{20,24},{21,25... | collective-permute-start | bytes 1572872 | tf_op jit(solution)/shard_map/ppermute | solution.py:434
  148.8 22.4 %collective-permute-start.23 = (bf16[2,128,1024]{2,1,0:T(8,128)(2,1)}, bf16[2,128,1024]{2,1,0:T(8,128)(2,1)S(1)}, u32[]{:S(2)}, u32[]{:S(2)}) collective-permute-start(bf16[2,128,1024]{2,1,0:T(8,128)(2,1)} %collective-permute-done.22.refs_3_.refs_2_), channel_id=1, source_target_pairs={{0,2},{1,3},{2,0},{3,1},{4,6},{5,7},{6,4},{7,5},{8,10},{9,11},{10,... | collective-permute-start | bytes 1572872 | tf_op jit(solution)/shard_map/ppermute | solution.py:430
  155.6 8.3 %copy-start.6 = (bf16[2,128,1024]{2,1,0:T(8,128)(2,1)S(1)}, bf16[2,128,1024]{2,1,0:T(8,128)(2,1)}, u32[]{:S(2)}) copy-start(bf16[2,128,1024]{2,1,0:T(8,128)(2,1)} %copy-done.4) | copy-start | bytes 1572868
  156.8 21.2 %collective-permute-start.34 = (bf16[2,128,1024]{2,1,0:T(8,128)(2,1)S(1)}, bf16[2,128,1024]{2,1,0:T(8,128)(2,1)S(1)}, u32[]{:S(2)}, u32[]{:S(2)}) collective-permute-start(bf16[2,128,1024]{2,1,0:T(8,128)(2,1)S(1)} %broadcast_select_fusion.2.refs_2_), channel_id=1, source_target_pairs={{0,2},{1,3},{2,0},{3,1},{4,6},{5,7},{6,4},{7,5},{8,10},{9,11},{10,... | collective-permute-start | bytes 1572872 | tf_op jit(solution)/shard_map/ppermute | solution.py:430
  157.2 20.8 %collective-permute-start.35 = (bf16[2,128,1024]{2,1,0:T(8,128)(2,1)}, bf16[2,128,1024]{2,1,0:T(8,128)(2,1)S(1)}, u32[]{:S(2)}, u32[]{:S(2)}) collective-permute-start(bf16[2,128,1024]{2,1,0:T(8,128)(2,1)} %collective-permute-done.32), channel_id=1, source_target_pairs={{4,0},{5,1},{6,2},{7,3},{8,12},{9,13},{10,14},{11,15},{20,16},{21,... | collective-permute-start | bytes 1572872 | tf_op jit(solution)/shard_map/ppermute | solution.py:434
  158.5 1.0 copy-start.5
  159.6 1.0 copy-start.8
  163.9 3.4 %copy-start.3 = (f32[2,128,8192]{2,1,0:T(8,128)S(1)}, f32[2,128,8192]{2,1,0:T(8,128)}, u32[]{:S(2)}) copy-start(f32[2,128,8192]{2,1,0:T(8,128)} %refs_0_.1) | copy-start | bytes 25165828
  172.4 16.8 %collective-permute-start.29 = (bf16[2,128,1024]{2,1,0:T(8,128)(2,1)S(1)}, bf16[2,128,1024]{2,1,0:T(8,128)(2,1)S(1)}, u32[]{:S(2)}, u32[]{:S(2)}) collective-permute-start(bf16[2,128,1024]{2,1,0:T(8,128)(2,1)S(1)} %broadcast_select_fusion.3.refs_1_), channel_id=1, source_target_pairs={{0,2},{1,3},{2,0},{3,1},{4,6},{5,7},{6,4},{7,5},{8,10},{9,11},{10,... | collective-permute-start | bytes 1572872 | tf_op jit(solution)/shard_map/ppermute | solution.py:430
  175.3 14.0 %collective-permute-start.30 = (bf16[2,128,1024]{2,1,0:T(8,128)(2,1)S(1)}, bf16[2,128,1024]{2,1,0:T(8,128)(2,1)S(1)}, u32[]{:S(2)}, u32[]{:S(2)}) collective-permute-start(bf16[2,128,1024]{2,1,0:T(8,128)(2,1)S(1)} %collective-permute-done.24), channel_id=1, source_target_pairs={{4,0},{5,1},{6,2},{7,3},{8,12},{9,13},{10,14},{11,15},{20,16},{21,... | collective-permute-start | bytes 1572872 | tf_op jit(solution)/shard_map/ppermute | solution.py:434
  179.1 21.4 %collective-permute-start.37 = (bf16[2,128,1024]{2,1,0:T(8,128)(2,1)S(1)}, bf16[2,128,1024]{2,1,0:T(8,128)(2,1)S(1)}, u32[]{:S(2)}, u32[]{:S(2)}) collective-permute-start(bf16[2,128,1024]{2,1,0:T(8,128)(2,1)S(1)} %broadcast_select_fusion.refs_6_.refs_2_), channel_id=1, source_target_pairs={{0,2},{1,3},{2,0},{3,1},{4,6},{5,7},{6,4},{7,5},{8,10},{9,11},{10,... | collective-permute-start | bytes 1572872 | tf_op jit(solution)/shard_map/ppermute | solution.py:430
  202.8 18.5 %collective-permute-start.39 = (bf16[2,128,4096]{2,1,0:T(8,128)(2,1)S(1)}, bf16[2,128,4096]{2,1,0:T(8,128)(2,1)S(1)}, u32[]{:S(2)}, u32[]{:S(2)}) collective-permute-start(bf16[2,128,4096]{2,1,0:T(8,128)(2,1)S(1)} %get-tuple-element.133), channel_id=1, source_target_pairs={{0,1},{1,0},{2,3},{3,2},{4,5},{5,4},{6,7},{7,6},{8,9},{9,8},{10,11... | collective-permute-start | bytes 6291464 | tf_op jit(solution)/shard_map/ppermute | solution.py:427
  205.3 16.0 %collective-permute-start.40 = (bf16[2,128,4096]{2,1,0:T(8,128)(2,1)S(1)}, bf16[2,128,4096]{2,1,0:T(8,128)(2,1)S(1)}, u32[]{:S(2)}, u32[]{:S(2)}) collective-permute-start(bf16[2,128,4096]{2,1,0:T(8,128)(2,1)S(1)} %get-tuple-element.134), channel_id=1, source_target_pairs={{0,1},{1,0},{2,3},{3,2},{4,5},{5,4},{6,7},{7,6},{8,9},{9,8},{10,11... | collective-permute-start | bytes 6291464 | tf_op jit(solution)/shard_map/ppermute | solution.py:427
  205.4 13.1 %collective-permute-start.36 = (bf16[2,128,1024]{2,1,0:T(8,128)(2,1)S(1)}, bf16[2,128,1024]{2,1,0:T(8,128)(2,1)S(1)}, u32[]{:S(2)}, u32[]{:S(2)}) collective-permute-start(bf16[2,128,1024]{2,1,0:T(8,128)(2,1)S(1)} %broadcast_select_fusion.1.refs_5_.refs_1_), channel_id=1, source_target_pairs={{0,2},{1,3},{2,0},{3,1},{4,6},{5,7},{6,4},{7,5},{8,10},{9,11},{10,... | collective-permute-start | bytes 1572872 | tf_op jit(solution)/shard_map/ppermute | solution.py:430
  205.4 13.1 %collective-permute-start.38 = (bf16[2,128,1024]{2,1,0:T(8,128)(2,1)S(1)}, bf16[2,128,1024]{2,1,0:T(8,128)(2,1)S(1)}, u32[]{:S(2)}, u32[]{:S(2)}) collective-permute-start(bf16[2,128,1024]{2,1,0:T(8,128)(2,1)S(1)} %collective-permute-done.37.refs_4_), channel_id=1, source_target_pairs={{0,1},{1,0},{2,3},{3,2},{4,5},{5,4},{6,7},{7,6},{8,9},{9,8},{10,11... | collective-permute-start | bytes 1572872 | tf_op jit(solution)/shard_map/ppermute | solution.py:427
  218.5 2.8 %collective-permute-start.41 = (bf16[2,128,1024]{2,1,0:T(8,128)(2,1)S(1)}, bf16[2,128,1024]{2,1,0:T(8,128)(2,1)S(1)}, u32[]{:S(2)}, u32[]{:S(2)}) collective-permute-start(bf16[2,128,1024]{2,1,0:T(8,128)(2,1)S(1)} %collective-permute-done.36.refs_3_), channel_id=1, source_target_pairs={{0,1},{1,0},{2,3},{3,2},{4,5},{5,4},{6,7},{7,6},{8,9},{9,8},{10,11... | collective-permute-start | bytes 1572872 | tf_op jit(solution)/shard_map/ppermute | solution.py:427

commit v6 on v5

--- a/solution.py
+++ b/solution.py
@@ -519,17 +519,18 @@
             pieces["result", stream] = apply([spectrum], early)
             close(stream, ("beside", 2), "far inner", "outward", "result")
         else:
-            close(stream, ("beside", 2), "far inner", "outward")
+            pieces["slab", stream] = apply([], early, 1)[0]
+            close(stream, ("beside", 2), "far inner", "outward", "slab")
     for stream in (lead, last):
         from_next = jnp.where(at_ends, pieces["outward", stream], pieces["inner", stream])
         pieces[("next", 0), stream] = from_next
         pieces[("next", 2), stream] = across(from_next)
         pieces["far outward", stream] = along(pieces["far inner", stream], outward)
-        if stream == lead:
-            pieces["slab", stream] = apply([], early, 1)[0]
+        if stream == last:
+            pieces["slab", stream] = apply([pieces["slab", lead]], later, 1)[0]
+            close(stream, ("next", 2), "far outward", "slab")
         else:
-            pieces["slab", stream] = apply([pieces["slab", lead]], later, 1)[0]
-        close(stream, ("next", 2), "far outward", "slab")
+            close(stream, ("next", 2), "far outward")
     for stream in (lead, last):
         from_far = jnp.where(at_ends, pieces["far outward", stream], pieces["far inner", stream])
         pieces[("far", 0), stream] = from_far

time: 228 us -> 230 us (level)
  starting transfers between devices: 73.8 us -> 63.5 us
  Pallas kernels: 50.3 us -> 57.8 us
  waiting for transfers between devices: 84.1 us -> 89.9 us
    ppermute x20, waiting for transfers between devices: 28.5 us -> 37.1 us  [along(): return lax.ppermute(value, 'ty', pairs)]
    ppermute x16, starting transfers between devices: 17.7 us -> 9.92 us  [across(): return lax.ppermute(value, 'ty', [(i, i ^ 2) for i in range(count)])]
    pallas_call x3, Pallas kernels: 19 us -> 23.1 us  [forward(): pl.pallas_call(functools.partial(forward_kernel, base=base, images=images...]
    ppermute x20, starting transfers between devices: 50.8 us -> 47.2 us  [along(): return lax.ppermute(value, 'ty', pairs)]
    pallas_call x6, Pallas kernels: 22 us -> 25.4 us  [backward(): pl.pallas_call(functools.partial(kernel, slots=slots, held=held, parts=le...]
  transfers between devices with their start and end apart: 42 -> 42, of which waited for: 22 -> 23; matrix products, arithmetic and copies ran while one was open for 3% -> 3% of each run, Pallas kernels for 14% -> 17%
where the time goes in v6:
time: 230 us
  waiting for transfers between devices  89.9 us (39%)
  starting transfers between devices  63.5 us (28%)
  Pallas kernels  57.8 us (25%)
  local copies, waits for them, and re-layouts  11.2 us (5%)
  other arithmetic  6.67 us (3%)
    ppermute x16, waiting for transfers between devices, across(): return lax.ppermute(value, 'ty', [(i, i ^ 2) for i in range(count)])  50.3 us
    ppermute x20, starting transfers between devices, along(): return lax.ppermute(value, 'ty', pairs)  47.2 us
    ppermute x20, waiting for transfers between devices, along(): return lax.ppermute(value, 'ty', pairs)  37.1 us
    pallas_call x6, Pallas kernels, backward(): pl.pallas_call(functools.partial(kernel, slots=slots, held=held, parts=le...  25.4 us
    pallas_call x3, Pallas kernels, forward(): pl.pallas_call(functools.partial(forward_kernel, base=base, images=images...  23.1 us
    unnamed x28, local copies, waits for them, and re-layouts  10.5 us
    ppermute x16, starting transfers between devices, across(): return lax.ppermute(value, 'ty', [(i, i ^ 2) for i in range(count)])  9.92 us
    ppermute x6, starting transfers between devices, sibling(): return lax.ppermute(value, 'ty', [(i, i ^ 1) for i in range(count)])  6.3 us
  transfers between devices with their start and end apart: 42, of which 23 were waited for; matrix products, arithmetic and copies ran while one was open for 3% of the time, Pallas kernels for 17%

profile of v6, /device:TPU:11, one launch (start us, length us, event | category | flops | bytes accessed | tf_op | source)
XLA Modules:
  0.0 229.6 jit_solution(3134303834962736967)
XLA Ops:
  0.0 3.4 %copy-done.2 = f32[2,128,8192]{2,1,0:T(8,128)S(1)} copy-done((f32[2,128,8192]{2,1,0:T(8,128)S(1)}, f32[2,128,8192]{2,1,0:T(8,128)}, u32[]{:S(2)}) %copy-start.2) | copy-done | bytes 8388632
  3.4 1.9 low_part.3.refs_1_
  6.1 1.8 low_part.2.refs_0_
  8.9 3.3 %forward.3.refs_2_ = bf16[2,256,1024]{2,1,0:T(8,128)(2,1)S(1)} custom-call(s32[3,16]{1,0:T(4,128)S(1)} %pad_add_fusion.meta_ref, bf16[1024,1024]{1,0:T(8,128)(2,1)S(1)} %copy-done, bf16[1024,512]{1,0:T(8,128)(2,1)S(1)} %copy-done.1, bf16[128,8192]{1,0:T(8,128)(2,1)} %low_part.2.refs_0_, bf16[128,8192]{1,0:T(8,128)(2,1)} %low_part.3.refs_1_), custom_call_target="tpu_custom_call" | custom-call | flops 1024 | bytes 1024 | tf_op jit(solution)/shard_map/forward/pallas_call | solution.py:257
  13.2 3.3 %forward.4 = (bf16[2,128,1024]{2,1,0:T(8,128)(2,1)S(1)}, bf16[2,128,1024]{2,1,0:T(8,128)(2,1)S(1)}) custom-call(s32[3,16]{1,0:T(4,128)S(1)} %pad_add_fusion.meta_ref, bf16[1024,1024]{1,0:T(8,128)(2,1)S(1)} %copy-done, bf16[1024,512]{1,0:T(8,128)(2,1)S(1)} %copy-done.1, bf16[128,8192]{1,0:T(8,128)(2,1)} %collective-permute-done.refs_0_.refs_2_, ...), custom_call_target="tpu_custom_call" | custom-call | flops 1024 | bytes 1024 | tf_op jit(solution)/shard_map/forward/pallas_call | solution.py:257
  16.5 1.3 collective-permute-start.2
  18.1 16.4 %forward.5 = (bf16[2,128,1024]{2,1,0:T(8,128)(2,1)S(1)}, bf16[2,128,1024]{2,1,0:T(8,128)(2,1)S(1)}, bf16[2,128,1024]{2,1,0:T(8,128)(2,1)S(1)}, bf16[2,128,1024]{...) custom-call(s32[3,16]{1,0:T(4,128)S(1)} %pad_add_fusion.meta_ref, ...), custom_call_target="tpu_custom_call" | custom-call | flops 1024 | bytes 1024 | tf_op jit(solution)/shard_map/forward/pallas_call | solution.py:257
  34.7 1.3 collective-permute-start.3
  36.0 1.3 collective-permute-start.4
  37.3 3.6 %collective-permute-done.11 = bf16[2,128,1024]{2,1,0:T(8,128)(2,1)S(1)} collective-permute-done((bf16[2,128,1024]{2,1,0:T(8,128)(2,1)S(1)}, bf16[2,128,1024]{2,1,0:T(8,128)(2,1)S(1)}, u32[]{:S(2)}, u32[]{:S(2)}) %collective-permute-start.11) | collective-permute-done | bytes 524320 | tf_op jit(solution)/shard_map/ppermute | solution.py:430
  41.2 1.3 collective-permute-start.12
  42.5 1.3 collective-permute-start.13
  43.7 6.7 %collective-permute-done.3 = bf16[2,128,1024]{2,1,0:T(8,128)(2,1)S(1)} collective-permute-done((bf16[2,128,1024]{2,1,0:T(8,128)(2,1)S(1)}, bf16[2,128,1024]{2,1,0:T(8,128)(2,1)S(1)}, u32[]{:S(2)}, u32[]{:S(2)}) %collective-permute-start.3) | collective-permute-done | bytes 524320 | tf_op jit(solution)/shard_map/ppermute | solution.py:434
  50.5 1.7 collective-permute-done.4
  52.4 1.3 collective-permute-start.6
  54.0 3.5 %collective-permute-start.5 = (bf16[2,128,1024]{2,1,0:T(8,128)(2,1)S(1)}, bf16[2,128,1024]{2,1,0:T(8,128)(2,1)S(1)}, u32[]{:S(2)}, u32[]{:S(2)}) collective-permute-start(bf16[2,128,1024]{2,1,0:T(8,128)(2,1)S(1)} %add_convert_fusion.7), channel_id=1, source_target_pairs={{4,8},{5,9},{6,10},{7,11},{8,4},{9,5},{10,6},{11,7},{20,24},{21,25... | collective-permute-start | bytes 1572872 | tf_op jit(solution)/shard_map/ppermute | solution.py:434
  57.6 4.1 %collective-permute-done.12 = bf16[2,128,1024]{2,1,0:T(8,128)(2,1)S(1)} collective-permute-done((bf16[2,128,1024]{2,1,0:T(8,128)(2,1)S(1)}, bf16[2,128,1024]{2,1,0:T(8,128)(2,1)S(1)}, u32[]{:S(2)}, u32[]{:S(2)}) %collective-permute-start.12) | collective-permute-done | bytes 524320 | tf_op jit(solution)/shard_map/ppermute | solution.py:434
  61.7 1.7 collective-permute-done.13
  63.6 1.3 collective-permute-start.15
  65.2 3.5 %collective-permute-start.14 = (bf16[2,128,1024]{2,1,0:T(8,128)(2,1)S(1)}, bf16[2,128,1024]{2,1,0:T(8,128)(2,1)S(1)}, u32[]{:S(2)}, u32[]{:S(2)}) collective-permute-start(bf16[2,128,1024]{2,1,0:T(8,128)(2,1)S(1)} %add_convert_fusion.3), channel_id=1, source_target_pairs={{4,8},{5,9},{6,10},{7,11},{8,4},{9,5},{10,6},{11,7},{20,24},{21,25... | collective-permute-start | bytes 1572872 | tf_op jit(solution)/shard_map/ppermute | solution.py:434
  68.7 4.2 %collective-permute-done.6 = bf16[2,128,1024]{2,1,0:T(8,128)(2,1)S(1)} collective-permute-done((bf16[2,128,1024]{2,1,0:T(8,128)(2,1)S(1)}, bf16[2,128,1024]{2,1,0:T(8,128)(2,1)S(1)}, u32[]{:S(2)}, u32[]{:S(2)}) %collective-permute-start.6) | collective-permute-done | bytes 524320 | tf_op jit(solution)/shard_map/ppermute | solution.py:434
  73.0 1.7 collective-permute-done.7
  74.9 3.5 %collective-permute-start.9 = (bf16[2,128,1024]{2,1,0:T(8,128)(2,1)S(1)}, bf16[2,128,1024]{2,1,0:T(8,128)(2,1)S(1)}, u32[]{:S(2)}, u32[]{:S(2)}) collective-permute-start(bf16[2,128,1024]{2,1,0:T(8,128)(2,1)S(1)} %add_convert_fusion.6), channel_id=1, source_target_pairs={{4,8},{5,9},{6,10},{7,11},{8,4},{9,5},{10,6},{11,7},{20,24},{21,25... | collective-permute-start | bytes 1572872 | tf_op jit(solution)/shard_map/ppermute | solution.py:434
  78.5 1.5 collective-permute-start.8
  80.3 3.3 %collective-permute-done.15 = bf16[2,128,1024]{2,1,0:T(8,128)(2,1)S(1)} collective-permute-done((bf16[2,128,1024]{2,1,0:T(8,128)(2,1)S(1)}, bf16[2,128,1024]{2,1,0:T(8,128)(2,1)S(1)}, u32[]{:S(2)}, u32[]{:S(2)}) %collective-permute-start.15) | collective-permute-done | bytes 524320 | tf_op jit(solution)/shard_map/ppermute | solution.py:434
  83.9 8.7 %collective-permute-start.18 = (bf16[2,128,1024]{2,1,0:T(8,128)(2,1)S(1)}, bf16[2,128,1024]{2,1,0:T(8,128)(2,1)S(1)}, u32[]{:S(2)}, u32[]{:S(2)}) collective-permute-start(bf16[2,128,1024]{2,1,0:T(8,128)(2,1)S(1)} %add_convert_fusion.2), channel_id=1, source_target_pairs={{4,8},{5,9},{6,10},{7,11},{8,4},{9,5},{10,6},{11,7},{20,24},{21,25... | collective-permute-start | bytes 1572872 | tf_op jit(solution)/shard_map/ppermute | solution.py:434
  93.0 1.1 collective-permute-done.8
  94.1 3.2 %collective-permute-done.10 = bf16[2,128,1024]{2,1,0:T(8,128)(2,1)S(1)} collective-permute-done((bf16[2,128,1024]{2,1,0:T(8,128)(2,1)S(1)}, bf16[2,128,1024]{2,1,0:T(8,128)(2,1)S(1)}, u32[]{:S(2)}, u32[]{:S(2)}) %collective-permute-start.10) | collective-permute-done | bytes 524320 | tf_op jit(solution)/shard_map/ppermute | solution.py:434
  97.7 5.1 %collective-permute-done.18 = bf16[2,128,1024]{2,1,0:T(8,128)(2,1)S(1)} collective-permute-done((bf16[2,128,1024]{2,1,0:T(8,128)(2,1)S(1)}, bf16[2,128,1024]{2,1,0:T(8,128)(2,1)S(1)}, u32[]{:S(2)}, u32[]{:S(2)}) %collective-permute-start.18) | collective-permute-done | bytes 524320 | tf_op jit(solution)/shard_map/ppermute | solution.py:434
  102.8 3.9 %collective-permute-done.17 = bf16[2,128,1024]{2,1,0:T(8,128)(2,1)S(1)} collective-permute-done((bf16[2,128,1024]{2,1,0:T(8,128)(2,1)S(1)}, bf16[2,128,1024]{2,1,0:T(8,128)(2,1)S(1)}, u32[]{:S(2)}, u32[]{:S(2)}) %collective-permute-start.17) | collective-permute-done | bytes 524320 | tf_op jit(solution)/shard_map/ppermute | solution.py:430
  107.4 5.6 %middle.1 = (bf16[2,128,1024]{2,1,0:T(8,128)(2,1)}, bf16[2,128,1024]{2,1,0:T(8,128)(2,1)S(1)}) custom-call(bf16[2,128,1024]{2,1,0:T(8,128)(2,1)S(1)} %add_convert_fusion.refs_0_, bf16[2,128,1024]{2,1,0:T(8,128)(2,1)S(1)} %add_convert_fusion.4.refs_1_, bf16[1,256,1024]{2,1,0:T(8,128)(2,1)S(1)} %copy-done.11, bf16[1024,1024]{1,0:T(8,128)(2,1)S(1)} %copy-done.10, ...), custom_call_target="tpu_custom_call" | custom-call | flops 1024 | bytes 1024 | tf_op jit(solution)/shard_map/middle/pallas_call | solution.py:295
  113.3 6.9 %collective-permute-start.27 = (bf16[2,128,1024]{2,1,0:T(8,128)(2,1)S(1)}, bf16[2,128,1024]{2,1,0:T(8,128)(2,1)}, u32[]{:S(2)}, u32[]{:S(2)}) collective-permute-start(bf16[2,128,1024]{2,1,0:T(8,128)(2,1)S(1)} %get-tuple-element.112.refs_2_.refs_1_), channel_id=1, source_target_pairs={{4,8},{5,9},{6,10},{7,11},{8,4},{9,5},{10,6},{11,7},{20,24},{21,25... | collective-permute-start | bytes 1572872 | tf_op jit(solution)/shard_map/ppermute | solution.py:434
  121.0 2.8 %collective-permute-start.21 = (bf16[2,128,1024]{2,1,0:T(8,128)(2,1)}, bf16[2,128,1024]{2,1,0:T(8,128)(2,1)}, u32[]{:S(2)}, u32[]{:S(2)}) collective-permute-start(bf16[2,128,1024]{2,1,0:T(8,128)(2,1)} %get-tuple-element.109.refs_1_.refs_0_), channel_id=1, source_target_pairs={{4,8},{5,9},{6,10},{7,11},{8,4},{9,5},{10,6},{11,7},{20,24},{21,25... | collective-permute-start | bytes 1572872 | tf_op jit(solution)/shard_map/ppermute | solution.py:434
  123.9 1.5 collective-permute-start.20
  125.4 6.6 %collective-permute-done.27 = bf16[2,128,1024]{2,1,0:T(8,128)(2,1)} collective-permute-done((bf16[2,128,1024]{2,1,0:T(8,128)(2,1)S(1)}, bf16[2,128,1024]{2,1,0:T(8,128)(2,1)}, u32[]{:S(2)}, u32[]{:S(2)}) %collective-permute-start.27) | collective-permute-done | bytes 524320 | tf_op jit(solution)/shard_map/ppermute | solution.py:434
  132.0 0.9 collective-permute-done.26.refs_6_.refs_5_
  133.7 2.1 collective-permute-start.33
  135.8 3.7 %collective-permute-start.32 = (bf16[2,128,1024]{2,1,0:T(8,128)(2,1)}, bf16[2,128,1024]{2,1,0:T(8,128)(2,1)}, u32[]{:S(2)}, u32[]{:S(2)}) collective-permute-start(bf16[2,128,1024]{2,1,0:T(8,128)(2,1)} %collective-permute-done.28.refs_4_.refs_3_), channel_id=1, source_target_pairs={{4,8},{5,9},{6,10},{7,11},{8,4},{9,5},{10,6},{11,7},{20,24},{21,25... | collective-permute-start | bytes 1572872 | tf_op jit(solution)/shard_map/ppermute | solution.py:434
  139.9 3.4 %collective-permute-done.21 = bf16[2,128,1024]{2,1,0:T(8,128)(2,1)} collective-permute-done((bf16[2,128,1024]{2,1,0:T(8,128)(2,1)}, bf16[2,128,1024]{2,1,0:T(8,128)(2,1)}, u32[]{:S(2)}, u32[]{:S(2)}) %collective-permute-start.21) | collective-permute-done | bytes 524320 | tf_op jit(solution)/shard_map/ppermute | solution.py:434
  143.2 0.9 collective-permute-done.20.refs_5_.refs_4_
  144.1 1.3 collective-permute-start.25
  145.5 3.1 %collective-permute-start.24 = (bf16[2,128,1024]{2,1,0:T(8,128)(2,1)}, bf16[2,128,1024]{2,1,0:T(8,128)(2,1)S(1)}, u32[]{:S(2)}, u32[]{:S(2)}) collective-permute-start(bf16[2,128,1024]{2,1,0:T(8,128)(2,1)} %collective-permute-done.22.refs_3_.refs_2_), channel_id=1, source_target_pairs={{4,8},{5,9},{6,10},{7,11},{8,4},{9,5},{10,6},{11,7},{20,24},{21,25... | collective-permute-start | bytes 1572872 | tf_op jit(solution)/shard_map/ppermute | solution.py:434
  148.6 1.0 copy-done.5
  149.6 1.0 copy-done.8
  150.7 5.0 %backward.7.refs_0_ = bf16[2,128,8192]{2,1,0:T(8,128)(2,1)S(1)} custom-call(s32[3,16]{1,0:T(4,128)S(1)} %pad_add_fusion.meta_ref, bf16[1024,1024]{1,0:T(8,128)(2,1)S(1)} %copy-done, bf16[1024,512]{1,0:T(8,128)(2,1)S(1)} %copy-done.1, bf16[2,128,1024]{2,1,0:T(8,128)(2,1)} %get-tuple-element.109.refs_1_.refs_0_, bf16[2,128,1024]{2,1,0:T(8,128)(2,1)S(1)} %copy-done.5, ...), custom_call_target="tpu_custom_call" | custom-call | flops 1024 | bytes 1024 | tf_op jit(solution)/shard_map/backward/pallas_call | solution.py:279
  156.0 1.1 broadcast_select_fusion.2.refs_2_
  157.1 1.3 collective-permute-start.35
  158.4 1.3 collective-permute-start.36
  159.7 3.4 %copy-done.3 = f32[2,128,8192]{2,1,0:T(8,128)S(1)} copy-done((f32[2,128,8192]{2,1,0:T(8,128)S(1)}, f32[2,128,8192]{2,1,0:T(8,128)}, u32[]{:S(2)}) %copy-start.3) | copy-done | bytes 8388632
  163.1 4.8 %backward.6.refs_0_ = f32[2,128,8192]{2,1,0:T(8,128)S(1)} custom-call(s32[3,16]{1,0:T(4,128)S(1)} %pad_add_fusion.meta_ref, bf16[1024,1024]{1,0:T(8,128)(2,1)S(1)} %copy-done, bf16[1024,512]{1,0:T(8,128)(2,1)S(1)} %copy-done.1, f32[2,128,8192]{2,1,0:T(8,128)S(1)} %copy-done.3, bf16[2,128,1024]{2,1,0:T(8,128)(2,1)} %get-tuple-element.109.refs_1_.refs_0_, ...), custom_call_target="tpu_custom_call" | custom-call | flops 1024 | bytes 1024 | tf_op jit(solution)/shard_map/backward/pallas_call | solution.py:279
  167.9 1.1 broadcast_select_fusion.3.refs_1_
  169.3 1.3 collective-permute-start.30
  170.6 8.4 %collective-permute-done.35.refs_8_.refs_4_ = bf16[2,128,1024]{2,1,0:T(8,128)(2,1)S(1)} collective-permute-done((bf16[2,128,1024]{2,1,0:T(8,128)(2,1)S(1)}, bf16[2,128,1024]{2,1,0:T(8,128)(2,1)S(1)}, u32[]{:S(2)}, u32[]{:S(2)}) %collective-permute-start.35) | collective-permute-done | bytes 524320 | tf_op jit(solution)/shard_map/ppermute | solution.py:430
  179.0 1.1 broadcast_select_fusion.refs_6_.refs_2_
  180.2 2.8 %backward.8.refs_0_ = bf16[2,128,8192]{2,1,0:T(8,128)(2,1)S(1)} custom-call(s32[3,16]{1,0:T(4,128)S(1)} %pad_add_fusion.meta_ref, bf16[1024,1024]{1,0:T(8,128)(2,1)S(1)} %copy-done, bf16[1024,512]{1,0:T(8,128)(2,1)S(1)} %copy-done.1, bf16[2,128,8192]{2,1,0:T(8,128)(2,1)S(1)} %backward.7.refs_0_, bf16[2,128,1024]{2,1,0:T(8,128)(2,1)S(1)} %broadcast_select_fusion.3.refs_1_, ...), custom_call_target="tpu_custom_call" | custom-call | flops 1024 | bytes 1024 | tf_op jit(solution)/shard_map/backward/pallas_call | solution.py:279
  183.1 7.2 %collective-permute-done.29.refs_7_.refs_3_ = bf16[2,128,1024]{2,1,0:T(8,128)(2,1)S(1)} collective-permute-done((bf16[2,128,1024]{2,1,0:T(8,128)(2,1)S(1)}, bf16[2,128,1024]{2,1,0:T(8,128)(2,1)S(1)}, u32[]{:S(2)}, u32[]{:S(2)}) %collective-permute-start.29) | collective-permute-done | bytes 524320 | tf_op jit(solution)/shard_map/ppermute | solution.py:430
  190.3 11.2 %collective-permute-done.37.refs_4_ = bf16[2,128,1024]{2,1,0:T(8,128)(2,1)S(1)} collective-permute-done((bf16[2,128,1024]{2,1,0:T(8,128)(2,1)S(1)}, bf16[2,128,1024]{2,1,0:T(8,128)(2,1)S(1)}, u32[]{:S(2)}, u32[]{:S(2)}) %collective-permute-start.37) | collective-permute-done | bytes 524320 | tf_op jit(solution)/shard_map/ppermute | solution.py:430
  201.5 2.3 %backward.10 = (bf16[2,128,4096]{2,1,0:T(8,128)(2,1)S(1)}, bf16[2,128,4096]{2,1,0:T(8,128)(2,1)S(1)}) custom-call(s32[3,16]{1,0:T(4,128)S(1)} %pad_add_fusion.meta_ref, bf16[1024,1024]{1,0:T(8,128)(2,1)S(1)} %copy-done, bf16[1024,512]{1,0:T(8,128)(2,1)S(1)} %copy-done.1, bf16[2,128,8192]{2,1,0:T(8,128)(2,1)S(1)} %backward.8.refs_0_, ...), custom_call_target="tpu_custom_call" | custom-call | flops 1024 | bytes 1024 | tf_op jit(solution)/shard_map/backward/pallas_call | solution.py:279
  203.9 3.4 %collective-permute-start.39 = (bf16[2,128,4096]{2,1,0:T(8,128)(2,1)S(1)}, bf16[2,128,4096]{2,1,0:T(8,128)(2,1)S(1)}, u32[]{:S(2)}, u32[]{:S(2)}) collective-permute-start(bf16[2,128,4096]{2,1,0:T(8,128)(2,1)S(1)} %get-tuple-element.133), channel_id=1, source_target_pairs={{0,1},{1,0},{2,3},{3,2},{4,5},{5,4},{6,7},{7,6},{8,9},{9,8},{10,11... | collective-permute-start | bytes 6291464 | tf_op jit(solution)/shard_map/ppermute | solution.py:427
  208.3 4.1 %backward.9.refs_0_ = f32[2,128,8192]{2,1,0:T(8,128)S(1)} custom-call(s32[3,16]{1,0:T(4,128)S(1)} %pad_add_fusion.meta_ref, bf16[1024,1024]{1,0:T(8,128)(2,1)S(1)} %copy-done, bf16[1024,512]{1,0:T(8,128)(2,1)S(1)} %copy-done.1, f32[2,128,8192]{2,1,0:T(8,128)S(1)} %backward.6.refs_0_, bf16[2,128,1024]{2,1,0:T(8,128)(2,1)S(1)} %broadcast_select_fusion.3.refs_1_, ...), custom_call_target="tpu_custom_call" | custom-call | flops 1024 | bytes 1024 | tf_op jit(solution)/shard_map/backward/pallas_call | solution.py:279
  212.4 8.0 %collective-permute-done.34.refs_3_ = bf16[2,128,1024]{2,1,0:T(8,128)(2,1)S(1)} collective-permute-done((bf16[2,128,1024]{2,1,0:T(8,128)(2,1)S(1)}, bf16[2,128,1024]{2,1,0:T(8,128)(2,1)S(1)}, u32[]{:S(2)}, u32[]{:S(2)}) %collective-permute-start.34) | collective-permute-done | bytes 524320 | tf_op jit(solution)/shard_map/ppermute | solution.py:430
  220.4 1.3 collective-permute-start.41
  221.7 1.5 collective-permute-done.41.refs_5_
  223.2 6.3 %backward.11 = f32[2,128,8192]{2,1,0:T(8,128)} custom-call(s32[3,16]{1,0:T(4,128)S(1)} %pad_add_fusion.meta_ref, bf16[1024,1024]{1,0:T(8,128)(2,1)S(1)} %copy-done, bf16[1024,512]{1,0:T(8,128)(2,1)S(1)} %copy-done.1, f32[2,128,8192]{2,1,0:T(8,128)S(1)} %backward.9.refs_0_, bf16[2,128,4096]{2,1,0:T(8,128)(2,1)S(1)} %collective-permute-done.39.refs_1_, ...), custom_call_target="tpu_custom_call" | custom-call | flops 1024 | bytes 1024 | tf_op jit(solution)/shard_map/backward/pallas_call | solution.py:279
  (81 shorter events, 10.6 us)
Async XLA Ops:
  0.0 3.4 %copy-start.2 = (f32[2,128,8192]{2,1,0:T(8,128)S(1)}, f32[2,128,8192]{2,1,0:T(8,128)}, u32[]{:S(2)}) copy-start(f32[2,128,8192]{2,1,0:T(8,128)} %refs_0_.1) | copy-start | bytes 25165828
  5.3 3.4 %copy-start.12 = (s32[16]{0:T(128)S(1)}, s32[16]{0:T(128)}, u32[]{:S(2)}) copy-start(s32[16]{0:T(128)} %param.12) | copy-start | bytes 196
  5.3 3.4 %copy-start.13 = (s32[16]{0:T(128)S(1)}, s32[16]{0:T(128)}, u32[]{:S(2)}) copy-start(s32[16]{0:T(128)} %param.13) | copy-start | bytes 196
  5.3 3.6 %copy-start = (bf16[1024,1024]{1,0:T(8,128)(2,1)S(1)}, bf16[1024,1024]{1,0:T(8,128)(2,1)}, u32[]{:S(2)}) copy-start(bf16[1024,1024]{1,0:T(8,128)(2,1)} %pupil_ref.17) | copy-start | bytes 6291460
  5.3 3.6 %copy-start.1 = (bf16[1024,512]{1,0:T(8,128)(2,1)S(1)}, bf16[1024,512]{1,0:T(8,128)(2,1)}, u32[]{:S(2)}) copy-start(bf16[1024,512]{1,0:T(8,128)(2,1)} %constant.42.clone.band_ref) | copy-start | bytes 3145732
  5.3 7.0 %collective-permute-start.1 = (bf16[128,8192]{1,0:T(8,128)(2,1)}, bf16[128,8192]{1,0:T(8,128)(2,1)}, u32[]{:S(2)}, u32[]{:S(2)}) collective-permute-start(bf16[128,8192]{1,0:T(8,128)(2,1)} %low_part.3.refs_1_), channel_id=1, source_target_pairs={{0,1},{1,0},{2,3},{3,2},{4,5},{5,4},{6,7},{7,6},{8,9},{9,8},{10,11... | collective-permute-start | bytes 6291464 | tf_op jit(solution)/shard_map/ppermute | solution.py:427
  7.9 5.3 %collective-permute-start = (bf16[128,8192]{1,0:T(8,128)(2,1)}, bf16[128,8192]{1,0:T(8,128)(2,1)}, u32[]{:S(2)}, u32[]{:S(2)}) collective-permute-start(bf16[128,8192]{1,0:T(8,128)(2,1)} %low_part.2.refs_0_), channel_id=1, source_target_pairs={{0,1},{1,0},{2,3},{3,2},{4,5},{5,4},{6,7},{7,6},{8,9},{9,8},{10,11... | collective-permute-start | bytes 6291464 | tf_op jit(solution)/shard_map/ppermute | solution.py:427
  16.5 18.0 %collective-permute-start.2 = (bf16[2,128,1024]{2,1,0:T(8,128)(2,1)S(1)}, bf16[2,128,1024]{2,1,0:T(8,128)(2,1)S(1)}, u32[]{:S(2)}, u32[]{:S(2)}) collective-permute-start(bf16[2,128,1024]{2,1,0:T(8,128)(2,1)S(1)} %get-tuple-element.75), channel_id=1, source_target_pairs={{0,2},{1,3},{2,0},{3,1},{4,6},{5,7},{6,4},{7,5},{8,10},{9,11},{10,... | collective-permute-start | bytes 1572872 | tf_op jit(solution)/shard_map/ppermute | solution.py:430
  17.8 23.1 %collective-permute-start.11 = (bf16[2,128,1024]{2,1,0:T(8,128)(2,1)S(1)}, bf16[2,128,1024]{2,1,0:T(8,128)(2,1)S(1)}, u32[]{:S(2)}, u32[]{:S(2)}) collective-permute-start(bf16[2,128,1024]{2,1,0:T(8,128)(2,1)S(1)} %get-tuple-element.71), channel_id=1, source_target_pairs={{0,2},{1,3},{2,0},{3,1},{4,6},{5,7},{6,4},{7,5},{8,10},{9,11},{10,... | collective-permute-start | bytes 1572872 | tf_op jit(solution)/shard_map/ppermute | solution.py:430
  34.7 15.8 %collective-permute-start.3 = (bf16[2,128,1024]{2,1,0:T(8,128)(2,1)S(1)}, bf16[2,128,1024]{2,1,0:T(8,128)(2,1)S(1)}, u32[]{:S(2)}, u32[]{:S(2)}) collective-permute-start(bf16[2,128,1024]{2,1,0:T(8,128)(2,1)S(1)} %fusion), channel_id=1, source_target_pairs={{0,4},{1,5},{2,6},{3,7},{12,8},{13,9},{14,10},{15,11},{16,20},{17,... | collective-permute-start | bytes 1572872 | tf_op jit(solution)/shard_map/ppermute | solution.py:434
  36.0 16.2 %collective-permute-start.4 = (bf16[2,128,1024]{2,1,0:T(8,128)(2,1)S(1)}, bf16[2,128,1024]{2,1,0:T(8,128)(2,1)S(1)}, u32[]{:S(2)}, u32[]{:S(2)}) collective-permute-start(bf16[2,128,1024]{2,1,0:T(8,128)(2,1)S(1)} %get-tuple-element.80), channel_id=1, source_target_pairs={{0,2},{1,3},{2,0},{3,1},{4,6},{5,7},{6,4},{7,5},{8,10},{9,11},{10,... | collective-permute-start | bytes 1572872 | tf_op jit(solution)/shard_map/ppermute | solution.py:430
  41.2 20.6 %collective-permute-start.12 = (bf16[2,128,1024]{2,1,0:T(8,128)(2,1)S(1)}, bf16[2,128,1024]{2,1,0:T(8,128)(2,1)S(1)}, u32[]{:S(2)}, u32[]{:S(2)}) collective-permute-start(bf16[2,128,1024]{2,1,0:T(8,128)(2,1)S(1)} %fusion.2), channel_id=1, source_target_pairs={{0,4},{1,5},{2,6},{3,7},{12,8},{13,9},{14,10},{15,11},{16,20},{17,... | collective-permute-start | bytes 1572872 | tf_op jit(solution)/shard_map/ppermute | solution.py:434
  42.5 21.0 %collective-permute-start.13 = (bf16[2,128,1024]{2,1,0:T(8,128)(2,1)S(1)}, bf16[2,128,1024]{2,1,0:T(8,128)(2,1)S(1)}, u32[]{:S(2)}, u32[]{:S(2)}) collective-permute-start(bf16[2,128,1024]{2,1,0:T(8,128)(2,1)S(1)} %get-tuple-element.97), channel_id=1, source_target_pairs={{0,2},{1,3},{2,0},{3,1},{4,6},{5,7},{6,4},{7,5},{8,10},{9,11},{10,... | collective-permute-start | bytes 1572872 | tf_op jit(solution)/shard_map/ppermute | solution.py:430
  52.4 20.6 %collective-permute-start.6 = (bf16[2,128,1024]{2,1,0:T(8,128)(2,1)S(1)}, bf16[2,128,1024]{2,1,0:T(8,128)(2,1)S(1)}, u32[]{:S(2)}, u32[]{:S(2)}) collective-permute-start(bf16[2,128,1024]{2,1,0:T(8,128)(2,1)S(1)} %fusion.1), channel_id=1, source_target_pairs={{0,4},{1,5},{2,6},{3,7},{12,8},{13,9},{14,10},{15,11},{16,20},{17,... | collective-permute-start | bytes 1572872 | tf_op jit(solution)/shard_map/ppermute | solution.py:434
  54.0 19.0 %collective-permute-start.5 = (bf16[2,128,1024]{2,1,0:T(8,128)(2,1)S(1)}, bf16[2,128,1024]{2,1,0:T(8,128)(2,1)S(1)}, u32[]{:S(2)}, u32[]{:S(2)}) collective-permute-start(bf16[2,128,1024]{2,1,0:T(8,128)(2,1)S(1)} %add_convert_fusion.7), channel_id=1, source_target_pairs={{4,8},{5,9},{6,10},{7,11},{8,4},{9,5},{10,6},{11,7},{20,24},{21,25... | collective-permute-start | bytes 1572872 | tf_op jit(solution)/shard_map/ppermute | solution.py:434
  57.5 17.2 %collective-permute-start.7 = (bf16[2,128,1024]{2,1,0:T(8,128)(2,1)S(1)}, bf16[2,128,1024]{2,1,0:T(8,128)(2,1)S(1)}, u32[]{:S(2)}, u32[]{:S(2)}) collective-permute-start(bf16[2,128,1024]{2,1,0:T(8,128)(2,1)S(1)} %get-tuple-element.85), channel_id=1, source_target_pairs={{0,2},{1,3},{2,0},{3,1},{4,6},{5,7},{6,4},{7,5},{8,10},{9,11},{10,... | collective-permute-start | bytes 1572872 | tf_op jit(solution)/shard_map/ppermute | solution.py:430
  63.6 20.0 %collective-permute-start.15 = (bf16[2,128,1024]{2,1,0:T(8,128)(2,1)S(1)}, bf16[2,128,1024]{2,1,0:T(8,128)(2,1)S(1)}, u32[]{:S(2)}, u32[]{:S(2)}) collective-permute-start(bf16[2,128,1024]{2,1,0:T(8,128)(2,1)S(1)} %fusion.3), channel_id=1, source_target_pairs={{0,4},{1,5},{2,6},{3,7},{12,8},{13,9},{14,10},{15,11},{16,20},{17,... | collective-permute-start | bytes 1572872 | tf_op jit(solution)/shard_map/ppermute | solution.py:434
  65.2 18.4 %collective-permute-start.14 = (bf16[2,128,1024]{2,1,0:T(8,128)(2,1)S(1)}, bf16[2,128,1024]{2,1,0:T(8,128)(2,1)S(1)}, u32[]{:S(2)}, u32[]{:S(2)}) collective-permute-start(bf16[2,128,1024]{2,1,0:T(8,128)(2,1)S(1)} %add_convert_fusion.3), channel_id=1, source_target_pairs={{4,8},{5,9},{6,10},{7,11},{8,4},{9,5},{10,6},{11,7},{20,24},{21,25... | collective-permute-start | bytes 1572872 | tf_op jit(solution)/shard_map/ppermute | solution.py:434
  73.0 10.7 %collective-permute-start.16 = (bf16[2,128,1024]{2,1,0:T(8,128)(2,1)S(1)}, bf16[2,128,1024]{2,1,0:T(8,128)(2,1)S(1)}, u32[]{:S(2)}, u32[]{:S(2)}) collective-permute-start(bf16[2,128,1024]{2,1,0:T(8,128)(2,1)S(1)} %get-tuple-element.102), channel_id=1, source_target_pairs={{0,2},{1,3},{2,0},{3,1},{4,6},{5,7},{6,4},{7,5},{8,10},{9,11},{10,... | collective-permute-start | bytes 1572872 | tf_op jit(solution)/shard_map/ppermute | solution.py:430
  74.9 18.0 %collective-permute-start.9 = (bf16[2,128,1024]{2,1,0:T(8,128)(2,1)S(1)}, bf16[2,128,1024]{2,1,0:T(8,128)(2,1)S(1)}, u32[]{:S(2)}, u32[]{:S(2)}) collective-permute-start(bf16[2,128,1024]{2,1,0:T(8,128)(2,1)S(1)} %add_convert_fusion.6), channel_id=1, source_target_pairs={{4,8},{5,9},{6,10},{7,11},{8,4},{9,5},{10,6},{11,7},{20,24},{21,25... | collective-permute-start | bytes 1572872 | tf_op jit(solution)/shard_map/ppermute | solution.py:434
  78.5 15.6 %collective-permute-start.8 = (bf16[2,128,1024]{2,1,0:T(8,128)(2,1)S(1)}, bf16[2,128,1024]{2,1,0:T(8,128)(2,1)S(1)}, u32[]{:S(2)}, u32[]{:S(2)}) collective-permute-start(bf16[2,128,1024]{2,1,0:T(8,128)(2,1)S(1)} %get-tuple-element.87), channel_id=1, source_target_pairs={{0,2},{1,3},{2,0},{3,1},{4,6},{5,7},{6,4},{7,5},{8,10},{9,11},{10,... | collective-permute-start | bytes 1572872 | tf_op jit(solution)/shard_map/ppermute | solution.py:430
  83.6 13.7 %collective-permute-start.10 = (bf16[2,128,1024]{2,1,0:T(8,128)(2,1)S(1)}, bf16[2,128,1024]{2,1,0:T(8,128)(2,1)S(1)}, u32[]{:S(2)}, u32[]{:S(2)}) collective-permute-start(bf16[2,128,1024]{2,1,0:T(8,128)(2,1)S(1)} %add_convert_fusion.5), channel_id=1, source_target_pairs={{0,4},{1,5},{2,6},{3,7},{12,8},{13,9},{14,10},{15,11},{4,0},{5,1},... | collective-permute-start | bytes 1572872 | tf_op jit(solution)/shard_map/ppermute | solution.py:434
  83.9 18.9 %collective-permute-start.18 = (bf16[2,128,1024]{2,1,0:T(8,128)(2,1)S(1)}, bf16[2,128,1024]{2,1,0:T(8,128)(2,1)S(1)}, u32[]{:S(2)}, u32[]{:S(2)}) collective-permute-start(bf16[2,128,1024]{2,1,0:T(8,128)(2,1)S(1)} %add_convert_fusion.2), channel_id=1, source_target_pairs={{4,8},{5,9},{6,10},{7,11},{8,4},{9,5},{10,6},{11,7},{20,24},{21,25... | collective-permute-start | bytes 1572872 | tf_op jit(solution)/shard_map/ppermute | solution.py:434
  92.6 14.1 %collective-permute-start.17 = (bf16[2,128,1024]{2,1,0:T(8,128)(2,1)S(1)}, bf16[2,128,1024]{2,1,0:T(8,128)(2,1)S(1)}, u32[]{:S(2)}, u32[]{:S(2)}) collective-permute-start(bf16[2,128,1024]{2,1,0:T(8,128)(2,1)S(1)} %get-tuple-element.104), channel_id=1, source_target_pairs={{0,2},{1,3},{2,0},{3,1},{4,6},{5,7},{6,4},{7,5},{8,10},{9,11},{10,... | collective-permute-start | bytes 1572872 | tf_op jit(solution)/shard_map/ppermute | solution.py:430
  92.9 14.1 %collective-permute-start.19 = (bf16[2,128,1024]{2,1,0:T(8,128)(2,1)S(1)}, bf16[2,128,1024]{2,1,0:T(8,128)(2,1)S(1)}, u32[]{:S(2)}, u32[]{:S(2)}) collective-permute-start(bf16[2,128,1024]{2,1,0:T(8,128)(2,1)S(1)} %add_convert_fusion.1), channel_id=1, source_target_pairs={{0,4},{1,5},{2,6},{3,7},{12,8},{13,9},{14,10},{15,11},{4,0},{5,1},... | collective-permute-start | bytes 1572872 | tf_op jit(solution)/shard_map/ppermute | solution.py:434
  97.3 10.1 %copy-start.9 = (bf16[1024,1024]{1,0:T(8,128)(2,1)S(1)}, bf16[1024,1024]{1,0:T(8,128)(2,1)}, u32[]{:S(2)}) copy-start(bf16[1024,1024]{1,0:T(8,128)(2,1)} %constant.44.clone.refs_4_) | copy-start | bytes 6291460
  97.3 10.1 %copy-start.10 = (bf16[1024,1024]{1,0:T(8,128)(2,1)S(1)}, bf16[1024,1024]{1,0:T(8,128)(2,1)}, u32[]{:S(2)}) copy-start(bf16[1024,1024]{1,0:T(8,128)(2,1)} %constant.43.clone.refs_3_) | copy-start | bytes 6291460
  97.3 10.1 %copy-start.11 = (bf16[1,256,1024]{2,1,0:T(8,128)(2,1)S(1)}, bf16[1,256,1024]{2,1,0:T(8,128)(2,1)}, u32[]{:S(2)}) copy-start(bf16[1,256,1024]{2,1,0:T(8,128)(2,1)} %refs_2_.1) | copy-start | bytes 1572868
  113.0 10.9 %collective-permute-start.28 = (bf16[2,128,1024]{2,1,0:T(8,128)(2,1)S(1)}, bf16[2,128,1024]{2,1,0:T(8,128)(2,1)}, u32[]{:S(2)}, u32[]{:S(2)}) collective-permute-start(bf16[2,128,1024]{2,1,0:T(8,128)(2,1)S(1)} %get-tuple-element.112.refs_2_.refs_1_), channel_id=1, source_target_pairs={{0,4},{1,5},{2,6},{3,7},{12,8},{13,9},{14,10},{15,11},{4,0},{5,1},... | collective-permute-start | bytes 1572872 | tf_op jit(solution)/shard_map/ppermute | solution.py:434
  113.3 18.7 %collective-permute-start.27 = (bf16[2,128,1024]{2,1,0:T(8,128)(2,1)S(1)}, bf16[2,128,1024]{2,1,0:T(8,128)(2,1)}, u32[]{:S(2)}, u32[]{:S(2)}) collective-permute-start(bf16[2,128,1024]{2,1,0:T(8,128)(2,1)S(1)} %get-tuple-element.112.refs_2_.refs_1_), channel_id=1, source_target_pairs={{4,8},{5,9},{6,10},{7,11},{8,4},{9,5},{10,6},{11,7},{20,24},{21,25... | collective-permute-start | bytes 1572872 | tf_op jit(solution)/shard_map/ppermute | solution.py:434
  120.2 12.8 %collective-permute-start.26 = (bf16[2,128,1024]{2,1,0:T(8,128)(2,1)S(1)}, bf16[2,128,1024]{2,1,0:T(8,128)(2,1)S(1)}, u32[]{:S(2)}, u32[]{:S(2)}) collective-permute-start(bf16[2,128,1024]{2,1,0:T(8,128)(2,1)S(1)} %get-tuple-element.112.refs_2_.refs_1_), channel_id=1, source_target_pairs={{0,2},{1,3},{2,0},{3,1},{4,6},{5,7},{6,4},{7,5},{8,10},{9,11},{10,... | collective-permute-start | bytes 1572872 | tf_op jit(solution)/shard_map/ppermute | solution.py:430
  120.2 0.8 copy-start.4
  121.0 18.4 %collective-permute-start.22 = (bf16[2,128,1024]{2,1,0:T(8,128)(2,1)}, bf16[2,128,1024]{2,1,0:T(8,128)(2,1)}, u32[]{:S(2)}, u32[]{:S(2)}) collective-permute-start(bf16[2,128,1024]{2,1,0:T(8,128)(2,1)} %get-tuple-element.109.refs_1_.refs_0_), channel_id=1, source_target_pairs={{0,4},{1,5},{2,6},{3,7},{12,8},{13,9},{14,10},{15,11},{4,0},{5,1},... | collective-permute-start | bytes 1572872 | tf_op jit(solution)/shard_map/ppermute | solution.py:434
  121.0 22.2 %collective-permute-start.21 = (bf16[2,128,1024]{2,1,0:T(8,128)(2,1)}, bf16[2,128,1024]{2,1,0:T(8,128)(2,1)}, u32[]{:S(2)}, u32[]{:S(2)}) collective-permute-start(bf16[2,128,1024]{2,1,0:T(8,128)(2,1)} %get-tuple-element.109.refs_1_.refs_0_), channel_id=1, source_target_pairs={{4,8},{5,9},{6,10},{7,11},{8,4},{9,5},{10,6},{11,7},{20,24},{21,25... | collective-permute-start | bytes 1572872 | tf_op jit(solution)/shard_map/ppermute | solution.py:434
  123.9 20.3 %collective-permute-start.20 = (bf16[2,128,1024]{2,1,0:T(8,128)(2,1)}, bf16[2,128,1024]{2,1,0:T(8,128)(2,1)}, u32[]{:S(2)}, u32[]{:S(2)}) collective-permute-start(bf16[2,128,1024]{2,1,0:T(8,128)(2,1)} %get-tuple-element.109.refs_1_.refs_0_), channel_id=1, source_target_pairs={{0,2},{1,3},{2,0},{3,1},{4,6},{5,7},{6,4},{7,5},{8,10},{9,11},{10,... | collective-permute-start | bytes 1572872 | tf_op jit(solution)/shard_map/ppermute | solution.py:430
  132.9 0.8 copy-start.7
  133.7 22.0 %collective-permute-start.33 = (bf16[2,128,1024]{2,1,0:T(8,128)(2,1)}, bf16[2,128,1024]{2,1,0:T(8,128)(2,1)}, u32[]{:S(2)}, u32[]{:S(2)}) collective-permute-start(bf16[2,128,1024]{2,1,0:T(8,128)(2,1)} %collective-permute-done.27), channel_id=1, source_target_pairs={{4,0},{5,1},{6,2},{7,3},{8,12},{9,13},{10,14},{11,15},{20,16},{21,... | collective-permute-start | bytes 1572872 | tf_op jit(solution)/shard_map/ppermute | solution.py:434
  135.8 20.2 %collective-permute-start.32 = (bf16[2,128,1024]{2,1,0:T(8,128)(2,1)}, bf16[2,128,1024]{2,1,0:T(8,128)(2,1)}, u32[]{:S(2)}, u32[]{:S(2)}) collective-permute-start(bf16[2,128,1024]{2,1,0:T(8,128)(2,1)} %collective-permute-done.28.refs_4_.refs_3_), channel_id=1, source_target_pairs={{4,8},{5,9},{6,10},{7,11},{8,4},{9,5},{10,6},{11,7},{20,24},{21,25... | collective-permute-start | bytes 1572872 | tf_op jit(solution)/shard_map/ppermute | solution.py:434
  139.5 16.5 %collective-permute-start.31 = (bf16[2,128,1024]{2,1,0:T(8,128)(2,1)}, bf16[2,128,1024]{2,1,0:T(8,128)(2,1)}, u32[]{:S(2)}, u32[]{:S(2)}) collective-permute-start(bf16[2,128,1024]{2,1,0:T(8,128)(2,1)} %collective-permute-done.28.refs_4_.refs_3_), channel_id=1, source_target_pairs={{0,2},{1,3},{2,0},{3,1},{4,6},{5,7},{6,4},{7,5},{8,10},{9,11},{10,... | collective-permute-start | bytes 1572872 | tf_op jit(solution)/shard_map/ppermute | solution.py:430
  144.1 23.8 %collective-permute-start.25 = (bf16[2,128,1024]{2,1,0:T(8,128)(2,1)}, bf16[2,128,1024]{2,1,0:T(8,128)(2,1)S(1)}, u32[]{:S(2)}, u32[]{:S(2)}) collective-permute-start(bf16[2,128,1024]{2,1,0:T(8,128)(2,1)} %collective-permute-done.21), channel_id=1, source_target_pairs={{4,0},{5,1},{6,2},{7,3},{8,12},{9,13},{10,14},{11,15},{20,16},{21,... | collective-permute-start | bytes 1572872 | tf_op jit(solution)/shard_map/ppermute | solution.py:434
  145.5 22.4 %collective-permute-start.24 = (bf16[2,128,1024]{2,1,0:T(8,128)(2,1)}, bf16[2,128,1024]{2,1,0:T(8,128)(2,1)S(1)}, u32[]{:S(2)}, u32[]{:S(2)}) collective-permute-start(bf16[2,128,1024]{2,1,0:T(8,128)(2,1)} %collective-permute-done.22.refs_3_.refs_2_), channel_id=1, source_target_pairs={{4,8},{5,9},{6,10},{7,11},{8,4},{9,5},{10,6},{11,7},{20,24},{21,25... | collective-permute-start | bytes 1572872 | tf_op jit(solution)/shard_map/ppermute | solution.py:434
  148.6 1.0 copy-start.5
  149.6 1.0 copy-start.8
  150.7 9.1 %copy-start.6 = (bf16[2,128,1024]{2,1,0:T(8,128)(2,1)S(1)}, bf16[2,128,1024]{2,1,0:T(8,128)(2,1)}, u32[]{:S(2)}) copy-start(bf16[2,128,1024]{2,1,0:T(8,128)(2,1)} %copy-done.4) | copy-start | bytes 1572868
  155.7 12.2 %collective-permute-start.23 = (bf16[2,128,1024]{2,1,0:T(8,128)(2,1)}, bf16[2,128,1024]{2,1,0:T(8,128)(2,1)S(1)}, u32[]{:S(2)}, u32[]{:S(2)}) collective-permute-start(bf16[2,128,1024]{2,1,0:T(8,128)(2,1)} %collective-permute-done.22.refs_3_.refs_2_), channel_id=1, source_target_pairs={{0,2},{1,3},{2,0},{3,1},{4,6},{5,7},{6,4},{7,5},{8,10},{9,11},{10,... | collective-permute-start | bytes 1572872 | tf_op jit(solution)/shard_map/ppermute | solution.py:430
  157.1 22.0 %collective-permute-start.35 = (bf16[2,128,1024]{2,1,0:T(8,128)(2,1)S(1)}, bf16[2,128,1024]{2,1,0:T(8,128)(2,1)S(1)}, u32[]{:S(2)}, u32[]{:S(2)}) collective-permute-start(bf16[2,128,1024]{2,1,0:T(8,128)(2,1)S(1)} %broadcast_select_fusion.2.refs_2_), channel_id=1, source_target_pairs={{0,2},{1,3},{2,0},{3,1},{4,6},{5,7},{6,4},{7,5},{8,10},{9,11},{10,... | collective-permute-start | bytes 1572872 | tf_op jit(solution)/shard_map/ppermute | solution.py:430
  158.4 20.6 %collective-permute-start.36 = (bf16[2,128,1024]{2,1,0:T(8,128)(2,1)}, bf16[2,128,1024]{2,1,0:T(8,128)(2,1)S(1)}, u32[]{:S(2)}, u32[]{:S(2)}) collective-permute-start(bf16[2,128,1024]{2,1,0:T(8,128)(2,1)} %collective-permute-done.32), channel_id=1, source_target_pairs={{4,0},{5,1},{6,2},{7,3},{8,12},{9,13},{10,14},{11,15},{20,16},{21,... | collective-permute-start | bytes 1572872 | tf_op jit(solution)/shard_map/ppermute | solution.py:434
  159.7 3.4 %copy-start.3 = (f32[2,128,8192]{2,1,0:T(8,128)S(1)}, f32[2,128,8192]{2,1,0:T(8,128)}, u32[]{:S(2)}) copy-start(f32[2,128,8192]{2,1,0:T(8,128)} %refs_0_.1) | copy-start | bytes 25165828
  169.0 21.2 %collective-permute-start.29 = (bf16[2,128,1024]{2,1,0:T(8,128)(2,1)S(1)}, bf16[2,128,1024]{2,1,0:T(8,128)(2,1)S(1)}, u32[]{:S(2)}, u32[]{:S(2)}) collective-permute-start(bf16[2,128,1024]{2,1,0:T(8,128)(2,1)S(1)} %broadcast_select_fusion.3.refs_1_), channel_id=1, source_target_pairs={{0,2},{1,3},{2,0},{3,1},{4,6},{5,7},{6,4},{7,5},{8,10},{9,11},{10,... | collective-permute-start | bytes 1572872 | tf_op jit(solution)/shard_map/ppermute | solution.py:430
  169.3 21.0 %collective-permute-start.30 = (bf16[2,128,1024]{2,1,0:T(8,128)(2,1)S(1)}, bf16[2,128,1024]{2,1,0:T(8,128)(2,1)S(1)}, u32[]{:S(2)}, u32[]{:S(2)}) collective-permute-start(bf16[2,128,1024]{2,1,0:T(8,128)(2,1)S(1)} %collective-permute-done.24), channel_id=1, source_target_pairs={{4,0},{5,1},{6,2},{7,3},{8,12},{9,13},{10,14},{11,15},{20,16},{21,... | collective-permute-start | bytes 1572872 | tf_op jit(solution)/shard_map/ppermute | solution.py:434
  180.1 21.4 %collective-permute-start.37 = (bf16[2,128,1024]{2,1,0:T(8,128)(2,1)S(1)}, bf16[2,128,1024]{2,1,0:T(8,128)(2,1)S(1)}, u32[]{:S(2)}, u32[]{:S(2)}) collective-permute-start(bf16[2,128,1024]{2,1,0:T(8,128)(2,1)S(1)} %broadcast_select_fusion.refs_6_.refs_2_), channel_id=1, source_target_pairs={{0,2},{1,3},{2,0},{3,1},{4,6},{5,7},{6,4},{7,5},{8,10},{9,11},{10,... | collective-permute-start | bytes 1572872 | tf_op jit(solution)/shard_map/ppermute | solution.py:430
  203.9 19.4 %collective-permute-start.39 = (bf16[2,128,4096]{2,1,0:T(8,128)(2,1)S(1)}, bf16[2,128,4096]{2,1,0:T(8,128)(2,1)S(1)}, u32[]{:S(2)}, u32[]{:S(2)}) collective-permute-start(bf16[2,128,4096]{2,1,0:T(8,128)(2,1)S(1)} %get-tuple-element.133), channel_id=1, source_target_pairs={{0,1},{1,0},{2,3},{3,2},{4,5},{5,4},{6,7},{7,6},{8,9},{9,8},{10,11... | collective-permute-start | bytes 6291464 | tf_op jit(solution)/shard_map/ppermute | solution.py:427
  207.3 16.0 %collective-permute-start.40 = (bf16[2,128,4096]{2,1,0:T(8,128)(2,1)S(1)}, bf16[2,128,4096]{2,1,0:T(8,128)(2,1)S(1)}, u32[]{:S(2)}, u32[]{:S(2)}) collective-permute-start(bf16[2,128,4096]{2,1,0:T(8,128)(2,1)S(1)} %get-tuple-element.134), channel_id=1, source_target_pairs={{0,1},{1,0},{2,3},{3,2},{4,5},{5,4},{6,7},{7,6},{8,9},{9,8},{10,11... | collective-permute-start | bytes 6291464 | tf_op jit(solution)/shard_map/ppermute | solution.py:427
  207.3 13.1 %collective-permute-start.34 = (bf16[2,128,1024]{2,1,0:T(8,128)(2,1)S(1)}, bf16[2,128,1024]{2,1,0:T(8,128)(2,1)S(1)}, u32[]{:S(2)}, u32[]{:S(2)}) collective-permute-start(bf16[2,128,1024]{2,1,0:T(8,128)(2,1)S(1)} %broadcast_select_fusion.1.refs_5_.refs_1_), channel_id=1, source_target_pairs={{0,2},{1,3},{2,0},{3,1},{4,6},{5,7},{6,4},{7,5},{8,10},{9,11},{10,... | collective-permute-start | bytes 1572872 | tf_op jit(solution)/shard_map/ppermute | solution.py:430
  207.6 12.9 %collective-permute-start.38 = (bf16[2,128,1024]{2,1,0:T(8,128)(2,1)S(1)}, bf16[2,128,1024]{2,1,0:T(8,128)(2,1)S(1)}, u32[]{:S(2)}, u32[]{:S(2)}) collective-permute-start(bf16[2,128,1024]{2,1,0:T(8,128)(2,1)S(1)} %collective-permute-done.37.refs_4_), channel_id=1, source_target_pairs={{0,1},{1,0},{2,3},{3,2},{4,5},{5,4},{6,7},{7,6},{8,9},{9,8},{10,11... | collective-permute-start | bytes 1572872 | tf_op jit(solution)/shard_map/ppermute | solution.py:427
  220.4 2.8 %collective-permute-start.41 = (bf16[2,128,1024]{2,1,0:T(8,128)(2,1)S(1)}, bf16[2,128,1024]{2,1,0:T(8,128)(2,1)S(1)}, u32[]{:S(2)}, u32[]{:S(2)}) collective-permute-start(bf16[2,128,1024]{2,1,0:T(8,128)(2,1)S(1)} %collective-permute-done.34.refs_3_), channel_id=1, source_target_pairs={{0,1},{1,0},{2,3},{3,2},{4,5},{5,4},{6,7},{7,6},{8,9},{9,8},{10,11... | collective-permute-start | bytes 1572872 | tf_op jit(solution)/shard_map/ppermute | solution.py:427

commit v7 on v6

--- a/solution.py
+++ b/solution.py
@@ -535,15 +535,14 @@
         from_far = jnp.where(at_ends, pieces["far outward", stream], pieces["far inner", stream])
         pieces[("far", 0), stream] = from_far
         pieces[("far", 2), stream] = across(from_far)
-    slab, pieces[("far", 2), lead] = together((pieces["slab", last], pieces[("far", 2), lead]))
-    slab = [sibling(chunk) for chunk in apply([slab], late, 2)]
+    chunks = apply([pieces["slab", last]], late, 4)
+    slab = [sibling(chunk) for chunk in chunks]
     result = apply([pieces["result", last]], later + late)
+    arriving, result, slab[0], slab[1] = together(
+        (pieces[("far", 2), last], result, slab[0], slab[1])
+    )
+    pieces[("far", 2), last] = arriving
     for stream in (lead, last):
-        if stream == last:
-            arriving, result, twin = together(
-                (pieces[("far", 2), stream], result, pieces[("far", 3), lead])
-            )
-            pieces[("far", 2), stream], pieces[("far", 3), lead] = arriving, twin
         pieces[("far", 3), stream] = sibling(pieces[("far", 2), stream])
     return apply([result] + slab, [("far", 2), ("far", 3)])
 

time: 230 us -> 234 us (1.017)
  the two profiles are of different devices: /device:TPU:11 before, /device:TPU:16 now
where the time goes in v7:
time: 234 us; the launch traced here: 232 us
  waiting for transfers between devices  95.6 us (41%)
  Pallas kernels  57.3 us (24%)
  starting transfers between devices  55.5 us (24%)
  local copies, waits for them, and re-layouts  15.6 us (7%)
  other arithmetic  7.78 us (3%)
    ppermute x16, waiting for transfers between devices, across(): return lax.ppermute(value, 'ty', [(i, i ^ 2) for i in range(count)])  63.8 us
    ppermute x20, starting transfers between devices, along(): return lax.ppermute(value, 'ty', pairs)  37.8 us
    ppermute x20, waiting for transfers between devices, along(): return lax.ppermute(value, 'ty', pairs)  28.9 us
    pallas_call x6, Pallas kernels, backward(): pl.pallas_call(functools.partial(kernel, slots=slots, held=held, parts=le...  25.6 us
    pallas_call x3, Pallas kernels, forward(): pl.pallas_call(functools.partial(forward_kernel, base=base, images=images...  23.1 us
    ppermute x16, starting transfers between devices, across(): return lax.ppermute(value, 'ty', [(i, i ^ 2) for i in range(count)])  15.9 us
    unnamed x40, local copies, waits for them, and re-layouts  15 us
    pallas_call x1, Pallas kernels, middle(): pl.pallas_call(functools.partial(middle_kernel, terms=len(streams[0]), st...  4.83 us
  transfers between devices with their start and end apart: 44, of which 26 were waited for; matrix products, arithmetic and copies ran while one was open for 3% of the time, Pallas kernels for 18%

profile of v7, /device:TPU:16, one launch (start us, length us, event | category | flops | bytes accessed | tf_op | source)
XLA Modules:
  0.0 232.4 jit_solution(1185418798837792495)
XLA Ops:
  0.0 3.4 %copy-done.2 = f32[2,128,8192]{2,1,0:T(8,128)S(1)} copy-done((f32[2,128,8192]{2,1,0:T(8,128)S(1)}, f32[2,128,8192]{2,1,0:T(8,128)}, u32[]{:S(2)}) %copy-start.2) | copy-done | bytes 8388632
  3.4 1.8 low_part.2.refs_0_
  5.4 1.9 low_part.3.refs_1_
  8.8 3.3 %forward.3.refs_2_ = bf16[2,256,1024]{2,1,0:T(8,128)(2,1)S(1)} custom-call(s32[3,16]{1,0:T(4,128)S(1)} %pad_add_fusion.meta_ref, bf16[1024,1024]{1,0:T(8,128)(2,1)S(1)} %copy-done, bf16[1024,512]{1,0:T(8,128)(2,1)S(1)} %copy-done.1, bf16[128,8192]{1,0:T(8,128)(2,1)} %low_part.2.refs_0_, bf16[128,8192]{1,0:T(8,128)(2,1)} %low_part.3.refs_1_), custom_call_target="tpu_custom_call" | custom-call | flops 1024 | bytes 1024 | tf_op jit(solution)/shard_map/forward/pallas_call | solution.py:257
  12.9 3.3 %forward.4 = (bf16[2,128,1024]{2,1,0:T(8,128)(2,1)S(1)}, bf16[2,128,1024]{2,1,0:T(8,128)(2,1)S(1)}) custom-call(s32[3,16]{1,0:T(4,128)S(1)} %pad_add_fusion.meta_ref, bf16[1024,1024]{1,0:T(8,128)(2,1)S(1)} %copy-done, bf16[1024,512]{1,0:T(8,128)(2,1)S(1)} %copy-done.1, bf16[128,8192]{1,0:T(8,128)(2,1)} %collective-permute-done.refs_0_.refs_2_, ...), custom_call_target="tpu_custom_call" | custom-call | flops 1024 | bytes 1024 | tf_op jit(solution)/shard_map/forward/pallas_call | solution.py:257
  16.2 1.6 collective-permute-start.2
  18.3 16.5 %forward.5 = (bf16[2,128,1024]{2,1,0:T(8,128)(2,1)S(1)}, bf16[2,128,1024]{2,1,0:T(8,128)(2,1)S(1)}, bf16[2,128,1024]{2,1,0:T(8,128)(2,1)S(1)}, bf16[2,128,1024]{...) custom-call(s32[3,16]{1,0:T(4,128)S(1)} %pad_add_fusion.meta_ref, ...), custom_call_target="tpu_custom_call" | custom-call | flops 1024 | bytes 1024 | tf_op jit(solution)/shard_map/forward/pallas_call | solution.py:257
  35.0 1.3 collective-permute-start.3
  36.3 5.9 %collective-permute-done.11 = bf16[2,128,1024]{2,1,0:T(8,128)(2,1)S(1)} collective-permute-done((bf16[2,128,1024]{2,1,0:T(8,128)(2,1)S(1)}, bf16[2,128,1024]{2,1,0:T(8,128)(2,1)S(1)}, u32[]{:S(2)}, u32[]{:S(2)}) %collective-permute-start.11) | collective-permute-done | bytes 524320 | tf_op jit(solution)/shard_map/ppermute | solution.py:430
  42.5 1.3 collective-permute-start.12
  43.8 1.6 collective-permute-start.13
  45.4 5.7 %collective-permute-done.3 = bf16[2,128,1024]{2,1,0:T(8,128)(2,1)S(1)} collective-permute-done((bf16[2,128,1024]{2,1,0:T(8,128)(2,1)S(1)}, bf16[2,128,1024]{2,1,0:T(8,128)(2,1)S(1)}, u32[]{:S(2)}, u32[]{:S(2)}) %collective-permute-start.3) | collective-permute-done | bytes 524320 | tf_op jit(solution)/shard_map/ppermute | solution.py:434
  51.1 2.4 %collective-permute-done.4 = bf16[2,128,1024]{2,1,0:T(8,128)(2,1)S(1)} collective-permute-done((bf16[2,128,1024]{2,1,0:T(8,128)(2,1)S(1)}, bf16[2,128,1024]{2,1,0:T(8,128)(2,1)S(1)}, u32[]{:S(2)}, u32[]{:S(2)}) %collective-permute-start.4) | collective-permute-done | bytes 524320 | tf_op jit(solution)/shard_map/ppermute | solution.py:430
  53.7 1.3 collective-permute-start.6
  55.3 2.4 %collective-permute-start.5 = (bf16[2,128,1024]{2,1,0:T(8,128)(2,1)S(1)}, bf16[2,128,1024]{2,1,0:T(8,128)(2,1)S(1)}, u32[]{:S(2)}, u32[]{:S(2)}) collective-permute-start(bf16[2,128,1024]{2,1,0:T(8,128)(2,1)S(1)} %add_convert_fusion.7), channel_id=1, source_target_pairs={{4,8},{5,9},{6,10},{7,11},{8,4},{9,5},{10,6},{11,7},{20,24},{21,25... | collective-permute-start | bytes 1572872 | tf_op jit(solution)/shard_map/ppermute | solution.py:434
  57.7 1.8 collective-permute-start.7
  59.5 2.8 %collective-permute-done.12 = bf16[2,128,1024]{2,1,0:T(8,128)(2,1)S(1)} collective-permute-done((bf16[2,128,1024]{2,1,0:T(8,128)(2,1)S(1)}, bf16[2,128,1024]{2,1,0:T(8,128)(2,1)S(1)}, u32[]{:S(2)}, u32[]{:S(2)}) %collective-permute-start.12) | collective-permute-done | bytes 524320 | tf_op jit(solution)/shard_map/ppermute | solution.py:434
  62.3 2.4 %collective-permute-done.13 = bf16[2,128,1024]{2,1,0:T(8,128)(2,1)S(1)} collective-permute-done((bf16[2,128,1024]{2,1,0:T(8,128)(2,1)S(1)}, bf16[2,128,1024]{2,1,0:T(8,128)(2,1)S(1)}, u32[]{:S(2)}, u32[]{:S(2)}) %collective-permute-start.13) | collective-permute-done | bytes 524320 | tf_op jit(solution)/shard_map/ppermute | solution.py:430
  64.9 1.3 collective-permute-start.15
  66.5 2.4 %collective-permute-start.14 = (bf16[2,128,1024]{2,1,0:T(8,128)(2,1)S(1)}, bf16[2,128,1024]{2,1,0:T(8,128)(2,1)S(1)}, u32[]{:S(2)}, u32[]{:S(2)}) collective-permute-start(bf16[2,128,1024]{2,1,0:T(8,128)(2,1)S(1)} %add_convert_fusion.3), channel_id=1, source_target_pairs={{4,8},{5,9},{6,10},{7,11},{8,4},{9,5},{10,6},{11,7},{20,24},{21,25... | collective-permute-start | bytes 1572872 | tf_op jit(solution)/shard_map/ppermute | solution.py:434
  68.9 4.6 %collective-permute-done.6 = bf16[2,128,1024]{2,1,0:T(8,128)(2,1)S(1)} collective-permute-done((bf16[2,128,1024]{2,1,0:T(8,128)(2,1)S(1)}, bf16[2,128,1024]{2,1,0:T(8,128)(2,1)S(1)}, u32[]{:S(2)}, u32[]{:S(2)}) %collective-permute-start.6) | collective-permute-done | bytes 524320 | tf_op jit(solution)/shard_map/ppermute | solution.py:434
  73.7 1.5 collective-permute-done.7
  75.4 4.9 %collective-permute-start.9 = (bf16[2,128,1024]{2,1,0:T(8,128)(2,1)S(1)}, bf16[2,128,1024]{2,1,0:T(8,128)(2,1)S(1)}, u32[]{:S(2)}, u32[]{:S(2)}) collective-permute-start(bf16[2,128,1024]{2,1,0:T(8,128)(2,1)S(1)} %add_convert_fusion.6), channel_id=1, source_target_pairs={{4,8},{5,9},{6,10},{7,11},{8,4},{9,5},{10,6},{11,7},{20,24},{21,25... | collective-permute-start | bytes 1572872 | tf_op jit(solution)/shard_map/ppermute | solution.py:434
  80.7 4.1 %collective-permute-done.15 = bf16[2,128,1024]{2,1,0:T(8,128)(2,1)S(1)} collective-permute-done((bf16[2,128,1024]{2,1,0:T(8,128)(2,1)S(1)}, bf16[2,128,1024]{2,1,0:T(8,128)(2,1)S(1)}, u32[]{:S(2)}, u32[]{:S(2)}) %collective-permute-start.15) | collective-permute-done | bytes 524320 | tf_op jit(solution)/shard_map/ppermute | solution.py:434
  84.9 3.1 %collective-permute-done.16 = bf16[2,128,1024]{2,1,0:T(8,128)(2,1)S(1)} collective-permute-done((bf16[2,128,1024]{2,1,0:T(8,128)(2,1)S(1)}, bf16[2,128,1024]{2,1,0:T(8,128)(2,1)S(1)}, u32[]{:S(2)}, u32[]{:S(2)}) %collective-permute-start.16) | collective-permute-done | bytes 524320 | tf_op jit(solution)/shard_map/ppermute | solution.py:430
  88.3 2.5 %collective-permute-start.18 = (bf16[2,128,1024]{2,1,0:T(8,128)(2,1)S(1)}, bf16[2,128,1024]{2,1,0:T(8,128)(2,1)S(1)}, u32[]{:S(2)}, u32[]{:S(2)}) collective-permute-start(bf16[2,128,1024]{2,1,0:T(8,128)(2,1)S(1)} %add_convert_fusion.2), channel_id=1, source_target_pairs={{4,8},{5,9},{6,10},{7,11},{8,4},{9,5},{10,6},{11,7},{20,24},{21,25... | collective-permute-start | bytes 1572872 | tf_op jit(solution)/shard_map/ppermute | solution.py:434
  91.1 1.2 collective-permute-done.9
  92.3 1.2 collective-permute-start.17
  93.5 2.5 %collective-permute-done.10 = bf16[2,128,1024]{2,1,0:T(8,128)(2,1)S(1)} collective-permute-done((bf16[2,128,1024]{2,1,0:T(8,128)(2,1)S(1)}, bf16[2,128,1024]{2,1,0:T(8,128)(2,1)S(1)}, u32[]{:S(2)}, u32[]{:S(2)}) %collective-permute-start.10) | collective-permute-done | bytes 524320 | tf_op jit(solution)/shard_map/ppermute | solution.py:434
  96.0 3.3 %collective-permute-done.8 = bf16[2,128,1024]{2,1,0:T(8,128)(2,1)S(1)} collective-permute-done((bf16[2,128,1024]{2,1,0:T(8,128)(2,1)S(1)}, bf16[2,128,1024]{2,1,0:T(8,128)(2,1)S(1)}, u32[]{:S(2)}, u32[]{:S(2)}) %collective-permute-start.8) | collective-permute-done | bytes 524320 | tf_op jit(solution)/shard_map/ppermute | solution.py:430
  99.6 4.8 %collective-permute-done.18 = bf16[2,128,1024]{2,1,0:T(8,128)(2,1)S(1)} collective-permute-done((bf16[2,128,1024]{2,1,0:T(8,128)(2,1)S(1)}, bf16[2,128,1024]{2,1,0:T(8,128)(2,1)S(1)}, u32[]{:S(2)}, u32[]{:S(2)}) %collective-permute-start.18) | collective-permute-done | bytes 524320 | tf_op jit(solution)/shard_map/ppermute | solution.py:434
  104.5 2.8 %collective-permute-done.19 = bf16[2,128,1024]{2,1,0:T(8,128)(2,1)S(1)} collective-permute-done((bf16[2,128,1024]{2,1,0:T(8,128)(2,1)S(1)}, bf16[2,128,1024]{2,1,0:T(8,128)(2,1)S(1)}, u32[]{:S(2)}, u32[]{:S(2)}) %collective-permute-start.19) | collective-permute-done | bytes 524320 | tf_op jit(solution)/shard_map/ppermute | solution.py:434
  107.2 3.3 %collective-permute-done.17 = bf16[2,128,1024]{2,1,0:T(8,128)(2,1)S(1)} collective-permute-done((bf16[2,128,1024]{2,1,0:T(8,128)(2,1)S(1)}, bf16[2,128,1024]{2,1,0:T(8,128)(2,1)S(1)}, u32[]{:S(2)}, u32[]{:S(2)}) %collective-permute-start.17) | collective-permute-done | bytes 524320 | tf_op jit(solution)/shard_map/ppermute | solution.py:430
  110.9 4.8 %middle.1 = (bf16[2,128,1024]{2,1,0:T(8,128)(2,1)S(1)}, bf16[2,128,1024]{2,1,0:T(8,128)(2,1)S(1)}) custom-call(bf16[2,128,1024]{2,1,0:T(8,128)(2,1)S(1)} %add_convert_fusion.refs_0_, bf16[2,128,1024]{2,1,0:T(8,128)(2,1)S(1)} %add_convert_fusion.4.refs_1_, bf16[1,256,1024]{2,1,0:T(8,128)(2,1)S(1)} %copy-done.17, bf16[1024,1024]{1,0:T(8,128)(2,1)S(1)} %copy-done.15, ...), custom_call_target="tpu_custom_call" | custom-call | flops 1024 | bytes 1024 | tf_op jit(solution)/shard_map/middle/pallas_call | solution.py:295
  115.8 2.2 collective-permute-start.27
  118.9 1.7 collective-permute-start.20
  120.6 3.9 %collective-permute-start.21 = (bf16[2,128,1024]{2,1,0:T(8,128)(2,1)S(1)}, bf16[2,128,1024]{2,1,0:T(8,128)(2,1)}, u32[]{:S(2)}, u32[]{:S(2)}) collective-permute-start(bf16[2,128,1024]{2,1,0:T(8,128)(2,1)S(1)} %get-tuple-element.110.refs_1_.refs_0_), channel_id=1, source_target_pairs={{4,8},{5,9},{6,10},{7,11},{8,4},{9,5},{10,6},{11,7},{20,24},{21,25... | collective-permute-start | bytes 1572872 | tf_op jit(solution)/shard_map/ppermute | solution.py:434
  124.6 6.0 %collective-permute-done.26.refs_6_.refs_5_ = bf16[2,128,1024]{2,1,0:T(8,128)(2,1)S(1)} collective-permute-done((bf16[2,128,1024]{2,1,0:T(8,128)(2,1)S(1)}, bf16[2,128,1024]{2,1,0:T(8,128)(2,1)S(1)}, u32[]{:S(2)}, u32[]{:S(2)}) %collective-permute-start.26) | collective-permute-done | bytes 524320 | tf_op jit(solution)/shard_map/ppermute | solution.py:430
  132.6 2.0 collective-permute-start.31
  134.6 4.0 %collective-permute-start.32 = (bf16[2,128,1024]{2,1,0:T(8,128)(2,1)}, bf16[2,128,1024]{2,1,0:T(8,128)(2,1)}, u32[]{:S(2)}, u32[]{:S(2)}) collective-permute-start(bf16[2,128,1024]{2,1,0:T(8,128)(2,1)} %collective-permute-done.28.refs_4_.refs_3_), channel_id=1, source_target_pairs={{4,8},{5,9},{6,10},{7,11},{8,4},{9,5},{10,6},{11,7},{20,24},{21,25... | collective-permute-start | bytes 1572872 | tf_op jit(solution)/shard_map/ppermute | solution.py:434
  138.7 3.1 %collective-permute-done.20.refs_5_.refs_4_ = bf16[2,128,1024]{2,1,0:T(8,128)(2,1)S(1)} collective-permute-done((bf16[2,128,1024]{2,1,0:T(8,128)(2,1)S(1)}, bf16[2,128,1024]{2,1,0:T(8,128)(2,1)S(1)}, u32[]{:S(2)}, u32[]{:S(2)}) %collective-permute-start.20) | collective-permute-done | bytes 524320 | tf_op jit(solution)/shard_map/ppermute | solution.py:430
  142.6 2.4 %collective-permute-start.33 = (bf16[2,128,1024]{2,1,0:T(8,128)(2,1)}, bf16[2,128,1024]{2,1,0:T(8,128)(2,1)}, u32[]{:S(2)}, u32[]{:S(2)}) collective-permute-start(bf16[2,128,1024]{2,1,0:T(8,128)(2,1)} %collective-permute-done.27), channel_id=1, source_target_pairs={{4,0},{5,1},{6,2},{7,3},{8,12},{9,13},{10,14},{11,15},{20,16},{21,... | collective-permute-start | bytes 1572872 | tf_op jit(solution)/shard_map/ppermute | solution.py:434
  145.9 2.6 %collective-permute-start.24 = (bf16[2,128,1024]{2,1,0:T(8,128)(2,1)}, bf16[2,128,1024]{2,1,0:T(8,128)(2,1)}, u32[]{:S(2)}, u32[]{:S(2)}) collective-permute-start(bf16[2,128,1024]{2,1,0:T(8,128)(2,1)} %collective-permute-done.22.refs_3_.refs_2_), channel_id=1, source_target_pairs={{4,8},{5,9},{6,10},{7,11},{8,4},{9,5},{10,6},{11,7},{20,24},{21,25... | collective-permute-start | bytes 1572872 | tf_op jit(solution)/shard_map/ppermute | solution.py:434
  148.5 4.6 %collective-permute-done.31.refs_4_ = bf16[2,128,1024]{2,1,0:T(8,128)(2,1)S(1)} collective-permute-done((bf16[2,128,1024]{2,1,0:T(8,128)(2,1)}, bf16[2,128,1024]{2,1,0:T(8,128)(2,1)S(1)}, u32[]{:S(2)}, u32[]{:S(2)}) %collective-permute-start.31) | collective-permute-done | bytes 524320 | tf_op jit(solution)/shard_map/ppermute | solution.py:430
  153.8 2.5 %collective-permute-start.25 = (bf16[2,128,1024]{2,1,0:T(8,128)(2,1)}, bf16[2,128,1024]{2,1,0:T(8,128)(2,1)}, u32[]{:S(2)}, u32[]{:S(2)}) collective-permute-start(bf16[2,128,1024]{2,1,0:T(8,128)(2,1)} %collective-permute-done.21), channel_id=1, source_target_pairs={{4,0},{5,1},{6,2},{7,3},{8,12},{9,13},{10,14},{11,15},{20,16},{21,... | collective-permute-start | bytes 1572872 | tf_op jit(solution)/shard_map/ppermute | solution.py:434
  160.5 3.9 %backward.7.refs_0_ = bf16[2,128,8192]{2,1,0:T(8,128)(2,1)S(1)} custom-call(s32[3,16]{1,0:T(4,128)S(1)} %pad_add_fusion.meta_ref, bf16[1024,1024]{1,0:T(8,128)(2,1)S(1)} %copy-done, bf16[1024,512]{1,0:T(8,128)(2,1)S(1)} %copy-done.1, bf16[2,128,1024]{2,1,0:T(8,128)(2,1)S(1)} %copy-done.7, bf16[2,128,1024]{2,1,0:T(8,128)(2,1)S(1)} %copy-done.9, ...), custom_call_target="tpu_custom_call" | custom-call | flops 1024 | bytes 1024 | tf_op jit(solution)/shard_map/backward/pallas_call | solution.py:279
  164.4 3.4 %copy-done.3 = f32[2,128,8192]{2,1,0:T(8,128)S(1)} copy-done((f32[2,128,8192]{2,1,0:T(8,128)S(1)}, f32[2,128,8192]{2,1,0:T(8,128)}, u32[]{:S(2)}) %copy-start.3) | copy-done | bytes 8388632
  167.8 3.6 %backward.6.refs_0_ = f32[2,128,8192]{2,1,0:T(8,128)S(1)} custom-call(s32[3,16]{1,0:T(4,128)S(1)} %pad_add_fusion.meta_ref, bf16[1024,1024]{1,0:T(8,128)(2,1)S(1)} %copy-done, bf16[1024,512]{1,0:T(8,128)(2,1)S(1)} %copy-done.1, f32[2,128,8192]{2,1,0:T(8,128)S(1)} %copy-done.3, bf16[2,128,1024]{2,1,0:T(8,128)(2,1)S(1)} %copy-done.7, ...), custom_call_target="tpu_custom_call" | custom-call | flops 1024 | bytes 1024 | tf_op jit(solution)/shard_map/backward/pallas_call | solution.py:279
  171.4 1.2 broadcast_select_fusion.2.refs_2_
  172.7 1.3 collective-permute-start.36
  174.0 1.1 broadcast_select_fusion.3.refs_1_
  175.1 2.1 collective-permute-start.29
  177.2 1.3 collective-permute-start.30
  178.5 3.7 %backward.8.refs_0_ = bf16[2,128,8192]{2,1,0:T(8,128)(2,1)S(1)} custom-call(s32[3,16]{1,0:T(4,128)S(1)} %pad_add_fusion.meta_ref, bf16[1024,1024]{1,0:T(8,128)(2,1)S(1)} %copy-done, bf16[1024,512]{1,0:T(8,128)(2,1)S(1)} %copy-done.1, bf16[2,128,8192]{2,1,0:T(8,128)(2,1)S(1)} %backward.7.refs_0_, bf16[2,128,1024]{2,1,0:T(8,128)(2,1)S(1)} %broadcast_select_fusion.3.refs_1_, ...), custom_call_target="tpu_custom_call" | custom-call | flops 1024 | bytes 1024 | tf_op jit(solution)/shard_map/backward/pallas_call | solution.py:279
  182.2 5.2 %collective-permute-done.35.refs_8_.refs_4_ = bf16[2,128,1024]{2,1,0:T(8,128)(2,1)S(1)} collective-permute-done((bf16[2,128,1024]{2,1,0:T(8,128)(2,1)S(1)}, bf16[2,128,1024]{2,1,0:T(8,128)(2,1)S(1)}, u32[]{:S(2)}, u32[]{:S(2)}) %collective-permute-start.35) | collective-permute-done | bytes 524320 | tf_op jit(solution)/shard_map/ppermute | solution.py:430
  187.5 1.1 broadcast_select_fusion.refs_6_.refs_2_
  188.6 9.1 %collective-permute-done.29.refs_7_.refs_3_ = bf16[2,128,1024]{2,1,0:T(8,128)(2,1)S(1)} collective-permute-done((bf16[2,128,1024]{2,1,0:T(8,128)(2,1)S(1)}, bf16[2,128,1024]{2,1,0:T(8,128)(2,1)S(1)}, u32[]{:S(2)}, u32[]{:S(2)}) %collective-permute-start.29) | collective-permute-done | bytes 524320 | tf_op jit(solution)/shard_map/ppermute | solution.py:430
  198.8 1.2 collective-permute-start.34
  200.0 3.2 %backward.10 = (bf16[2,128,2048]{2,1,0:T(8,128)(2,1)S(1)}, bf16[2,128,2048]{2,1,0:T(8,128)(2,1)S(1)}, bf16[2,128,2048]{2,1,0:T(8,128)(2,1)S(1)}, bf16[2,128,2048]{2,1,0:T(8,128)(2,1)S(1)}) custom-call(s32[3,16]{1,0:T(4,128)S(1)} %pad_add_fusion.meta_ref, bf16[1024,1024]{1,0:T(8,128)(2,1)S(1)} %copy-done, bf16[1024,512]{1,0:T(8,128)(2,1)S(1)} %copy-done.1, ...), custom_call_target="tpu_custom_call" | custom-call | flops 1024 | bytes 1024 | tf_op jit(solution)/shard_map/backward/pallas_call | solution.py:279
  204.6 9.1 %collective-permute-done.34.refs_5_ = bf16[2,128,1024]{2,1,0:T(8,128)(2,1)S(1)} collective-permute-done((bf16[2,128,1024]{2,1,0:T(8,128)(2,1)S(1)}, bf16[2,128,1024]{2,1,0:T(8,128)(2,1)S(1)}, u32[]{:S(2)}, u32[]{:S(2)}) %collective-permute-start.34) | collective-permute-done | bytes 524320 | tf_op jit(solution)/shard_map/ppermute | solution.py:430
  213.7 5.0 %backward.9.refs_0_ = f32[2,128,8192]{2,1,0:T(8,128)S(1)} custom-call(s32[3,16]{1,0:T(4,128)S(1)} %pad_add_fusion.meta_ref, bf16[1024,1024]{1,0:T(8,128)(2,1)S(1)} %copy-done, bf16[1024,512]{1,0:T(8,128)(2,1)S(1)} %copy-done.1, f32[2,128,8192]{2,1,0:T(8,128)S(1)} %backward.6.refs_0_, bf16[2,128,1024]{2,1,0:T(8,128)(2,1)S(1)} %broadcast_select_fusion.3.refs_1_, ...), custom_call_target="tpu_custom_call" | custom-call | flops 1024 | bytes 1024 | tf_op jit(solution)/shard_map/backward/pallas_call | solution.py:279
  218.7 4.8 %collective-permute-done.41.refs_6_ = bf16[2,128,1024]{2,1,0:T(8,128)(2,1)S(1)} collective-permute-done((bf16[2,128,1024]{2,1,0:T(8,128)(2,1)S(1)}, bf16[2,128,1024]{2,1,0:T(8,128)(2,1)S(1)}, u32[]{:S(2)}, u32[]{:S(2)}) %collective-permute-start.41) | collective-permute-done | bytes 524320 | tf_op jit(solution)/shard_map/ppermute | solution.py:430
  223.9 1.4 collective-permute-done.43.refs_8_
  226.1 6.3 %backward.11 = f32[2,128,8192]{2,1,0:T(8,128)} custom-call(s32[3,16]{1,0:T(4,128)S(1)} %pad_add_fusion.meta_ref, bf16[1024,1024]{1,0:T(8,128)(2,1)S(1)} %copy-done, bf16[1024,512]{1,0:T(8,128)(2,1)S(1)} %copy-done.1, f32[2,128,8192]{2,1,0:T(8,128)S(1)} %backward.9.refs_0_, bf16[2,128,2048]{2,1,0:T(8,128)(2,1)S(1)} %collective-permute-done.37.refs_1_, ...), custom_call_target="tpu_custom_call" | custom-call | flops 1024 | bytes 1024 | tf_op jit(solution)/shard_map/backward/pallas_call | solution.py:279
  (97 shorter events, 19.9 us)
Async XLA Ops:
  0.0 3.4 %copy-start.2 = (f32[2,128,8192]{2,1,0:T(8,128)S(1)}, f32[2,128,8192]{2,1,0:T(8,128)}, u32[]{:S(2)}) copy-start(f32[2,128,8192]{2,1,0:T(8,128)} %refs_0_.1) | copy-start | bytes 25165828
  5.2 3.3 %copy-start.18 = (s32[16]{0:T(128)S(1)}, s32[16]{0:T(128)}, u32[]{:S(2)}) copy-start(s32[16]{0:T(128)} %param.12) | copy-start | bytes 196
  5.2 3.3 %copy-start.19 = (s32[16]{0:T(128)S(1)}, s32[16]{0:T(128)}, u32[]{:S(2)}) copy-start(s32[16]{0:T(128)} %param.13) | copy-start | bytes 196
  5.3 3.5 %copy-start = (bf16[1024,1024]{1,0:T(8,128)(2,1)S(1)}, bf16[1024,1024]{1,0:T(8,128)(2,1)}, u32[]{:S(2)}) copy-start(bf16[1024,1024]{1,0:T(8,128)(2,1)} %pupil_ref.17) | copy-start | bytes 6291460
  5.3 3.5 %copy-start.1 = (bf16[1024,512]{1,0:T(8,128)(2,1)S(1)}, bf16[1024,512]{1,0:T(8,128)(2,1)}, u32[]{:S(2)}) copy-start(bf16[1024,512]{1,0:T(8,128)(2,1)} %constant.42.clone.band_ref) | copy-start | bytes 3145732
  5.3 6.8 %collective-permute-start = (bf16[128,8192]{1,0:T(8,128)(2,1)}, bf16[128,8192]{1,0:T(8,128)(2,1)}, u32[]{:S(2)}, u32[]{:S(2)}) collective-permute-start(bf16[128,8192]{1,0:T(8,128)(2,1)} %low_part.2.refs_0_), channel_id=1, source_target_pairs={{0,1},{1,0},{2,3},{3,2},{4,5},{5,4},{6,7},{7,6},{8,9},{9,8},{10,11... | collective-permute-start | bytes 6291464 | tf_op jit(solution)/shard_map/ppermute | solution.py:427
  7.3 5.6 %collective-permute-start.1 = (bf16[128,8192]{1,0:T(8,128)(2,1)}, bf16[128,8192]{1,0:T(8,128)(2,1)}, u32[]{:S(2)}, u32[]{:S(2)}) collective-permute-start(bf16[128,8192]{1,0:T(8,128)(2,1)} %low_part.3.refs_1_), channel_id=1, source_target_pairs={{0,1},{1,0},{2,3},{3,2},{4,5},{5,4},{6,7},{7,6},{8,9},{9,8},{10,11... | collective-permute-start | bytes 6291464 | tf_op jit(solution)/shard_map/ppermute | solution.py:427
  16.2 18.6 %collective-permute-start.2 = (bf16[2,128,1024]{2,1,0:T(8,128)(2,1)S(1)}, bf16[2,128,1024]{2,1,0:T(8,128)(2,1)S(1)}, u32[]{:S(2)}, u32[]{:S(2)}) collective-permute-start(bf16[2,128,1024]{2,1,0:T(8,128)(2,1)S(1)} %get-tuple-element.76), channel_id=1, source_target_pairs={{0,2},{1,3},{2,0},{3,1},{4,6},{5,7},{6,4},{7,5},{8,10},{9,11},{10,... | collective-permute-start | bytes 1572872 | tf_op jit(solution)/shard_map/ppermute | solution.py:430
  17.8 24.5 %collective-permute-start.11 = (bf16[2,128,1024]{2,1,0:T(8,128)(2,1)S(1)}, bf16[2,128,1024]{2,1,0:T(8,128)(2,1)S(1)}, u32[]{:S(2)}, u32[]{:S(2)}) collective-permute-start(bf16[2,128,1024]{2,1,0:T(8,128)(2,1)S(1)} %get-tuple-element.72), channel_id=1, source_target_pairs={{0,2},{1,3},{2,0},{3,1},{4,6},{5,7},{6,4},{7,5},{8,10},{9,11},{10,... | collective-permute-start | bytes 1572872 | tf_op jit(solution)/shard_map/ppermute | solution.py:430
  35.0 16.1 %collective-permute-start.3 = (bf16[2,128,1024]{2,1,0:T(8,128)(2,1)S(1)}, bf16[2,128,1024]{2,1,0:T(8,128)(2,1)S(1)}, u32[]{:S(2)}, u32[]{:S(2)}) collective-permute-start(bf16[2,128,1024]{2,1,0:T(8,128)(2,1)S(1)} %fusion), channel_id=1, source_target_pairs={{0,4},{1,5},{2,6},{3,7},{12,8},{13,9},{14,10},{15,11},{16,20},{17,... | collective-permute-start | bytes 1572872 | tf_op jit(solution)/shard_map/ppermute | solution.py:434
  36.3 17.2 %collective-permute-start.4 = (bf16[2,128,1024]{2,1,0:T(8,128)(2,1)S(1)}, bf16[2,128,1024]{2,1,0:T(8,128)(2,1)S(1)}, u32[]{:S(2)}, u32[]{:S(2)}) collective-permute-start(bf16[2,128,1024]{2,1,0:T(8,128)(2,1)S(1)} %get-tuple-element.81), channel_id=1, source_target_pairs={{0,2},{1,3},{2,0},{3,1},{4,6},{5,7},{6,4},{7,5},{8,10},{9,11},{10,... | collective-permute-start | bytes 1572872 | tf_op jit(solution)/shard_map/ppermute | solution.py:430
  42.5 19.8 %collective-permute-start.12 = (bf16[2,128,1024]{2,1,0:T(8,128)(2,1)S(1)}, bf16[2,128,1024]{2,1,0:T(8,128)(2,1)S(1)}, u32[]{:S(2)}, u32[]{:S(2)}) collective-permute-start(bf16[2,128,1024]{2,1,0:T(8,128)(2,1)S(1)} %fusion.2), channel_id=1, source_target_pairs={{0,4},{1,5},{2,6},{3,7},{12,8},{13,9},{14,10},{15,11},{16,20},{17,... | collective-permute-start | bytes 1572872 | tf_op jit(solution)/shard_map/ppermute | solution.py:434
  43.8 21.0 %collective-permute-start.13 = (bf16[2,128,1024]{2,1,0:T(8,128)(2,1)S(1)}, bf16[2,128,1024]{2,1,0:T(8,128)(2,1)S(1)}, u32[]{:S(2)}, u32[]{:S(2)}) collective-permute-start(bf16[2,128,1024]{2,1,0:T(8,128)(2,1)S(1)} %get-tuple-element.98), channel_id=1, source_target_pairs={{0,2},{1,3},{2,0},{3,1},{4,6},{5,7},{6,4},{7,5},{8,10},{9,11},{10,... | collective-permute-start | bytes 1572872 | tf_op jit(solution)/shard_map/ppermute | solution.py:430
  53.7 19.8 %collective-permute-start.6 = (bf16[2,128,1024]{2,1,0:T(8,128)(2,1)S(1)}, bf16[2,128,1024]{2,1,0:T(8,128)(2,1)S(1)}, u32[]{:S(2)}, u32[]{:S(2)}) collective-permute-start(bf16[2,128,1024]{2,1,0:T(8,128)(2,1)S(1)} %fusion.1), channel_id=1, source_target_pairs={{0,4},{1,5},{2,6},{3,7},{12,8},{13,9},{14,10},{15,11},{16,20},{17,... | collective-permute-start | bytes 1572872 | tf_op jit(solution)/shard_map/ppermute | solution.py:434
  55.3 18.4 %collective-permute-start.5 = (bf16[2,128,1024]{2,1,0:T(8,128)(2,1)S(1)}, bf16[2,128,1024]{2,1,0:T(8,128)(2,1)S(1)}, u32[]{:S(2)}, u32[]{:S(2)}) collective-permute-start(bf16[2,128,1024]{2,1,0:T(8,128)(2,1)S(1)} %add_convert_fusion.7), channel_id=1, source_target_pairs={{4,8},{5,9},{6,10},{7,11},{8,4},{9,5},{10,6},{11,7},{20,24},{21,25... | collective-permute-start | bytes 1572872 | tf_op jit(solution)/shard_map/ppermute | solution.py:434
  57.7 17.5 %collective-permute-start.7 = (bf16[2,128,1024]{2,1,0:T(8,128)(2,1)S(1)}, bf16[2,128,1024]{2,1,0:T(8,128)(2,1)S(1)}, u32[]{:S(2)}, u32[]{:S(2)}) collective-permute-start(bf16[2,128,1024]{2,1,0:T(8,128)(2,1)S(1)} %get-tuple-element.86), channel_id=1, source_target_pairs={{0,2},{1,3},{2,0},{3,1},{4,6},{5,7},{6,4},{7,5},{8,10},{9,11},{10,... | collective-permute-start | bytes 1572872 | tf_op jit(solution)/shard_map/ppermute | solution.py:430
  64.9 19.8 %collective-permute-start.15 = (bf16[2,128,1024]{2,1,0:T(8,128)(2,1)S(1)}, bf16[2,128,1024]{2,1,0:T(8,128)(2,1)S(1)}, u32[]{:S(2)}, u32[]{:S(2)}) collective-permute-start(bf16[2,128,1024]{2,1,0:T(8,128)(2,1)S(1)} %fusion.3), channel_id=1, source_target_pairs={{0,4},{1,5},{2,6},{3,7},{12,8},{13,9},{14,10},{15,11},{16,20},{17,... | collective-permute-start | bytes 1572872 | tf_op jit(solution)/shard_map/ppermute | solution.py:434
  66.5 18.4 %collective-permute-start.14 = (bf16[2,128,1024]{2,1,0:T(8,128)(2,1)S(1)}, bf16[2,128,1024]{2,1,0:T(8,128)(2,1)S(1)}, u32[]{:S(2)}, u32[]{:S(2)}) collective-permute-start(bf16[2,128,1024]{2,1,0:T(8,128)(2,1)S(1)} %add_convert_fusion.3), channel_id=1, source_target_pairs={{4,8},{5,9},{6,10},{7,11},{8,4},{9,5},{10,6},{11,7},{20,24},{21,25... | collective-permute-start | bytes 1572872 | tf_op jit(solution)/shard_map/ppermute | solution.py:434
  73.5 14.5 %collective-permute-start.16 = (bf16[2,128,1024]{2,1,0:T(8,128)(2,1)S(1)}, bf16[2,128,1024]{2,1,0:T(8,128)(2,1)S(1)}, u32[]{:S(2)}, u32[]{:S(2)}) collective-permute-start(bf16[2,128,1024]{2,1,0:T(8,128)(2,1)S(1)} %get-tuple-element.103), channel_id=1, source_target_pairs={{0,2},{1,3},{2,0},{3,1},{4,6},{5,7},{6,4},{7,5},{8,10},{9,11},{10,... | collective-permute-start | bytes 1572872 | tf_op jit(solution)/shard_map/ppermute | solution.py:430
  75.4 16.9 %collective-permute-start.9 = (bf16[2,128,1024]{2,1,0:T(8,128)(2,1)S(1)}, bf16[2,128,1024]{2,1,0:T(8,128)(2,1)S(1)}, u32[]{:S(2)}, u32[]{:S(2)}) collective-permute-start(bf16[2,128,1024]{2,1,0:T(8,128)(2,1)S(1)} %add_convert_fusion.6), channel_id=1, source_target_pairs={{4,8},{5,9},{6,10},{7,11},{8,4},{9,5},{10,6},{11,7},{20,24},{21,25... | collective-permute-start | bytes 1572872 | tf_op jit(solution)/shard_map/ppermute | solution.py:434
  80.6 15.4 %collective-permute-start.10 = (bf16[2,128,1024]{2,1,0:T(8,128)(2,1)S(1)}, bf16[2,128,1024]{2,1,0:T(8,128)(2,1)S(1)}, u32[]{:S(2)}, u32[]{:S(2)}) collective-permute-start(bf16[2,128,1024]{2,1,0:T(8,128)(2,1)S(1)} %add_convert_fusion.5), channel_id=1, source_target_pairs={{0,4},{1,5},{2,6},{3,7},{12,8},{13,9},{14,10},{15,11},{4,0},{5,1},... | collective-permute-start | bytes 1572872 | tf_op jit(solution)/shard_map/ppermute | solution.py:434
  84.8 14.5 %collective-permute-start.8 = (bf16[2,128,1024]{2,1,0:T(8,128)(2,1)S(1)}, bf16[2,128,1024]{2,1,0:T(8,128)(2,1)S(1)}, u32[]{:S(2)}, u32[]{:S(2)}) collective-permute-start(bf16[2,128,1024]{2,1,0:T(8,128)(2,1)S(1)} %get-tuple-element.88), channel_id=1, source_target_pairs={{0,2},{1,3},{2,0},{3,1},{4,6},{5,7},{6,4},{7,5},{8,10},{9,11},{10,... | collective-permute-start | bytes 1572872 | tf_op jit(solution)/shard_map/ppermute | solution.py:430
  88.3 16.2 %collective-permute-start.18 = (bf16[2,128,1024]{2,1,0:T(8,128)(2,1)S(1)}, bf16[2,128,1024]{2,1,0:T(8,128)(2,1)S(1)}, u32[]{:S(2)}, u32[]{:S(2)}) collective-permute-start(bf16[2,128,1024]{2,1,0:T(8,128)(2,1)S(1)} %add_convert_fusion.2), channel_id=1, source_target_pairs={{4,8},{5,9},{6,10},{7,11},{8,4},{9,5},{10,6},{11,7},{20,24},{21,25... | collective-permute-start | bytes 1572872 | tf_op jit(solution)/shard_map/ppermute | solution.py:434
  91.0 16.2 %collective-permute-start.19 = (bf16[2,128,1024]{2,1,0:T(8,128)(2,1)S(1)}, bf16[2,128,1024]{2,1,0:T(8,128)(2,1)S(1)}, u32[]{:S(2)}, u32[]{:S(2)}) collective-permute-start(bf16[2,128,1024]{2,1,0:T(8,128)(2,1)S(1)} %add_convert_fusion.1), channel_id=1, source_target_pairs={{0,4},{1,5},{2,6},{3,7},{12,8},{13,9},{14,10},{15,11},{4,0},{5,1},... | collective-permute-start | bytes 1572872 | tf_op jit(solution)/shard_map/ppermute | solution.py:434
  92.3 18.2 %collective-permute-start.17 = (bf16[2,128,1024]{2,1,0:T(8,128)(2,1)S(1)}, bf16[2,128,1024]{2,1,0:T(8,128)(2,1)S(1)}, u32[]{:S(2)}, u32[]{:S(2)}) collective-permute-start(bf16[2,128,1024]{2,1,0:T(8,128)(2,1)S(1)} %get-tuple-element.105), channel_id=1, source_target_pairs={{0,2},{1,3},{2,0},{3,1},{4,6},{5,7},{6,4},{7,5},{8,10},{9,11},{10,... | collective-permute-start | bytes 1572872 | tf_op jit(solution)/shard_map/ppermute | solution.py:430
  99.3 11.6 %copy-start.15 = (bf16[1024,1024]{1,0:T(8,128)(2,1)S(1)}, bf16[1024,1024]{1,0:T(8,128)(2,1)}, u32[]{:S(2)}) copy-start(bf16[1024,1024]{1,0:T(8,128)(2,1)} %constant.43.clone.refs_3_) | copy-start | bytes 6291460
  99.3 11.6 %copy-start.16 = (bf16[1024,1024]{1,0:T(8,128)(2,1)S(1)}, bf16[1024,1024]{1,0:T(8,128)(2,1)}, u32[]{:S(2)}) copy-start(bf16[1024,1024]{1,0:T(8,128)(2,1)} %constant.44.clone.refs_4_) | copy-start | bytes 6291460
  99.3 11.6 %copy-start.17 = (bf16[1,256,1024]{2,1,0:T(8,128)(2,1)S(1)}, bf16[1,256,1024]{2,1,0:T(8,128)(2,1)}, u32[]{:S(2)}) copy-start(bf16[1,256,1024]{2,1,0:T(8,128)(2,1)} %refs_2_.1) | copy-start | bytes 1572868
  115.7 14.8 %collective-permute-start.26 = (bf16[2,128,1024]{2,1,0:T(8,128)(2,1)S(1)}, bf16[2,128,1024]{2,1,0:T(8,128)(2,1)S(1)}, u32[]{:S(2)}, u32[]{:S(2)}) collective-permute-start(bf16[2,128,1024]{2,1,0:T(8,128)(2,1)S(1)} %get-tuple-element.113.refs_2_.refs_1_), channel_id=1, source_target_pairs={{0,2},{1,3},{2,0},{3,1},{4,6},{5,7},{6,4},{7,5},{8,10},{9,11},{10,... | collective-permute-start | bytes 1572872 | tf_op jit(solution)/shard_map/ppermute | solution.py:430
  115.8 16.8 %collective-permute-start.27 = (bf16[2,128,1024]{2,1,0:T(8,128)(2,1)S(1)}, bf16[2,128,1024]{2,1,0:T(8,128)(2,1)}, u32[]{:S(2)}, u32[]{:S(2)}) collective-permute-start(bf16[2,128,1024]{2,1,0:T(8,128)(2,1)S(1)} %get-tuple-element.113.refs_2_.refs_1_), channel_id=1, source_target_pairs={{4,8},{5,9},{6,10},{7,11},{8,4},{9,5},{10,6},{11,7},{20,24},{21,25... | collective-permute-start | bytes 1572872 | tf_op jit(solution)/shard_map/ppermute | solution.py:434
  118.0 14.6 %collective-permute-start.28 = (bf16[2,128,1024]{2,1,0:T(8,128)(2,1)S(1)}, bf16[2,128,1024]{2,1,0:T(8,128)(2,1)}, u32[]{:S(2)}, u32[]{:S(2)}) collective-permute-start(bf16[2,128,1024]{2,1,0:T(8,128)(2,1)S(1)} %get-tuple-element.113.refs_2_.refs_1_), channel_id=1, source_target_pairs={{0,4},{1,5},{2,6},{3,7},{12,8},{13,9},{14,10},{15,11},{4,0},{5,1},... | collective-permute-start | bytes 1572872 | tf_op jit(solution)/shard_map/ppermute | solution.py:434
  118.1 0.8 copy-start.8
  118.9 22.9 %collective-permute-start.20 = (bf16[2,128,1024]{2,1,0:T(8,128)(2,1)S(1)}, bf16[2,128,1024]{2,1,0:T(8,128)(2,1)S(1)}, u32[]{:S(2)}, u32[]{:S(2)}) collective-permute-start(bf16[2,128,1024]{2,1,0:T(8,128)(2,1)S(1)} %get-tuple-element.110.refs_1_.refs_0_), channel_id=1, source_target_pairs={{0,2},{1,3},{2,0},{3,1},{4,6},{5,7},{6,4},{7,5},{8,10},{9,11},{10,... | collective-permute-start | bytes 1572872 | tf_op jit(solution)/shard_map/ppermute | solution.py:430
  120.6 24.4 %collective-permute-start.21 = (bf16[2,128,1024]{2,1,0:T(8,128)(2,1)S(1)}, bf16[2,128,1024]{2,1,0:T(8,128)(2,1)}, u32[]{:S(2)}, u32[]{:S(2)}) collective-permute-start(bf16[2,128,1024]{2,1,0:T(8,128)(2,1)S(1)} %get-tuple-element.110.refs_1_.refs_0_), channel_id=1, source_target_pairs={{4,8},{5,9},{6,10},{7,11},{8,4},{9,5},{10,6},{11,7},{20,24},{21,25... | collective-permute-start | bytes 1572872 | tf_op jit(solution)/shard_map/ppermute | solution.py:434
  130.6 0.8 copy-start.10
  131.4 13.7 %collective-permute-start.22 = (bf16[2,128,1024]{2,1,0:T(8,128)(2,1)S(1)}, bf16[2,128,1024]{2,1,0:T(8,128)(2,1)}, u32[]{:S(2)}, u32[]{:S(2)}) collective-permute-start(bf16[2,128,1024]{2,1,0:T(8,128)(2,1)S(1)} %get-tuple-element.110.refs_1_.refs_0_), channel_id=1, source_target_pairs={{0,4},{1,5},{2,6},{3,7},{12,8},{13,9},{14,10},{15,11},{4,0},{5,1},... | collective-permute-start | bytes 1572872 | tf_op jit(solution)/shard_map/ppermute | solution.py:434
  131.4 0.8 copy-start.6
  132.6 20.4 %collective-permute-start.31 = (bf16[2,128,1024]{2,1,0:T(8,128)(2,1)}, bf16[2,128,1024]{2,1,0:T(8,128)(2,1)S(1)}, u32[]{:S(2)}, u32[]{:S(2)}) collective-permute-start(bf16[2,128,1024]{2,1,0:T(8,128)(2,1)} %collective-permute-done.28.refs_4_.refs_3_), channel_id=1, source_target_pairs={{0,2},{1,3},{2,0},{3,1},{4,6},{5,7},{6,4},{7,5},{8,10},{9,11},{10,... | collective-permute-start | bytes 1572872 | tf_op jit(solution)/shard_map/ppermute | solution.py:430
  134.6 36.8 %collective-permute-start.32 = (bf16[2,128,1024]{2,1,0:T(8,128)(2,1)}, bf16[2,128,1024]{2,1,0:T(8,128)(2,1)}, u32[]{:S(2)}, u32[]{:S(2)}) collective-permute-start(bf16[2,128,1024]{2,1,0:T(8,128)(2,1)} %collective-permute-done.28.refs_4_.refs_3_), channel_id=1, source_target_pairs={{4,8},{5,9},{6,10},{7,11},{8,4},{9,5},{10,6},{11,7},{20,24},{21,25... | collective-permute-start | bytes 1572872 | tf_op jit(solution)/shard_map/ppermute | solution.py:434
  141.8 0.8 copy-start.12
  142.6 28.8 %collective-permute-start.33 = (bf16[2,128,1024]{2,1,0:T(8,128)(2,1)}, bf16[2,128,1024]{2,1,0:T(8,128)(2,1)}, u32[]{:S(2)}, u32[]{:S(2)}) collective-permute-start(bf16[2,128,1024]{2,1,0:T(8,128)(2,1)} %collective-permute-done.27), channel_id=1, source_target_pairs={{4,0},{5,1},{6,2},{7,3},{8,12},{9,13},{10,14},{11,15},{20,16},{21,... | collective-permute-start | bytes 1572872 | tf_op jit(solution)/shard_map/ppermute | solution.py:434
  145.0 29.0 %collective-permute-start.23 = (bf16[2,128,1024]{2,1,0:T(8,128)(2,1)}, bf16[2,128,1024]{2,1,0:T(8,128)(2,1)}, u32[]{:S(2)}, u32[]{:S(2)}) collective-permute-start(bf16[2,128,1024]{2,1,0:T(8,128)(2,1)} %collective-permute-done.22.refs_3_.refs_2_), channel_id=1, source_target_pairs={{0,2},{1,3},{2,0},{3,1},{4,6},{5,7},{6,4},{7,5},{8,10},{9,11},{10,... | collective-permute-start | bytes 1572872 | tf_op jit(solution)/shard_map/ppermute | solution.py:430
  145.9 28.1 %collective-permute-start.24 = (bf16[2,128,1024]{2,1,0:T(8,128)(2,1)}, bf16[2,128,1024]{2,1,0:T(8,128)(2,1)}, u32[]{:S(2)}, u32[]{:S(2)}) collective-permute-start(bf16[2,128,1024]{2,1,0:T(8,128)(2,1)} %collective-permute-done.22.refs_3_.refs_2_), channel_id=1, source_target_pairs={{4,8},{5,9},{6,10},{7,11},{8,4},{9,5},{10,6},{11,7},{20,24},{21,25... | collective-permute-start | bytes 1572872 | tf_op jit(solution)/shard_map/ppermute | solution.py:434
  153.0 0.8 copy-start.4
  153.8 20.2 %collective-permute-start.25 = (bf16[2,128,1024]{2,1,0:T(8,128)(2,1)}, bf16[2,128,1024]{2,1,0:T(8,128)(2,1)}, u32[]{:S(2)}, u32[]{:S(2)}) collective-permute-start(bf16[2,128,1024]{2,1,0:T(8,128)(2,1)} %collective-permute-done.21), channel_id=1, source_target_pairs={{4,0},{5,1},{6,2},{7,3},{8,12},{9,13},{10,14},{11,15},{20,16},{21,... | collective-permute-start | bytes 1572872 | tf_op jit(solution)/shard_map/ppermute | solution.py:434
  156.3 1.0 copy-start.7
  157.3 1.0 copy-start.9
  158.4 1.0 copy-start.11
  159.4 1.0 copy-start.13
  160.5 3.9 %copy-start.14 = (bf16[2,128,1024]{2,1,0:T(8,128)(2,1)S(1)}, bf16[2,128,1024]{2,1,0:T(8,128)(2,1)}, u32[]{:S(2)}) copy-start(bf16[2,128,1024]{2,1,0:T(8,128)(2,1)} %copy-done.12) | copy-start | bytes 1572868
  164.4 3.4 %copy-start.3 = (f32[2,128,8192]{2,1,0:T(8,128)S(1)}, f32[2,128,8192]{2,1,0:T(8,128)}, u32[]{:S(2)}) copy-start(f32[2,128,8192]{2,1,0:T(8,128)} %refs_0_.1) | copy-start | bytes 25165828
  171.4 7.1 %copy-start.5 = (bf16[2,128,1024]{2,1,0:T(8,128)(2,1)S(1)}, bf16[2,128,1024]{2,1,0:T(8,128)(2,1)}, u32[]{:S(2)}) copy-start(bf16[2,128,1024]{2,1,0:T(8,128)(2,1)} %copy-done.4) | copy-start | bytes 1572868
  172.6 14.9 %collective-permute-start.35 = (bf16[2,128,1024]{2,1,0:T(8,128)(2,1)S(1)}, bf16[2,128,1024]{2,1,0:T(8,128)(2,1)S(1)}, u32[]{:S(2)}, u32[]{:S(2)}) collective-permute-start(bf16[2,128,1024]{2,1,0:T(8,128)(2,1)S(1)} %broadcast_select_fusion.2.refs_2_), channel_id=1, source_target_pairs={{0,2},{1,3},{2,0},{3,1},{4,6},{5,7},{6,4},{7,5},{8,10},{9,11},{10,... | collective-permute-start | bytes 1572872 | tf_op jit(solution)/shard_map/ppermute | solution.py:430
  172.7 14.8 %collective-permute-start.36 = (bf16[2,128,1024]{2,1,0:T(8,128)(2,1)}, bf16[2,128,1024]{2,1,0:T(8,128)(2,1)S(1)}, u32[]{:S(2)}, u32[]{:S(2)}) collective-permute-start(bf16[2,128,1024]{2,1,0:T(8,128)(2,1)} %collective-permute-done.32), channel_id=1, source_target_pairs={{4,0},{5,1},{6,2},{7,3},{8,12},{9,13},{10,14},{11,15},{20,16},{21,... | collective-permute-start | bytes 1572872 | tf_op jit(solution)/shard_map/ppermute | solution.py:434
  175.1 22.5 %collective-permute-start.29 = (bf16[2,128,1024]{2,1,0:T(8,128)(2,1)S(1)}, bf16[2,128,1024]{2,1,0:T(8,128)(2,1)S(1)}, u32[]{:S(2)}, u32[]{:S(2)}) collective-permute-start(bf16[2,128,1024]{2,1,0:T(8,128)(2,1)S(1)} %broadcast_select_fusion.3.refs_1_), channel_id=1, source_target_pairs={{0,2},{1,3},{2,0},{3,1},{4,6},{5,7},{6,4},{7,5},{8,10},{9,11},{10,... | collective-permute-start | bytes 1572872 | tf_op jit(solution)/shard_map/ppermute | solution.py:430
  177.2 20.4 %collective-permute-start.30 = (bf16[2,128,1024]{2,1,0:T(8,128)(2,1)}, bf16[2,128,1024]{2,1,0:T(8,128)(2,1)S(1)}, u32[]{:S(2)}, u32[]{:S(2)}) collective-permute-start(bf16[2,128,1024]{2,1,0:T(8,128)(2,1)} %collective-permute-done.24), channel_id=1, source_target_pairs={{4,0},{5,1},{6,2},{7,3},{8,12},{9,13},{10,14},{11,15},{20,16},{21,... | collective-permute-start | bytes 1572872 | tf_op jit(solution)/shard_map/ppermute | solution.py:434
  198.8 14.9 %collective-permute-start.34 = (bf16[2,128,1024]{2,1,0:T(8,128)(2,1)S(1)}, bf16[2,128,1024]{2,1,0:T(8,128)(2,1)S(1)}, u32[]{:S(2)}, u32[]{:S(2)}) collective-permute-start(bf16[2,128,1024]{2,1,0:T(8,128)(2,1)S(1)} %broadcast_select_fusion.1.refs_5_.refs_1_), channel_id=1, source_target_pairs={{0,2},{1,3},{2,0},{3,1},{4,6},{5,7},{6,4},{7,5},{8,10},{9,11},{10,... | collective-permute-start | bytes 1572872 | tf_op jit(solution)/shard_map/ppermute | solution.py:430
  203.1 20.3 %collective-permute-start.37 = (bf16[2,128,2048]{2,1,0:T(8,128)(2,1)S(1)}, bf16[2,128,2048]{2,1,0:T(8,128)(2,1)S(1)}, u32[]{:S(2)}, u32[]{:S(2)}) collective-permute-start(bf16[2,128,2048]{2,1,0:T(8,128)(2,1)S(1)} %get-tuple-element.131), channel_id=1, source_target_pairs={{0,1},{1,0},{2,3},{3,2},{4,5},{5,4},{6,7},{7,6},{8,9},{9,8},{10,11... | collective-permute-start | bytes 3145736 | tf_op jit(solution)/shard_map/ppermute | solution.py:427
  203.2 20.2 %collective-permute-start.38 = (bf16[2,128,2048]{2,1,0:T(8,128)(2,1)S(1)}, bf16[2,128,2048]{2,1,0:T(8,128)(2,1)S(1)}, u32[]{:S(2)}, u32[]{:S(2)}) collective-permute-start(bf16[2,128,2048]{2,1,0:T(8,128)(2,1)S(1)} %get-tuple-element.132), channel_id=1, source_target_pairs={{0,1},{1,0},{2,3},{3,2},{4,5},{5,4},{6,7},{7,6},{8,9},{9,8},{10,11... | collective-permute-start | bytes 3145736 | tf_op jit(solution)/shard_map/ppermute | solution.py:427
  203.7 19.7 %collective-permute-start.41 = (bf16[2,128,1024]{2,1,0:T(8,128)(2,1)S(1)}, bf16[2,128,1024]{2,1,0:T(8,128)(2,1)S(1)}, u32[]{:S(2)}, u32[]{:S(2)}) collective-permute-start(bf16[2,128,1024]{2,1,0:T(8,128)(2,1)S(1)} %broadcast_select_fusion.refs_6_.refs_2_), channel_id=1, source_target_pairs={{0,2},{1,3},{2,0},{3,1},{4,6},{5,7},{6,4},{7,5},{8,10},{9,11},{10,... | collective-permute-start | bytes 1572872 | tf_op jit(solution)/shard_map/ppermute | solution.py:430
  204.6 19.3 %collective-permute-start.39 = (bf16[2,128,2048]{2,1,0:T(8,128)(2,1)S(1)}, bf16[2,128,2048]{2,1,0:T(8,128)(2,1)S(1)}, u32[]{:S(2)}, u32[]{:S(2)}) collective-permute-start(bf16[2,128,2048]{2,1,0:T(8,128)(2,1)S(1)} %get-tuple-element.136), channel_id=1, source_target_pairs={{0,1},{1,0},{2,3},{3,2},{4,5},{5,4},{6,7},{7,6},{8,9},{9,8},{10,11... | collective-permute-start | bytes 3145736 | tf_op jit(solution)/shard_map/ppermute | solution.py:427
  213.7 10.3 %collective-permute-start.40 = (bf16[2,128,2048]{2,1,0:T(8,128)(2,1)S(1)}, bf16[2,128,2048]{2,1,0:T(8,128)(2,1)S(1)}, u32[]{:S(2)}, u32[]{:S(2)}) collective-permute-start(bf16[2,128,2048]{2,1,0:T(8,128)(2,1)S(1)} %get-tuple-element.137), channel_id=1, source_target_pairs={{0,1},{1,0},{2,3},{3,2},{4,5},{5,4},{6,7},{7,6},{8,9},{9,8},{10,11... | collective-permute-start | bytes 3145736 | tf_op jit(solution)/shard_map/ppermute | solution.py:427
  223.4 1.9 collective-permute-start.43
  223.4 2.6 %collective-permute-start.42 = (bf16[2,128,1024]{2,1,0:T(8,128)(2,1)S(1)}, bf16[2,128,1024]{2,1,0:T(8,128)(2,1)S(1)}, u32[]{:S(2)}, u32[]{:S(2)}) collective-permute-start(bf16[2,128,1024]{2,1,0:T(8,128)(2,1)S(1)} %collective-permute-done.34.refs_5_), channel_id=1, source_target_pairs={{0,1},{1,0},{2,3},{3,2},{4,5},{5,4},{6,7},{7,6},{8,9},{9,8},{10,11... | collective-permute-start | bytes 1572872 | tf_op jit(solution)/shard_map/ppermute | solution.py:427

commit v8 on v7

--- a/solution.py
+++ b/solution.py
@@ -535,15 +535,14 @@
         from_far = jnp.where(at_ends, pieces["far outward", stream], pieces["far inner", stream])
         pieces[("far", 0), stream] = from_far
         pieces[("far", 2), stream] = across(from_far)
-    chunks = apply([pieces["slab", last]], late, 4)
-    slab = [sibling(chunk) for chunk in chunks]
+    slab = [sibling(chunk) for chunk in apply([pieces["slab", last]], late, 4)]
     result = apply([pieces["result", last]], later + late)
-    arriving, result, slab[0], slab[1] = together(
-        (pieces[("far", 2), last], result, slab[0], slab[1])
+    pieces[("far", 2), lead], result = together((pieces[("far", 2), lead], result))
+    pieces[("far", 3), lead] = sibling(pieces[("far", 2), lead])
+    pieces[("far", 2), last], pieces[("far", 3), lead] = together(
+        (pieces[("far", 2), last], pieces[("far", 3), lead])
     )
-    pieces[("far", 2), last] = arriving
-    for stream in (lead, last):
-        pieces[("far", 3), stream] = sibling(pieces[("far", 2), stream])
+    pieces[("far", 3), last] = sibling(pieces[("far", 2), last])
     return apply([result] + slab, [("far", 2), ("far", 3)])
 
 

time: 234 us -> 234 us (level)
  the two profiles are of different devices: /device:TPU:16 before, /device:TPU:0 now
where the time goes in v8:
time: 234 us; the launch traced here: 233 us
  waiting for transfers between devices  85.4 us (36%)
  starting transfers between devices  83.4 us (36%)
  Pallas kernels  42.5 us (18%)
  local copies, waits for them, and re-layouts  15.7 us (7%)
  other arithmetic  5.63 us (2%)
    ppermute x16, waiting for transfers between devices, across(): return lax.ppermute(value, 'ty', [(i, i ^ 2) for i in range(count)])  58.5 us
    ppermute x20, starting transfers between devices, along(): return lax.ppermute(value, 'ty', pairs)  47.6 us
    ppermute x16, starting transfers between devices, across(): return lax.ppermute(value, 'ty', [(i, i ^ 2) for i in range(count)])  34 us
    ppermute x20, waiting for transfers between devices, along(): return lax.ppermute(value, 'ty', pairs)  22.2 us
    pallas_call x6, Pallas kernels, backward(): pl.pallas_call(functools.partial(kernel, slots=slots, held=held, parts=le...  18.9 us
    unnamed x38, local copies, waits for them, and re-layouts  15 us
    pallas_call x3, Pallas kernels, forward(): pl.pallas_call(functools.partial(forward_kernel, base=base, images=images...  15 us
    pallas_call x1, Pallas kernels, middle(): pl.pallas_call(functools.partial(middle_kernel, terms=len(streams[0]), st...  4.83 us
  transfers between devices with their start and end apart: 44, of which 24 were waited for; matrix products, arithmetic and copies ran while one was open for 2% of the time, Pallas kernels for 12%

profile of v8, /device:TPU:0, one launch (start us, length us, event | category | flops | bytes accessed | tf_op | source)
XLA Modules:
  0.0 233.1 jit_solution(14739008422195681653)
XLA Ops:
  0.0 3.4 %copy-done.2 = f32[2,128,8192]{2,1,0:T(8,128)S(1)} copy-done((f32[2,128,8192]{2,1,0:T(8,128)S(1)}, f32[2,128,8192]{2,1,0:T(8,128)}, u32[]{:S(2)}) %copy-start.2) | copy-done | bytes 8388632
  3.4 1.8 low_part.2.refs_0_
  5.8 1.9 low_part.3.refs_1_
  8.8 2.3 forward.3.refs_2_
  11.1 1.8 collective-permute-done.1.refs_1_.refs_3_
  12.9 2.3 forward.4
  15.2 4.0 %collective-permute-start.2 = (bf16[2,128,1024]{2,1,0:T(8,128)(2,1)S(1)}, bf16[2,128,1024]{2,1,0:T(8,128)(2,1)S(1)}, u32[]{:S(2)}, u32[]{:S(2)}) collective-permute-start(bf16[2,128,1024]{2,1,0:T(8,128)(2,1)S(1)} %get-tuple-element.76), channel_id=1, source_target_pairs={{0,2},{1,3},{2,0},{3,1},{4,6},{5,7},{6,4},{7,5},{8,10},{9,11},{10,... | collective-permute-start | bytes 1572872 | tf_op jit(solution)/shard_map/ppermute | solution.py:430
  19.3 10.4 %forward.5 = (bf16[2,128,1024]{2,1,0:T(8,128)(2,1)S(1)}, bf16[2,128,1024]{2,1,0:T(8,128)(2,1)S(1)}, bf16[2,128,1024]{2,1,0:T(8,128)(2,1)S(1)}, bf16[2,128,1024]{...) custom-call(s32[3,16]{1,0:T(4,128)S(1)} %pad_add_fusion.meta_ref, ...), custom_call_target="tpu_custom_call" | custom-call | flops 1024 | bytes 1024 | tf_op jit(solution)/shard_map/forward/pallas_call | solution.py:257
  29.7 2.3 collective-permute-done.2
  32.1 3.6 %collective-permute-start.3 = (bf16[2,128,1024]{2,1,0:T(8,128)(2,1)S(1)}, bf16[2,128,1024]{2,1,0:T(8,128)(2,1)S(1)}, u32[]{:S(2)}, u32[]{:S(2)}) collective-permute-start(bf16[2,128,1024]{2,1,0:T(8,128)(2,1)S(1)} %fusion), channel_id=1, source_target_pairs={{0,4},{1,5},{2,6},{3,7},{12,8},{13,9},{14,10},{15,11},{16,20},{17,... | collective-permute-start | bytes 1572872 | tf_op jit(solution)/shard_map/ppermute | solution.py:434
  35.7 5.8 %collective-permute-start.4 = (bf16[2,128,1024]{2,1,0:T(8,128)(2,1)S(1)}, bf16[2,128,1024]{2,1,0:T(8,128)(2,1)S(1)}, u32[]{:S(2)}, u32[]{:S(2)}) collective-permute-start(bf16[2,128,1024]{2,1,0:T(8,128)(2,1)S(1)} %get-tuple-element.81), channel_id=1, source_target_pairs={{0,2},{1,3},{2,0},{3,1},{4,6},{5,7},{6,4},{7,5},{8,10},{9,11},{10,... | collective-permute-start | bytes 1572872 | tf_op jit(solution)/shard_map/ppermute | solution.py:430
  41.5 1.2 collective-permute-done.11
  42.9 4.1 %collective-permute-start.12 = (bf16[2,128,1024]{2,1,0:T(8,128)(2,1)S(1)}, bf16[2,128,1024]{2,1,0:T(8,128)(2,1)S(1)}, u32[]{:S(2)}, u32[]{:S(2)}) collective-permute-start(bf16[2,128,1024]{2,1,0:T(8,128)(2,1)S(1)} %fusion.2), channel_id=1, source_target_pairs={{0,4},{1,5},{2,6},{3,7},{12,8},{13,9},{14,10},{15,11},{16,20},{17,... | collective-permute-start | bytes 1572872 | tf_op jit(solution)/shard_map/ppermute | solution.py:434
  47.0 2.1 collective-permute-start.13
  49.0 4.7 %collective-permute-done.4 = bf16[2,128,1024]{2,1,0:T(8,128)(2,1)S(1)} collective-permute-done((bf16[2,128,1024]{2,1,0:T(8,128)(2,1)S(1)}, bf16[2,128,1024]{2,1,0:T(8,128)(2,1)S(1)}, u32[]{:S(2)}, u32[]{:S(2)}) %collective-permute-start.4) | collective-permute-done | bytes 524320 | tf_op jit(solution)/shard_map/ppermute | solution.py:430
  53.9 4.3 %collective-permute-start.6 = (bf16[2,128,1024]{2,1,0:T(8,128)(2,1)S(1)}, bf16[2,128,1024]{2,1,0:T(8,128)(2,1)S(1)}, u32[]{:S(2)}, u32[]{:S(2)}) collective-permute-start(bf16[2,128,1024]{2,1,0:T(8,128)(2,1)S(1)} %fusion.1), channel_id=1, source_target_pairs={{0,4},{1,5},{2,6},{3,7},{12,8},{13,9},{14,10},{15,11},{16,20},{17,... | collective-permute-start | bytes 1572872 | tf_op jit(solution)/shard_map/ppermute | solution.py:434
  59.2 2.1 collective-permute-start.7
  61.2 3.7 %collective-permute-done.13 = bf16[2,128,1024]{2,1,0:T(8,128)(2,1)S(1)} collective-permute-done((bf16[2,128,1024]{2,1,0:T(8,128)(2,1)S(1)}, bf16[2,128,1024]{2,1,0:T(8,128)(2,1)S(1)}, u32[]{:S(2)}, u32[]{:S(2)}) %collective-permute-start.13) | collective-permute-done | bytes 524320 | tf_op jit(solution)/shard_map/ppermute | solution.py:430
  65.1 4.3 %collective-permute-start.15 = (bf16[2,128,1024]{2,1,0:T(8,128)(2,1)S(1)}, bf16[2,128,1024]{2,1,0:T(8,128)(2,1)S(1)}, u32[]{:S(2)}, u32[]{:S(2)}) collective-permute-start(bf16[2,128,1024]{2,1,0:T(8,128)(2,1)S(1)} %fusion.3), channel_id=1, source_target_pairs={{0,4},{1,5},{2,6},{3,7},{12,8},{13,9},{14,10},{15,11},{16,20},{17,... | collective-permute-start | bytes 1572872 | tf_op jit(solution)/shard_map/ppermute | solution.py:434
  70.5 5.1 %collective-permute-start.16 = (bf16[2,128,1024]{2,1,0:T(8,128)(2,1)S(1)}, bf16[2,128,1024]{2,1,0:T(8,128)(2,1)S(1)}, u32[]{:S(2)}, u32[]{:S(2)}) collective-permute-start(bf16[2,128,1024]{2,1,0:T(8,128)(2,1)S(1)} %get-tuple-element.103), channel_id=1, source_target_pairs={{0,2},{1,3},{2,0},{3,1},{4,6},{5,7},{6,4},{7,5},{8,10},{9,11},{10,... | collective-permute-start | bytes 1572872 | tf_op jit(solution)/shard_map/ppermute | solution.py:430
  77.4 5.5 %collective-permute-start.10 = (bf16[2,128,1024]{2,1,0:T(8,128)(2,1)S(1)}, bf16[2,128,1024]{2,1,0:T(8,128)(2,1)S(1)}, u32[]{:S(2)}, u32[]{:S(2)}) collective-permute-start(bf16[2,128,1024]{2,1,0:T(8,128)(2,1)S(1)} %add_convert_fusion.5), channel_id=1, source_target_pairs={{0,4},{1,5},{2,6},{3,7},{12,8},{13,9},{14,10},{15,11},{4,0},{5,1},... | collective-permute-start | bytes 1572872 | tf_op jit(solution)/shard_map/ppermute | solution.py:434
  82.9 3.9 %collective-permute-start.8 = (bf16[2,128,1024]{2,1,0:T(8,128)(2,1)S(1)}, bf16[2,128,1024]{2,1,0:T(8,128)(2,1)S(1)}, u32[]{:S(2)}, u32[]{:S(2)}) collective-permute-start(bf16[2,128,1024]{2,1,0:T(8,128)(2,1)S(1)} %get-tuple-element.88), channel_id=1, source_target_pairs={{0,2},{1,3},{2,0},{3,1},{4,6},{5,7},{6,4},{7,5},{8,10},{9,11},{10,... | collective-permute-start | bytes 1572872 | tf_op jit(solution)/shard_map/ppermute | solution.py:430
  89.2 6.8 %collective-permute-start.19 = (bf16[2,128,1024]{2,1,0:T(8,128)(2,1)S(1)}, bf16[2,128,1024]{2,1,0:T(8,128)(2,1)S(1)}, u32[]{:S(2)}, u32[]{:S(2)}) collective-permute-start(bf16[2,128,1024]{2,1,0:T(8,128)(2,1)S(1)} %add_convert_fusion.1), channel_id=1, source_target_pairs={{0,4},{1,5},{2,6},{3,7},{12,8},{13,9},{14,10},{15,11},{4,0},{5,1},... | collective-permute-start | bytes 1572872 | tf_op jit(solution)/shard_map/ppermute | solution.py:434
  96.0 1.3 collective-permute-start.17
  97.3 1.7 collective-permute-done.8
  99.4 6.4 %collective-permute-done.19 = bf16[2,128,1024]{2,1,0:T(8,128)(2,1)S(1)} collective-permute-done((bf16[2,128,1024]{2,1,0:T(8,128)(2,1)S(1)}, bf16[2,128,1024]{2,1,0:T(8,128)(2,1)S(1)}, u32[]{:S(2)}, u32[]{:S(2)}) %collective-permute-start.19) | collective-permute-done | bytes 524320 | tf_op jit(solution)/shard_map/ppermute | solution.py:434
  105.8 5.1 %collective-permute-done.17 = bf16[2,128,1024]{2,1,0:T(8,128)(2,1)S(1)} collective-permute-done((bf16[2,128,1024]{2,1,0:T(8,128)(2,1)S(1)}, bf16[2,128,1024]{2,1,0:T(8,128)(2,1)S(1)}, u32[]{:S(2)}, u32[]{:S(2)}) %collective-permute-start.17) | collective-permute-done | bytes 524320 | tf_op jit(solution)/shard_map/ppermute | solution.py:430
  111.2 4.8 %middle.1 = (bf16[2,128,1024]{2,1,0:T(8,128)(2,1)S(1)}, bf16[2,128,1024]{2,1,0:T(8,128)(2,1)S(1)}) custom-call(bf16[2,128,1024]{2,1,0:T(8,128)(2,1)S(1)} %add_convert_fusion.refs_0_, bf16[2,128,1024]{2,1,0:T(8,128)(2,1)S(1)} %add_convert_fusion.4.refs_1_, bf16[1,256,1024]{2,1,0:T(8,128)(2,1)S(1)} %copy-done.16, bf16[1024,1024]{1,0:T(8,128)(2,1)S(1)} %copy-done.14, ...), custom_call_target="tpu_custom_call" | custom-call | flops 1024 | bytes 1024 | tf_op jit(solution)/shard_map/middle/pallas_call | solution.py:295
  116.1 1.8 collective-permute-start.26
  117.9 1.5 collective-permute-start.27
  119.4 3.0 %collective-permute-start.28 = (bf16[2,128,1024]{2,1,0:T(8,128)(2,1)S(1)}, bf16[2,128,1024]{2,1,0:T(8,128)(2,1)}, u32[]{:S(2)}, u32[]{:S(2)}) collective-permute-start(bf16[2,128,1024]{2,1,0:T(8,128)(2,1)S(1)} %get-tuple-element.113.refs_0_.refs_1_), channel_id=1, source_target_pairs={{0,4},{1,5},{2,6},{3,7},{12,8},{13,9},{14,10},{15,11},{4,0},{5,1},... | collective-permute-start | bytes 1572872 | tf_op jit(solution)/shard_map/ppermute | solution.py:434
  123.6 1.5 collective-permute-start.21
  125.0 5.9 %collective-permute-done.26.refs_4_.refs_5_ = bf16[2,128,1024]{2,1,0:T(8,128)(2,1)S(1)} collective-permute-done((bf16[2,128,1024]{2,1,0:T(8,128)(2,1)S(1)}, bf16[2,128,1024]{2,1,0:T(8,128)(2,1)S(1)}, u32[]{:S(2)}, u32[]{:S(2)}) %collective-permute-start.26) | collective-permute-done | bytes 524320 | tf_op jit(solution)/shard_map/ppermute | solution.py:430
  131.7 2.2 collective-permute-start.22
  134.7 2.1 collective-permute-start.32
  136.8 1.5 collective-permute-start.33
  138.2 3.9 %collective-permute-done.20.refs_5_.refs_6_ = bf16[2,128,1024]{2,1,0:T(8,128)(2,1)S(1)} collective-permute-done((bf16[2,128,1024]{2,1,0:T(8,128)(2,1)S(1)}, bf16[2,128,1024]{2,1,0:T(8,128)(2,1)S(1)}, u32[]{:S(2)}, u32[]{:S(2)}) %collective-permute-start.20) | collective-permute-done | bytes 524320 | tf_op jit(solution)/shard_map/ppermute | solution.py:430
  142.9 2.7 %collective-permute-done.22.refs_3_.refs_4_ = bf16[2,128,1024]{2,1,0:T(8,128)(2,1)} collective-permute-done((bf16[2,128,1024]{2,1,0:T(8,128)(2,1)S(1)}, bf16[2,128,1024]{2,1,0:T(8,128)(2,1)}, u32[]{:S(2)}, u32[]{:S(2)}) %collective-permute-start.22) | collective-permute-done | bytes 524320 | tf_op jit(solution)/shard_map/ppermute | solution.py:434
  145.6 1.3 collective-permute-start.34
  146.9 1.2 collective-permute-start.23
  148.1 1.5 collective-permute-start.24
  149.5 3.8 %collective-permute-done.32.refs_3_ = bf16[2,128,1024]{2,1,0:T(8,128)(2,1)S(1)} collective-permute-done((bf16[2,128,1024]{2,1,0:T(8,128)(2,1)}, bf16[2,128,1024]{2,1,0:T(8,128)(2,1)S(1)}, u32[]{:S(2)}, u32[]{:S(2)}) %collective-permute-start.32) | collective-permute-done | bytes 524320 | tf_op jit(solution)/shard_map/ppermute | solution.py:430
  154.2 1.3 collective-permute-start.25
  155.5 3.4 %copy-done.3 = f32[2,128,8192]{2,1,0:T(8,128)S(1)} copy-done((f32[2,128,8192]{2,1,0:T(8,128)S(1)}, f32[2,128,8192]{2,1,0:T(8,128)}, u32[]{:S(2)}) %copy-start.3) | copy-done | bytes 8388632
  163.0 2.6 %backward.7.refs_0_ = f32[2,128,8192]{2,1,0:T(8,128)S(1)} custom-call(s32[3,16]{1,0:T(4,128)S(1)} %pad_add_fusion.meta_ref, bf16[1024,1024]{1,0:T(8,128)(2,1)S(1)} %copy-done, bf16[1024,512]{1,0:T(8,128)(2,1)S(1)} %copy-done.1, f32[2,128,8192]{2,1,0:T(8,128)S(1)} %copy-done.3, bf16[2,128,1024]{2,1,0:T(8,128)(2,1)S(1)} %copy-done.7, ...), custom_call_target="tpu_custom_call" | custom-call | flops 1024 | bytes 1024 | tf_op jit(solution)/shard_map/backward/pallas_call | solution.py:279
  165.6 3.2 %backward.6.refs_0_ = bf16[2,128,8192]{2,1,0:T(8,128)(2,1)S(1)} custom-call(s32[3,16]{1,0:T(4,128)S(1)} %pad_add_fusion.meta_ref, bf16[1024,1024]{1,0:T(8,128)(2,1)S(1)} %copy-done, bf16[1024,512]{1,0:T(8,128)(2,1)S(1)} %copy-done.1, bf16[2,128,1024]{2,1,0:T(8,128)(2,1)S(1)} %copy-done.7, bf16[2,128,1024]{2,1,0:T(8,128)(2,1)S(1)} %copy-done.9, ...), custom_call_target="tpu_custom_call" | custom-call | flops 1024 | bytes 1024 | tf_op jit(solution)/shard_map/backward/pallas_call | solution.py:279
  168.9 2.9 %collective-permute-done.25 = bf16[2,128,1024]{2,1,0:T(8,128)(2,1)} collective-permute-done((bf16[2,128,1024]{2,1,0:T(8,128)(2,1)}, bf16[2,128,1024]{2,1,0:T(8,128)(2,1)}, u32[]{:S(2)}, u32[]{:S(2)}) %collective-permute-start.25) | collective-permute-done | bytes 524320 | tf_op jit(solution)/shard_map/ppermute | solution.py:434
  171.8 1.1 broadcast_select_fusion.1.refs_1_
  173.1 1.3 collective-permute-start.36
  174.4 1.1 broadcast_select_fusion.3.refs_2_
  175.5 2.0 collective-permute-start.29
  177.4 1.3 collective-permute-start.30
  178.7 2.8 %backward.8.refs_0_ = bf16[2,128,8192]{2,1,0:T(8,128)(2,1)S(1)} custom-call(s32[3,16]{1,0:T(4,128)S(1)} %pad_add_fusion.meta_ref, bf16[1024,1024]{1,0:T(8,128)(2,1)S(1)} %copy-done, bf16[1024,512]{1,0:T(8,128)(2,1)S(1)} %copy-done.1, bf16[2,128,8192]{2,1,0:T(8,128)(2,1)S(1)} %backward.6.refs_0_, bf16[2,128,1024]{2,1,0:T(8,128)(2,1)S(1)} %broadcast_select_fusion.1.refs_1_, ...), custom_call_target="tpu_custom_call" | custom-call | flops 1024 | bytes 1024 | tf_op jit(solution)/shard_map/backward/pallas_call | solution.py:279
  181.6 6.2 %collective-permute-done.35.refs_7_.refs_3_ = bf16[2,128,1024]{2,1,0:T(8,128)(2,1)S(1)} collective-permute-done((bf16[2,128,1024]{2,1,0:T(8,128)(2,1)S(1)}, bf16[2,128,1024]{2,1,0:T(8,128)(2,1)S(1)}, u32[]{:S(2)}, u32[]{:S(2)}) %collective-permute-start.35) | collective-permute-done | bytes 524320 | tf_op jit(solution)/shard_map/ppermute | solution.py:430
  187.8 4.3 %collective-permute-done.36 = bf16[2,128,1024]{2,1,0:T(8,128)(2,1)S(1)} collective-permute-done((bf16[2,128,1024]{2,1,0:T(8,128)(2,1)}, bf16[2,128,1024]{2,1,0:T(8,128)(2,1)S(1)}, u32[]{:S(2)}, u32[]{:S(2)}) %collective-permute-start.36) | collective-permute-done | bytes 524320 | tf_op jit(solution)/shard_map/ppermute | solution.py:434
  192.1 3.7 %collective-permute-done.29.refs_8_.refs_4_ = bf16[2,128,1024]{2,1,0:T(8,128)(2,1)S(1)} collective-permute-done((bf16[2,128,1024]{2,1,0:T(8,128)(2,1)S(1)}, bf16[2,128,1024]{2,1,0:T(8,128)(2,1)S(1)}, u32[]{:S(2)}, u32[]{:S(2)}) %collective-permute-start.29) | collective-permute-done | bytes 524320 | tf_op jit(solution)/shard_map/ppermute | solution.py:430
  195.8 5.8 %collective-permute-done.30 = bf16[2,128,1024]{2,1,0:T(8,128)(2,1)S(1)} collective-permute-done((bf16[2,128,1024]{2,1,0:T(8,128)(2,1)}, bf16[2,128,1024]{2,1,0:T(8,128)(2,1)S(1)}, u32[]{:S(2)}, u32[]{:S(2)}) %collective-permute-start.30) | collective-permute-done | bytes 524320 | tf_op jit(solution)/shard_map/ppermute | solution.py:434
  202.4 1.5 collective-permute-start.41
  203.8 3.3 %backward.9.refs_0_ = f32[2,128,8192]{2,1,0:T(8,128)S(1)} custom-call(s32[3,16]{1,0:T(4,128)S(1)} %pad_add_fusion.meta_ref, bf16[1024,1024]{1,0:T(8,128)(2,1)S(1)} %copy-done, bf16[1024,512]{1,0:T(8,128)(2,1)S(1)} %copy-done.1, f32[2,128,8192]{2,1,0:T(8,128)S(1)} %backward.7.refs_0_, bf16[2,128,1024]{2,1,0:T(8,128)(2,1)S(1)} %broadcast_select_fusion.1.refs_1_, ...), custom_call_target="tpu_custom_call" | custom-call | flops 1024 | bytes 1024 | tf_op jit(solution)/shard_map/backward/pallas_call | solution.py:279
  207.1 2.4 %backward.10 = (bf16[2,128,2048]{2,1,0:T(8,128)(2,1)S(1)}, bf16[2,128,2048]{2,1,0:T(8,128)(2,1)S(1)}, bf16[2,128,2048]{2,1,0:T(8,128)(2,1)S(1)}, bf16[2,128,2048]{2,1,0:T(8,128)(2,1)S(1)}) custom-call(s32[3,16]{1,0:T(4,128)S(1)} %pad_add_fusion.meta_ref, bf16[1024,1024]{1,0:T(8,128)(2,1)S(1)} %copy-done, bf16[1024,512]{1,0:T(8,128)(2,1)S(1)} %copy-done.1, ...), custom_call_target="tpu_custom_call" | custom-call | flops 1024 | bytes 1024 | tf_op jit(solution)/shard_map/backward/pallas_call | solution.py:279
  210.1 6.4 %collective-permute-done.31.refs_6_ = bf16[2,128,1024]{2,1,0:T(8,128)(2,1)S(1)} collective-permute-done((bf16[2,128,1024]{2,1,0:T(8,128)(2,1)S(1)}, bf16[2,128,1024]{2,1,0:T(8,128)(2,1)S(1)}, u32[]{:S(2)}, u32[]{:S(2)}) %collective-permute-start.31) | collective-permute-done | bytes 524320 | tf_op jit(solution)/shard_map/ppermute | solution.py:430
  216.6 8.5 %collective-permute-done.41.refs_5_ = bf16[2,128,1024]{2,1,0:T(8,128)(2,1)S(1)} collective-permute-done((bf16[2,128,1024]{2,1,0:T(8,128)(2,1)S(1)}, bf16[2,128,1024]{2,1,0:T(8,128)(2,1)S(1)}, u32[]{:S(2)}, u32[]{:S(2)}) %collective-permute-start.41) | collective-permute-done | bytes 524320 | tf_op jit(solution)/shard_map/ppermute | solution.py:430
  225.6 2.1 collective-permute-done.40.refs_4_
  228.5 4.6 %backward.11 = f32[2,128,8192]{2,1,0:T(8,128)} custom-call(s32[3,16]{1,0:T(4,128)S(1)} %pad_add_fusion.meta_ref, bf16[1024,1024]{1,0:T(8,128)(2,1)S(1)} %copy-done, bf16[1024,512]{1,0:T(8,128)(2,1)S(1)} %copy-done.1, f32[2,128,8192]{2,1,0:T(8,128)S(1)} %backward.9.refs_0_, bf16[2,128,2048]{2,1,0:T(8,128)(2,1)S(1)} %collective-permute-done.37.refs_1_, ...), custom_call_target="tpu_custom_call" | custom-call | flops 1024 | bytes 1024 | tf_op jit(solution)/shard_map/backward/pallas_call | solution.py:279
  (95 shorter events, 20.9 us)
Async XLA Ops:
  0.0 3.4 %copy-start.2 = (f32[2,128,8192]{2,1,0:T(8,128)S(1)}, f32[2,128,8192]{2,1,0:T(8,128)}, u32[]{:S(2)}) copy-start(f32[2,128,8192]{2,1,0:T(8,128)} %refs_0_.1) | copy-start | bytes 25165828
  5.2 3.3 %copy-start.17 = (s32[16]{0:T(128)S(1)}, s32[16]{0:T(128)}, u32[]{:S(2)}) copy-start(s32[16]{0:T(128)} %param.12) | copy-start | bytes 196
  5.2 3.3 %copy-start.18 = (s32[16]{0:T(128)S(1)}, s32[16]{0:T(128)}, u32[]{:S(2)}) copy-start(s32[16]{0:T(128)} %param.13) | copy-start | bytes 196
  5.3 3.5 %copy-start = (bf16[1024,1024]{1,0:T(8,128)(2,1)S(1)}, bf16[1024,1024]{1,0:T(8,128)(2,1)}, u32[]{:S(2)}) copy-start(bf16[1024,1024]{1,0:T(8,128)(2,1)} %pupil_ref.17) | copy-start | bytes 6291460
  5.3 3.5 %copy-start.1 = (bf16[1024,512]{1,0:T(8,128)(2,1)S(1)}, bf16[1024,512]{1,0:T(8,128)(2,1)}, u32[]{:S(2)}) copy-start(bf16[1024,512]{1,0:T(8,128)(2,1)} %constant.42.clone.band_ref) | copy-start | bytes 3145732
  5.3 5.8 %collective-permute-start = (bf16[128,8192]{1,0:T(8,128)(2,1)}, bf16[128,8192]{1,0:T(8,128)(2,1)}, u32[]{:S(2)}, u32[]{:S(2)}) collective-permute-start(bf16[128,8192]{1,0:T(8,128)(2,1)} %low_part.2.refs_0_), channel_id=1, source_target_pairs={{0,1},{1,0},{2,3},{3,2},{4,5},{5,4},{6,7},{7,6},{8,9},{9,8},{10,11... | collective-permute-start | bytes 6291464 | tf_op jit(solution)/shard_map/ppermute | solution.py:427
  7.7 5.2 %collective-permute-start.1 = (bf16[128,8192]{1,0:T(8,128)(2,1)}, bf16[128,8192]{1,0:T(8,128)(2,1)}, u32[]{:S(2)}, u32[]{:S(2)}) collective-permute-start(bf16[128,8192]{1,0:T(8,128)(2,1)} %low_part.3.refs_1_), channel_id=1, source_target_pairs={{0,1},{1,0},{2,3},{3,2},{4,5},{5,4},{6,7},{7,6},{8,9},{9,8},{10,11... | collective-permute-start | bytes 6291464 | tf_op jit(solution)/shard_map/ppermute | solution.py:427
  15.2 16.7 %collective-permute-start.2 = (bf16[2,128,1024]{2,1,0:T(8,128)(2,1)S(1)}, bf16[2,128,1024]{2,1,0:T(8,128)(2,1)S(1)}, u32[]{:S(2)}, u32[]{:S(2)}) collective-permute-start(bf16[2,128,1024]{2,1,0:T(8,128)(2,1)S(1)} %get-tuple-element.76), channel_id=1, source_target_pairs={{0,2},{1,3},{2,0},{3,1},{4,6},{5,7},{6,4},{7,5},{8,10},{9,11},{10,... | collective-permute-start | bytes 1572872 | tf_op jit(solution)/shard_map/ppermute | solution.py:430
  19.2 23.5 %collective-permute-start.11 = (bf16[2,128,1024]{2,1,0:T(8,128)(2,1)S(1)}, bf16[2,128,1024]{2,1,0:T(8,128)(2,1)S(1)}, u32[]{:S(2)}, u32[]{:S(2)}) collective-permute-start(bf16[2,128,1024]{2,1,0:T(8,128)(2,1)S(1)} %get-tuple-element.72), channel_id=1, source_target_pairs={{0,2},{1,3},{2,0},{3,1},{4,6},{5,7},{6,4},{7,5},{8,10},{9,11},{10,... | collective-permute-start | bytes 1572872 | tf_op jit(solution)/shard_map/ppermute | solution.py:430
  32.1 16.9 %collective-permute-start.3 = (bf16[2,128,1024]{2,1,0:T(8,128)(2,1)S(1)}, bf16[2,128,1024]{2,1,0:T(8,128)(2,1)S(1)}, u32[]{:S(2)}, u32[]{:S(2)}) collective-permute-start(bf16[2,128,1024]{2,1,0:T(8,128)(2,1)S(1)} %fusion), channel_id=1, source_target_pairs={{0,4},{1,5},{2,6},{3,7},{12,8},{13,9},{14,10},{15,11},{16,20},{17,... | collective-permute-start | bytes 1572872 | tf_op jit(solution)/shard_map/ppermute | solution.py:434
  35.7 18.0 %collective-permute-start.4 = (bf16[2,128,1024]{2,1,0:T(8,128)(2,1)S(1)}, bf16[2,128,1024]{2,1,0:T(8,128)(2,1)S(1)}, u32[]{:S(2)}, u32[]{:S(2)}) collective-permute-start(bf16[2,128,1024]{2,1,0:T(8,128)(2,1)S(1)} %get-tuple-element.81), channel_id=1, source_target_pairs={{0,2},{1,3},{2,0},{3,1},{4,6},{5,7},{6,4},{7,5},{8,10},{9,11},{10,... | collective-permute-start | bytes 1572872 | tf_op jit(solution)/shard_map/ppermute | solution.py:430
  42.9 18.4 %collective-permute-start.12 = (bf16[2,128,1024]{2,1,0:T(8,128)(2,1)S(1)}, bf16[2,128,1024]{2,1,0:T(8,128)(2,1)S(1)}, u32[]{:S(2)}, u32[]{:S(2)}) collective-permute-start(bf16[2,128,1024]{2,1,0:T(8,128)(2,1)S(1)} %fusion.2), channel_id=1, source_target_pairs={{0,4},{1,5},{2,6},{3,7},{12,8},{13,9},{14,10},{15,11},{16,20},{17,... | collective-permute-start | bytes 1572872 | tf_op jit(solution)/shard_map/ppermute | solution.py:434
  47.0 18.0 %collective-permute-start.13 = (bf16[2,128,1024]{2,1,0:T(8,128)(2,1)S(1)}, bf16[2,128,1024]{2,1,0:T(8,128)(2,1)S(1)}, u32[]{:S(2)}, u32[]{:S(2)}) collective-permute-start(bf16[2,128,1024]{2,1,0:T(8,128)(2,1)S(1)} %get-tuple-element.98), channel_id=1, source_target_pairs={{0,2},{1,3},{2,0},{3,1},{4,6},{5,7},{6,4},{7,5},{8,10},{9,11},{10,... | collective-permute-start | bytes 1572872 | tf_op jit(solution)/shard_map/ppermute | solution.py:430
  53.9 16.6 %collective-permute-start.6 = (bf16[2,128,1024]{2,1,0:T(8,128)(2,1)S(1)}, bf16[2,128,1024]{2,1,0:T(8,128)(2,1)S(1)}, u32[]{:S(2)}, u32[]{:S(2)}) collective-permute-start(bf16[2,128,1024]{2,1,0:T(8,128)(2,1)S(1)} %fusion.1), channel_id=1, source_target_pairs={{0,4},{1,5},{2,6},{3,7},{12,8},{13,9},{14,10},{15,11},{16,20},{17,... | collective-permute-start | bytes 1572872 | tf_op jit(solution)/shard_map/ppermute | solution.py:434
  58.5 17.1 %collective-permute-start.5 = (bf16[2,128,1024]{2,1,0:T(8,128)(2,1)S(1)}, bf16[2,128,1024]{2,1,0:T(8,128)(2,1)S(1)}, u32[]{:S(2)}, u32[]{:S(2)}) collective-permute-start(bf16[2,128,1024]{2,1,0:T(8,128)(2,1)S(1)} %add_convert_fusion.7), channel_id=1, source_target_pairs={{4,8},{5,9},{6,10},{7,11},{8,4},{9,5},{10,6},{11,7},{20,24},{21,25... | collective-permute-start | bytes 1572872 | tf_op jit(solution)/shard_map/ppermute | solution.py:434
  59.2 17.0 %collective-permute-start.7 = (bf16[2,128,1024]{2,1,0:T(8,128)(2,1)S(1)}, bf16[2,128,1024]{2,1,0:T(8,128)(2,1)S(1)}, u32[]{:S(2)}, u32[]{:S(2)}) collective-permute-start(bf16[2,128,1024]{2,1,0:T(8,128)(2,1)S(1)} %get-tuple-element.86), channel_id=1, source_target_pairs={{0,2},{1,3},{2,0},{3,1},{4,6},{5,7},{6,4},{7,5},{8,10},{9,11},{10,... | collective-permute-start | bytes 1572872 | tf_op jit(solution)/shard_map/ppermute | solution.py:430
  65.1 17.8 %collective-permute-start.15 = (bf16[2,128,1024]{2,1,0:T(8,128)(2,1)S(1)}, bf16[2,128,1024]{2,1,0:T(8,128)(2,1)S(1)}, u32[]{:S(2)}, u32[]{:S(2)}) collective-permute-start(bf16[2,128,1024]{2,1,0:T(8,128)(2,1)S(1)} %fusion.3), channel_id=1, source_target_pairs={{0,4},{1,5},{2,6},{3,7},{12,8},{13,9},{14,10},{15,11},{16,20},{17,... | collective-permute-start | bytes 1572872 | tf_op jit(solution)/shard_map/ppermute | solution.py:434
  69.7 17.1 %collective-permute-start.14 = (bf16[2,128,1024]{2,1,0:T(8,128)(2,1)S(1)}, bf16[2,128,1024]{2,1,0:T(8,128)(2,1)S(1)}, u32[]{:S(2)}, u32[]{:S(2)}) collective-permute-start(bf16[2,128,1024]{2,1,0:T(8,128)(2,1)S(1)} %add_convert_fusion.3), channel_id=1, source_target_pairs={{4,8},{5,9},{6,10},{7,11},{8,4},{9,5},{10,6},{11,7},{20,24},{21,25... | collective-permute-start | bytes 1572872 | tf_op jit(solution)/shard_map/ppermute | solution.py:434
  70.5 17.3 %collective-permute-start.16 = (bf16[2,128,1024]{2,1,0:T(8,128)(2,1)S(1)}, bf16[2,128,1024]{2,1,0:T(8,128)(2,1)S(1)}, u32[]{:S(2)}, u32[]{:S(2)}) collective-permute-start(bf16[2,128,1024]{2,1,0:T(8,128)(2,1)S(1)} %get-tuple-element.103), channel_id=1, source_target_pairs={{0,2},{1,3},{2,0},{3,1},{4,6},{5,7},{6,4},{7,5},{8,10},{9,11},{10,... | collective-permute-start | bytes 1572872 | tf_op jit(solution)/shard_map/ppermute | solution.py:430
  76.4 19.5 %collective-permute-start.9 = (bf16[2,128,1024]{2,1,0:T(8,128)(2,1)S(1)}, bf16[2,128,1024]{2,1,0:T(8,128)(2,1)S(1)}, u32[]{:S(2)}, u32[]{:S(2)}) collective-permute-start(bf16[2,128,1024]{2,1,0:T(8,128)(2,1)S(1)} %add_convert_fusion.6), channel_id=1, source_target_pairs={{4,8},{5,9},{6,10},{7,11},{8,4},{9,5},{10,6},{11,7},{20,24},{21,25... | collective-permute-start | bytes 1572872 | tf_op jit(solution)/shard_map/ppermute | solution.py:434
  77.4 19.9 %collective-permute-start.10 = (bf16[2,128,1024]{2,1,0:T(8,128)(2,1)S(1)}, bf16[2,128,1024]{2,1,0:T(8,128)(2,1)S(1)}, u32[]{:S(2)}, u32[]{:S(2)}) collective-permute-start(bf16[2,128,1024]{2,1,0:T(8,128)(2,1)S(1)} %add_convert_fusion.5), channel_id=1, source_target_pairs={{0,4},{1,5},{2,6},{3,7},{12,8},{13,9},{14,10},{15,11},{4,0},{5,1},... | collective-permute-start | bytes 1572872 | tf_op jit(solution)/shard_map/ppermute | solution.py:434
  82.9 16.1 %collective-permute-start.8 = (bf16[2,128,1024]{2,1,0:T(8,128)(2,1)S(1)}, bf16[2,128,1024]{2,1,0:T(8,128)(2,1)S(1)}, u32[]{:S(2)}, u32[]{:S(2)}) collective-permute-start(bf16[2,128,1024]{2,1,0:T(8,128)(2,1)S(1)} %get-tuple-element.88), channel_id=1, source_target_pairs={{0,2},{1,3},{2,0},{3,1},{4,6},{5,7},{6,4},{7,5},{8,10},{9,11},{10,... | collective-permute-start | bytes 1572872 | tf_op jit(solution)/shard_map/ppermute | solution.py:430
  88.0 11.3 %collective-permute-start.18 = (bf16[2,128,1024]{2,1,0:T(8,128)(2,1)S(1)}, bf16[2,128,1024]{2,1,0:T(8,128)(2,1)S(1)}, u32[]{:S(2)}, u32[]{:S(2)}) collective-permute-start(bf16[2,128,1024]{2,1,0:T(8,128)(2,1)S(1)} %add_convert_fusion.2), channel_id=1, source_target_pairs={{4,8},{5,9},{6,10},{7,11},{8,4},{9,5},{10,6},{11,7},{20,24},{21,25... | collective-permute-start | bytes 1572872 | tf_op jit(solution)/shard_map/ppermute | solution.py:434
  89.2 16.6 %collective-permute-start.19 = (bf16[2,128,1024]{2,1,0:T(8,128)(2,1)S(1)}, bf16[2,128,1024]{2,1,0:T(8,128)(2,1)S(1)}, u32[]{:S(2)}, u32[]{:S(2)}) collective-permute-start(bf16[2,128,1024]{2,1,0:T(8,128)(2,1)S(1)} %add_convert_fusion.1), channel_id=1, source_target_pairs={{0,4},{1,5},{2,6},{3,7},{12,8},{13,9},{14,10},{15,11},{4,0},{5,1},... | collective-permute-start | bytes 1572872 | tf_op jit(solution)/shard_map/ppermute | solution.py:434
  96.0 14.9 %collective-permute-start.17 = (bf16[2,128,1024]{2,1,0:T(8,128)(2,1)S(1)}, bf16[2,128,1024]{2,1,0:T(8,128)(2,1)S(1)}, u32[]{:S(2)}, u32[]{:S(2)}) collective-permute-start(bf16[2,128,1024]{2,1,0:T(8,128)(2,1)S(1)} %get-tuple-element.105), channel_id=1, source_target_pairs={{0,2},{1,3},{2,0},{3,1},{4,6},{5,7},{6,4},{7,5},{8,10},{9,11},{10,... | collective-permute-start | bytes 1572872 | tf_op jit(solution)/shard_map/ppermute | solution.py:430
  99.0 12.2 %copy-start.14 = (bf16[1024,1024]{1,0:T(8,128)(2,1)S(1)}, bf16[1024,1024]{1,0:T(8,128)(2,1)}, u32[]{:S(2)}) copy-start(bf16[1024,1024]{1,0:T(8,128)(2,1)} %constant.43.clone.refs_3_) | copy-start | bytes 6291460
  99.0 12.2 %copy-start.15 = (bf16[1024,1024]{1,0:T(8,128)(2,1)S(1)}, bf16[1024,1024]{1,0:T(8,128)(2,1)}, u32[]{:S(2)}) copy-start(bf16[1024,1024]{1,0:T(8,128)(2,1)} %constant.44.clone.refs_4_) | copy-start | bytes 6291460
  99.0 12.2 %copy-start.16 = (bf16[1,256,1024]{2,1,0:T(8,128)(2,1)S(1)}, bf16[1,256,1024]{2,1,0:T(8,128)(2,1)}, u32[]{:S(2)}) copy-start(bf16[1,256,1024]{2,1,0:T(8,128)(2,1)} %refs_2_.1) | copy-start | bytes 1572868
  116.1 14.8 %collective-permute-start.26 = (bf16[2,128,1024]{2,1,0:T(8,128)(2,1)S(1)}, bf16[2,128,1024]{2,1,0:T(8,128)(2,1)S(1)}, u32[]{:S(2)}, u32[]{:S(2)}) collective-permute-start(bf16[2,128,1024]{2,1,0:T(8,128)(2,1)S(1)} %get-tuple-element.113.refs_0_.refs_1_), channel_id=1, source_target_pairs={{0,2},{1,3},{2,0},{3,1},{4,6},{5,7},{6,4},{7,5},{8,10},{9,11},{10,... | collective-permute-start | bytes 1572872 | tf_op jit(solution)/shard_map/ppermute | solution.py:430
  117.9 16.8 %collective-permute-start.27 = (bf16[2,128,1024]{2,1,0:T(8,128)(2,1)S(1)}, bf16[2,128,1024]{2,1,0:T(8,128)(2,1)}, u32[]{:S(2)}, u32[]{:S(2)}) collective-permute-start(bf16[2,128,1024]{2,1,0:T(8,128)(2,1)S(1)} %get-tuple-element.113.refs_0_.refs_1_), channel_id=1, source_target_pairs={{4,8},{5,9},{6,10},{7,11},{8,4},{9,5},{10,6},{11,7},{20,24},{21,25... | collective-permute-start | bytes 1572872 | tf_op jit(solution)/shard_map/ppermute | solution.py:434
  119.4 15.4 %collective-permute-start.28 = (bf16[2,128,1024]{2,1,0:T(8,128)(2,1)S(1)}, bf16[2,128,1024]{2,1,0:T(8,128)(2,1)}, u32[]{:S(2)}, u32[]{:S(2)}) collective-permute-start(bf16[2,128,1024]{2,1,0:T(8,128)(2,1)S(1)} %get-tuple-element.113.refs_0_.refs_1_), channel_id=1, source_target_pairs={{0,4},{1,5},{2,6},{3,7},{12,8},{13,9},{14,10},{15,11},{4,0},{5,1},... | collective-permute-start | bytes 1572872 | tf_op jit(solution)/shard_map/ppermute | solution.py:434
  122.4 0.8 copy-start.6
  123.2 19.0 %collective-permute-start.20 = (bf16[2,128,1024]{2,1,0:T(8,128)(2,1)S(1)}, bf16[2,128,1024]{2,1,0:T(8,128)(2,1)S(1)}, u32[]{:S(2)}, u32[]{:S(2)}) collective-permute-start(bf16[2,128,1024]{2,1,0:T(8,128)(2,1)S(1)} %get-tuple-element.110.refs_1_.refs_2_), channel_id=1, source_target_pairs={{0,2},{1,3},{2,0},{3,1},{4,6},{5,7},{6,4},{7,5},{8,10},{9,11},{10,... | collective-permute-start | bytes 1572872 | tf_op jit(solution)/shard_map/ppermute | solution.py:430
  123.6 19.4 %collective-permute-start.21 = (bf16[2,128,1024]{2,1,0:T(8,128)(2,1)S(1)}, bf16[2,128,1024]{2,1,0:T(8,128)(2,1)}, u32[]{:S(2)}, u32[]{:S(2)}) collective-permute-start(bf16[2,128,1024]{2,1,0:T(8,128)(2,1)S(1)} %get-tuple-element.110.refs_1_.refs_2_), channel_id=1, source_target_pairs={{4,8},{5,9},{6,10},{7,11},{8,4},{9,5},{10,6},{11,7},{20,24},{21,25... | collective-permute-start | bytes 1572872 | tf_op jit(solution)/shard_map/ppermute | solution.py:434
  130.9 0.8 copy-start.10
  131.7 13.9 %collective-permute-start.22 = (bf16[2,128,1024]{2,1,0:T(8,128)(2,1)S(1)}, bf16[2,128,1024]{2,1,0:T(8,128)(2,1)}, u32[]{:S(2)}, u32[]{:S(2)}) collective-permute-start(bf16[2,128,1024]{2,1,0:T(8,128)(2,1)S(1)} %get-tuple-element.110.refs_1_.refs_2_), channel_id=1, source_target_pairs={{0,4},{1,5},{2,6},{3,7},{12,8},{13,9},{14,10},{15,11},{4,0},{5,1},... | collective-permute-start | bytes 1572872 | tf_op jit(solution)/shard_map/ppermute | solution.py:434
  133.9 0.8 copy-start.8
  134.7 18.6 %collective-permute-start.32 = (bf16[2,128,1024]{2,1,0:T(8,128)(2,1)}, bf16[2,128,1024]{2,1,0:T(8,128)(2,1)S(1)}, u32[]{:S(2)}, u32[]{:S(2)}) collective-permute-start(bf16[2,128,1024]{2,1,0:T(8,128)(2,1)} %collective-permute-done.28.refs_2_.refs_3_), channel_id=1, source_target_pairs={{0,2},{1,3},{2,0},{3,1},{4,6},{5,7},{6,4},{7,5},{8,10},{9,11},{10,... | collective-permute-start | bytes 1572872 | tf_op jit(solution)/shard_map/ppermute | solution.py:430
  136.8 32.1 %collective-permute-start.33 = (bf16[2,128,1024]{2,1,0:T(8,128)(2,1)}, bf16[2,128,1024]{2,1,0:T(8,128)(2,1)}, u32[]{:S(2)}, u32[]{:S(2)}) collective-permute-start(bf16[2,128,1024]{2,1,0:T(8,128)(2,1)} %collective-permute-done.28.refs_2_.refs_3_), channel_id=1, source_target_pairs={{4,8},{5,9},{6,10},{7,11},{8,4},{9,5},{10,6},{11,7},{20,24},{21,25... | collective-permute-start | bytes 1572872 | tf_op jit(solution)/shard_map/ppermute | solution.py:434
  142.1 0.8 copy-start.12
  145.6 23.3 %collective-permute-start.34 = (bf16[2,128,1024]{2,1,0:T(8,128)(2,1)}, bf16[2,128,1024]{2,1,0:T(8,128)(2,1)}, u32[]{:S(2)}, u32[]{:S(2)}) collective-permute-start(bf16[2,128,1024]{2,1,0:T(8,128)(2,1)} %collective-permute-done.27), channel_id=1, source_target_pairs={{4,0},{5,1},{6,2},{7,3},{8,12},{9,13},{10,14},{11,15},{20,16},{21,... | collective-permute-start | bytes 1572872 | tf_op jit(solution)/shard_map/ppermute | solution.py:434
  146.9 22.0 %collective-permute-start.23 = (bf16[2,128,1024]{2,1,0:T(8,128)(2,1)}, bf16[2,128,1024]{2,1,0:T(8,128)(2,1)}, u32[]{:S(2)}, u32[]{:S(2)}) collective-permute-start(bf16[2,128,1024]{2,1,0:T(8,128)(2,1)} %collective-permute-done.22.refs_3_.refs_4_), channel_id=1, source_target_pairs={{0,2},{1,3},{2,0},{3,1},{4,6},{5,7},{6,4},{7,5},{8,10},{9,11},{10,... | collective-permute-start | bytes 1572872 | tf_op jit(solution)/shard_map/ppermute | solution.py:430
  148.1 20.8 %collective-permute-start.24 = (bf16[2,128,1024]{2,1,0:T(8,128)(2,1)}, bf16[2,128,1024]{2,1,0:T(8,128)(2,1)}, u32[]{:S(2)}, u32[]{:S(2)}) collective-permute-start(bf16[2,128,1024]{2,1,0:T(8,128)(2,1)} %collective-permute-done.22.refs_3_.refs_4_), channel_id=1, source_target_pairs={{4,8},{5,9},{6,10},{7,11},{8,4},{9,5},{10,6},{11,7},{20,24},{21,25... | collective-permute-start | bytes 1572872 | tf_op jit(solution)/shard_map/ppermute | solution.py:434
  153.4 0.8 copy-start.4
  154.2 17.6 %collective-permute-start.25 = (bf16[2,128,1024]{2,1,0:T(8,128)(2,1)}, bf16[2,128,1024]{2,1,0:T(8,128)(2,1)}, u32[]{:S(2)}, u32[]{:S(2)}) collective-permute-start(bf16[2,128,1024]{2,1,0:T(8,128)(2,1)} %collective-permute-done.21), channel_id=1, source_target_pairs={{4,0},{5,1},{6,2},{7,3},{8,12},{9,13},{10,14},{11,15},{20,16},{21,... | collective-permute-start | bytes 1572872 | tf_op jit(solution)/shard_map/ppermute | solution.py:434
  155.5 3.4 %copy-start.3 = (f32[2,128,8192]{2,1,0:T(8,128)S(1)}, f32[2,128,8192]{2,1,0:T(8,128)}, u32[]{:S(2)}) copy-start(f32[2,128,8192]{2,1,0:T(8,128)} %refs_0_.1) | copy-start | bytes 25165828
  158.9 1.0 copy-start.7
  159.9 1.0 copy-start.9
  160.9 1.0 copy-start.11
  162.0 1.0 copy-start.13
  168.9 9.9 %copy-start.5 = (bf16[2,128,1024]{2,1,0:T(8,128)(2,1)S(1)}, bf16[2,128,1024]{2,1,0:T(8,128)(2,1)}, u32[]{:S(2)}) copy-start(bf16[2,128,1024]{2,1,0:T(8,128)(2,1)} %copy-done.4) | copy-start | bytes 1572868
  172.9 14.9 %collective-permute-start.35 = (bf16[2,128,1024]{2,1,0:T(8,128)(2,1)S(1)}, bf16[2,128,1024]{2,1,0:T(8,128)(2,1)S(1)}, u32[]{:S(2)}, u32[]{:S(2)}) collective-permute-start(bf16[2,128,1024]{2,1,0:T(8,128)(2,1)S(1)} %broadcast_select_fusion.1.refs_1_), channel_id=1, source_target_pairs={{0,2},{1,3},{2,0},{3,1},{4,6},{5,7},{6,4},{7,5},{8,10},{9,11},{10,... | collective-permute-start | bytes 1572872 | tf_op jit(solution)/shard_map/ppermute | solution.py:430
  173.1 19.1 %collective-permute-start.36 = (bf16[2,128,1024]{2,1,0:T(8,128)(2,1)}, bf16[2,128,1024]{2,1,0:T(8,128)(2,1)S(1)}, u32[]{:S(2)}, u32[]{:S(2)}) collective-permute-start(bf16[2,128,1024]{2,1,0:T(8,128)(2,1)} %collective-permute-done.33), channel_id=1, source_target_pairs={{4,0},{5,1},{6,2},{7,3},{8,12},{9,13},{10,14},{11,15},{20,16},{21,... | collective-permute-start | bytes 1572872 | tf_op jit(solution)/shard_map/ppermute | solution.py:434
  175.5 20.3 %collective-permute-start.29 = (bf16[2,128,1024]{2,1,0:T(8,128)(2,1)S(1)}, bf16[2,128,1024]{2,1,0:T(8,128)(2,1)S(1)}, u32[]{:S(2)}, u32[]{:S(2)}) collective-permute-start(bf16[2,128,1024]{2,1,0:T(8,128)(2,1)S(1)} %broadcast_select_fusion.3.refs_2_), channel_id=1, source_target_pairs={{0,2},{1,3},{2,0},{3,1},{4,6},{5,7},{6,4},{7,5},{8,10},{9,11},{10,... | collective-permute-start | bytes 1572872 | tf_op jit(solution)/shard_map/ppermute | solution.py:430
  177.4 24.1 %collective-permute-start.30 = (bf16[2,128,1024]{2,1,0:T(8,128)(2,1)}, bf16[2,128,1024]{2,1,0:T(8,128)(2,1)S(1)}, u32[]{:S(2)}, u32[]{:S(2)}) collective-permute-start(bf16[2,128,1024]{2,1,0:T(8,128)(2,1)} %collective-permute-done.24), channel_id=1, source_target_pairs={{4,0},{5,1},{6,2},{7,3},{8,12},{9,13},{10,14},{11,15},{20,16},{21,... | collective-permute-start | bytes 1572872 | tf_op jit(solution)/shard_map/ppermute | solution.py:434
  201.6 14.9 %collective-permute-start.31 = (bf16[2,128,1024]{2,1,0:T(8,128)(2,1)S(1)}, bf16[2,128,1024]{2,1,0:T(8,128)(2,1)S(1)}, u32[]{:S(2)}, u32[]{:S(2)}) collective-permute-start(bf16[2,128,1024]{2,1,0:T(8,128)(2,1)S(1)} %broadcast_select_fusion.2.refs_6_.refs_2_), channel_id=1, source_target_pairs={{0,2},{1,3},{2,0},{3,1},{4,6},{5,7},{6,4},{7,5},{8,10},{9,11},{10,... | collective-permute-start | bytes 1572872 | tf_op jit(solution)/shard_map/ppermute | solution.py:430
  202.4 22.7 %collective-permute-start.41 = (bf16[2,128,1024]{2,1,0:T(8,128)(2,1)S(1)}, bf16[2,128,1024]{2,1,0:T(8,128)(2,1)S(1)}, u32[]{:S(2)}, u32[]{:S(2)}) collective-permute-start(bf16[2,128,1024]{2,1,0:T(8,128)(2,1)S(1)} %broadcast_select_fusion.refs_5_.refs_1_), channel_id=1, source_target_pairs={{0,2},{1,3},{2,0},{3,1},{4,6},{5,7},{6,4},{7,5},{8,10},{9,11},{10,... | collective-permute-start | bytes 1572872 | tf_op jit(solution)/shard_map/ppermute | solution.py:430
  209.5 16.1 %collective-permute-start.37 = (bf16[2,128,2048]{2,1,0:T(8,128)(2,1)S(1)}, bf16[2,128,2048]{2,1,0:T(8,128)(2,1)S(1)}, u32[]{:S(2)}, u32[]{:S(2)}) collective-permute-start(bf16[2,128,2048]{2,1,0:T(8,128)(2,1)S(1)} %get-tuple-element.132), channel_id=1, source_target_pairs={{0,1},{1,0},{2,3},{3,2},{4,5},{5,4},{6,7},{7,6},{8,9},{9,8},{10,11... | collective-permute-start | bytes 3145736 | tf_op jit(solution)/shard_map/ppermute | solution.py:427
  209.6 16.0 %collective-permute-start.38 = (bf16[2,128,2048]{2,1,0:T(8,128)(2,1)S(1)}, bf16[2,128,2048]{2,1,0:T(8,128)(2,1)S(1)}, u32[]{:S(2)}, u32[]{:S(2)}) collective-permute-start(bf16[2,128,2048]{2,1,0:T(8,128)(2,1)S(1)} %get-tuple-element.133), channel_id=1, source_target_pairs={{0,1},{1,0},{2,3},{3,2},{4,5},{5,4},{6,7},{7,6},{8,9},{9,8},{10,11... | collective-permute-start | bytes 3145736 | tf_op jit(solution)/shard_map/ppermute | solution.py:427
  210.1 15.5 %collective-permute-start.39 = (bf16[2,128,2048]{2,1,0:T(8,128)(2,1)S(1)}, bf16[2,128,2048]{2,1,0:T(8,128)(2,1)S(1)}, u32[]{:S(2)}, u32[]{:S(2)}) collective-permute-start(bf16[2,128,2048]{2,1,0:T(8,128)(2,1)S(1)} %get-tuple-element.134), channel_id=1, source_target_pairs={{0,1},{1,0},{2,3},{3,2},{4,5},{5,4},{6,7},{7,6},{8,9},{9,8},{10,11... | collective-permute-start | bytes 3145736 | tf_op jit(solution)/shard_map/ppermute | solution.py:427
  216.6 8.5 %collective-permute-start.42 = (bf16[2,128,1024]{2,1,0:T(8,128)(2,1)S(1)}, bf16[2,128,1024]{2,1,0:T(8,128)(2,1)S(1)}, u32[]{:S(2)}, u32[]{:S(2)}) collective-permute-start(bf16[2,128,1024]{2,1,0:T(8,128)(2,1)S(1)} %collective-permute-done.31.refs_6_), channel_id=1, source_target_pairs={{0,1},{1,0},{2,3},{3,2},{4,5},{5,4},{6,7},{7,6},{8,9},{9,8},{10,11... | collective-permute-start | bytes 1572872 | tf_op jit(solution)/shard_map/ppermute | solution.py:427
  225.1 2.7 %collective-permute-start.40 = (bf16[2,128,2048]{2,1,0:T(8,128)(2,1)S(1)}, bf16[2,128,2048]{2,1,0:T(8,128)(2,1)S(1)}, u32[]{:S(2)}, u32[]{:S(2)}) collective-permute-start(bf16[2,128,2048]{2,1,0:T(8,128)(2,1)S(1)} %get-tuple-element.135), channel_id=1, source_target_pairs={{0,1},{1,0},{2,3},{3,2},{4,5},{5,4},{6,7},{7,6},{8,9},{9,8},{10,11... | collective-permute-start | bytes 3145736 | tf_op jit(solution)/shard_map/ppermute | solution.py:427
  225.1 3.4 %collective-permute-start.43 = (bf16[2,128,1024]{2,1,0:T(8,128)(2,1)S(1)}, bf16[2,128,1024]{2,1,0:T(8,128)(2,1)S(1)}, u32[]{:S(2)}, u32[]{:S(2)}) collective-permute-start(bf16[2,128,1024]{2,1,0:T(8,128)(2,1)S(1)} %collective-permute-done.41.refs_5_), channel_id=1, source_target_pairs={{0,1},{1,0},{2,3},{3,2},{4,5},{5,4},{6,7},{7,6},{8,9},{9,8},{10,11... | collective-permute-start | bytes 1572872 | tf_op jit(solution)/shard_map/ppermute | solution.py:427

commit v9 on v8

--- a/solution.py
+++ b/solution.py
@@ -535,14 +535,18 @@
         from_far = jnp.where(at_ends, pieces["far outward", stream], pieces["far inner", stream])
         pieces[("far", 0), stream] = from_far
         pieces[("far", 2), stream] = across(from_far)
-    slab = [sibling(chunk) for chunk in apply([pieces["slab", last]], late, 4)]
-    result = apply([pieces["result", last]], later + late)
-    pieces[("far", 2), lead], result = together((pieces[("far", 2), lead], result))
-    pieces[("far", 3), lead] = sibling(pieces[("far", 2), lead])
-    pieces[("far", 2), last], pieces[("far", 3), lead] = together(
-        (pieces[("far", 2), last], pieces[("far", 3), lead])
-    )
-    pieces[("far", 3), last] = sibling(pieces[("far", 2), last])
+    far_other = pieces[("far", 2), lead]
+    slab, far_other = together((pieces["slab", last], far_other))
+    chunks = apply([slab], late, 4)
+    twin = sibling(far_other)
+    slab = [sibling(chunk) for chunk in chunks[:-1]]
+    result, twin = together((pieces["result", last], twin))
+    result = apply([result], later + late)
+    chunk, result = together((chunks[-1], result))
+    slab.append(sibling(chunk))
+    arriving, result = together((pieces[("far", 2), last], result))
+    pieces[("far", 2), lead], pieces[("far", 3), lead] = far_other, twin
+    pieces[("far", 2), last], pieces[("far", 3), last] = arriving, sibling(arriving)
     return apply([result] + slab, [("far", 2), ("far", 3)])
 
 

time: 234 us -> 226 us (0.966)
  the two profiles are of different devices: /device:TPU:0 before, /device:TPU:11 now
where the time goes in v9:
time: 226 us; the launch traced here: 224 us
  waiting for transfers between devices  84.9 us (38%)
  starting transfers between devices  69.2 us (31%)
  Pallas kernels  51.2 us (23%)
  local copies, waits for them, and re-layouts  11.2 us (5%)
  other arithmetic  6.66 us (3%)
    ppermute x16, waiting for transfers between devices, across(): return lax.ppermute(value, 'ty', [(i, i ^ 2) for i in range(count)])  53.8 us
    ppermute x20, starting transfers between devices, along(): return lax.ppermute(value, 'ty', pairs)  48.4 us
    ppermute x20, waiting for transfers between devices, along(): return lax.ppermute(value, 'ty', pairs)  27.7 us
    pallas_call x6, Pallas kernels, backward(): pl.pallas_call(functools.partial(kernel, slots=slots, held=held, parts=le...  22.9 us
    pallas_call x3, Pallas kernels, forward(): pl.pallas_call(functools.partial(forward_kernel, base=base, images=images...  19 us
    ppermute x16, starting transfers between devices, across(): return lax.ppermute(value, 'ty', [(i, i ^ 2) for i in range(count)])  15 us
    unnamed x28, local copies, waits for them, and re-layouts  10.5 us
    ppermute x8, starting transfers between devices, sibling(): return lax.ppermute(value, 'ty', [(i, i ^ 1) for i in range(count)])  5.82 us
  transfers between devices with their start and end apart: 44, of which 24 were waited for; matrix products, arithmetic and copies ran while one was open for 3% of the time, Pallas kernels for 16%

profile of v9, /device:TPU:11, one launch (start us, length us, event | category | flops | bytes accessed | tf_op | source)
XLA Modules:
  0.0 223.8 jit_solution(14550948825715036075)
XLA Ops:
  0.0 3.4 %copy-done.2 = f32[2,128,8192]{2,1,0:T(8,128)S(1)} copy-done((f32[2,128,8192]{2,1,0:T(8,128)S(1)}, f32[2,128,8192]{2,1,0:T(8,128)}, u32[]{:S(2)}) %copy-start.2) | copy-done | bytes 8388632
  3.4 1.9 low_part.3.refs_1_
  6.1 1.8 low_part.2.refs_0_
  9.0 2.3 %forward.3.refs_2_ = bf16[2,256,1024]{2,1,0:T(8,128)(2,1)S(1)} custom-call(s32[3,16]{1,0:T(4,128)S(1)} %pad_add_fusion.meta_ref, bf16[1024,1024]{1,0:T(8,128)(2,1)S(1)} %copy-done, bf16[1024,512]{1,0:T(8,128)(2,1)S(1)} %copy-done.1, bf16[128,8192]{1,0:T(8,128)(2,1)} %low_part.2.refs_0_, bf16[128,8192]{1,0:T(8,128)(2,1)} %low_part.3.refs_1_), custom_call_target="tpu_custom_call" | custom-call | flops 1024 | bytes 1024 | tf_op jit(solution)/shard_map/forward/pallas_call | solution.py:257
  11.3 1.9 collective-permute-done.refs_0_.refs_2_
  13.2 2.3 %forward.4 = (bf16[2,128,1024]{2,1,0:T(8,128)(2,1)S(1)}, bf16[2,128,1024]{2,1,0:T(8,128)(2,1)S(1)}) custom-call(s32[3,16]{1,0:T(4,128)S(1)} %pad_add_fusion.meta_ref, bf16[1024,1024]{1,0:T(8,128)(2,1)S(1)} %copy-done, bf16[1024,512]{1,0:T(8,128)(2,1)S(1)} %copy-done.1, bf16[128,8192]{1,0:T(8,128)(2,1)} %collective-permute-done.refs_0_.refs_2_, ...), custom_call_target="tpu_custom_call" | custom-call | flops 1024 | bytes 1024 | tf_op jit(solution)/shard_map/forward/pallas_call | solution.py:257
  15.5 2.3 %collective-permute-start.2 = (bf16[2,128,1024]{2,1,0:T(8,128)(2,1)S(1)}, bf16[2,128,1024]{2,1,0:T(8,128)(2,1)S(1)}, u32[]{:S(2)}, u32[]{:S(2)}) collective-permute-start(bf16[2,128,1024]{2,1,0:T(8,128)(2,1)S(1)} %get-tuple-element.80), channel_id=1, source_target_pairs={{0,2},{1,3},{2,0},{3,1},{4,6},{5,7},{6,4},{7,5},{8,10},{9,11},{10,... | collective-permute-start | bytes 1572872 | tf_op jit(solution)/shard_map/ppermute | solution.py:430
  17.9 14.4 %forward.5 = (bf16[2,128,1024]{2,1,0:T(8,128)(2,1)S(1)}, bf16[2,128,1024]{2,1,0:T(8,128)(2,1)S(1)}, bf16[2,128,1024]{2,1,0:T(8,128)(2,1)S(1)}, bf16[2,128,1024]{...) custom-call(s32[3,16]{1,0:T(4,128)S(1)} %pad_add_fusion.meta_ref, ...), custom_call_target="tpu_custom_call" | custom-call | flops 1024 | bytes 1024 | tf_op jit(solution)/shard_map/forward/pallas_call | solution.py:257
  32.5 1.3 collective-permute-start.3
  33.8 3.5 %collective-permute-start.4 = (bf16[2,128,1024]{2,1,0:T(8,128)(2,1)S(1)}, bf16[2,128,1024]{2,1,0:T(8,128)(2,1)S(1)}, u32[]{:S(2)}, u32[]{:S(2)}) collective-permute-start(bf16[2,128,1024]{2,1,0:T(8,128)(2,1)S(1)} %get-tuple-element.85), channel_id=1, source_target_pairs={{0,2},{1,3},{2,0},{3,1},{4,6},{5,7},{6,4},{7,5},{8,10},{9,11},{10,... | collective-permute-start | bytes 1572872 | tf_op jit(solution)/shard_map/ppermute | solution.py:430
  37.3 3.2 %collective-permute-done.11 = bf16[2,128,1024]{2,1,0:T(8,128)(2,1)S(1)} collective-permute-done((bf16[2,128,1024]{2,1,0:T(8,128)(2,1)S(1)}, bf16[2,128,1024]{2,1,0:T(8,128)(2,1)S(1)}, u32[]{:S(2)}, u32[]{:S(2)}) %collective-permute-start.11) | collective-permute-done | bytes 524320 | tf_op jit(solution)/shard_map/ppermute | solution.py:430
  40.7 1.3 collective-permute-start.12
  42.0 1.8 collective-permute-start.13
  43.8 4.5 %collective-permute-done.3 = bf16[2,128,1024]{2,1,0:T(8,128)(2,1)S(1)} collective-permute-done((bf16[2,128,1024]{2,1,0:T(8,128)(2,1)S(1)}, bf16[2,128,1024]{2,1,0:T(8,128)(2,1)S(1)}, u32[]{:S(2)}, u32[]{:S(2)}) %collective-permute-start.3) | collective-permute-done | bytes 524320 | tf_op jit(solution)/shard_map/ppermute | solution.py:434
  48.3 3.5 %collective-permute-done.4 = bf16[2,128,1024]{2,1,0:T(8,128)(2,1)S(1)} collective-permute-done((bf16[2,128,1024]{2,1,0:T(8,128)(2,1)S(1)}, bf16[2,128,1024]{2,1,0:T(8,128)(2,1)S(1)}, u32[]{:S(2)}, u32[]{:S(2)}) %collective-permute-start.4) | collective-permute-done | bytes 524320 | tf_op jit(solution)/shard_map/ppermute | solution.py:430
  51.9 1.3 collective-permute-start.6
  53.5 4.5 %collective-permute-start.5 = (bf16[2,128,1024]{2,1,0:T(8,128)(2,1)S(1)}, bf16[2,128,1024]{2,1,0:T(8,128)(2,1)S(1)}, u32[]{:S(2)}, u32[]{:S(2)}) collective-permute-start(bf16[2,128,1024]{2,1,0:T(8,128)(2,1)S(1)} %add_convert_fusion.7), channel_id=1, source_target_pairs={{4,8},{5,9},{6,10},{7,11},{8,4},{9,5},{10,6},{11,7},{20,24},{21,25... | collective-permute-start | bytes 1572872 | tf_op jit(solution)/shard_map/ppermute | solution.py:434
  58.0 1.3 collective-permute-start.7
  59.4 3.5 %collective-permute-done.13 = bf16[2,128,1024]{2,1,0:T(8,128)(2,1)S(1)} collective-permute-done((bf16[2,128,1024]{2,1,0:T(8,128)(2,1)S(1)}, bf16[2,128,1024]{2,1,0:T(8,128)(2,1)S(1)}, u32[]{:S(2)}, u32[]{:S(2)}) %collective-permute-start.13) | collective-permute-done | bytes 524320 | tf_op jit(solution)/shard_map/ppermute | solution.py:430
  63.2 1.3 collective-permute-start.15
  64.7 4.5 %collective-permute-start.14 = (bf16[2,128,1024]{2,1,0:T(8,128)(2,1)S(1)}, bf16[2,128,1024]{2,1,0:T(8,128)(2,1)S(1)}, u32[]{:S(2)}, u32[]{:S(2)}) collective-permute-start(bf16[2,128,1024]{2,1,0:T(8,128)(2,1)S(1)} %add_convert_fusion.3), channel_id=1, source_target_pairs={{4,8},{5,9},{6,10},{7,11},{8,4},{9,5},{10,6},{11,7},{20,24},{21,25... | collective-permute-start | bytes 1572872 | tf_op jit(solution)/shard_map/ppermute | solution.py:434
  69.2 1.4 collective-permute-done.6
  70.8 3.4 %collective-permute-done.7 = bf16[2,128,1024]{2,1,0:T(8,128)(2,1)S(1)} collective-permute-done((bf16[2,128,1024]{2,1,0:T(8,128)(2,1)S(1)}, bf16[2,128,1024]{2,1,0:T(8,128)(2,1)S(1)}, u32[]{:S(2)}, u32[]{:S(2)}) %collective-permute-start.7) | collective-permute-done | bytes 524320 | tf_op jit(solution)/shard_map/ppermute | solution.py:430
  74.5 4.3 %collective-permute-start.9 = (bf16[2,128,1024]{2,1,0:T(8,128)(2,1)S(1)}, bf16[2,128,1024]{2,1,0:T(8,128)(2,1)S(1)}, u32[]{:S(2)}, u32[]{:S(2)}) collective-permute-start(bf16[2,128,1024]{2,1,0:T(8,128)(2,1)S(1)} %add_convert_fusion.6), channel_id=1, source_target_pairs={{4,8},{5,9},{6,10},{7,11},{8,4},{9,5},{10,6},{11,7},{20,24},{21,25... | collective-permute-start | bytes 1572872 | tf_op jit(solution)/shard_map/ppermute | solution.py:434
  78.8 1.5 collective-permute-start.8
  80.5 1.4 collective-permute-done.15
  82.4 10.0 %collective-permute-start.18 = (bf16[2,128,1024]{2,1,0:T(8,128)(2,1)S(1)}, bf16[2,128,1024]{2,1,0:T(8,128)(2,1)S(1)}, u32[]{:S(2)}, u32[]{:S(2)}) collective-permute-start(bf16[2,128,1024]{2,1,0:T(8,128)(2,1)S(1)} %add_convert_fusion.2), channel_id=1, source_target_pairs={{4,8},{5,9},{6,10},{7,11},{8,4},{9,5},{10,6},{11,7},{20,24},{21,25... | collective-permute-start | bytes 1572872 | tf_op jit(solution)/shard_map/ppermute | solution.py:434
  93.3 1.6 collective-permute-done.10
  95.3 7.0 %collective-permute-done.18 = bf16[2,128,1024]{2,1,0:T(8,128)(2,1)S(1)} collective-permute-done((bf16[2,128,1024]{2,1,0:T(8,128)(2,1)S(1)}, bf16[2,128,1024]{2,1,0:T(8,128)(2,1)S(1)}, u32[]{:S(2)}, u32[]{:S(2)}) %collective-permute-start.18) | collective-permute-done | bytes 524320 | tf_op jit(solution)/shard_map/ppermute | solution.py:434
  102.3 4.1 %collective-permute-done.17 = bf16[2,128,1024]{2,1,0:T(8,128)(2,1)S(1)} collective-permute-done((bf16[2,128,1024]{2,1,0:T(8,128)(2,1)S(1)}, bf16[2,128,1024]{2,1,0:T(8,128)(2,1)S(1)}, u32[]{:S(2)}, u32[]{:S(2)}) %collective-permute-start.17) | collective-permute-done | bytes 524320 | tf_op jit(solution)/shard_map/ppermute | solution.py:430
  106.8 5.6 %middle.1 = (bf16[2,128,1024]{2,1,0:T(8,128)(2,1)}, bf16[2,128,1024]{2,1,0:T(8,128)(2,1)S(1)}) custom-call(bf16[2,128,1024]{2,1,0:T(8,128)(2,1)S(1)} %add_convert_fusion.refs_0_, bf16[2,128,1024]{2,1,0:T(8,128)(2,1)S(1)} %add_convert_fusion.4.refs_1_, bf16[1,256,1024]{2,1,0:T(8,128)(2,1)S(1)} %copy-done.11, bf16[1024,1024]{1,0:T(8,128)(2,1)S(1)} %copy-done.10, ...), custom_call_target="tpu_custom_call" | custom-call | flops 1024 | bytes 1024 | tf_op jit(solution)/shard_map/middle/pallas_call | solution.py:295
  112.4 6.8 %collective-permute-start.27 = (bf16[2,128,1024]{2,1,0:T(8,128)(2,1)S(1)}, bf16[2,128,1024]{2,1,0:T(8,128)(2,1)}, u32[]{:S(2)}, u32[]{:S(2)}) collective-permute-start(bf16[2,128,1024]{2,1,0:T(8,128)(2,1)S(1)} %get-tuple-element.117.refs_2_.refs_1_), channel_id=1, source_target_pairs={{4,8},{5,9},{6,10},{7,11},{8,4},{9,5},{10,6},{11,7},{20,24},{21,25... | collective-permute-start | bytes 1572872 | tf_op jit(solution)/shard_map/ppermute | solution.py:434
  119.8 0.8 copy-done.4
  120.6 2.4 %collective-permute-start.21 = (bf16[2,128,1024]{2,1,0:T(8,128)(2,1)}, bf16[2,128,1024]{2,1,0:T(8,128)(2,1)}, u32[]{:S(2)}, u32[]{:S(2)}) collective-permute-start(bf16[2,128,1024]{2,1,0:T(8,128)(2,1)} %get-tuple-element.114.refs_1_.refs_0_), channel_id=1, source_target_pairs={{4,8},{5,9},{6,10},{7,11},{8,4},{9,5},{10,6},{11,7},{20,24},{21,25... | collective-permute-start | bytes 1572872 | tf_op jit(solution)/shard_map/ppermute | solution.py:434
  123.5 7.7 %collective-permute-done.27 = bf16[2,128,1024]{2,1,0:T(8,128)(2,1)} collective-permute-done((bf16[2,128,1024]{2,1,0:T(8,128)(2,1)S(1)}, bf16[2,128,1024]{2,1,0:T(8,128)(2,1)}, u32[]{:S(2)}, u32[]{:S(2)}) %collective-permute-start.27) | collective-permute-done | bytes 524320 | tf_op jit(solution)/shard_map/ppermute | solution.py:434
  131.2 0.9 collective-permute-done.26.refs_6_.refs_5_
  132.9 2.1 collective-permute-start.33
  135.0 2.5 %collective-permute-start.32 = (bf16[2,128,1024]{2,1,0:T(8,128)(2,1)}, bf16[2,128,1024]{2,1,0:T(8,128)(2,1)}, u32[]{:S(2)}, u32[]{:S(2)}) collective-permute-start(bf16[2,128,1024]{2,1,0:T(8,128)(2,1)} %collective-permute-done.28.refs_4_.refs_3_), channel_id=1, source_target_pairs={{4,8},{5,9},{6,10},{7,11},{8,4},{9,5},{10,6},{11,7},{20,24},{21,25... | collective-permute-start | bytes 1572872 | tf_op jit(solution)/shard_map/ppermute | solution.py:434
  137.6 1.0 collective-permute-start.31
  138.6 3.9 %collective-permute-done.21 = bf16[2,128,1024]{2,1,0:T(8,128)(2,1)} collective-permute-done((bf16[2,128,1024]{2,1,0:T(8,128)(2,1)}, bf16[2,128,1024]{2,1,0:T(8,128)(2,1)}, u32[]{:S(2)}, u32[]{:S(2)}) %collective-permute-start.21) | collective-permute-done | bytes 524320 | tf_op jit(solution)/shard_map/ppermute | solution.py:434
  142.5 0.9 collective-permute-done.20.refs_5_.refs_4_
  143.4 1.3 collective-permute-start.25
  144.7 2.2 collective-permute-start.24
  146.9 1.0 copy-done.5
  147.9 1.0 copy-done.8
  149.0 5.0 %backward.7.refs_0_ = bf16[2,128,8192]{2,1,0:T(8,128)(2,1)S(1)} custom-call(s32[3,16]{1,0:T(4,128)S(1)} %pad_add_fusion.meta_ref, bf16[1024,1024]{1,0:T(8,128)(2,1)S(1)} %copy-done, bf16[1024,512]{1,0:T(8,128)(2,1)S(1)} %copy-done.1, bf16[2,128,1024]{2,1,0:T(8,128)(2,1)} %get-tuple-element.114.refs_1_.refs_0_, bf16[2,128,1024]{2,1,0:T(8,128)(2,1)S(1)} %copy-done.5, ...), custom_call_target="tpu_custom_call" | custom-call | flops 1024 | bytes 1024 | tf_op jit(solution)/shard_map/backward/pallas_call | solution.py:279
  154.6 1.1 broadcast_select_fusion.2.refs_2_
  155.7 1.0 collective-permute-start.35
  156.7 1.3 collective-permute-start.36
  158.1 3.4 %copy-done.3 = f32[2,128,8192]{2,1,0:T(8,128)S(1)} copy-done((f32[2,128,8192]{2,1,0:T(8,128)S(1)}, f32[2,128,8192]{2,1,0:T(8,128)}, u32[]{:S(2)}) %copy-start.3) | copy-done | bytes 8388632
  161.4 4.8 %backward.6.refs_0_ = f32[2,128,8192]{2,1,0:T(8,128)S(1)} custom-call(s32[3,16]{1,0:T(4,128)S(1)} %pad_add_fusion.meta_ref, bf16[1024,1024]{1,0:T(8,128)(2,1)S(1)} %copy-done, bf16[1024,512]{1,0:T(8,128)(2,1)S(1)} %copy-done.1, f32[2,128,8192]{2,1,0:T(8,128)S(1)} %copy-done.3, bf16[2,128,1024]{2,1,0:T(8,128)(2,1)} %get-tuple-element.114.refs_1_.refs_0_, ...), custom_call_target="tpu_custom_call" | custom-call | flops 1024 | bytes 1024 | tf_op jit(solution)/shard_map/backward/pallas_call | solution.py:279
  166.2 1.1 broadcast_select_fusion.3.refs_1_
  167.9 1.3 collective-permute-start.30
  169.3 7.5 %collective-permute-done.35.refs_4_.refs_8_ = bf16[2,128,1024]{2,1,0:T(8,128)(2,1)S(1)} collective-permute-done((bf16[2,128,1024]{2,1,0:T(8,128)(2,1)S(1)}, bf16[2,128,1024]{2,1,0:T(8,128)(2,1)S(1)}, u32[]{:S(2)}, u32[]{:S(2)}) %collective-permute-start.35) | collective-permute-done | bytes 524320 | tf_op jit(solution)/shard_map/ppermute | solution.py:430
  176.8 1.1 broadcast_select_fusion.refs_2_.refs_6_
  178.0 2.9 %backward.8.refs_0_ = bf16[2,128,8192]{2,1,0:T(8,128)(2,1)S(1)} custom-call(s32[3,16]{1,0:T(4,128)S(1)} %pad_add_fusion.meta_ref, bf16[1024,1024]{1,0:T(8,128)(2,1)S(1)} %copy-done, bf16[1024,512]{1,0:T(8,128)(2,1)S(1)} %copy-done.1, bf16[2,128,8192]{2,1,0:T(8,128)(2,1)S(1)} %backward.7.refs_0_, bf16[2,128,1024]{2,1,0:T(8,128)(2,1)S(1)} %broadcast_select_fusion.3.refs_1_, ...), custom_call_target="tpu_custom_call" | custom-call | flops 1024 | bytes 1024 | tf_op jit(solution)/shard_map/backward/pallas_call | solution.py:279
  180.8 7.2 %collective-permute-done.29.refs_3_.refs_7_ = bf16[2,128,1024]{2,1,0:T(8,128)(2,1)S(1)} collective-permute-done((bf16[2,128,1024]{2,1,0:T(8,128)(2,1)S(1)}, bf16[2,128,1024]{2,1,0:T(8,128)(2,1)S(1)}, u32[]{:S(2)}, u32[]{:S(2)}) %collective-permute-start.29) | collective-permute-done | bytes 524320 | tf_op jit(solution)/shard_map/ppermute | solution.py:430
  188.0 11.2 %collective-permute-done.37.refs_6_ = bf16[2,128,1024]{2,1,0:T(8,128)(2,1)S(1)} collective-permute-done((bf16[2,128,1024]{2,1,0:T(8,128)(2,1)S(1)}, bf16[2,128,1024]{2,1,0:T(8,128)(2,1)S(1)}, u32[]{:S(2)}, u32[]{:S(2)}) %collective-permute-start.37) | collective-permute-done | bytes 524320 | tf_op jit(solution)/shard_map/ppermute | solution.py:430
  199.2 3.1 %collective-permute-start.38 = (bf16[2,128,1024]{2,1,0:T(8,128)(2,1)S(1)}, bf16[2,128,1024]{2,1,0:T(8,128)(2,1)S(1)}, u32[]{:S(2)}, u32[]{:S(2)}) collective-permute-start(bf16[2,128,1024]{2,1,0:T(8,128)(2,1)S(1)} %collective-permute-done.37.refs_6_), channel_id=1, source_target_pairs={{0,1},{1,0},{2,3},{3,2},{4,5},{5,4},{6,7},{7,6},{8,9},{9,8},{10,11... | collective-permute-start | bytes 1572872 | tf_op jit(solution)/shard_map/ppermute | solution.py:427
  202.5 1.5 backward.9
  204.8 3.3 %backward.10.refs_0_ = f32[2,128,8192]{2,1,0:T(8,128)S(1)} custom-call(s32[3,16]{1,0:T(4,128)S(1)} %pad_add_fusion.meta_ref, bf16[1024,1024]{1,0:T(8,128)(2,1)S(1)} %copy-done, bf16[1024,512]{1,0:T(8,128)(2,1)S(1)} %copy-done.1, f32[2,128,8192]{2,1,0:T(8,128)S(1)} %backward.6.refs_0_, bf16[2,128,1024]{2,1,0:T(8,128)(2,1)S(1)} %broadcast_select_fusion.3.refs_1_, ...), custom_call_target="tpu_custom_call" | custom-call | flops 1024 | bytes 1024 | tf_op jit(solution)/shard_map/backward/pallas_call | solution.py:279
  208.4 7.6 %collective-permute-done.34.refs_5_ = bf16[2,128,1024]{2,1,0:T(8,128)(2,1)S(1)} collective-permute-done((bf16[2,128,1024]{2,1,0:T(8,128)(2,1)S(1)}, bf16[2,128,1024]{2,1,0:T(8,128)(2,1)S(1)}, u32[]{:S(2)}, u32[]{:S(2)}) %collective-permute-start.34) | collective-permute-done | bytes 524320 | tf_op jit(solution)/shard_map/ppermute | solution.py:430
  216.8 1.5 collective-permute-done.43.refs_7_
  218.3 5.5 %backward.11 = f32[2,128,8192]{2,1,0:T(8,128)} custom-call(s32[3,16]{1,0:T(4,128)S(1)} %pad_add_fusion.meta_ref, bf16[1024,1024]{1,0:T(8,128)(2,1)S(1)} %copy-done, bf16[1024,512]{1,0:T(8,128)(2,1)S(1)} %copy-done.1, f32[2,128,8192]{2,1,0:T(8,128)S(1)} %backward.10.refs_0_, bf16[2,128,2048]{2,1,0:T(8,128)(2,1)S(1)} %collective-permute-done.39.refs_1_, ...), custom_call_target="tpu_custom_call" | custom-call | flops 1024 | bytes 1024 | tf_op jit(solution)/shard_map/backward/pallas_call | solution.py:279
  (85 shorter events, 11.3 us)
Async XLA Ops:
  0.0 3.4 %copy-start.2 = (f32[2,128,8192]{2,1,0:T(8,128)S(1)}, f32[2,128,8192]{2,1,0:T(8,128)}, u32[]{:S(2)}) copy-start(f32[2,128,8192]{2,1,0:T(8,128)} %refs_0_.1) | copy-start | bytes 25165828
  5.3 3.4 %copy-start.12 = (s32[16]{0:T(128)S(1)}, s32[16]{0:T(128)}, u32[]{:S(2)}) copy-start(s32[16]{0:T(128)} %param.12) | copy-start | bytes 196
  5.3 3.4 %copy-start.13 = (s32[16]{0:T(128)S(1)}, s32[16]{0:T(128)}, u32[]{:S(2)}) copy-start(s32[16]{0:T(128)} %param.13) | copy-start | bytes 196
  5.3 3.6 %copy-start = (bf16[1024,1024]{1,0:T(8,128)(2,1)S(1)}, bf16[1024,1024]{1,0:T(8,128)(2,1)}, u32[]{:S(2)}) copy-start(bf16[1024,1024]{1,0:T(8,128)(2,1)} %pupil_ref.17) | copy-start | bytes 6291460
  5.3 3.6 %copy-start.1 = (bf16[1024,512]{1,0:T(8,128)(2,1)S(1)}, bf16[1024,512]{1,0:T(8,128)(2,1)}, u32[]{:S(2)}) copy-start(bf16[1024,512]{1,0:T(8,128)(2,1)} %constant.42.clone.band_ref) | copy-start | bytes 3145732
  5.3 5.9 %collective-permute-start.1 = (bf16[128,8192]{1,0:T(8,128)(2,1)}, bf16[128,8192]{1,0:T(8,128)(2,1)}, u32[]{:S(2)}, u32[]{:S(2)}) collective-permute-start(bf16[128,8192]{1,0:T(8,128)(2,1)} %low_part.3.refs_1_), channel_id=1, source_target_pairs={{0,1},{1,0},{2,3},{3,2},{4,5},{5,4},{6,7},{7,6},{8,9},{9,8},{10,11... | collective-permute-start | bytes 6291464 | tf_op jit(solution)/shard_map/ppermute | solution.py:427
  7.9 5.3 %collective-permute-start = (bf16[128,8192]{1,0:T(8,128)(2,1)}, bf16[128,8192]{1,0:T(8,128)(2,1)}, u32[]{:S(2)}, u32[]{:S(2)}) collective-permute-start(bf16[128,8192]{1,0:T(8,128)(2,1)} %low_part.2.refs_0_), channel_id=1, source_target_pairs={{0,1},{1,0},{2,3},{3,2},{4,5},{5,4},{6,7},{7,6},{8,9},{9,8},{10,11... | collective-permute-start | bytes 6291464 | tf_op jit(solution)/shard_map/ppermute | solution.py:427
  15.5 16.8 %collective-permute-start.2 = (bf16[2,128,1024]{2,1,0:T(8,128)(2,1)S(1)}, bf16[2,128,1024]{2,1,0:T(8,128)(2,1)S(1)}, u32[]{:S(2)}, u32[]{:S(2)}) collective-permute-start(bf16[2,128,1024]{2,1,0:T(8,128)(2,1)S(1)} %get-tuple-element.80), channel_id=1, source_target_pairs={{0,2},{1,3},{2,0},{3,1},{4,6},{5,7},{6,4},{7,5},{8,10},{9,11},{10,... | collective-permute-start | bytes 1572872 | tf_op jit(solution)/shard_map/ppermute | solution.py:430
  17.8 22.7 %collective-permute-start.11 = (bf16[2,128,1024]{2,1,0:T(8,128)(2,1)S(1)}, bf16[2,128,1024]{2,1,0:T(8,128)(2,1)S(1)}, u32[]{:S(2)}, u32[]{:S(2)}) collective-permute-start(bf16[2,128,1024]{2,1,0:T(8,128)(2,1)S(1)} %get-tuple-element.76), channel_id=1, source_target_pairs={{0,2},{1,3},{2,0},{3,1},{4,6},{5,7},{6,4},{7,5},{8,10},{9,11},{10,... | collective-permute-start | bytes 1572872 | tf_op jit(solution)/shard_map/ppermute | solution.py:430
  32.5 15.8 %collective-permute-start.3 = (bf16[2,128,1024]{2,1,0:T(8,128)(2,1)S(1)}, bf16[2,128,1024]{2,1,0:T(8,128)(2,1)S(1)}, u32[]{:S(2)}, u32[]{:S(2)}) collective-permute-start(bf16[2,128,1024]{2,1,0:T(8,128)(2,1)S(1)} %fusion), channel_id=1, source_target_pairs={{0,4},{1,5},{2,6},{3,7},{12,8},{13,9},{14,10},{15,11},{16,20},{17,... | collective-permute-start | bytes 1572872 | tf_op jit(solution)/shard_map/ppermute | solution.py:434
  33.8 17.9 %collective-permute-start.4 = (bf16[2,128,1024]{2,1,0:T(8,128)(2,1)S(1)}, bf16[2,128,1024]{2,1,0:T(8,128)(2,1)S(1)}, u32[]{:S(2)}, u32[]{:S(2)}) collective-permute-start(bf16[2,128,1024]{2,1,0:T(8,128)(2,1)S(1)} %get-tuple-element.85), channel_id=1, source_target_pairs={{0,2},{1,3},{2,0},{3,1},{4,6},{5,7},{6,4},{7,5},{8,10},{9,11},{10,... | collective-permute-start | bytes 1572872 | tf_op jit(solution)/shard_map/ppermute | solution.py:430
  40.7 18.7 %collective-permute-start.12 = (bf16[2,128,1024]{2,1,0:T(8,128)(2,1)S(1)}, bf16[2,128,1024]{2,1,0:T(8,128)(2,1)S(1)}, u32[]{:S(2)}, u32[]{:S(2)}) collective-permute-start(bf16[2,128,1024]{2,1,0:T(8,128)(2,1)S(1)} %fusion.2), channel_id=1, source_target_pairs={{0,4},{1,5},{2,6},{3,7},{12,8},{13,9},{14,10},{15,11},{16,20},{17,... | collective-permute-start | bytes 1572872 | tf_op jit(solution)/shard_map/ppermute | solution.py:434
  42.0 21.0 %collective-permute-start.13 = (bf16[2,128,1024]{2,1,0:T(8,128)(2,1)S(1)}, bf16[2,128,1024]{2,1,0:T(8,128)(2,1)S(1)}, u32[]{:S(2)}, u32[]{:S(2)}) collective-permute-start(bf16[2,128,1024]{2,1,0:T(8,128)(2,1)S(1)} %get-tuple-element.102), channel_id=1, source_target_pairs={{0,2},{1,3},{2,0},{3,1},{4,6},{5,7},{6,4},{7,5},{8,10},{9,11},{10,... | collective-permute-start | bytes 1572872 | tf_op jit(solution)/shard_map/ppermute | solution.py:430
  51.9 18.7 %collective-permute-start.6 = (bf16[2,128,1024]{2,1,0:T(8,128)(2,1)S(1)}, bf16[2,128,1024]{2,1,0:T(8,128)(2,1)S(1)}, u32[]{:S(2)}, u32[]{:S(2)}) collective-permute-start(bf16[2,128,1024]{2,1,0:T(8,128)(2,1)S(1)} %fusion.1), channel_id=1, source_target_pairs={{0,4},{1,5},{2,6},{3,7},{12,8},{13,9},{14,10},{15,11},{16,20},{17,... | collective-permute-start | bytes 1572872 | tf_op jit(solution)/shard_map/ppermute | solution.py:434
  53.5 17.3 %collective-permute-start.5 = (bf16[2,128,1024]{2,1,0:T(8,128)(2,1)S(1)}, bf16[2,128,1024]{2,1,0:T(8,128)(2,1)S(1)}, u32[]{:S(2)}, u32[]{:S(2)}) collective-permute-start(bf16[2,128,1024]{2,1,0:T(8,128)(2,1)S(1)} %add_convert_fusion.7), channel_id=1, source_target_pairs={{4,8},{5,9},{6,10},{7,11},{8,4},{9,5},{10,6},{11,7},{20,24},{21,25... | collective-permute-start | bytes 1572872 | tf_op jit(solution)/shard_map/ppermute | solution.py:434
  58.0 16.2 %collective-permute-start.7 = (bf16[2,128,1024]{2,1,0:T(8,128)(2,1)S(1)}, bf16[2,128,1024]{2,1,0:T(8,128)(2,1)S(1)}, u32[]{:S(2)}, u32[]{:S(2)}) collective-permute-start(bf16[2,128,1024]{2,1,0:T(8,128)(2,1)S(1)} %get-tuple-element.90), channel_id=1, source_target_pairs={{0,2},{1,3},{2,0},{3,1},{4,6},{5,7},{6,4},{7,5},{8,10},{9,11},{10,... | collective-permute-start | bytes 1572872 | tf_op jit(solution)/shard_map/ppermute | solution.py:430
  63.2 18.7 %collective-permute-start.15 = (bf16[2,128,1024]{2,1,0:T(8,128)(2,1)S(1)}, bf16[2,128,1024]{2,1,0:T(8,128)(2,1)S(1)}, u32[]{:S(2)}, u32[]{:S(2)}) collective-permute-start(bf16[2,128,1024]{2,1,0:T(8,128)(2,1)S(1)} %fusion.3), channel_id=1, source_target_pairs={{0,4},{1,5},{2,6},{3,7},{12,8},{13,9},{14,10},{15,11},{16,20},{17,... | collective-permute-start | bytes 1572872 | tf_op jit(solution)/shard_map/ppermute | solution.py:434
  64.7 17.2 %collective-permute-start.14 = (bf16[2,128,1024]{2,1,0:T(8,128)(2,1)S(1)}, bf16[2,128,1024]{2,1,0:T(8,128)(2,1)S(1)}, u32[]{:S(2)}, u32[]{:S(2)}) collective-permute-start(bf16[2,128,1024]{2,1,0:T(8,128)(2,1)S(1)} %add_convert_fusion.3), channel_id=1, source_target_pairs={{4,8},{5,9},{6,10},{7,11},{8,4},{9,5},{10,6},{11,7},{20,24},{21,25... | collective-permute-start | bytes 1572872 | tf_op jit(solution)/shard_map/ppermute | solution.py:434
  70.7 11.4 %collective-permute-start.16 = (bf16[2,128,1024]{2,1,0:T(8,128)(2,1)S(1)}, bf16[2,128,1024]{2,1,0:T(8,128)(2,1)S(1)}, u32[]{:S(2)}, u32[]{:S(2)}) collective-permute-start(bf16[2,128,1024]{2,1,0:T(8,128)(2,1)S(1)} %get-tuple-element.107), channel_id=1, source_target_pairs={{0,2},{1,3},{2,0},{3,1},{4,6},{5,7},{6,4},{7,5},{8,10},{9,11},{10,... | collective-permute-start | bytes 1572872 | tf_op jit(solution)/shard_map/ppermute | solution.py:430
  74.5 18.7 %collective-permute-start.9 = (bf16[2,128,1024]{2,1,0:T(8,128)(2,1)S(1)}, bf16[2,128,1024]{2,1,0:T(8,128)(2,1)S(1)}, u32[]{:S(2)}, u32[]{:S(2)}) collective-permute-start(bf16[2,128,1024]{2,1,0:T(8,128)(2,1)S(1)} %add_convert_fusion.6), channel_id=1, source_target_pairs={{4,8},{5,9},{6,10},{7,11},{8,4},{9,5},{10,6},{11,7},{20,24},{21,25... | collective-permute-start | bytes 1572872 | tf_op jit(solution)/shard_map/ppermute | solution.py:434
  78.8 14.6 %collective-permute-start.8 = (bf16[2,128,1024]{2,1,0:T(8,128)(2,1)S(1)}, bf16[2,128,1024]{2,1,0:T(8,128)(2,1)S(1)}, u32[]{:S(2)}, u32[]{:S(2)}) collective-permute-start(bf16[2,128,1024]{2,1,0:T(8,128)(2,1)S(1)} %get-tuple-element.92), channel_id=1, source_target_pairs={{0,2},{1,3},{2,0},{3,1},{4,6},{5,7},{6,4},{7,5},{8,10},{9,11},{10,... | collective-permute-start | bytes 1572872 | tf_op jit(solution)/shard_map/ppermute | solution.py:430
  81.9 13.0 %collective-permute-start.10 = (bf16[2,128,1024]{2,1,0:T(8,128)(2,1)S(1)}, bf16[2,128,1024]{2,1,0:T(8,128)(2,1)S(1)}, u32[]{:S(2)}, u32[]{:S(2)}) collective-permute-start(bf16[2,128,1024]{2,1,0:T(8,128)(2,1)S(1)} %add_convert_fusion.5), channel_id=1, source_target_pairs={{0,4},{1,5},{2,6},{3,7},{12,8},{13,9},{14,10},{15,11},{4,0},{5,1},... | collective-permute-start | bytes 1572872 | tf_op jit(solution)/shard_map/ppermute | solution.py:434
  82.4 20.0 %collective-permute-start.18 = (bf16[2,128,1024]{2,1,0:T(8,128)(2,1)S(1)}, bf16[2,128,1024]{2,1,0:T(8,128)(2,1)S(1)}, u32[]{:S(2)}, u32[]{:S(2)}) collective-permute-start(bf16[2,128,1024]{2,1,0:T(8,128)(2,1)S(1)} %add_convert_fusion.2), channel_id=1, source_target_pairs={{4,8},{5,9},{6,10},{7,11},{8,4},{9,5},{10,6},{11,7},{20,24},{21,25... | collective-permute-start | bytes 1572872 | tf_op jit(solution)/shard_map/ppermute | solution.py:434
  92.4 14.1 %collective-permute-start.17 = (bf16[2,128,1024]{2,1,0:T(8,128)(2,1)S(1)}, bf16[2,128,1024]{2,1,0:T(8,128)(2,1)S(1)}, u32[]{:S(2)}, u32[]{:S(2)}) collective-permute-start(bf16[2,128,1024]{2,1,0:T(8,128)(2,1)S(1)} %get-tuple-element.109), channel_id=1, source_target_pairs={{0,2},{1,3},{2,0},{3,1},{4,6},{5,7},{6,4},{7,5},{8,10},{9,11},{10,... | collective-permute-start | bytes 1572872 | tf_op jit(solution)/shard_map/ppermute | solution.py:430
  93.1 13.3 %collective-permute-start.19 = (bf16[2,128,1024]{2,1,0:T(8,128)(2,1)S(1)}, bf16[2,128,1024]{2,1,0:T(8,128)(2,1)S(1)}, u32[]{:S(2)}, u32[]{:S(2)}) collective-permute-start(bf16[2,128,1024]{2,1,0:T(8,128)(2,1)S(1)} %add_convert_fusion.1), channel_id=1, source_target_pairs={{0,4},{1,5},{2,6},{3,7},{12,8},{13,9},{14,10},{15,11},{4,0},{5,1},... | collective-permute-start | bytes 1572872 | tf_op jit(solution)/shard_map/ppermute | solution.py:434
  94.9 11.9 %copy-start.9 = (bf16[1024,1024]{1,0:T(8,128)(2,1)S(1)}, bf16[1024,1024]{1,0:T(8,128)(2,1)}, u32[]{:S(2)}) copy-start(bf16[1024,1024]{1,0:T(8,128)(2,1)} %constant.44.clone.refs_4_) | copy-start | bytes 6291460
  94.9 11.9 %copy-start.10 = (bf16[1024,1024]{1,0:T(8,128)(2,1)S(1)}, bf16[1024,1024]{1,0:T(8,128)(2,1)}, u32[]{:S(2)}) copy-start(bf16[1024,1024]{1,0:T(8,128)(2,1)} %constant.43.clone.refs_3_) | copy-start | bytes 6291460
  94.9 11.9 %copy-start.11 = (bf16[1,256,1024]{2,1,0:T(8,128)(2,1)S(1)}, bf16[1,256,1024]{2,1,0:T(8,128)(2,1)}, u32[]{:S(2)}) copy-start(bf16[1,256,1024]{2,1,0:T(8,128)(2,1)} %refs_2_.1) | copy-start | bytes 1572868
  112.4 10.6 %collective-permute-start.28 = (bf16[2,128,1024]{2,1,0:T(8,128)(2,1)S(1)}, bf16[2,128,1024]{2,1,0:T(8,128)(2,1)}, u32[]{:S(2)}, u32[]{:S(2)}) collective-permute-start(bf16[2,128,1024]{2,1,0:T(8,128)(2,1)S(1)} %get-tuple-element.117.refs_2_.refs_1_), channel_id=1, source_target_pairs={{0,4},{1,5},{2,6},{3,7},{12,8},{13,9},{14,10},{15,11},{4,0},{5,1},... | collective-permute-start | bytes 1572872 | tf_op jit(solution)/shard_map/ppermute | solution.py:434
  112.4 18.8 %collective-permute-start.27 = (bf16[2,128,1024]{2,1,0:T(8,128)(2,1)S(1)}, bf16[2,128,1024]{2,1,0:T(8,128)(2,1)}, u32[]{:S(2)}, u32[]{:S(2)}) collective-permute-start(bf16[2,128,1024]{2,1,0:T(8,128)(2,1)S(1)} %get-tuple-element.117.refs_2_.refs_1_), channel_id=1, source_target_pairs={{4,8},{5,9},{6,10},{7,11},{8,4},{9,5},{10,6},{11,7},{20,24},{21,25... | collective-permute-start | bytes 1572872 | tf_op jit(solution)/shard_map/ppermute | solution.py:434
  119.2 12.9 %collective-permute-start.26 = (bf16[2,128,1024]{2,1,0:T(8,128)(2,1)S(1)}, bf16[2,128,1024]{2,1,0:T(8,128)(2,1)S(1)}, u32[]{:S(2)}, u32[]{:S(2)}) collective-permute-start(bf16[2,128,1024]{2,1,0:T(8,128)(2,1)S(1)} %get-tuple-element.117.refs_2_.refs_1_), channel_id=1, source_target_pairs={{0,2},{1,3},{2,0},{3,1},{4,6},{5,7},{6,4},{7,5},{8,10},{9,11},{10,... | collective-permute-start | bytes 1572872 | tf_op jit(solution)/shard_map/ppermute | solution.py:430
  119.8 0.8 copy-start.4
  120.6 16.9 %collective-permute-start.22 = (bf16[2,128,1024]{2,1,0:T(8,128)(2,1)}, bf16[2,128,1024]{2,1,0:T(8,128)(2,1)}, u32[]{:S(2)}, u32[]{:S(2)}) collective-permute-start(bf16[2,128,1024]{2,1,0:T(8,128)(2,1)} %get-tuple-element.114.refs_1_.refs_0_), channel_id=1, source_target_pairs={{0,4},{1,5},{2,6},{3,7},{12,8},{13,9},{14,10},{15,11},{4,0},{5,1},... | collective-permute-start | bytes 1572872 | tf_op jit(solution)/shard_map/ppermute | solution.py:434
  120.6 21.8 %collective-permute-start.21 = (bf16[2,128,1024]{2,1,0:T(8,128)(2,1)}, bf16[2,128,1024]{2,1,0:T(8,128)(2,1)}, u32[]{:S(2)}, u32[]{:S(2)}) collective-permute-start(bf16[2,128,1024]{2,1,0:T(8,128)(2,1)} %get-tuple-element.114.refs_1_.refs_0_), channel_id=1, source_target_pairs={{4,8},{5,9},{6,10},{7,11},{8,4},{9,5},{10,6},{11,7},{20,24},{21,25... | collective-permute-start | bytes 1572872 | tf_op jit(solution)/shard_map/ppermute | solution.py:434
  123.1 20.3 %collective-permute-start.20 = (bf16[2,128,1024]{2,1,0:T(8,128)(2,1)}, bf16[2,128,1024]{2,1,0:T(8,128)(2,1)}, u32[]{:S(2)}, u32[]{:S(2)}) collective-permute-start(bf16[2,128,1024]{2,1,0:T(8,128)(2,1)} %get-tuple-element.114.refs_1_.refs_0_), channel_id=1, source_target_pairs={{0,2},{1,3},{2,0},{3,1},{4,6},{5,7},{6,4},{7,5},{8,10},{9,11},{10,... | collective-permute-start | bytes 1572872 | tf_op jit(solution)/shard_map/ppermute | solution.py:430
  132.1 0.8 copy-start.7
  132.9 21.1 %collective-permute-start.33 = (bf16[2,128,1024]{2,1,0:T(8,128)(2,1)}, bf16[2,128,1024]{2,1,0:T(8,128)(2,1)}, u32[]{:S(2)}, u32[]{:S(2)}) collective-permute-start(bf16[2,128,1024]{2,1,0:T(8,128)(2,1)} %collective-permute-done.27), channel_id=1, source_target_pairs={{4,0},{5,1},{6,2},{7,3},{8,12},{9,13},{10,14},{11,15},{20,16},{21,... | collective-permute-start | bytes 1572872 | tf_op jit(solution)/shard_map/ppermute | solution.py:434
  135.0 19.1 %collective-permute-start.32 = (bf16[2,128,1024]{2,1,0:T(8,128)(2,1)}, bf16[2,128,1024]{2,1,0:T(8,128)(2,1)}, u32[]{:S(2)}, u32[]{:S(2)}) collective-permute-start(bf16[2,128,1024]{2,1,0:T(8,128)(2,1)} %collective-permute-done.28.refs_4_.refs_3_), channel_id=1, source_target_pairs={{4,8},{5,9},{6,10},{7,11},{8,4},{9,5},{10,6},{11,7},{20,24},{21,25... | collective-permute-start | bytes 1572872 | tf_op jit(solution)/shard_map/ppermute | solution.py:434
  137.6 17.0 %collective-permute-start.31 = (bf16[2,128,1024]{2,1,0:T(8,128)(2,1)}, bf16[2,128,1024]{2,1,0:T(8,128)(2,1)}, u32[]{:S(2)}, u32[]{:S(2)}) collective-permute-start(bf16[2,128,1024]{2,1,0:T(8,128)(2,1)} %collective-permute-done.28.refs_4_.refs_3_), channel_id=1, source_target_pairs={{0,2},{1,3},{2,0},{3,1},{4,6},{5,7},{6,4},{7,5},{8,10},{9,11},{10,... | collective-permute-start | bytes 1572872 | tf_op jit(solution)/shard_map/ppermute | solution.py:430
  143.4 22.8 %collective-permute-start.25 = (bf16[2,128,1024]{2,1,0:T(8,128)(2,1)}, bf16[2,128,1024]{2,1,0:T(8,128)(2,1)S(1)}, u32[]{:S(2)}, u32[]{:S(2)}) collective-permute-start(bf16[2,128,1024]{2,1,0:T(8,128)(2,1)} %collective-permute-done.21), channel_id=1, source_target_pairs={{4,0},{5,1},{6,2},{7,3},{8,12},{9,13},{10,14},{11,15},{20,16},{21,... | collective-permute-start | bytes 1572872 | tf_op jit(solution)/shard_map/ppermute | solution.py:434
  144.7 21.5 %collective-permute-start.24 = (bf16[2,128,1024]{2,1,0:T(8,128)(2,1)}, bf16[2,128,1024]{2,1,0:T(8,128)(2,1)S(1)}, u32[]{:S(2)}, u32[]{:S(2)}) collective-permute-start(bf16[2,128,1024]{2,1,0:T(8,128)(2,1)} %collective-permute-done.22.refs_3_.refs_2_), channel_id=1, source_target_pairs={{4,8},{5,9},{6,10},{7,11},{8,4},{9,5},{10,6},{11,7},{20,24},{21,25... | collective-permute-start | bytes 1572872 | tf_op jit(solution)/shard_map/ppermute | solution.py:434
  146.9 1.0 copy-start.5
  147.9 1.0 copy-start.8
  149.0 9.1 %copy-start.6 = (bf16[2,128,1024]{2,1,0:T(8,128)(2,1)S(1)}, bf16[2,128,1024]{2,1,0:T(8,128)(2,1)}, u32[]{:S(2)}) copy-start(bf16[2,128,1024]{2,1,0:T(8,128)(2,1)} %copy-done.4) | copy-start | bytes 1572868
  154.0 12.2 %collective-permute-start.23 = (bf16[2,128,1024]{2,1,0:T(8,128)(2,1)}, bf16[2,128,1024]{2,1,0:T(8,128)(2,1)S(1)}, u32[]{:S(2)}, u32[]{:S(2)}) collective-permute-start(bf16[2,128,1024]{2,1,0:T(8,128)(2,1)} %collective-permute-done.22.refs_3_.refs_2_), channel_id=1, source_target_pairs={{0,2},{1,3},{2,0},{3,1},{4,6},{5,7},{6,4},{7,5},{8,10},{9,11},{10,... | collective-permute-start | bytes 1572872 | tf_op jit(solution)/shard_map/ppermute | solution.py:430
  155.7 21.1 %collective-permute-start.35 = (bf16[2,128,1024]{2,1,0:T(8,128)(2,1)S(1)}, bf16[2,128,1024]{2,1,0:T(8,128)(2,1)S(1)}, u32[]{:S(2)}, u32[]{:S(2)}) collective-permute-start(bf16[2,128,1024]{2,1,0:T(8,128)(2,1)S(1)} %broadcast_select_fusion.2.refs_2_), channel_id=1, source_target_pairs={{0,2},{1,3},{2,0},{3,1},{4,6},{5,7},{6,4},{7,5},{8,10},{9,11},{10,... | collective-permute-start | bytes 1572872 | tf_op jit(solution)/shard_map/ppermute | solution.py:430
  156.7 20.1 %collective-permute-start.36 = (bf16[2,128,1024]{2,1,0:T(8,128)(2,1)}, bf16[2,128,1024]{2,1,0:T(8,128)(2,1)S(1)}, u32[]{:S(2)}, u32[]{:S(2)}) collective-permute-start(bf16[2,128,1024]{2,1,0:T(8,128)(2,1)} %collective-permute-done.32), channel_id=1, source_target_pairs={{4,0},{5,1},{6,2},{7,3},{8,12},{9,13},{10,14},{11,15},{20,16},{21,... | collective-permute-start | bytes 1572872 | tf_op jit(solution)/shard_map/ppermute | solution.py:434
  158.0 3.4 %copy-start.3 = (f32[2,128,8192]{2,1,0:T(8,128)S(1)}, f32[2,128,8192]{2,1,0:T(8,128)}, u32[]{:S(2)}) copy-start(f32[2,128,8192]{2,1,0:T(8,128)} %refs_0_.1) | copy-start | bytes 25165828
  167.3 20.7 %collective-permute-start.29 = (bf16[2,128,1024]{2,1,0:T(8,128)(2,1)S(1)}, bf16[2,128,1024]{2,1,0:T(8,128)(2,1)S(1)}, u32[]{:S(2)}, u32[]{:S(2)}) collective-permute-start(bf16[2,128,1024]{2,1,0:T(8,128)(2,1)S(1)} %broadcast_select_fusion.3.refs_1_), channel_id=1, source_target_pairs={{0,2},{1,3},{2,0},{3,1},{4,6},{5,7},{6,4},{7,5},{8,10},{9,11},{10,... | collective-permute-start | bytes 1572872 | tf_op jit(solution)/shard_map/ppermute | solution.py:430
  167.9 20.1 %collective-permute-start.30 = (bf16[2,128,1024]{2,1,0:T(8,128)(2,1)S(1)}, bf16[2,128,1024]{2,1,0:T(8,128)(2,1)S(1)}, u32[]{:S(2)}, u32[]{:S(2)}) collective-permute-start(bf16[2,128,1024]{2,1,0:T(8,128)(2,1)S(1)} %collective-permute-done.24), channel_id=1, source_target_pairs={{4,0},{5,1},{6,2},{7,3},{8,12},{9,13},{10,14},{11,15},{20,16},{21,... | collective-permute-start | bytes 1572872 | tf_op jit(solution)/shard_map/ppermute | solution.py:434
  177.9 21.4 %collective-permute-start.37 = (bf16[2,128,1024]{2,1,0:T(8,128)(2,1)S(1)}, bf16[2,128,1024]{2,1,0:T(8,128)(2,1)S(1)}, u32[]{:S(2)}, u32[]{:S(2)}) collective-permute-start(bf16[2,128,1024]{2,1,0:T(8,128)(2,1)S(1)} %broadcast_select_fusion.refs_2_.refs_6_), channel_id=1, source_target_pairs={{0,2},{1,3},{2,0},{3,1},{4,6},{5,7},{6,4},{7,5},{8,10},{9,11},{10,... | collective-permute-start | bytes 1572872 | tf_op jit(solution)/shard_map/ppermute | solution.py:430
  199.2 5.6 %collective-permute-start.38 = (bf16[2,128,1024]{2,1,0:T(8,128)(2,1)S(1)}, bf16[2,128,1024]{2,1,0:T(8,128)(2,1)S(1)}, u32[]{:S(2)}, u32[]{:S(2)}) collective-permute-start(bf16[2,128,1024]{2,1,0:T(8,128)(2,1)S(1)} %collective-permute-done.37.refs_6_), channel_id=1, source_target_pairs={{0,1},{1,0},{2,3},{3,2},{4,5},{5,4},{6,7},{7,6},{8,9},{9,8},{10,11... | collective-permute-start | bytes 1572872 | tf_op jit(solution)/shard_map/ppermute | solution.py:427
  202.4 13.6 %collective-permute-start.34 = (bf16[2,128,1024]{2,1,0:T(8,128)(2,1)S(1)}, bf16[2,128,1024]{2,1,0:T(8,128)(2,1)S(1)}, u32[]{:S(2)}, u32[]{:S(2)}) collective-permute-start(bf16[2,128,1024]{2,1,0:T(8,128)(2,1)S(1)} %broadcast_select_fusion.1.refs_1_.refs_5_), channel_id=1, source_target_pairs={{0,2},{1,3},{2,0},{3,1},{4,6},{5,7},{6,4},{7,5},{8,10},{9,11},{10,... | collective-permute-start | bytes 1572872 | tf_op jit(solution)/shard_map/ppermute | solution.py:430
  204.0 14.3 %collective-permute-start.39 = (bf16[2,128,2048]{2,1,0:T(8,128)(2,1)S(1)}, bf16[2,128,2048]{2,1,0:T(8,128)(2,1)S(1)}, u32[]{:S(2)}, u32[]{:S(2)}) collective-permute-start(bf16[2,128,2048]{2,1,0:T(8,128)(2,1)S(1)} %get-tuple-element.141), channel_id=1, source_target_pairs={{0,1},{1,0},{2,3},{3,2},{4,5},{5,4},{6,7},{7,6},{8,9},{9,8},{10,11... | collective-permute-start | bytes 3145736 | tf_op jit(solution)/shard_map/ppermute | solution.py:427
  204.3 14.0 %collective-permute-start.40 = (bf16[2,128,2048]{2,1,0:T(8,128)(2,1)S(1)}, bf16[2,128,2048]{2,1,0:T(8,128)(2,1)S(1)}, u32[]{:S(2)}, u32[]{:S(2)}) collective-permute-start(bf16[2,128,2048]{2,1,0:T(8,128)(2,1)S(1)} %get-tuple-element.142), channel_id=1, source_target_pairs={{0,1},{1,0},{2,3},{3,2},{4,5},{5,4},{6,7},{7,6},{8,9},{9,8},{10,11... | collective-permute-start | bytes 3145736 | tf_op jit(solution)/shard_map/ppermute | solution.py:427
  204.6 13.8 %collective-permute-start.41 = (bf16[2,128,2048]{2,1,0:T(8,128)(2,1)S(1)}, bf16[2,128,2048]{2,1,0:T(8,128)(2,1)S(1)}, u32[]{:S(2)}, u32[]{:S(2)}) collective-permute-start(bf16[2,128,2048]{2,1,0:T(8,128)(2,1)S(1)} %get-tuple-element.143), channel_id=1, source_target_pairs={{0,1},{1,0},{2,3},{3,2},{4,5},{5,4},{6,7},{7,6},{8,9},{9,8},{10,11... | collective-permute-start | bytes 3145736 | tf_op jit(solution)/shard_map/ppermute | solution.py:427
  208.1 10.2 %collective-permute-start.42 = (bf16[2,128,2048]{2,1,0:T(8,128)(2,1)S(1)}, bf16[2,128,2048]{2,1,0:T(8,128)(2,1)S(1)}, u32[]{:S(2)}, u32[]{:S(2)}) collective-permute-start(bf16[2,128,2048]{2,1,0:T(8,128)(2,1)S(1)} %get-tuple-element.144), channel_id=1, source_target_pairs={{0,1},{1,0},{2,3},{3,2},{4,5},{5,4},{6,7},{7,6},{8,9},{9,8},{10,11... | collective-permute-start | bytes 3145736 | tf_op jit(solution)/shard_map/ppermute | solution.py:427
  216.0 2.3 %collective-permute-start.43 = (bf16[2,128,1024]{2,1,0:T(8,128)(2,1)S(1)}, bf16[2,128,1024]{2,1,0:T(8,128)(2,1)S(1)}, u32[]{:S(2)}, u32[]{:S(2)}) collective-permute-start(bf16[2,128,1024]{2,1,0:T(8,128)(2,1)S(1)} %collective-permute-done.34.refs_5_), channel_id=1, source_target_pairs={{0,1},{1,0},{2,3},{3,2},{4,5},{5,4},{6,7},{7,6},{8,9},{9,8},{10,11... | collective-permute-start | bytes 1572872 | tf_op jit(solution)/shard_map/ppermute | solution.py:427

commit v10 on v9

--- a/solution.py
+++ b/solution.py
@@ -538,12 +538,10 @@
     far_other = pieces[("far", 2), lead]
     slab, far_other = together((pieces["slab", last], far_other))
     chunks = apply([slab], late, 4)
+    result = apply([pieces["result", last]], later + late)
+    far_other, result = together((far_other, result))
     twin = sibling(far_other)
-    slab = [sibling(chunk) for chunk in chunks[:-1]]
-    result, twin = together((pieces["result", last], twin))
-    result = apply([result], later + late)
-    chunk, result = together((chunks[-1], result))
-    slab.append(sibling(chunk))
+    slab = [sibling(chunk) for chunk in chunks]
     arriving, result = together((pieces[("far", 2), last], result))
     pieces[("far", 2), lead], pieces[("far", 3), lead] = far_other, twin
     pieces[("far", 2), last], pieces[("far", 3), last] = arriving, sibling(arriving)

time: 226 us -> 227 us (level)
  starting transfers between devices: 69.2 us -> 62.1 us
  Pallas kernels: 51.2 us -> 57.8 us
  local copies, waits for them, and re-layouts: 11.2 us -> 15.7 us
    ppermute x20, starting transfers between devices: 48.4 us -> 33.9 us  [along(): return lax.ppermute(value, 'ty', pairs)]
    ppermute x16, starting transfers between devices: 15 us -> 22.6 us  [across(): return lax.ppermute(value, 'ty', [(i, i ^ 2) for i in range(count)])]
    unnamed x28 -> x50, local copies, waits for them, and re-layouts: 10.5 us -> 15 us
    ppermute x20, waiting for transfers between devices: 27.7 us -> 23.2 us  [along(): return lax.ppermute(value, 'ty', pairs)]
    pallas_call x3, Pallas kernels: 19 us -> 23.1 us  [forward(): pl.pallas_call(functools.partial(forward_kernel, base=base, images=images...]
    pallas_call x6, Pallas kernels: 22.9 us -> 26.2 us  [backward(): pl.pallas_call(functools.partial(kernel, slots=slots, held=held, parts=le...]
    ppermute x16, waiting for transfers between devices: 53.8 us -> 56.2 us  [across(): return lax.ppermute(value, 'ty', [(i, i ^ 2) for i in range(count)])]
  transfers between devices with their start and end apart: 44 -> 44, of which waited for: 24 -> 20; matrix products, arithmetic and copies ran while one was open for 3% -> 3% of each run, Pallas kernels for 16% -> 18%
where the time goes in v10:
time: 227 us; the launch traced here: 226 us
  waiting for transfers between devices  83.3 us (37%)
  starting transfers between devices  62.1 us (27%)
  Pallas kernels  57.8 us (25%)
  local copies, waits for them, and re-layouts  15.7 us (7%)
  other arithmetic  6.68 us (3%)
    ppermute x16, waiting for transfers between devices, across(): return lax.ppermute(value, 'ty', [(i, i ^ 2) for i in range(count)])  56.2 us
    ppermute x20, starting transfers between devices, along(): return lax.ppermute(value, 'ty', pairs)  33.9 us
    pallas_call x6, Pallas kernels, backward(): pl.pallas_call(functools.partial(kernel, slots=slots, held=held, parts=le...  26.2 us
    ppermute x20, waiting for transfers between devices, along(): return lax.ppermute(value, 'ty', pairs)  23.2 us
    pallas_call x3, Pallas kernels, forward(): pl.pallas_call(functools.partial(forward_kernel, base=base, images=images...  23.1 us
    ppermute x16, starting transfers between devices, across(): return lax.ppermute(value, 'ty', [(i, i ^ 2) for i in range(count)])  22.6 us
    unnamed x50, local copies, waits for them, and re-layouts  15 us
    ppermute x8, starting transfers between devices, sibling(): return lax.ppermute(value, 'ty', [(i, i ^ 1) for i in range(count)])  5.6 us
  transfers between devices with their start and end apart: 44, of which 20 were waited for; matrix products, arithmetic and copies ran while one was open for 3% of the time, Pallas kernels for 18%

profile of v10, /device:TPU:11, one launch (start us, length us, event | category | flops | bytes accessed | tf_op | source)
XLA Modules:
  0.0 226.1 jit_solution(13409173872706123944)
XLA Ops:
  0.0 3.4 %copy-done.2 = f32[2,128,8192]{2,1,0:T(8,128)S(1)} copy-done((f32[2,128,8192]{2,1,0:T(8,128)S(1)}, f32[2,128,8192]{2,1,0:T(8,128)}, u32[]{:S(2)}) %copy-start.2) | copy-done | bytes 8388632
  3.4 1.9 low_part.3.refs_1_
  6.0 1.8 low_part.2.refs_0_
  8.9 3.3 %forward.3.refs_2_ = bf16[2,256,1024]{2,1,0:T(8,128)(2,1)S(1)} custom-call(s32[3,16]{1,0:T(4,128)S(1)} %pad_add_fusion.meta_ref, bf16[1024,1024]{1,0:T(8,128)(2,1)S(1)} %copy-done, bf16[1024,512]{1,0:T(8,128)(2,1)S(1)} %copy-done.1, bf16[128,8192]{1,0:T(8,128)(2,1)} %low_part.2.refs_0_, bf16[128,8192]{1,0:T(8,128)(2,1)} %low_part.3.refs_1_), custom_call_target="tpu_custom_call" | custom-call | flops 1024 | bytes 1024 | tf_op jit(solution)/shard_map/forward/pallas_call | solution.py:257
  13.2 3.3 %forward.4 = (bf16[2,128,1024]{2,1,0:T(8,128)(2,1)S(1)}, bf16[2,128,1024]{2,1,0:T(8,128)(2,1)S(1)}) custom-call(s32[3,16]{1,0:T(4,128)S(1)} %pad_add_fusion.meta_ref, bf16[1024,1024]{1,0:T(8,128)(2,1)S(1)} %copy-done, bf16[1024,512]{1,0:T(8,128)(2,1)S(1)} %copy-done.1, bf16[128,8192]{1,0:T(8,128)(2,1)} %collective-permute-done.refs_0_.refs_2_, ...), custom_call_target="tpu_custom_call" | custom-call | flops 1024 | bytes 1024 | tf_op jit(solution)/shard_map/forward/pallas_call | solution.py:257
  16.5 1.3 collective-permute-start.2
  18.0 16.4 %forward.5 = (bf16[2,128,1024]{2,1,0:T(8,128)(2,1)S(1)}, bf16[2,128,1024]{2,1,0:T(8,128)(2,1)S(1)}, bf16[2,128,1024]{2,1,0:T(8,128)(2,1)S(1)}, bf16[2,128,1024]{...) custom-call(s32[3,16]{1,0:T(4,128)S(1)} %pad_add_fusion.meta_ref, ...), custom_call_target="tpu_custom_call" | custom-call | flops 1024 | bytes 1024 | tf_op jit(solution)/shard_map/forward/pallas_call | solution.py:257
  34.7 1.3 collective-permute-start.3
  36.0 3.4 %collective-permute-start.4 = (bf16[2,128,1024]{2,1,0:T(8,128)(2,1)S(1)}, bf16[2,128,1024]{2,1,0:T(8,128)(2,1)S(1)}, u32[]{:S(2)}, u32[]{:S(2)}) collective-permute-start(bf16[2,128,1024]{2,1,0:T(8,128)(2,1)S(1)} %get-tuple-element.83), channel_id=1, source_target_pairs={{0,2},{1,3},{2,0},{3,1},{4,6},{5,7},{6,4},{7,5},{8,10},{9,11},{10,... | collective-permute-start | bytes 1572872 | tf_op jit(solution)/shard_map/ppermute | solution.py:430
  39.3 1.6 collective-permute-done.11
  41.1 1.3 collective-permute-start.12
  42.4 1.3 collective-permute-start.13
  43.7 4.5 %collective-permute-done.3 = bf16[2,128,1024]{2,1,0:T(8,128)(2,1)S(1)} collective-permute-done((bf16[2,128,1024]{2,1,0:T(8,128)(2,1)S(1)}, bf16[2,128,1024]{2,1,0:T(8,128)(2,1)S(1)}, u32[]{:S(2)}, u32[]{:S(2)}) %collective-permute-start.3) | collective-permute-done | bytes 524320 | tf_op jit(solution)/shard_map/ppermute | solution.py:434
  48.2 4.0 %collective-permute-done.4 = bf16[2,128,1024]{2,1,0:T(8,128)(2,1)S(1)} collective-permute-done((bf16[2,128,1024]{2,1,0:T(8,128)(2,1)S(1)}, bf16[2,128,1024]{2,1,0:T(8,128)(2,1)S(1)}, u32[]{:S(2)}, u32[]{:S(2)}) %collective-permute-start.4) | collective-permute-done | bytes 524320 | tf_op jit(solution)/shard_map/ppermute | solution.py:430
  52.4 1.3 collective-permute-start.6
  54.0 3.2 %collective-permute-start.5 = (bf16[2,128,1024]{2,1,0:T(8,128)(2,1)S(1)}, bf16[2,128,1024]{2,1,0:T(8,128)(2,1)S(1)}, u32[]{:S(2)}, u32[]{:S(2)}) collective-permute-start(bf16[2,128,1024]{2,1,0:T(8,128)(2,1)S(1)} %add_convert_fusion.7), channel_id=1, source_target_pairs={{4,8},{5,9},{6,10},{7,11},{8,4},{9,5},{10,6},{11,7},{20,24},{21,25... | collective-permute-start | bytes 1572872 | tf_op jit(solution)/shard_map/ppermute | solution.py:434
  57.5 1.9 collective-permute-done.12
  59.4 4.0 %collective-permute-done.13 = bf16[2,128,1024]{2,1,0:T(8,128)(2,1)S(1)} collective-permute-done((bf16[2,128,1024]{2,1,0:T(8,128)(2,1)S(1)}, bf16[2,128,1024]{2,1,0:T(8,128)(2,1)S(1)}, u32[]{:S(2)}, u32[]{:S(2)}) %collective-permute-start.13) | collective-permute-done | bytes 524320 | tf_op jit(solution)/shard_map/ppermute | solution.py:430
  63.6 1.3 collective-permute-start.15
  65.2 3.2 %collective-permute-start.14 = (bf16[2,128,1024]{2,1,0:T(8,128)(2,1)S(1)}, bf16[2,128,1024]{2,1,0:T(8,128)(2,1)S(1)}, u32[]{:S(2)}, u32[]{:S(2)}) collective-permute-start(bf16[2,128,1024]{2,1,0:T(8,128)(2,1)S(1)} %add_convert_fusion.3), channel_id=1, source_target_pairs={{4,8},{5,9},{6,10},{7,11},{8,4},{9,5},{10,6},{11,7},{20,24},{21,25... | collective-permute-start | bytes 1572872 | tf_op jit(solution)/shard_map/ppermute | solution.py:434
  68.4 2.2 collective-permute-done.6
  70.6 5.6 %collective-permute-start.16 = (bf16[2,128,1024]{2,1,0:T(8,128)(2,1)S(1)}, bf16[2,128,1024]{2,1,0:T(8,128)(2,1)S(1)}, u32[]{:S(2)}, u32[]{:S(2)}) collective-permute-start(bf16[2,128,1024]{2,1,0:T(8,128)(2,1)S(1)} %get-tuple-element.105), channel_id=1, source_target_pairs={{0,2},{1,3},{2,0},{3,1},{4,6},{5,7},{6,4},{7,5},{8,10},{9,11},{10,... | collective-permute-start | bytes 1572872 | tf_op jit(solution)/shard_map/ppermute | solution.py:430
  76.5 1.9 collective-permute-start.9
  78.8 3.1 %collective-permute-done.15 = bf16[2,128,1024]{2,1,0:T(8,128)(2,1)S(1)} collective-permute-done((bf16[2,128,1024]{2,1,0:T(8,128)(2,1)S(1)}, bf16[2,128,1024]{2,1,0:T(8,128)(2,1)S(1)}, u32[]{:S(2)}, u32[]{:S(2)}) %collective-permute-start.15) | collective-permute-done | bytes 524320 | tf_op jit(solution)/shard_map/ppermute | solution.py:434
  81.9 6.8 %collective-permute-done.16 = bf16[2,128,1024]{2,1,0:T(8,128)(2,1)S(1)} collective-permute-done((bf16[2,128,1024]{2,1,0:T(8,128)(2,1)S(1)}, bf16[2,128,1024]{2,1,0:T(8,128)(2,1)S(1)}, u32[]{:S(2)}, u32[]{:S(2)}) %collective-permute-start.16) | collective-permute-done | bytes 524320 | tf_op jit(solution)/shard_map/ppermute | solution.py:430
  88.9 2.1 collective-permute-start.18
  91.0 1.5 collective-permute-start.17
  92.9 6.7 %collective-permute-done.8 = bf16[2,128,1024]{2,1,0:T(8,128)(2,1)S(1)} collective-permute-done((bf16[2,128,1024]{2,1,0:T(8,128)(2,1)S(1)}, bf16[2,128,1024]{2,1,0:T(8,128)(2,1)S(1)}, u32[]{:S(2)}, u32[]{:S(2)}) %collective-permute-start.8) | collective-permute-done | bytes 524320 | tf_op jit(solution)/shard_map/ppermute | solution.py:430
  100.0 1.6 collective-permute-done.18
  101.6 8.6 %collective-permute-done.17 = bf16[2,128,1024]{2,1,0:T(8,128)(2,1)S(1)} collective-permute-done((bf16[2,128,1024]{2,1,0:T(8,128)(2,1)S(1)}, bf16[2,128,1024]{2,1,0:T(8,128)(2,1)S(1)}, u32[]{:S(2)}, u32[]{:S(2)}) %collective-permute-start.17) | collective-permute-done | bytes 524320 | tf_op jit(solution)/shard_map/ppermute | solution.py:430
  110.6 4.8 %middle.1 = (bf16[2,128,1024]{2,1,0:T(8,128)(2,1)S(1)}, bf16[2,128,1024]{2,1,0:T(8,128)(2,1)S(1)}) custom-call(bf16[2,128,1024]{2,1,0:T(8,128)(2,1)S(1)} %add_convert_fusion.refs_0_, bf16[2,128,1024]{2,1,0:T(8,128)(2,1)S(1)} %add_convert_fusion.4.refs_1_, bf16[1,256,1024]{2,1,0:T(8,128)(2,1)S(1)} %copy-done.18, bf16[1024,1024]{1,0:T(8,128)(2,1)S(1)} %copy-done.17, ...), custom_call_target="tpu_custom_call" | custom-call | flops 1024 | bytes 1024 | tf_op jit(solution)/shard_map/middle/pallas_call | solution.py:295
  115.5 1.9 collective-permute-start.27
  117.5 1.9 collective-permute-start.26
  120.4 3.1 %collective-permute-start.21 = (bf16[2,128,1024]{2,1,0:T(8,128)(2,1)S(1)}, bf16[2,128,1024]{2,1,0:T(8,128)(2,1)}, u32[]{:S(2)}, u32[]{:S(2)}) collective-permute-start(bf16[2,128,1024]{2,1,0:T(8,128)(2,1)S(1)} %get-tuple-element.112.refs_1_.refs_0_), channel_id=1, source_target_pairs={{4,8},{5,9},{6,10},{7,11},{8,4},{9,5},{10,6},{11,7},{20,24},{21,25... | collective-permute-start | bytes 1572872 | tf_op jit(solution)/shard_map/ppermute | solution.py:434
  123.5 5.3 %collective-permute-done.28.refs_4_.refs_3_ = bf16[2,128,1024]{2,1,0:T(8,128)(2,1)} collective-permute-done((bf16[2,128,1024]{2,1,0:T(8,128)(2,1)S(1)}, bf16[2,128,1024]{2,1,0:T(8,128)(2,1)}, u32[]{:S(2)}, u32[]{:S(2)}) %collective-permute-start.28) | collective-permute-done | bytes 524320 | tf_op jit(solution)/shard_map/ppermute | solution.py:434
  128.8 1.8 collective-permute-start.20
  132.2 2.0 collective-permute-start.33
  134.2 2.2 collective-permute-start.32
  136.3 3.7 %collective-permute-done.22.refs_3_.refs_2_ = bf16[2,128,1024]{2,1,0:T(8,128)(2,1)} collective-permute-done((bf16[2,128,1024]{2,1,0:T(8,128)(2,1)S(1)}, bf16[2,128,1024]{2,1,0:T(8,128)(2,1)}, u32[]{:S(2)}, u32[]{:S(2)}) %collective-permute-start.22) | collective-permute-done | bytes 524320 | tf_op jit(solution)/shard_map/ppermute | solution.py:434
  140.0 1.8 collective-permute-start.31
  142.6 2.7 %collective-permute-start.25 = (bf16[2,128,1024]{2,1,0:T(8,128)(2,1)}, bf16[2,128,1024]{2,1,0:T(8,128)(2,1)}, u32[]{:S(2)}, u32[]{:S(2)}) collective-permute-start(bf16[2,128,1024]{2,1,0:T(8,128)(2,1)} %collective-permute-done.21), channel_id=1, source_target_pairs={{4,0},{5,1},{6,2},{7,3},{8,12},{9,13},{10,14},{11,15},{20,16},{21,... | collective-permute-start | bytes 1572872 | tf_op jit(solution)/shard_map/ppermute | solution.py:434
  145.3 3.0 %collective-permute-start.24 = (bf16[2,128,1024]{2,1,0:T(8,128)(2,1)}, bf16[2,128,1024]{2,1,0:T(8,128)(2,1)}, u32[]{:S(2)}, u32[]{:S(2)}) collective-permute-start(bf16[2,128,1024]{2,1,0:T(8,128)(2,1)} %collective-permute-done.22.refs_3_.refs_2_), channel_id=1, source_target_pairs={{4,8},{5,9},{6,10},{7,11},{8,4},{9,5},{10,6},{11,7},{20,24},{21,25... | collective-permute-start | bytes 1572872 | tf_op jit(solution)/shard_map/ppermute | solution.py:434
  150.0 1.5 collective-permute-start.23
  153.6 1.0 copy-done.11
  155.7 4.8 %backward.7.refs_0_ = bf16[2,128,8192]{2,1,0:T(8,128)(2,1)S(1)} custom-call(s32[3,16]{1,0:T(4,128)S(1)} %pad_add_fusion.meta_ref, bf16[1024,1024]{1,0:T(8,128)(2,1)S(1)} %copy-done, bf16[1024,512]{1,0:T(8,128)(2,1)S(1)} %copy-done.1, bf16[2,128,1024]{2,1,0:T(8,128)(2,1)S(1)} %copy-done.5, bf16[2,128,1024]{2,1,0:T(8,128)(2,1)S(1)} %copy-done.8, ...), custom_call_target="tpu_custom_call" | custom-call | flops 1024 | bytes 1024 | tf_op jit(solution)/shard_map/backward/pallas_call | solution.py:279
  160.6 3.4 %copy-done.3 = f32[2,128,8192]{2,1,0:T(8,128)S(1)} copy-done((f32[2,128,8192]{2,1,0:T(8,128)S(1)}, f32[2,128,8192]{2,1,0:T(8,128)}, u32[]{:S(2)}) %copy-start.3) | copy-done | bytes 8388632
  163.9 4.6 %backward.6.refs_0_ = f32[2,128,8192]{2,1,0:T(8,128)S(1)} custom-call(s32[3,16]{1,0:T(4,128)S(1)} %pad_add_fusion.meta_ref, bf16[1024,1024]{1,0:T(8,128)(2,1)S(1)} %copy-done, bf16[1024,512]{1,0:T(8,128)(2,1)S(1)} %copy-done.1, f32[2,128,8192]{2,1,0:T(8,128)S(1)} %copy-done.3, bf16[2,128,1024]{2,1,0:T(8,128)(2,1)S(1)} %copy-done.6, ...), custom_call_target="tpu_custom_call" | custom-call | flops 1024 | bytes 1024 | tf_op jit(solution)/shard_map/backward/pallas_call | solution.py:279
  168.7 1.7 collective-permute-start.36
  170.5 1.1 broadcast_select_fusion.3.refs_1_
  171.6 1.1 collective-permute-start.29
  172.7 1.3 collective-permute-start.30
  174.0 3.0 %backward.8.refs_0_ = bf16[2,128,8192]{2,1,0:T(8,128)(2,1)S(1)} custom-call(s32[3,16]{1,0:T(4,128)S(1)} %pad_add_fusion.meta_ref, bf16[1024,1024]{1,0:T(8,128)(2,1)S(1)} %copy-done, bf16[1024,512]{1,0:T(8,128)(2,1)S(1)} %copy-done.1, bf16[2,128,8192]{2,1,0:T(8,128)(2,1)S(1)} %backward.7.refs_0_, bf16[2,128,1024]{2,1,0:T(8,128)(2,1)S(1)} %broadcast_select_fusion.3.refs_1_, ...), custom_call_target="tpu_custom_call" | custom-call | flops 1024 | bytes 1024 | tf_op jit(solution)/shard_map/backward/pallas_call | solution.py:279
  177.0 4.5 %collective-permute-done.35.refs_8_.refs_4_ = bf16[2,128,1024]{2,1,0:T(8,128)(2,1)S(1)} collective-permute-done((bf16[2,128,1024]{2,1,0:T(8,128)(2,1)S(1)}, bf16[2,128,1024]{2,1,0:T(8,128)(2,1)S(1)}, u32[]{:S(2)}, u32[]{:S(2)}) %collective-permute-start.35) | collective-permute-done | bytes 524320 | tf_op jit(solution)/shard_map/ppermute | solution.py:430
  181.5 1.1 broadcast_select_fusion.refs_6_.refs_2_
  183.0 9.7 %collective-permute-done.29.refs_7_.refs_3_ = bf16[2,128,1024]{2,1,0:T(8,128)(2,1)S(1)} collective-permute-done((bf16[2,128,1024]{2,1,0:T(8,128)(2,1)S(1)}, bf16[2,128,1024]{2,1,0:T(8,128)(2,1)S(1)}, u32[]{:S(2)}, u32[]{:S(2)}) %collective-permute-start.29) | collective-permute-done | bytes 524320 | tf_op jit(solution)/shard_map/ppermute | solution.py:430
  192.8 1.1 broadcast_select_fusion.1.refs_5_.refs_1_
  194.3 4.3 %backward.9.refs_0_ = f32[2,128,8192]{2,1,0:T(8,128)S(1)} custom-call(s32[3,16]{1,0:T(4,128)S(1)} %pad_add_fusion.meta_ref, bf16[1024,1024]{1,0:T(8,128)(2,1)S(1)} %copy-done, bf16[1024,512]{1,0:T(8,128)(2,1)S(1)} %copy-done.1, f32[2,128,8192]{2,1,0:T(8,128)S(1)} %backward.6.refs_0_, bf16[2,128,1024]{2,1,0:T(8,128)(2,1)S(1)} %broadcast_select_fusion.3.refs_1_, ...), custom_call_target="tpu_custom_call" | custom-call | flops 1024 | bytes 1024 | tf_op jit(solution)/shard_map/backward/pallas_call | solution.py:279
  198.5 5.5 %collective-permute-done.37.refs_6_ = bf16[2,128,1024]{2,1,0:T(8,128)(2,1)S(1)} collective-permute-done((bf16[2,128,1024]{2,1,0:T(8,128)(2,1)S(1)}, bf16[2,128,1024]{2,1,0:T(8,128)(2,1)S(1)}, u32[]{:S(2)}, u32[]{:S(2)}) %collective-permute-start.37) | collective-permute-done | bytes 524320 | tf_op jit(solution)/shard_map/ppermute | solution.py:430
  204.0 2.6 %collective-permute-start.43 = (bf16[2,128,1024]{2,1,0:T(8,128)(2,1)S(1)}, bf16[2,128,1024]{2,1,0:T(8,128)(2,1)S(1)}, u32[]{:S(2)}, u32[]{:S(2)}) collective-permute-start(bf16[2,128,1024]{2,1,0:T(8,128)(2,1)S(1)} %collective-permute-done.37.refs_6_), channel_id=1, source_target_pairs={{0,1},{1,0},{2,3},{3,2},{4,5},{5,4},{6,7},{7,6},{8,9},{9,8},{10,11... | collective-permute-start | bytes 1572872 | tf_op jit(solution)/shard_map/ppermute | solution.py:427
  206.6 3.2 %backward.10 = (bf16[2,128,2048]{2,1,0:T(8,128)(2,1)S(1)}, bf16[2,128,2048]{2,1,0:T(8,128)(2,1)S(1)}, bf16[2,128,2048]{2,1,0:T(8,128)(2,1)S(1)}, bf16[2,128,2048]{2,1,0:T(8,128)(2,1)S(1)}) custom-call(s32[3,16]{1,0:T(4,128)S(1)} %pad_add_fusion.meta_ref, bf16[1024,1024]{1,0:T(8,128)(2,1)S(1)} %copy-done, bf16[1024,512]{1,0:T(8,128)(2,1)S(1)} %copy-done.1, ...), custom_call_target="tpu_custom_call" | custom-call | flops 1024 | bytes 1024 | tf_op jit(solution)/shard_map/backward/pallas_call | solution.py:279
  210.5 4.8 %collective-permute-done.34.refs_5_ = bf16[2,128,1024]{2,1,0:T(8,128)(2,1)S(1)} collective-permute-done((bf16[2,128,1024]{2,1,0:T(8,128)(2,1)S(1)}, bf16[2,128,1024]{2,1,0:T(8,128)(2,1)S(1)}, u32[]{:S(2)}, u32[]{:S(2)}) %collective-permute-start.34) | collective-permute-done | bytes 524320 | tf_op jit(solution)/shard_map/ppermute | solution.py:430
  215.2 1.5 collective-permute-start.41
  216.7 3.0 %collective-permute-done.42.refs_7_ = bf16[2,128,1024]{2,1,0:T(8,128)(2,1)S(1)} collective-permute-done((bf16[2,128,1024]{2,1,0:T(8,128)(2,1)S(1)}, bf16[2,128,1024]{2,1,0:T(8,128)(2,1)S(1)}, u32[]{:S(2)}, u32[]{:S(2)}) %collective-permute-start.42) | collective-permute-done | bytes 524320 | tf_op jit(solution)/shard_map/ppermute | solution.py:427
  219.8 6.3 %backward.11 = f32[2,128,8192]{2,1,0:T(8,128)} custom-call(s32[3,16]{1,0:T(4,128)S(1)} %pad_add_fusion.meta_ref, bf16[1024,1024]{1,0:T(8,128)(2,1)S(1)} %copy-done, bf16[1024,512]{1,0:T(8,128)(2,1)S(1)} %copy-done.1, f32[2,128,8192]{2,1,0:T(8,128)S(1)} %backward.9.refs_0_, bf16[2,128,2048]{2,1,0:T(8,128)(2,1)S(1)} %collective-permute-done.38.refs_1_, ...), custom_call_target="tpu_custom_call" | custom-call | flops 1024 | bytes 1024 | tf_op jit(solution)/shard_map/backward/pallas_call | solution.py:279
  (107 shorter events, 16.5 us)
Async XLA Ops:
  0.0 3.4 %copy-start.2 = (f32[2,128,8192]{2,1,0:T(8,128)S(1)}, f32[2,128,8192]{2,1,0:T(8,128)}, u32[]{:S(2)}) copy-start(f32[2,128,8192]{2,1,0:T(8,128)} %refs_0_.1) | copy-start | bytes 25165828
  5.3 3.4 %copy-start.23 = (s32[16]{0:T(128)S(1)}, s32[16]{0:T(128)}, u32[]{:S(2)}) copy-start(s32[16]{0:T(128)} %param.12) | copy-start | bytes 196
  5.3 3.4 %copy-start.24 = (s32[16]{0:T(128)S(1)}, s32[16]{0:T(128)}, u32[]{:S(2)}) copy-start(s32[16]{0:T(128)} %param.13) | copy-start | bytes 196
  5.3 3.6 %copy-start = (bf16[1024,1024]{1,0:T(8,128)(2,1)S(1)}, bf16[1024,1024]{1,0:T(8,128)(2,1)}, u32[]{:S(2)}) copy-start(bf16[1024,1024]{1,0:T(8,128)(2,1)} %pupil_ref.17) | copy-start | bytes 6291460
  5.3 3.6 %copy-start.1 = (bf16[1024,512]{1,0:T(8,128)(2,1)S(1)}, bf16[1024,512]{1,0:T(8,128)(2,1)}, u32[]{:S(2)}) copy-start(bf16[1024,512]{1,0:T(8,128)(2,1)} %constant.42.clone.band_ref) | copy-start | bytes 3145732
  5.3 7.0 %collective-permute-start.1 = (bf16[128,8192]{1,0:T(8,128)(2,1)}, bf16[128,8192]{1,0:T(8,128)(2,1)}, u32[]{:S(2)}, u32[]{:S(2)}) collective-permute-start(bf16[128,8192]{1,0:T(8,128)(2,1)} %low_part.3.refs_1_), channel_id=1, source_target_pairs={{0,1},{1,0},{2,3},{3,2},{4,5},{5,4},{6,7},{7,6},{8,9},{9,8},{10,11... | collective-permute-start | bytes 6291464 | tf_op jit(solution)/shard_map/ppermute | solution.py:427
  7.9 5.3 %collective-permute-start = (bf16[128,8192]{1,0:T(8,128)(2,1)}, bf16[128,8192]{1,0:T(8,128)(2,1)}, u32[]{:S(2)}, u32[]{:S(2)}) collective-permute-start(bf16[128,8192]{1,0:T(8,128)(2,1)} %low_part.2.refs_0_), channel_id=1, source_target_pairs={{0,1},{1,0},{2,3},{3,2},{4,5},{5,4},{6,7},{7,6},{8,9},{9,8},{10,11... | collective-permute-start | bytes 6291464 | tf_op jit(solution)/shard_map/ppermute | solution.py:427
  16.5 18.0 %collective-permute-start.2 = (bf16[2,128,1024]{2,1,0:T(8,128)(2,1)S(1)}, bf16[2,128,1024]{2,1,0:T(8,128)(2,1)S(1)}, u32[]{:S(2)}, u32[]{:S(2)}) collective-permute-start(bf16[2,128,1024]{2,1,0:T(8,128)(2,1)S(1)} %get-tuple-element.78), channel_id=1, source_target_pairs={{0,2},{1,3},{2,0},{3,1},{4,6},{5,7},{6,4},{7,5},{8,10},{9,11},{10,... | collective-permute-start | bytes 1572872 | tf_op jit(solution)/shard_map/ppermute | solution.py:430
  17.8 23.1 %collective-permute-start.11 = (bf16[2,128,1024]{2,1,0:T(8,128)(2,1)S(1)}, bf16[2,128,1024]{2,1,0:T(8,128)(2,1)S(1)}, u32[]{:S(2)}, u32[]{:S(2)}) collective-permute-start(bf16[2,128,1024]{2,1,0:T(8,128)(2,1)S(1)} %get-tuple-element.74), channel_id=1, source_target_pairs={{0,2},{1,3},{2,0},{3,1},{4,6},{5,7},{6,4},{7,5},{8,10},{9,11},{10,... | collective-permute-start | bytes 1572872 | tf_op jit(solution)/shard_map/ppermute | solution.py:430
  34.7 13.5 %collective-permute-start.3 = (bf16[2,128,1024]{2,1,0:T(8,128)(2,1)S(1)}, bf16[2,128,1024]{2,1,0:T(8,128)(2,1)S(1)}, u32[]{:S(2)}, u32[]{:S(2)}) collective-permute-start(bf16[2,128,1024]{2,1,0:T(8,128)(2,1)S(1)} %fusion), channel_id=1, source_target_pairs={{0,4},{1,5},{2,6},{3,7},{12,8},{13,9},{14,10},{15,11},{16,20},{17,... | collective-permute-start | bytes 1572872 | tf_op jit(solution)/shard_map/ppermute | solution.py:434
  36.0 16.2 %collective-permute-start.4 = (bf16[2,128,1024]{2,1,0:T(8,128)(2,1)S(1)}, bf16[2,128,1024]{2,1,0:T(8,128)(2,1)S(1)}, u32[]{:S(2)}, u32[]{:S(2)}) collective-permute-start(bf16[2,128,1024]{2,1,0:T(8,128)(2,1)S(1)} %get-tuple-element.83), channel_id=1, source_target_pairs={{0,2},{1,3},{2,0},{3,1},{4,6},{5,7},{6,4},{7,5},{8,10},{9,11},{10,... | collective-permute-start | bytes 1572872 | tf_op jit(solution)/shard_map/ppermute | solution.py:430
  41.1 18.2 %collective-permute-start.12 = (bf16[2,128,1024]{2,1,0:T(8,128)(2,1)S(1)}, bf16[2,128,1024]{2,1,0:T(8,128)(2,1)S(1)}, u32[]{:S(2)}, u32[]{:S(2)}) collective-permute-start(bf16[2,128,1024]{2,1,0:T(8,128)(2,1)S(1)} %fusion.2), channel_id=1, source_target_pairs={{0,4},{1,5},{2,6},{3,7},{12,8},{13,9},{14,10},{15,11},{16,20},{17,... | collective-permute-start | bytes 1572872 | tf_op jit(solution)/shard_map/ppermute | solution.py:434
  42.4 21.0 %collective-permute-start.13 = (bf16[2,128,1024]{2,1,0:T(8,128)(2,1)S(1)}, bf16[2,128,1024]{2,1,0:T(8,128)(2,1)S(1)}, u32[]{:S(2)}, u32[]{:S(2)}) collective-permute-start(bf16[2,128,1024]{2,1,0:T(8,128)(2,1)S(1)} %get-tuple-element.100), channel_id=1, source_target_pairs={{0,2},{1,3},{2,0},{3,1},{4,6},{5,7},{6,4},{7,5},{8,10},{9,11},{10,... | collective-permute-start | bytes 1572872 | tf_op jit(solution)/shard_map/ppermute | solution.py:430
  52.4 18.2 %collective-permute-start.6 = (bf16[2,128,1024]{2,1,0:T(8,128)(2,1)S(1)}, bf16[2,128,1024]{2,1,0:T(8,128)(2,1)S(1)}, u32[]{:S(2)}, u32[]{:S(2)}) collective-permute-start(bf16[2,128,1024]{2,1,0:T(8,128)(2,1)S(1)} %fusion.1), channel_id=1, source_target_pairs={{0,4},{1,5},{2,6},{3,7},{12,8},{13,9},{14,10},{15,11},{16,20},{17,... | collective-permute-start | bytes 1572872 | tf_op jit(solution)/shard_map/ppermute | solution.py:434
  54.0 22.3 %collective-permute-start.5 = (bf16[2,128,1024]{2,1,0:T(8,128)(2,1)S(1)}, bf16[2,128,1024]{2,1,0:T(8,128)(2,1)S(1)}, u32[]{:S(2)}, u32[]{:S(2)}) collective-permute-start(bf16[2,128,1024]{2,1,0:T(8,128)(2,1)S(1)} %add_convert_fusion.7), channel_id=1, source_target_pairs={{4,8},{5,9},{6,10},{7,11},{8,4},{9,5},{10,6},{11,7},{20,24},{21,25... | collective-permute-start | bytes 1572872 | tf_op jit(solution)/shard_map/ppermute | solution.py:434
  57.2 19.1 %collective-permute-start.7 = (bf16[2,128,1024]{2,1,0:T(8,128)(2,1)S(1)}, bf16[2,128,1024]{2,1,0:T(8,128)(2,1)S(1)}, u32[]{:S(2)}, u32[]{:S(2)}) collective-permute-start(bf16[2,128,1024]{2,1,0:T(8,128)(2,1)S(1)} %get-tuple-element.88), channel_id=1, source_target_pairs={{0,2},{1,3},{2,0},{3,1},{4,6},{5,7},{6,4},{7,5},{8,10},{9,11},{10,... | collective-permute-start | bytes 1572872 | tf_op jit(solution)/shard_map/ppermute | solution.py:430
  63.6 18.2 %collective-permute-start.15 = (bf16[2,128,1024]{2,1,0:T(8,128)(2,1)S(1)}, bf16[2,128,1024]{2,1,0:T(8,128)(2,1)S(1)}, u32[]{:S(2)}, u32[]{:S(2)}) collective-permute-start(bf16[2,128,1024]{2,1,0:T(8,128)(2,1)S(1)} %fusion.3), channel_id=1, source_target_pairs={{0,4},{1,5},{2,6},{3,7},{12,8},{13,9},{14,10},{15,11},{16,20},{17,... | collective-permute-start | bytes 1572872 | tf_op jit(solution)/shard_map/ppermute | solution.py:434
  65.2 16.7 %collective-permute-start.14 = (bf16[2,128,1024]{2,1,0:T(8,128)(2,1)S(1)}, bf16[2,128,1024]{2,1,0:T(8,128)(2,1)S(1)}, u32[]{:S(2)}, u32[]{:S(2)}) collective-permute-start(bf16[2,128,1024]{2,1,0:T(8,128)(2,1)S(1)} %add_convert_fusion.3), channel_id=1, source_target_pairs={{4,8},{5,9},{6,10},{7,11},{8,4},{9,5},{10,6},{11,7},{20,24},{21,25... | collective-permute-start | bytes 1572872 | tf_op jit(solution)/shard_map/ppermute | solution.py:434
  70.6 18.0 %collective-permute-start.16 = (bf16[2,128,1024]{2,1,0:T(8,128)(2,1)S(1)}, bf16[2,128,1024]{2,1,0:T(8,128)(2,1)S(1)}, u32[]{:S(2)}, u32[]{:S(2)}) collective-permute-start(bf16[2,128,1024]{2,1,0:T(8,128)(2,1)S(1)} %get-tuple-element.105), channel_id=1, source_target_pairs={{0,2},{1,3},{2,0},{3,1},{4,6},{5,7},{6,4},{7,5},{8,10},{9,11},{10,... | collective-permute-start | bytes 1572872 | tf_op jit(solution)/shard_map/ppermute | solution.py:430
  76.5 16.3 %collective-permute-start.9 = (bf16[2,128,1024]{2,1,0:T(8,128)(2,1)S(1)}, bf16[2,128,1024]{2,1,0:T(8,128)(2,1)S(1)}, u32[]{:S(2)}, u32[]{:S(2)}) collective-permute-start(bf16[2,128,1024]{2,1,0:T(8,128)(2,1)S(1)} %add_convert_fusion.6), channel_id=1, source_target_pairs={{4,8},{5,9},{6,10},{7,11},{8,4},{9,5},{10,6},{11,7},{20,24},{21,25... | collective-permute-start | bytes 1572872 | tf_op jit(solution)/shard_map/ppermute | solution.py:434
  78.4 21.2 %collective-permute-start.8 = (bf16[2,128,1024]{2,1,0:T(8,128)(2,1)S(1)}, bf16[2,128,1024]{2,1,0:T(8,128)(2,1)S(1)}, u32[]{:S(2)}, u32[]{:S(2)}) collective-permute-start(bf16[2,128,1024]{2,1,0:T(8,128)(2,1)S(1)} %get-tuple-element.90), channel_id=1, source_target_pairs={{0,2},{1,3},{2,0},{3,1},{4,6},{5,7},{6,4},{7,5},{8,10},{9,11},{10,... | collective-permute-start | bytes 1572872 | tf_op jit(solution)/shard_map/ppermute | solution.py:430
  81.9 17.7 %collective-permute-start.10 = (bf16[2,128,1024]{2,1,0:T(8,128)(2,1)S(1)}, bf16[2,128,1024]{2,1,0:T(8,128)(2,1)S(1)}, u32[]{:S(2)}, u32[]{:S(2)}) collective-permute-start(bf16[2,128,1024]{2,1,0:T(8,128)(2,1)S(1)} %add_convert_fusion.5), channel_id=1, source_target_pairs={{0,4},{1,5},{2,6},{3,7},{12,8},{13,9},{14,10},{15,11},{4,0},{5,1},... | collective-permute-start | bytes 1572872 | tf_op jit(solution)/shard_map/ppermute | solution.py:434
  88.9 12.7 %collective-permute-start.18 = (bf16[2,128,1024]{2,1,0:T(8,128)(2,1)S(1)}, bf16[2,128,1024]{2,1,0:T(8,128)(2,1)S(1)}, u32[]{:S(2)}, u32[]{:S(2)}) collective-permute-start(bf16[2,128,1024]{2,1,0:T(8,128)(2,1)S(1)} %add_convert_fusion.2), channel_id=1, source_target_pairs={{4,8},{5,9},{6,10},{7,11},{8,4},{9,5},{10,6},{11,7},{20,24},{21,25... | collective-permute-start | bytes 1572872 | tf_op jit(solution)/shard_map/ppermute | solution.py:434
  91.0 19.2 %collective-permute-start.17 = (bf16[2,128,1024]{2,1,0:T(8,128)(2,1)S(1)}, bf16[2,128,1024]{2,1,0:T(8,128)(2,1)S(1)}, u32[]{:S(2)}, u32[]{:S(2)}) collective-permute-start(bf16[2,128,1024]{2,1,0:T(8,128)(2,1)S(1)} %get-tuple-element.107), channel_id=1, source_target_pairs={{0,2},{1,3},{2,0},{3,1},{4,6},{5,7},{6,4},{7,5},{8,10},{9,11},{10,... | collective-permute-start | bytes 1572872 | tf_op jit(solution)/shard_map/ppermute | solution.py:430
  92.8 17.4 %collective-permute-start.19 = (bf16[2,128,1024]{2,1,0:T(8,128)(2,1)S(1)}, bf16[2,128,1024]{2,1,0:T(8,128)(2,1)S(1)}, u32[]{:S(2)}, u32[]{:S(2)}) collective-permute-start(bf16[2,128,1024]{2,1,0:T(8,128)(2,1)S(1)} %add_convert_fusion.1), channel_id=1, source_target_pairs={{0,4},{1,5},{2,6},{3,7},{12,8},{13,9},{14,10},{15,11},{4,0},{5,1},... | collective-permute-start | bytes 1572872 | tf_op jit(solution)/shard_map/ppermute | solution.py:434
  99.6 11.0 %copy-start.16 = (bf16[1024,1024]{1,0:T(8,128)(2,1)S(1)}, bf16[1024,1024]{1,0:T(8,128)(2,1)}, u32[]{:S(2)}) copy-start(bf16[1024,1024]{1,0:T(8,128)(2,1)} %constant.44.clone.refs_4_) | copy-start | bytes 6291460
  99.6 11.0 %copy-start.17 = (bf16[1024,1024]{1,0:T(8,128)(2,1)S(1)}, bf16[1024,1024]{1,0:T(8,128)(2,1)}, u32[]{:S(2)}) copy-start(bf16[1024,1024]{1,0:T(8,128)(2,1)} %constant.43.clone.refs_3_) | copy-start | bytes 6291460
  99.6 11.0 %copy-start.18 = (bf16[1,256,1024]{2,1,0:T(8,128)(2,1)S(1)}, bf16[1,256,1024]{2,1,0:T(8,128)(2,1)}, u32[]{:S(2)}) copy-start(bf16[1,256,1024]{2,1,0:T(8,128)(2,1)} %refs_2_.1) | copy-start | bytes 1572868
  115.5 13.3 %collective-permute-start.28 = (bf16[2,128,1024]{2,1,0:T(8,128)(2,1)S(1)}, bf16[2,128,1024]{2,1,0:T(8,128)(2,1)}, u32[]{:S(2)}, u32[]{:S(2)}) collective-permute-start(bf16[2,128,1024]{2,1,0:T(8,128)(2,1)S(1)} %get-tuple-element.115.refs_2_.refs_1_), channel_id=1, source_target_pairs={{0,4},{1,5},{2,6},{3,7},{12,8},{13,9},{14,10},{15,11},{4,0},{5,1},... | collective-permute-start | bytes 1572872 | tf_op jit(solution)/shard_map/ppermute | solution.py:434
  115.5 15.8 %collective-permute-start.27 = (bf16[2,128,1024]{2,1,0:T(8,128)(2,1)S(1)}, bf16[2,128,1024]{2,1,0:T(8,128)(2,1)S(1)}, u32[]{:S(2)}, u32[]{:S(2)}) collective-permute-start(bf16[2,128,1024]{2,1,0:T(8,128)(2,1)S(1)} %get-tuple-element.115.refs_2_.refs_1_), channel_id=1, source_target_pairs={{4,8},{5,9},{6,10},{7,11},{8,4},{9,5},{10,6},{11,7},{20,24},{21,25... | collective-permute-start | bytes 1572872 | tf_op jit(solution)/shard_map/ppermute | solution.py:434
  117.5 13.9 %collective-permute-start.26 = (bf16[2,128,1024]{2,1,0:T(8,128)(2,1)S(1)}, bf16[2,128,1024]{2,1,0:T(8,128)(2,1)S(1)}, u32[]{:S(2)}, u32[]{:S(2)}) collective-permute-start(bf16[2,128,1024]{2,1,0:T(8,128)(2,1)S(1)} %get-tuple-element.115.refs_2_.refs_1_), channel_id=1, source_target_pairs={{0,2},{1,3},{2,0},{3,1},{4,6},{5,7},{6,4},{7,5},{8,10},{9,11},{10,... | collective-permute-start | bytes 1572872 | tf_op jit(solution)/shard_map/ppermute | solution.py:430
  120.1 19.9 %collective-permute-start.22 = (bf16[2,128,1024]{2,1,0:T(8,128)(2,1)S(1)}, bf16[2,128,1024]{2,1,0:T(8,128)(2,1)}, u32[]{:S(2)}, u32[]{:S(2)}) collective-permute-start(bf16[2,128,1024]{2,1,0:T(8,128)(2,1)S(1)} %get-tuple-element.112.refs_1_.refs_0_), channel_id=1, source_target_pairs={{0,4},{1,5},{2,6},{3,7},{12,8},{13,9},{14,10},{15,11},{4,0},{5,1},... | collective-permute-start | bytes 1572872 | tf_op jit(solution)/shard_map/ppermute | solution.py:434
  120.4 21.4 %collective-permute-start.21 = (bf16[2,128,1024]{2,1,0:T(8,128)(2,1)S(1)}, bf16[2,128,1024]{2,1,0:T(8,128)(2,1)}, u32[]{:S(2)}, u32[]{:S(2)}) collective-permute-start(bf16[2,128,1024]{2,1,0:T(8,128)(2,1)S(1)} %get-tuple-element.112.refs_1_.refs_0_), channel_id=1, source_target_pairs={{4,8},{5,9},{6,10},{7,11},{8,4},{9,5},{10,6},{11,7},{20,24},{21,25... | collective-permute-start | bytes 1572872 | tf_op jit(solution)/shard_map/ppermute | solution.py:434
  128.8 13.0 %collective-permute-start.20 = (bf16[2,128,1024]{2,1,0:T(8,128)(2,1)S(1)}, bf16[2,128,1024]{2,1,0:T(8,128)(2,1)S(1)}, u32[]{:S(2)}, u32[]{:S(2)}) collective-permute-start(bf16[2,128,1024]{2,1,0:T(8,128)(2,1)S(1)} %get-tuple-element.112.refs_1_.refs_0_), channel_id=1, source_target_pairs={{0,2},{1,3},{2,0},{3,1},{4,6},{5,7},{6,4},{7,5},{8,10},{9,11},{10,... | collective-permute-start | bytes 1572872 | tf_op jit(solution)/shard_map/ppermute | solution.py:430
  131.3 10.5 %copy-start.19 = (bf16[2,128,1024]{2,1,0:T(8,128)(2,1)}, bf16[2,128,1024]{2,1,0:T(8,128)(2,1)S(1)}, u32[]{:S(2)}) copy-start(bf16[2,128,1024]{2,1,0:T(8,128)(2,1)S(1)} %collective-permute-done.27) | copy-start | bytes 1572868
  132.2 17.1 %collective-permute-start.33 = (bf16[2,128,1024]{2,1,0:T(8,128)(2,1)S(1)}, bf16[2,128,1024]{2,1,0:T(8,128)(2,1)S(1)}, u32[]{:S(2)}, u32[]{:S(2)}) collective-permute-start(bf16[2,128,1024]{2,1,0:T(8,128)(2,1)S(1)} %collective-permute-done.27), channel_id=1, source_target_pairs={{4,0},{5,1},{6,2},{7,3},{8,12},{9,13},{10,14},{11,15},{20,16},{21,... | collective-permute-start | bytes 1572872 | tf_op jit(solution)/shard_map/ppermute | solution.py:434
  134.2 34.4 %collective-permute-start.32 = (bf16[2,128,1024]{2,1,0:T(8,128)(2,1)}, bf16[2,128,1024]{2,1,0:T(8,128)(2,1)}, u32[]{:S(2)}, u32[]{:S(2)}) collective-permute-start(bf16[2,128,1024]{2,1,0:T(8,128)(2,1)} %collective-permute-done.28.refs_4_.refs_3_), channel_id=1, source_target_pairs={{4,8},{5,9},{6,10},{7,11},{8,4},{9,5},{10,6},{11,7},{20,24},{21,25... | collective-permute-start | bytes 1572872 | tf_op jit(solution)/shard_map/ppermute | solution.py:434
  140.0 28.5 %collective-permute-start.31 = (bf16[2,128,1024]{2,1,0:T(8,128)(2,1)}, bf16[2,128,1024]{2,1,0:T(8,128)(2,1)}, u32[]{:S(2)}, u32[]{:S(2)}) collective-permute-start(bf16[2,128,1024]{2,1,0:T(8,128)(2,1)} %collective-permute-done.28.refs_4_.refs_3_), channel_id=1, source_target_pairs={{0,2},{1,3},{2,0},{3,1},{4,6},{5,7},{6,4},{7,5},{8,10},{9,11},{10,... | collective-permute-start | bytes 1572872 | tf_op jit(solution)/shard_map/ppermute | solution.py:430
  142.6 27.8 %collective-permute-start.25 = (bf16[2,128,1024]{2,1,0:T(8,128)(2,1)}, bf16[2,128,1024]{2,1,0:T(8,128)(2,1)}, u32[]{:S(2)}, u32[]{:S(2)}) collective-permute-start(bf16[2,128,1024]{2,1,0:T(8,128)(2,1)} %collective-permute-done.21), channel_id=1, source_target_pairs={{4,0},{5,1},{6,2},{7,3},{8,12},{9,13},{10,14},{11,15},{20,16},{21,... | collective-permute-start | bytes 1572872 | tf_op jit(solution)/shard_map/ppermute | solution.py:434
  145.3 25.1 %collective-permute-start.24 = (bf16[2,128,1024]{2,1,0:T(8,128)(2,1)}, bf16[2,128,1024]{2,1,0:T(8,128)(2,1)}, u32[]{:S(2)}, u32[]{:S(2)}) collective-permute-start(bf16[2,128,1024]{2,1,0:T(8,128)(2,1)} %collective-permute-done.22.refs_3_.refs_2_), channel_id=1, source_target_pairs={{4,8},{5,9},{6,10},{7,11},{8,4},{9,5},{10,6},{11,7},{20,24},{21,25... | collective-permute-start | bytes 1572872 | tf_op jit(solution)/shard_map/ppermute | solution.py:434
  150.0 20.4 %collective-permute-start.23 = (bf16[2,128,1024]{2,1,0:T(8,128)(2,1)}, bf16[2,128,1024]{2,1,0:T(8,128)(2,1)}, u32[]{:S(2)}, u32[]{:S(2)}) collective-permute-start(bf16[2,128,1024]{2,1,0:T(8,128)(2,1)} %collective-permute-done.22.refs_3_.refs_2_), channel_id=1, source_target_pairs={{0,2},{1,3},{2,0},{3,1},{4,6},{5,7},{6,4},{7,5},{8,10},{9,11},{10,... | collective-permute-start | bytes 1572872 | tf_op jit(solution)/shard_map/ppermute | solution.py:430
  151.5 1.0 copy-start.5
  152.6 1.0 copy-start.8
  153.6 1.0 copy-start.11
  154.7 1.0 copy-start.14
  155.7 4.8 %copy-start.6 = (bf16[2,128,1024]{2,1,0:T(8,128)(2,1)S(1)}, bf16[2,128,1024]{2,1,0:T(8,128)(2,1)}, u32[]{:S(2)}) copy-start(bf16[2,128,1024]{2,1,0:T(8,128)(2,1)} %copy-done.4) | copy-start | bytes 1572868
  155.7 4.8 %copy-start.9 = (bf16[2,128,1024]{2,1,0:T(8,128)(2,1)S(1)}, bf16[2,128,1024]{2,1,0:T(8,128)(2,1)}, u32[]{:S(2)}) copy-start(bf16[2,128,1024]{2,1,0:T(8,128)(2,1)} %copy-done.7) | copy-start | bytes 1572868
  155.7 4.8 %copy-start.12 = (bf16[2,128,1024]{2,1,0:T(8,128)(2,1)S(1)}, bf16[2,128,1024]{2,1,0:T(8,128)(2,1)}, u32[]{:S(2)}) copy-start(bf16[2,128,1024]{2,1,0:T(8,128)(2,1)} %copy-done.10) | copy-start | bytes 1572868
  155.7 4.8 %copy-start.15 = (bf16[2,128,1024]{2,1,0:T(8,128)(2,1)S(1)}, bf16[2,128,1024]{2,1,0:T(8,128)(2,1)}, u32[]{:S(2)}) copy-start(bf16[2,128,1024]{2,1,0:T(8,128)(2,1)} %copy-done.13) | copy-start | bytes 1572868
  160.6 3.4 %copy-start.3 = (f32[2,128,8192]{2,1,0:T(8,128)S(1)}, f32[2,128,8192]{2,1,0:T(8,128)}, u32[]{:S(2)}) copy-start(f32[2,128,8192]{2,1,0:T(8,128)} %refs_0_.1) | copy-start | bytes 25165828
  163.9 4.6 %copy-start.20 = (bf16[2,128,1024]{2,1,0:T(8,128)(2,1)S(1)}, bf16[2,128,1024]{2,1,0:T(8,128)(2,1)}, u32[]{:S(2)}) copy-start(bf16[2,128,1024]{2,1,0:T(8,128)(2,1)} %copy-done.19) | copy-start | bytes 1572868
  163.9 4.6 %copy-start.22 = (bf16[2,128,1024]{2,1,0:T(8,128)(2,1)S(1)}, bf16[2,128,1024]{2,1,0:T(8,128)(2,1)}, u32[]{:S(2)}) copy-start(bf16[2,128,1024]{2,1,0:T(8,128)(2,1)} %copy-done.21) | copy-start | bytes 1572868
  168.6 12.9 %collective-permute-start.35 = (bf16[2,128,1024]{2,1,0:T(8,128)(2,1)S(1)}, bf16[2,128,1024]{2,1,0:T(8,128)(2,1)S(1)}, u32[]{:S(2)}, u32[]{:S(2)}) collective-permute-start(bf16[2,128,1024]{2,1,0:T(8,128)(2,1)S(1)} %broadcast_select_fusion.2.refs_2_), channel_id=1, source_target_pairs={{0,2},{1,3},{2,0},{3,1},{4,6},{5,7},{6,4},{7,5},{8,10},{9,11},{10,... | collective-permute-start | bytes 1572872 | tf_op jit(solution)/shard_map/ppermute | solution.py:430
  168.7 12.8 %collective-permute-start.36 = (bf16[2,128,1024]{2,1,0:T(8,128)(2,1)}, bf16[2,128,1024]{2,1,0:T(8,128)(2,1)S(1)}, u32[]{:S(2)}, u32[]{:S(2)}) collective-permute-start(bf16[2,128,1024]{2,1,0:T(8,128)(2,1)} %collective-permute-done.32), channel_id=1, source_target_pairs={{4,0},{5,1},{6,2},{7,3},{8,12},{9,13},{10,14},{11,15},{20,16},{21,... | collective-permute-start | bytes 1572872 | tf_op jit(solution)/shard_map/ppermute | solution.py:434
  171.6 21.2 %collective-permute-start.29 = (bf16[2,128,1024]{2,1,0:T(8,128)(2,1)S(1)}, bf16[2,128,1024]{2,1,0:T(8,128)(2,1)S(1)}, u32[]{:S(2)}, u32[]{:S(2)}) collective-permute-start(bf16[2,128,1024]{2,1,0:T(8,128)(2,1)S(1)} %broadcast_select_fusion.3.refs_1_), channel_id=1, source_target_pairs={{0,2},{1,3},{2,0},{3,1},{4,6},{5,7},{6,4},{7,5},{8,10},{9,11},{10,... | collective-permute-start | bytes 1572872 | tf_op jit(solution)/shard_map/ppermute | solution.py:430
  172.7 20.1 %collective-permute-start.30 = (bf16[2,128,1024]{2,1,0:T(8,128)(2,1)}, bf16[2,128,1024]{2,1,0:T(8,128)(2,1)S(1)}, u32[]{:S(2)}, u32[]{:S(2)}) collective-permute-start(bf16[2,128,1024]{2,1,0:T(8,128)(2,1)} %collective-permute-done.24), channel_id=1, source_target_pairs={{4,0},{5,1},{6,2},{7,3},{8,12},{9,13},{10,14},{11,15},{20,16},{21,... | collective-permute-start | bytes 1572872 | tf_op jit(solution)/shard_map/ppermute | solution.py:434
  182.6 21.4 %collective-permute-start.37 = (bf16[2,128,1024]{2,1,0:T(8,128)(2,1)S(1)}, bf16[2,128,1024]{2,1,0:T(8,128)(2,1)S(1)}, u32[]{:S(2)}, u32[]{:S(2)}) collective-permute-start(bf16[2,128,1024]{2,1,0:T(8,128)(2,1)S(1)} %broadcast_select_fusion.refs_6_.refs_2_), channel_id=1, source_target_pairs={{0,2},{1,3},{2,0},{3,1},{4,6},{5,7},{6,4},{7,5},{8,10},{9,11},{10,... | collective-permute-start | bytes 1572872 | tf_op jit(solution)/shard_map/ppermute | solution.py:430
  193.9 21.4 %collective-permute-start.34 = (bf16[2,128,1024]{2,1,0:T(8,128)(2,1)S(1)}, bf16[2,128,1024]{2,1,0:T(8,128)(2,1)S(1)}, u32[]{:S(2)}, u32[]{:S(2)}) collective-permute-start(bf16[2,128,1024]{2,1,0:T(8,128)(2,1)S(1)} %broadcast_select_fusion.1.refs_5_.refs_1_), channel_id=1, source_target_pairs={{0,2},{1,3},{2,0},{3,1},{4,6},{5,7},{6,4},{7,5},{8,10},{9,11},{10,... | collective-permute-start | bytes 1572872 | tf_op jit(solution)/shard_map/ppermute | solution.py:430
  204.0 12.7 %collective-permute-start.43 = (bf16[2,128,1024]{2,1,0:T(8,128)(2,1)S(1)}, bf16[2,128,1024]{2,1,0:T(8,128)(2,1)S(1)}, u32[]{:S(2)}, u32[]{:S(2)}) collective-permute-start(bf16[2,128,1024]{2,1,0:T(8,128)(2,1)S(1)} %collective-permute-done.37.refs_6_), channel_id=1, source_target_pairs={{0,1},{1,0},{2,3},{3,2},{4,5},{5,4},{6,7},{7,6},{8,9},{9,8},{10,11... | collective-permute-start | bytes 1572872 | tf_op jit(solution)/shard_map/ppermute | solution.py:427
  209.8 10.0 %collective-permute-start.38 = (bf16[2,128,2048]{2,1,0:T(8,128)(2,1)S(1)}, bf16[2,128,2048]{2,1,0:T(8,128)(2,1)S(1)}, u32[]{:S(2)}, u32[]{:S(2)}) collective-permute-start(bf16[2,128,2048]{2,1,0:T(8,128)(2,1)S(1)} %get-tuple-element.137), channel_id=1, source_target_pairs={{0,1},{1,0},{2,3},{3,2},{4,5},{5,4},{6,7},{7,6},{8,9},{9,8},{10,11... | collective-permute-start | bytes 3145736 | tf_op jit(solution)/shard_map/ppermute | solution.py:427
  209.9 9.9 %collective-permute-start.39 = (bf16[2,128,2048]{2,1,0:T(8,128)(2,1)S(1)}, bf16[2,128,2048]{2,1,0:T(8,128)(2,1)S(1)}, u32[]{:S(2)}, u32[]{:S(2)}) collective-permute-start(bf16[2,128,2048]{2,1,0:T(8,128)(2,1)S(1)} %get-tuple-element.138), channel_id=1, source_target_pairs={{0,1},{1,0},{2,3},{3,2},{4,5},{5,4},{6,7},{7,6},{8,9},{9,8},{10,11... | collective-permute-start | bytes 3145736 | tf_op jit(solution)/shard_map/ppermute | solution.py:427
  210.4 9.4 %collective-permute-start.40 = (bf16[2,128,2048]{2,1,0:T(8,128)(2,1)S(1)}, bf16[2,128,2048]{2,1,0:T(8,128)(2,1)S(1)}, u32[]{:S(2)}, u32[]{:S(2)}) collective-permute-start(bf16[2,128,2048]{2,1,0:T(8,128)(2,1)S(1)} %get-tuple-element.139), channel_id=1, source_target_pairs={{0,1},{1,0},{2,3},{3,2},{4,5},{5,4},{6,7},{7,6},{8,9},{9,8},{10,11... | collective-permute-start | bytes 3145736 | tf_op jit(solution)/shard_map/ppermute | solution.py:427
  215.2 4.6 %collective-permute-start.41 = (bf16[2,128,2048]{2,1,0:T(8,128)(2,1)S(1)}, bf16[2,128,2048]{2,1,0:T(8,128)(2,1)S(1)}, u32[]{:S(2)}, u32[]{:S(2)}) collective-permute-start(bf16[2,128,2048]{2,1,0:T(8,128)(2,1)S(1)} %get-tuple-element.140), channel_id=1, source_target_pairs={{0,1},{1,0},{2,3},{3,2},{4,5},{5,4},{6,7},{7,6},{8,9},{9,8},{10,11... | collective-permute-start | bytes 3145736 | tf_op jit(solution)/shard_map/ppermute | solution.py:427
  216.7 3.0 %collective-permute-start.42 = (bf16[2,128,1024]{2,1,0:T(8,128)(2,1)S(1)}, bf16[2,128,1024]{2,1,0:T(8,128)(2,1)S(1)}, u32[]{:S(2)}, u32[]{:S(2)}) collective-permute-start(bf16[2,128,1024]{2,1,0:T(8,128)(2,1)S(1)} %collective-permute-done.34.refs_5_), channel_id=1, source_target_pairs={{0,1},{1,0},{2,3},{3,2},{4,5},{5,4},{6,7},{7,6},{8,9},{9,8},{10,11... | collective-permute-start | bytes 1572872 | tf_op jit(solution)/shard_map/ppermute | solution.py:427
  (5 other events, 4.0 us)

commit v11 on v9

--- a/solution.py
+++ b/solution.py
@@ -165,6 +165,8 @@
         out_ref[:, :, columns] = part_refs[0][:, :, columns] + chunk
     if parts == 1:
         out_ref[...] = part_refs[0][...]
+    if parts == 0:
+        out_ref[...] = jnp.zeros_like(out_ref)
     for slot, groups in zip(slots, held):
         of_image = [next(back_refs) if there else None for there in groups]
         subtract_image(meta_ref, slot, of_image, pupil_ref, band_ref, out_ref, win)
@@ -516,7 +518,7 @@
         pieces["far inner", stream] = along(pieces[("beside", 0), stream], inner)
         pieces["outward", stream] = along(pieces["inner", stream], outward)
         if stream == last:
-            pieces["result", stream] = apply([spectrum], early)
+            pieces["result", stream] = apply([], early)
             close(stream, ("beside", 2), "far inner", "outward", "result")
         else:
             pieces["slab", stream] = apply([], early, 1)[0]
@@ -541,7 +543,7 @@
     twin = sibling(far_other)
     slab = [sibling(chunk) for chunk in chunks[:-1]]
     result, twin = together((pieces["result", last], twin))
-    result = apply([result], later + late)
+    result = apply([spectrum, result], later + late)
     chunk, result = together((chunks[-1], result))
     slab.append(sibling(chunk))
     arriving, result = together((pieces[("far", 2), last], result))

time: 226 us -> 228 us (level)
  waiting for transfers between devices: 84.9 us -> 73.9 us
  starting transfers between devices: 69.2 us -> 76.5 us
  local copies, waits for them, and re-layouts: 11.2 us -> 14.6 us
    ppermute x16, waiting for transfers between devices: 53.8 us -> 46.7 us  [across(): return lax.ppermute(value, 'ty', [(i, i ^ 2) for i in range(count)])]
    ppermute x20, waiting for transfers between devices: 27.7 us -> 22.7 us  [along(): return lax.ppermute(value, 'ty', pairs)]
    ppermute x16, starting transfers between devices: 15 us -> 18.8 us  [across(): return lax.ppermute(value, 'ty', [(i, i ^ 2) for i in range(count)])]
    unnamed x28 -> x32, local copies, waits for them, and re-layouts: 10.5 us -> 13.9 us
  transfers between devices with their start and end apart: 44 -> 44, of which waited for: 24 -> 21; matrix products, arithmetic and copies ran while one was open for 3% -> 3% of each run, Pallas kernels for 16% -> 17%
where the time goes in v11:
time: 228 us; the launch traced here: 226 us
  starting transfers between devices  76.5 us (34%)
  waiting for transfers between devices  73.9 us (32%)
  Pallas kernels  53.3 us (23%)
  local copies, waits for them, and re-layouts  14.6 us (6%)
  other arithmetic  6.82 us (3%)
    ppermute x20, starting transfers between devices, along(): return lax.ppermute(value, 'ty', pairs)  50.1 us
    ppermute x16, waiting for transfers between devices, across(): return lax.ppermute(value, 'ty', [(i, i ^ 2) for i in range(count)])  46.7 us
    pallas_call x6, Pallas kernels, backward(): pl.pallas_call(functools.partial(kernel, slots=slots, held=held, parts=le...  24.9 us
    ppermute x20, waiting for transfers between devices, along(): return lax.ppermute(value, 'ty', pairs)  22.7 us
    pallas_call x3, Pallas kernels, forward(): pl.pallas_call(functools.partial(forward_kernel, base=base, images=images...  19 us
    ppermute x16, starting transfers between devices, across(): return lax.ppermute(value, 'ty', [(i, i ^ 2) for i in range(count)])  18.8 us
    unnamed x32, local copies, waits for them, and re-layouts  13.9 us
    ppermute x8, starting transfers between devices, sibling(): return lax.ppermute(value, 'ty', [(i, i ^ 1) for i in range(count)])  7.58 us
  transfers between devices with their start and end apart: 44, of which 21 were waited for; matrix products, arithmetic and copies ran while one was open for 3% of the time, Pallas kernels for 17%

profile of v11, /device:TPU:11, one launch (start us, length us, event | category | flops | bytes accessed | tf_op | source)
XLA Modules:
  0.0 225.6 jit_solution(4780010833927770549)
XLA Ops:
  0.0 3.4 %copy-done.2 = f32[2,128,8192]{2,1,0:T(8,128)S(1)} copy-done((f32[2,128,8192]{2,1,0:T(8,128)S(1)}, f32[2,128,8192]{2,1,0:T(8,128)}, u32[]{:S(2)}) %copy-start.2) | copy-done | bytes 8388632
  3.4 1.9 low_part.3.refs_1_
  6.1 1.8 low_part.2.refs_0_
  9.0 2.3 %forward.3.refs_2_ = bf16[2,256,1024]{2,1,0:T(8,128)(2,1)S(1)} custom-call(s32[3,16]{1,0:T(4,128)S(1)} %pad_add_fusion.meta_ref, bf16[1024,1024]{1,0:T(8,128)(2,1)S(1)} %copy-done, bf16[1024,512]{1,0:T(8,128)(2,1)S(1)} %copy-done.1, bf16[128,8192]{1,0:T(8,128)(2,1)} %low_part.2.refs_0_, bf16[128,8192]{1,0:T(8,128)(2,1)} %low_part.3.refs_1_), custom_call_target="tpu_custom_call" | custom-call | flops 1024 | bytes 1024 | tf_op jit(solution)/shard_map/forward/pallas_call | solution.py:259
  11.3 1.9 collective-permute-done.refs_0_.refs_2_
  13.2 2.3 %forward.4 = (bf16[2,128,1024]{2,1,0:T(8,128)(2,1)S(1)}, bf16[2,128,1024]{2,1,0:T(8,128)(2,1)S(1)}) custom-call(s32[3,16]{1,0:T(4,128)S(1)} %pad_add_fusion.meta_ref, bf16[1024,1024]{1,0:T(8,128)(2,1)S(1)} %copy-done, bf16[1024,512]{1,0:T(8,128)(2,1)S(1)} %copy-done.1, bf16[128,8192]{1,0:T(8,128)(2,1)} %collective-permute-done.refs_0_.refs_2_, ...), custom_call_target="tpu_custom_call" | custom-call | flops 1024 | bytes 1024 | tf_op jit(solution)/shard_map/forward/pallas_call | solution.py:259
  15.5 2.3 %collective-permute-start.2 = (bf16[2,128,1024]{2,1,0:T(8,128)(2,1)S(1)}, bf16[2,128,1024]{2,1,0:T(8,128)(2,1)S(1)}, u32[]{:S(2)}, u32[]{:S(2)}) collective-permute-start(bf16[2,128,1024]{2,1,0:T(8,128)(2,1)S(1)} %get-tuple-element.80), channel_id=1, source_target_pairs={{0,2},{1,3},{2,0},{3,1},{4,6},{5,7},{6,4},{7,5},{8,10},{9,11},{10,... | collective-permute-start | bytes 1572872 | tf_op jit(solution)/shard_map/ppermute | solution.py:432
  17.9 14.4 %forward.5 = (bf16[2,128,1024]{2,1,0:T(8,128)(2,1)S(1)}, bf16[2,128,1024]{2,1,0:T(8,128)(2,1)S(1)}, bf16[2,128,1024]{2,1,0:T(8,128)(2,1)S(1)}, bf16[2,128,1024]{...) custom-call(s32[3,16]{1,0:T(4,128)S(1)} %pad_add_fusion.meta_ref, ...), custom_call_target="tpu_custom_call" | custom-call | flops 1024 | bytes 1024 | tf_op jit(solution)/shard_map/forward/pallas_call | solution.py:259
  32.6 1.3 collective-permute-start.3
  33.9 3.5 %collective-permute-start.4 = (bf16[2,128,1024]{2,1,0:T(8,128)(2,1)S(1)}, bf16[2,128,1024]{2,1,0:T(8,128)(2,1)S(1)}, u32[]{:S(2)}, u32[]{:S(2)}) collective-permute-start(bf16[2,128,1024]{2,1,0:T(8,128)(2,1)S(1)} %get-tuple-element.85), channel_id=1, source_target_pairs={{0,2},{1,3},{2,0},{3,1},{4,6},{5,7},{6,4},{7,5},{8,10},{9,11},{10,... | collective-permute-start | bytes 1572872 | tf_op jit(solution)/shard_map/ppermute | solution.py:432
  37.4 3.2 %collective-permute-done.11 = bf16[2,128,1024]{2,1,0:T(8,128)(2,1)S(1)} collective-permute-done((bf16[2,128,1024]{2,1,0:T(8,128)(2,1)S(1)}, bf16[2,128,1024]{2,1,0:T(8,128)(2,1)S(1)}, u32[]{:S(2)}, u32[]{:S(2)}) %collective-permute-start.11) | collective-permute-done | bytes 524320 | tf_op jit(solution)/shard_map/ppermute | solution.py:432
  40.7 1.3 collective-permute-start.12
  42.0 1.8 collective-permute-start.13
  43.8 3.0 %collective-permute-done.3 = bf16[2,128,1024]{2,1,0:T(8,128)(2,1)S(1)} collective-permute-done((bf16[2,128,1024]{2,1,0:T(8,128)(2,1)S(1)}, bf16[2,128,1024]{2,1,0:T(8,128)(2,1)S(1)}, u32[]{:S(2)}, u32[]{:S(2)}) %collective-permute-start.3) | collective-permute-done | bytes 524320 | tf_op jit(solution)/shard_map/ppermute | solution.py:436
  46.8 4.9 %collective-permute-done.4 = bf16[2,128,1024]{2,1,0:T(8,128)(2,1)S(1)} collective-permute-done((bf16[2,128,1024]{2,1,0:T(8,128)(2,1)S(1)}, bf16[2,128,1024]{2,1,0:T(8,128)(2,1)S(1)}, u32[]{:S(2)}, u32[]{:S(2)}) %collective-permute-start.4) | collective-permute-done | bytes 524320 | tf_op jit(solution)/shard_map/ppermute | solution.py:432
  51.9 1.3 collective-permute-start.6
  53.5 4.0 %collective-permute-start.5 = (bf16[2,128,1024]{2,1,0:T(8,128)(2,1)S(1)}, bf16[2,128,1024]{2,1,0:T(8,128)(2,1)S(1)}, u32[]{:S(2)}, u32[]{:S(2)}) collective-permute-start(bf16[2,128,1024]{2,1,0:T(8,128)(2,1)S(1)} %add_convert_fusion.7), channel_id=1, source_target_pairs={{4,8},{5,9},{6,10},{7,11},{8,4},{9,5},{10,6},{11,7},{20,24},{21,25... | collective-permute-start | bytes 1572872 | tf_op jit(solution)/shard_map/ppermute | solution.py:436
  57.5 1.8 collective-permute-start.7
  59.3 3.7 %collective-permute-done.13 = bf16[2,128,1024]{2,1,0:T(8,128)(2,1)S(1)} collective-permute-done((bf16[2,128,1024]{2,1,0:T(8,128)(2,1)S(1)}, bf16[2,128,1024]{2,1,0:T(8,128)(2,1)S(1)}, u32[]{:S(2)}, u32[]{:S(2)}) %collective-permute-start.13) | collective-permute-done | bytes 524320 | tf_op jit(solution)/shard_map/ppermute | solution.py:432
  63.2 1.3 collective-permute-start.15
  64.8 4.0 %collective-permute-start.14 = (bf16[2,128,1024]{2,1,0:T(8,128)(2,1)S(1)}, bf16[2,128,1024]{2,1,0:T(8,128)(2,1)S(1)}, u32[]{:S(2)}, u32[]{:S(2)}) collective-permute-start(bf16[2,128,1024]{2,1,0:T(8,128)(2,1)S(1)} %add_convert_fusion.3), channel_id=1, source_target_pairs={{4,8},{5,9},{6,10},{7,11},{8,4},{9,5},{10,6},{11,7},{20,24},{21,25... | collective-permute-start | bytes 1572872 | tf_op jit(solution)/shard_map/ppermute | solution.py:436
  69.3 1.5 collective-permute-start.16
  70.8 3.4 %collective-permute-done.7 = bf16[2,128,1024]{2,1,0:T(8,128)(2,1)S(1)} collective-permute-done((bf16[2,128,1024]{2,1,0:T(8,128)(2,1)S(1)}, bf16[2,128,1024]{2,1,0:T(8,128)(2,1)S(1)}, u32[]{:S(2)}, u32[]{:S(2)}) %collective-permute-start.7) | collective-permute-done | bytes 524320 | tf_op jit(solution)/shard_map/ppermute | solution.py:432
  74.5 4.0 %collective-permute-start.9 = (bf16[2,128,1024]{2,1,0:T(8,128)(2,1)S(1)}, bf16[2,128,1024]{2,1,0:T(8,128)(2,1)S(1)}, u32[]{:S(2)}, u32[]{:S(2)}) collective-permute-start(bf16[2,128,1024]{2,1,0:T(8,128)(2,1)S(1)} %add_convert_fusion.6), channel_id=1, source_target_pairs={{4,8},{5,9},{6,10},{7,11},{8,4},{9,5},{10,6},{11,7},{20,24},{21,25... | collective-permute-start | bytes 1572872 | tf_op jit(solution)/shard_map/ppermute | solution.py:436
  78.5 1.6 collective-permute-start.8
  80.5 1.6 collective-permute-done.16
  82.4 10.2 %collective-permute-start.18 = (bf16[2,128,1024]{2,1,0:T(8,128)(2,1)S(1)}, bf16[2,128,1024]{2,1,0:T(8,128)(2,1)S(1)}, u32[]{:S(2)}, u32[]{:S(2)}) collective-permute-start(bf16[2,128,1024]{2,1,0:T(8,128)(2,1)S(1)} %add_convert_fusion.2), channel_id=1, source_target_pairs={{4,8},{5,9},{6,10},{7,11},{8,4},{9,5},{10,6},{11,7},{20,24},{21,25... | collective-permute-start | bytes 1572872 | tf_op jit(solution)/shard_map/ppermute | solution.py:436
  93.8 9.2 %collective-permute-done.18 = bf16[2,128,1024]{2,1,0:T(8,128)(2,1)S(1)} collective-permute-done((bf16[2,128,1024]{2,1,0:T(8,128)(2,1)S(1)}, bf16[2,128,1024]{2,1,0:T(8,128)(2,1)S(1)}, u32[]{:S(2)}, u32[]{:S(2)}) %collective-permute-start.18) | collective-permute-done | bytes 524320 | tf_op jit(solution)/shard_map/ppermute | solution.py:436
  103.0 3.7 %collective-permute-done.17 = bf16[2,128,1024]{2,1,0:T(8,128)(2,1)S(1)} collective-permute-done((bf16[2,128,1024]{2,1,0:T(8,128)(2,1)S(1)}, bf16[2,128,1024]{2,1,0:T(8,128)(2,1)S(1)}, u32[]{:S(2)}, u32[]{:S(2)}) %collective-permute-start.17) | collective-permute-done | bytes 524320 | tf_op jit(solution)/shard_map/ppermute | solution.py:432
  107.1 5.6 %middle.1 = (bf16[2,128,1024]{2,1,0:T(8,128)(2,1)}, bf16[2,128,1024]{2,1,0:T(8,128)(2,1)S(1)}) custom-call(bf16[2,128,1024]{2,1,0:T(8,128)(2,1)S(1)} %add_convert_fusion.refs_0_, bf16[2,128,1024]{2,1,0:T(8,128)(2,1)S(1)} %add_convert_fusion.4.refs_1_, bf16[1,256,1024]{2,1,0:T(8,128)(2,1)S(1)} %copy-done.11, bf16[1024,1024]{1,0:T(8,128)(2,1)S(1)} %copy-done.10, ...), custom_call_target="tpu_custom_call" | custom-call | flops 1024 | bytes 1024 | tf_op jit(solution)/shard_map/middle/pallas_call | solution.py:297
  112.7 7.3 %collective-permute-start.27 = (bf16[2,128,1024]{2,1,0:T(8,128)(2,1)S(1)}, bf16[2,128,1024]{2,1,0:T(8,128)(2,1)}, u32[]{:S(2)}, u32[]{:S(2)}) collective-permute-start(bf16[2,128,1024]{2,1,0:T(8,128)(2,1)S(1)} %get-tuple-element.117.refs_1_), channel_id=1, source_target_pairs={{4,8},{5,9},{6,10},{7,11},{8,4},{9,5},{10,6},{11,7},{20,24},{21,25... | collective-permute-start | bytes 1572872 | tf_op jit(solution)/shard_map/ppermute | solution.py:436
  121.5 2.4 %collective-permute-start.21 = (bf16[2,128,1024]{2,1,0:T(8,128)(2,1)}, bf16[2,128,1024]{2,1,0:T(8,128)(2,1)}, u32[]{:S(2)}, u32[]{:S(2)}) collective-permute-start(bf16[2,128,1024]{2,1,0:T(8,128)(2,1)} %get-tuple-element.114.refs_0_), channel_id=1, source_target_pairs={{4,8},{5,9},{6,10},{7,11},{8,4},{9,5},{10,6},{11,7},{20,24},{21,25... | collective-permute-start | bytes 1572872 | tf_op jit(solution)/shard_map/ppermute | solution.py:436
  123.8 1.5 collective-permute-start.20
  125.4 6.5 %collective-permute-done.27 = bf16[2,128,1024]{2,1,0:T(8,128)(2,1)} collective-permute-done((bf16[2,128,1024]{2,1,0:T(8,128)(2,1)S(1)}, bf16[2,128,1024]{2,1,0:T(8,128)(2,1)}, u32[]{:S(2)}, u32[]{:S(2)}) %collective-permute-start.27) | collective-permute-done | bytes 524320 | tf_op jit(solution)/shard_map/ppermute | solution.py:436
  131.8 0.9 collective-permute-done.26.refs_5_
  133.5 2.1 collective-permute-start.33
  135.7 3.8 %collective-permute-start.32 = (bf16[2,128,1024]{2,1,0:T(8,128)(2,1)}, bf16[2,128,1024]{2,1,0:T(8,128)(2,1)}, u32[]{:S(2)}, u32[]{:S(2)}) collective-permute-start(bf16[2,128,1024]{2,1,0:T(8,128)(2,1)} %collective-permute-done.28.refs_3_), channel_id=1, source_target_pairs={{4,8},{5,9},{6,10},{7,11},{8,4},{9,5},{10,6},{11,7},{20,24},{21,25... | collective-permute-start | bytes 1572872 | tf_op jit(solution)/shard_map/ppermute | solution.py:436
  139.8 3.3 %collective-permute-done.21 = bf16[2,128,1024]{2,1,0:T(8,128)(2,1)} collective-permute-done((bf16[2,128,1024]{2,1,0:T(8,128)(2,1)}, bf16[2,128,1024]{2,1,0:T(8,128)(2,1)}, u32[]{:S(2)}, u32[]{:S(2)}) %collective-permute-start.21) | collective-permute-done | bytes 524320 | tf_op jit(solution)/shard_map/ppermute | solution.py:436
  143.1 0.9 collective-permute-done.20.refs_4_
  144.0 1.3 collective-permute-start.25
  145.3 3.1 %collective-permute-start.24 = (bf16[2,128,1024]{2,1,0:T(8,128)(2,1)}, bf16[2,128,1024]{2,1,0:T(8,128)(2,1)S(1)}, u32[]{:S(2)}, u32[]{:S(2)}) collective-permute-start(bf16[2,128,1024]{2,1,0:T(8,128)(2,1)} %collective-permute-done.22.refs_2_), channel_id=1, source_target_pairs={{4,8},{5,9},{6,10},{7,11},{8,4},{9,5},{10,6},{11,7},{20,24},{21,25... | collective-permute-start | bytes 1572872 | tf_op jit(solution)/shard_map/ppermute | solution.py:436
  148.4 1.0 copy-done.6
  149.5 1.0 copy-done.8
  150.5 4.1 %backward.7.refs_0_ = bf16[2,128,8192]{2,1,0:T(8,128)(2,1)S(1)} custom-call(s32[3,16]{1,0:T(4,128)S(1)} %pad_add_fusion.meta_ref, bf16[1024,1024]{1,0:T(8,128)(2,1)S(1)} %copy-done, bf16[1024,512]{1,0:T(8,128)(2,1)S(1)} %copy-done.1, bf16[2,128,1024]{2,1,0:T(8,128)(2,1)} %get-tuple-element.114.refs_0_, bf16[2,128,1024]{2,1,0:T(8,128)(2,1)S(1)} %copy-done.6, ...), custom_call_target="tpu_custom_call" | custom-call | flops 1024 | bytes 1024 | tf_op jit(solution)/shard_map/backward/pallas_call | solution.py:281
  155.2 1.1 broadcast_select_fusion.2.refs_2_.refs_3_
  156.3 1.1 collective-permute-start.35
  157.4 1.3 collective-permute-start.36
  158.7 4.0 %backward.6.refs_1_ = f32[2,128,8192]{2,1,0:T(8,128)S(1)} custom-call(s32[3,16]{1,0:T(4,128)S(1)} %pad_add_fusion.meta_ref, bf16[1024,1024]{1,0:T(8,128)(2,1)S(1)} %copy-done, bf16[1024,512]{1,0:T(8,128)(2,1)S(1)} %copy-done.1, bf16[2,128,1024]{2,1,0:T(8,128)(2,1)} %get-tuple-element.114.refs_0_, bf16[2,128,1024]{2,1,0:T(8,128)(2,1)S(1)} %copy-done.6, ...), custom_call_target="tpu_custom_call" | custom-call | flops 1024 | bytes 1024 | tf_op jit(solution)/shard_map/backward/pallas_call | solution.py:281
  162.7 3.4 %copy-done.3 = f32[2,128,8192]{2,1,0:T(8,128)} copy-done((f32[2,128,8192]{2,1,0:T(8,128)}, f32[2,128,8192]{2,1,0:T(8,128)S(1)}, u32[]{:S(2)}) %copy-start.3) | copy-done | bytes 8388632
  166.1 1.1 broadcast_select_fusion.3.refs_1_.refs_2_
  167.2 1.4 collective-permute-start.29
  168.6 1.3 collective-permute-start.30
  169.9 6.4 %collective-permute-done.35.refs_4_.refs_9_ = bf16[2,128,1024]{2,1,0:T(8,128)(2,1)S(1)} collective-permute-done((bf16[2,128,1024]{2,1,0:T(8,128)(2,1)S(1)}, bf16[2,128,1024]{2,1,0:T(8,128)(2,1)S(1)}, u32[]{:S(2)}, u32[]{:S(2)}) %collective-permute-start.35) | collective-permute-done | bytes 524320 | tf_op jit(solution)/shard_map/ppermute | solution.py:432
  176.3 1.2 broadcast_select_fusion.refs_2_.refs_7_
  177.9 3.2 %backward.8.refs_0_ = bf16[2,128,8192]{2,1,0:T(8,128)(2,1)S(1)} custom-call(s32[3,16]{1,0:T(4,128)S(1)} %pad_add_fusion.meta_ref, bf16[1024,1024]{1,0:T(8,128)(2,1)S(1)} %copy-done, bf16[1024,512]{1,0:T(8,128)(2,1)S(1)} %copy-done.1, bf16[2,128,8192]{2,1,0:T(8,128)(2,1)S(1)} %backward.7.refs_0_, ...), custom_call_target="tpu_custom_call" | custom-call | flops 1024 | bytes 1024 | tf_op jit(solution)/shard_map/backward/pallas_call | solution.py:281
  181.1 6.4 %collective-permute-done.29.refs_3_.refs_8_ = bf16[2,128,1024]{2,1,0:T(8,128)(2,1)S(1)} collective-permute-done((bf16[2,128,1024]{2,1,0:T(8,128)(2,1)S(1)}, bf16[2,128,1024]{2,1,0:T(8,128)(2,1)S(1)}, u32[]{:S(2)}, u32[]{:S(2)}) %collective-permute-start.29) | collective-permute-done | bytes 524320 | tf_op jit(solution)/shard_map/ppermute | solution.py:432
  187.5 11.2 %collective-permute-done.37.refs_6_ = bf16[2,128,1024]{2,1,0:T(8,128)(2,1)S(1)} collective-permute-done((bf16[2,128,1024]{2,1,0:T(8,128)(2,1)S(1)}, bf16[2,128,1024]{2,1,0:T(8,128)(2,1)S(1)}, u32[]{:S(2)}, u32[]{:S(2)}) %collective-permute-start.37) | collective-permute-done | bytes 524320 | tf_op jit(solution)/shard_map/ppermute | solution.py:432
  198.7 4.3 %collective-permute-start.38 = (bf16[2,128,1024]{2,1,0:T(8,128)(2,1)S(1)}, bf16[2,128,1024]{2,1,0:T(8,128)(2,1)S(1)}, u32[]{:S(2)}, u32[]{:S(2)}) collective-permute-start(bf16[2,128,1024]{2,1,0:T(8,128)(2,1)S(1)} %collective-permute-done.37.refs_6_), channel_id=1, source_target_pairs={{0,1},{1,0},{2,3},{3,2},{4,5},{5,4},{6,7},{7,6},{8,9},{9,8},{10,11... | collective-permute-start | bytes 1572872 | tf_op jit(solution)/shard_map/ppermute | solution.py:429
  203.5 3.3 %backward.9 = (bf16[2,128,2048]{2,1,0:T(8,128)(2,1)}, bf16[2,128,2048]{2,1,0:T(8,128)(2,1)S(1)}, bf16[2,128,2048]{2,1,0:T(8,128)(2,1)S(1)}, bf16[2,128,2048]{2,1,0:T(8,128)(2,1)S(1)}) custom-call(s32[3,16]{1,0:T(4,128)S(1)} %pad_add_fusion.meta_ref, bf16[1024,1024]{1,0:T(8,128)(2,1)S(1)} %copy-done, bf16[1024,512]{1,0:T(8,128)(2,1)S(1)} %copy-done.1, ...), custom_call_target="tpu_custom_call" | custom-call | flops 1024 | bytes 1024 | tf_op jit(solution)/shard_map/backward/pallas_call | solution.py:281
  206.8 1.1 collective-permute-start.39
  208.4 3.4 %copy-done.4 = f32[2,128,8192]{2,1,0:T(8,128)S(1)} copy-done((f32[2,128,8192]{2,1,0:T(8,128)S(1)}, f32[2,128,8192]{2,1,0:T(8,128)}, u32[]{:S(2)}) %copy-start.4) | copy-done | bytes 8388632
  211.8 4.8 %backward.10.refs_0_ = f32[2,128,8192]{2,1,0:T(8,128)S(1)} custom-call(s32[3,16]{1,0:T(4,128)S(1)} %pad_add_fusion.meta_ref, bf16[1024,1024]{1,0:T(8,128)(2,1)S(1)} %copy-done, bf16[1024,512]{1,0:T(8,128)(2,1)S(1)} %copy-done.1, f32[2,128,8192]{2,1,0:T(8,128)S(1)} %bitcast.9, f32[2,128,8192]{2,1,0:T(8,128)S(1)} %copy-done.4, ...), custom_call_target="tpu_custom_call" | custom-call | flops 1024 | bytes 1024 | tf_op jit(solution)/shard_map/backward/pallas_call | solution.py:281
  217.5 2.6 %collective-permute-done.43.refs_7_ = bf16[2,128,1024]{2,1,0:T(8,128)(2,1)S(1)} collective-permute-done((bf16[2,128,1024]{2,1,0:T(8,128)(2,1)S(1)}, bf16[2,128,1024]{2,1,0:T(8,128)(2,1)S(1)}, u32[]{:S(2)}, u32[]{:S(2)}) %collective-permute-start.43) | collective-permute-done | bytes 524320 | tf_op jit(solution)/shard_map/ppermute | solution.py:429
  220.1 5.5 %backward.11 = f32[2,128,8192]{2,1,0:T(8,128)} custom-call(s32[3,16]{1,0:T(4,128)S(1)} %pad_add_fusion.meta_ref, bf16[1024,1024]{1,0:T(8,128)(2,1)S(1)} %copy-done, bf16[1024,512]{1,0:T(8,128)(2,1)S(1)} %copy-done.1, f32[2,128,8192]{2,1,0:T(8,128)S(1)} %backward.10.refs_0_, bf16[2,128,2048]{2,1,0:T(8,128)(2,1)S(1)} %collective-permute-done.39.refs_1_, ...), custom_call_target="tpu_custom_call" | custom-call | flops 1024 | bytes 1024 | tf_op jit(solution)/shard_map/backward/pallas_call | solution.py:281
  (90 shorter events, 11.6 us)
Async XLA Ops:
  0.0 3.4 %copy-start.2 = (f32[2,128,8192]{2,1,0:T(8,128)S(1)}, f32[2,128,8192]{2,1,0:T(8,128)}, u32[]{:S(2)}) copy-start(f32[2,128,8192]{2,1,0:T(8,128)} %refs_0_.1) | copy-start | bytes 25165828
  5.3 3.4 %copy-start.12 = (s32[16]{0:T(128)S(1)}, s32[16]{0:T(128)}, u32[]{:S(2)}) copy-start(s32[16]{0:T(128)} %param.12) | copy-start | bytes 196
  5.3 3.4 %copy-start.13 = (s32[16]{0:T(128)S(1)}, s32[16]{0:T(128)}, u32[]{:S(2)}) copy-start(s32[16]{0:T(128)} %param.13) | copy-start | bytes 196
  5.3 3.6 %copy-start = (bf16[1024,1024]{1,0:T(8,128)(2,1)S(1)}, bf16[1024,1024]{1,0:T(8,128)(2,1)}, u32[]{:S(2)}) copy-start(bf16[1024,1024]{1,0:T(8,128)(2,1)} %pupil_ref.17) | copy-start | bytes 6291460
  5.3 3.6 %copy-start.1 = (bf16[1024,512]{1,0:T(8,128)(2,1)S(1)}, bf16[1024,512]{1,0:T(8,128)(2,1)}, u32[]{:S(2)}) copy-start(bf16[1024,512]{1,0:T(8,128)(2,1)} %constant.42.clone.band_ref) | copy-start | bytes 3145732
  5.3 5.9 %collective-permute-start.1 = (bf16[128,8192]{1,0:T(8,128)(2,1)}, bf16[128,8192]{1,0:T(8,128)(2,1)}, u32[]{:S(2)}, u32[]{:S(2)}) collective-permute-start(bf16[128,8192]{1,0:T(8,128)(2,1)} %low_part.3.refs_1_), channel_id=1, source_target_pairs={{0,1},{1,0},{2,3},{3,2},{4,5},{5,4},{6,7},{7,6},{8,9},{9,8},{10,11... | collective-permute-start | bytes 6291464 | tf_op jit(solution)/shard_map/ppermute | solution.py:429
  7.9 5.3 %collective-permute-start = (bf16[128,8192]{1,0:T(8,128)(2,1)}, bf16[128,8192]{1,0:T(8,128)(2,1)}, u32[]{:S(2)}, u32[]{:S(2)}) collective-permute-start(bf16[128,8192]{1,0:T(8,128)(2,1)} %low_part.2.refs_0_), channel_id=1, source_target_pairs={{0,1},{1,0},{2,3},{3,2},{4,5},{5,4},{6,7},{7,6},{8,9},{9,8},{10,11... | collective-permute-start | bytes 6291464 | tf_op jit(solution)/shard_map/ppermute | solution.py:429
  15.5 16.8 %collective-permute-start.2 = (bf16[2,128,1024]{2,1,0:T(8,128)(2,1)S(1)}, bf16[2,128,1024]{2,1,0:T(8,128)(2,1)S(1)}, u32[]{:S(2)}, u32[]{:S(2)}) collective-permute-start(bf16[2,128,1024]{2,1,0:T(8,128)(2,1)S(1)} %get-tuple-element.80), channel_id=1, source_target_pairs={{0,2},{1,3},{2,0},{3,1},{4,6},{5,7},{6,4},{7,5},{8,10},{9,11},{10,... | collective-permute-start | bytes 1572872 | tf_op jit(solution)/shard_map/ppermute | solution.py:432
  17.9 22.7 %collective-permute-start.11 = (bf16[2,128,1024]{2,1,0:T(8,128)(2,1)S(1)}, bf16[2,128,1024]{2,1,0:T(8,128)(2,1)S(1)}, u32[]{:S(2)}, u32[]{:S(2)}) collective-permute-start(bf16[2,128,1024]{2,1,0:T(8,128)(2,1)S(1)} %get-tuple-element.76), channel_id=1, source_target_pairs={{0,2},{1,3},{2,0},{3,1},{4,6},{5,7},{6,4},{7,5},{8,10},{9,11},{10,... | collective-permute-start | bytes 1572872 | tf_op jit(solution)/shard_map/ppermute | solution.py:432
  32.6 14.3 %collective-permute-start.3 = (bf16[2,128,1024]{2,1,0:T(8,128)(2,1)S(1)}, bf16[2,128,1024]{2,1,0:T(8,128)(2,1)S(1)}, u32[]{:S(2)}, u32[]{:S(2)}) collective-permute-start(bf16[2,128,1024]{2,1,0:T(8,128)(2,1)S(1)} %fusion), channel_id=1, source_target_pairs={{0,4},{1,5},{2,6},{3,7},{12,8},{13,9},{14,10},{15,11},{16,20},{17,... | collective-permute-start | bytes 1572872 | tf_op jit(solution)/shard_map/ppermute | solution.py:436
  33.9 17.9 %collective-permute-start.4 = (bf16[2,128,1024]{2,1,0:T(8,128)(2,1)S(1)}, bf16[2,128,1024]{2,1,0:T(8,128)(2,1)S(1)}, u32[]{:S(2)}, u32[]{:S(2)}) collective-permute-start(bf16[2,128,1024]{2,1,0:T(8,128)(2,1)S(1)} %get-tuple-element.85), channel_id=1, source_target_pairs={{0,2},{1,3},{2,0},{3,1},{4,6},{5,7},{6,4},{7,5},{8,10},{9,11},{10,... | collective-permute-start | bytes 1572872 | tf_op jit(solution)/shard_map/ppermute | solution.py:432
  40.7 18.6 %collective-permute-start.12 = (bf16[2,128,1024]{2,1,0:T(8,128)(2,1)S(1)}, bf16[2,128,1024]{2,1,0:T(8,128)(2,1)S(1)}, u32[]{:S(2)}, u32[]{:S(2)}) collective-permute-start(bf16[2,128,1024]{2,1,0:T(8,128)(2,1)S(1)} %fusion.2), channel_id=1, source_target_pairs={{0,4},{1,5},{2,6},{3,7},{12,8},{13,9},{14,10},{15,11},{16,20},{17,... | collective-permute-start | bytes 1572872 | tf_op jit(solution)/shard_map/ppermute | solution.py:436
  42.0 21.0 %collective-permute-start.13 = (bf16[2,128,1024]{2,1,0:T(8,128)(2,1)S(1)}, bf16[2,128,1024]{2,1,0:T(8,128)(2,1)S(1)}, u32[]{:S(2)}, u32[]{:S(2)}) collective-permute-start(bf16[2,128,1024]{2,1,0:T(8,128)(2,1)S(1)} %get-tuple-element.102), channel_id=1, source_target_pairs={{0,2},{1,3},{2,0},{3,1},{4,6},{5,7},{6,4},{7,5},{8,10},{9,11},{10,... | collective-permute-start | bytes 1572872 | tf_op jit(solution)/shard_map/ppermute | solution.py:432
  51.9 17.4 %collective-permute-start.6 = (bf16[2,128,1024]{2,1,0:T(8,128)(2,1)S(1)}, bf16[2,128,1024]{2,1,0:T(8,128)(2,1)S(1)}, u32[]{:S(2)}, u32[]{:S(2)}) collective-permute-start(bf16[2,128,1024]{2,1,0:T(8,128)(2,1)S(1)} %fusion.1), channel_id=1, source_target_pairs={{0,4},{1,5},{2,6},{3,7},{12,8},{13,9},{14,10},{15,11},{16,20},{17,... | collective-permute-start | bytes 1572872 | tf_op jit(solution)/shard_map/ppermute | solution.py:436
  53.5 17.3 %collective-permute-start.5 = (bf16[2,128,1024]{2,1,0:T(8,128)(2,1)S(1)}, bf16[2,128,1024]{2,1,0:T(8,128)(2,1)S(1)}, u32[]{:S(2)}, u32[]{:S(2)}) collective-permute-start(bf16[2,128,1024]{2,1,0:T(8,128)(2,1)S(1)} %add_convert_fusion.7), channel_id=1, source_target_pairs={{4,8},{5,9},{6,10},{7,11},{8,4},{9,5},{10,6},{11,7},{20,24},{21,25... | collective-permute-start | bytes 1572872 | tf_op jit(solution)/shard_map/ppermute | solution.py:436
  57.5 16.7 %collective-permute-start.7 = (bf16[2,128,1024]{2,1,0:T(8,128)(2,1)S(1)}, bf16[2,128,1024]{2,1,0:T(8,128)(2,1)S(1)}, u32[]{:S(2)}, u32[]{:S(2)}) collective-permute-start(bf16[2,128,1024]{2,1,0:T(8,128)(2,1)S(1)} %get-tuple-element.90), channel_id=1, source_target_pairs={{0,2},{1,3},{2,0},{3,1},{4,6},{5,7},{6,4},{7,5},{8,10},{9,11},{10,... | collective-permute-start | bytes 1572872 | tf_op jit(solution)/shard_map/ppermute | solution.py:432
  63.2 17.4 %collective-permute-start.15 = (bf16[2,128,1024]{2,1,0:T(8,128)(2,1)S(1)}, bf16[2,128,1024]{2,1,0:T(8,128)(2,1)S(1)}, u32[]{:S(2)}, u32[]{:S(2)}) collective-permute-start(bf16[2,128,1024]{2,1,0:T(8,128)(2,1)S(1)} %fusion.3), channel_id=1, source_target_pairs={{0,4},{1,5},{2,6},{3,7},{12,8},{13,9},{14,10},{15,11},{16,20},{17,... | collective-permute-start | bytes 1572872 | tf_op jit(solution)/shard_map/ppermute | solution.py:436
  64.8 15.8 %collective-permute-start.14 = (bf16[2,128,1024]{2,1,0:T(8,128)(2,1)S(1)}, bf16[2,128,1024]{2,1,0:T(8,128)(2,1)S(1)}, u32[]{:S(2)}, u32[]{:S(2)}) collective-permute-start(bf16[2,128,1024]{2,1,0:T(8,128)(2,1)S(1)} %add_convert_fusion.3), channel_id=1, source_target_pairs={{4,8},{5,9},{6,10},{7,11},{8,4},{9,5},{10,6},{11,7},{20,24},{21,25... | collective-permute-start | bytes 1572872 | tf_op jit(solution)/shard_map/ppermute | solution.py:436
  69.3 12.9 %collective-permute-start.16 = (bf16[2,128,1024]{2,1,0:T(8,128)(2,1)S(1)}, bf16[2,128,1024]{2,1,0:T(8,128)(2,1)S(1)}, u32[]{:S(2)}, u32[]{:S(2)}) collective-permute-start(bf16[2,128,1024]{2,1,0:T(8,128)(2,1)S(1)} %get-tuple-element.107), channel_id=1, source_target_pairs={{0,2},{1,3},{2,0},{3,1},{4,6},{5,7},{6,4},{7,5},{8,10},{9,11},{10,... | collective-permute-start | bytes 1572872 | tf_op jit(solution)/shard_map/ppermute | solution.py:432
  74.5 18.5 %collective-permute-start.9 = (bf16[2,128,1024]{2,1,0:T(8,128)(2,1)S(1)}, bf16[2,128,1024]{2,1,0:T(8,128)(2,1)S(1)}, u32[]{:S(2)}, u32[]{:S(2)}) collective-permute-start(bf16[2,128,1024]{2,1,0:T(8,128)(2,1)S(1)} %add_convert_fusion.6), channel_id=1, source_target_pairs={{4,8},{5,9},{6,10},{7,11},{8,4},{9,5},{10,6},{11,7},{20,24},{21,25... | collective-permute-start | bytes 1572872 | tf_op jit(solution)/shard_map/ppermute | solution.py:436
  78.5 14.9 %collective-permute-start.8 = (bf16[2,128,1024]{2,1,0:T(8,128)(2,1)S(1)}, bf16[2,128,1024]{2,1,0:T(8,128)(2,1)S(1)}, u32[]{:S(2)}, u32[]{:S(2)}) collective-permute-start(bf16[2,128,1024]{2,1,0:T(8,128)(2,1)S(1)} %get-tuple-element.92), channel_id=1, source_target_pairs={{0,2},{1,3},{2,0},{3,1},{4,6},{5,7},{6,4},{7,5},{8,10},{9,11},{10,... | collective-permute-start | bytes 1572872 | tf_op jit(solution)/shard_map/ppermute | solution.py:432
  80.5 12.9 %collective-permute-start.10 = (bf16[2,128,1024]{2,1,0:T(8,128)(2,1)S(1)}, bf16[2,128,1024]{2,1,0:T(8,128)(2,1)S(1)}, u32[]{:S(2)}, u32[]{:S(2)}) collective-permute-start(bf16[2,128,1024]{2,1,0:T(8,128)(2,1)S(1)} %add_convert_fusion.5), channel_id=1, source_target_pairs={{0,4},{1,5},{2,6},{3,7},{12,8},{13,9},{14,10},{15,11},{4,0},{5,1},... | collective-permute-start | bytes 1572872 | tf_op jit(solution)/shard_map/ppermute | solution.py:436
  82.4 20.5 %collective-permute-start.18 = (bf16[2,128,1024]{2,1,0:T(8,128)(2,1)S(1)}, bf16[2,128,1024]{2,1,0:T(8,128)(2,1)S(1)}, u32[]{:S(2)}, u32[]{:S(2)}) collective-permute-start(bf16[2,128,1024]{2,1,0:T(8,128)(2,1)S(1)} %add_convert_fusion.2), channel_id=1, source_target_pairs={{4,8},{5,9},{6,10},{7,11},{8,4},{9,5},{10,6},{11,7},{20,24},{21,25... | collective-permute-start | bytes 1572872 | tf_op jit(solution)/shard_map/ppermute | solution.py:436
  92.6 14.1 %collective-permute-start.17 = (bf16[2,128,1024]{2,1,0:T(8,128)(2,1)S(1)}, bf16[2,128,1024]{2,1,0:T(8,128)(2,1)S(1)}, u32[]{:S(2)}, u32[]{:S(2)}) collective-permute-start(bf16[2,128,1024]{2,1,0:T(8,128)(2,1)S(1)} %get-tuple-element.109), channel_id=1, source_target_pairs={{0,2},{1,3},{2,0},{3,1},{4,6},{5,7},{6,4},{7,5},{8,10},{9,11},{10,... | collective-permute-start | bytes 1572872 | tf_op jit(solution)/shard_map/ppermute | solution.py:432
  93.0 13.7 %collective-permute-start.19 = (bf16[2,128,1024]{2,1,0:T(8,128)(2,1)S(1)}, bf16[2,128,1024]{2,1,0:T(8,128)(2,1)S(1)}, u32[]{:S(2)}, u32[]{:S(2)}) collective-permute-start(bf16[2,128,1024]{2,1,0:T(8,128)(2,1)S(1)} %add_convert_fusion.1), channel_id=1, source_target_pairs={{0,4},{1,5},{2,6},{3,7},{12,8},{13,9},{14,10},{15,11},{4,0},{5,1},... | collective-permute-start | bytes 1572872 | tf_op jit(solution)/shard_map/ppermute | solution.py:436
  93.4 13.7 %copy-start.9 = (bf16[1024,1024]{1,0:T(8,128)(2,1)S(1)}, bf16[1024,1024]{1,0:T(8,128)(2,1)}, u32[]{:S(2)}) copy-start(bf16[1024,1024]{1,0:T(8,128)(2,1)} %constant.44.clone.refs_4_) | copy-start | bytes 6291460
  93.4 13.7 %copy-start.10 = (bf16[1024,1024]{1,0:T(8,128)(2,1)S(1)}, bf16[1024,1024]{1,0:T(8,128)(2,1)}, u32[]{:S(2)}) copy-start(bf16[1024,1024]{1,0:T(8,128)(2,1)} %constant.43.clone.refs_3_) | copy-start | bytes 6291460
  93.4 13.7 %copy-start.11 = (bf16[1,256,1024]{2,1,0:T(8,128)(2,1)S(1)}, bf16[1,256,1024]{2,1,0:T(8,128)(2,1)}, u32[]{:S(2)}) copy-start(bf16[1,256,1024]{2,1,0:T(8,128)(2,1)} %refs_2_.1) | copy-start | bytes 1572868
  112.7 11.1 %collective-permute-start.28 = (bf16[2,128,1024]{2,1,0:T(8,128)(2,1)S(1)}, bf16[2,128,1024]{2,1,0:T(8,128)(2,1)}, u32[]{:S(2)}, u32[]{:S(2)}) collective-permute-start(bf16[2,128,1024]{2,1,0:T(8,128)(2,1)S(1)} %get-tuple-element.117.refs_1_), channel_id=1, source_target_pairs={{0,4},{1,5},{2,6},{3,7},{12,8},{13,9},{14,10},{15,11},{4,0},{5,1},... | collective-permute-start | bytes 1572872 | tf_op jit(solution)/shard_map/ppermute | solution.py:436
  112.7 19.1 %collective-permute-start.27 = (bf16[2,128,1024]{2,1,0:T(8,128)(2,1)S(1)}, bf16[2,128,1024]{2,1,0:T(8,128)(2,1)}, u32[]{:S(2)}, u32[]{:S(2)}) collective-permute-start(bf16[2,128,1024]{2,1,0:T(8,128)(2,1)S(1)} %get-tuple-element.117.refs_1_), channel_id=1, source_target_pairs={{4,8},{5,9},{6,10},{7,11},{8,4},{9,5},{10,6},{11,7},{20,24},{21,25... | collective-permute-start | bytes 1572872 | tf_op jit(solution)/shard_map/ppermute | solution.py:436
  120.1 12.7 %collective-permute-start.26 = (bf16[2,128,1024]{2,1,0:T(8,128)(2,1)S(1)}, bf16[2,128,1024]{2,1,0:T(8,128)(2,1)S(1)}, u32[]{:S(2)}, u32[]{:S(2)}) collective-permute-start(bf16[2,128,1024]{2,1,0:T(8,128)(2,1)S(1)} %get-tuple-element.117.refs_1_), channel_id=1, source_target_pairs={{0,2},{1,3},{2,0},{3,1},{4,6},{5,7},{6,4},{7,5},{8,10},{9,11},{10,... | collective-permute-start | bytes 1572872 | tf_op jit(solution)/shard_map/ppermute | solution.py:432
  120.6 0.8 copy-start.5
  121.5 18.0 %collective-permute-start.22 = (bf16[2,128,1024]{2,1,0:T(8,128)(2,1)}, bf16[2,128,1024]{2,1,0:T(8,128)(2,1)}, u32[]{:S(2)}, u32[]{:S(2)}) collective-permute-start(bf16[2,128,1024]{2,1,0:T(8,128)(2,1)} %get-tuple-element.114.refs_0_), channel_id=1, source_target_pairs={{0,4},{1,5},{2,6},{3,7},{12,8},{13,9},{14,10},{15,11},{4,0},{5,1},... | collective-permute-start | bytes 1572872 | tf_op jit(solution)/shard_map/ppermute | solution.py:436
  121.5 21.6 %collective-permute-start.21 = (bf16[2,128,1024]{2,1,0:T(8,128)(2,1)}, bf16[2,128,1024]{2,1,0:T(8,128)(2,1)}, u32[]{:S(2)}, u32[]{:S(2)}) collective-permute-start(bf16[2,128,1024]{2,1,0:T(8,128)(2,1)} %get-tuple-element.114.refs_0_), channel_id=1, source_target_pairs={{4,8},{5,9},{6,10},{7,11},{8,4},{9,5},{10,6},{11,7},{20,24},{21,25... | collective-permute-start | bytes 1572872 | tf_op jit(solution)/shard_map/ppermute | solution.py:436
  123.8 20.2 %collective-permute-start.20 = (bf16[2,128,1024]{2,1,0:T(8,128)(2,1)}, bf16[2,128,1024]{2,1,0:T(8,128)(2,1)}, u32[]{:S(2)}, u32[]{:S(2)}) collective-permute-start(bf16[2,128,1024]{2,1,0:T(8,128)(2,1)} %get-tuple-element.114.refs_0_), channel_id=1, source_target_pairs={{0,2},{1,3},{2,0},{3,1},{4,6},{5,7},{6,4},{7,5},{8,10},{9,11},{10,... | collective-permute-start | bytes 1572872 | tf_op jit(solution)/shard_map/ppermute | solution.py:432
  132.8 0.8 copy-start.7
  133.5 21.1 %collective-permute-start.33 = (bf16[2,128,1024]{2,1,0:T(8,128)(2,1)}, bf16[2,128,1024]{2,1,0:T(8,128)(2,1)}, u32[]{:S(2)}, u32[]{:S(2)}) collective-permute-start(bf16[2,128,1024]{2,1,0:T(8,128)(2,1)} %collective-permute-done.27), channel_id=1, source_target_pairs={{4,0},{5,1},{6,2},{7,3},{8,12},{9,13},{10,14},{11,15},{20,16},{21,... | collective-permute-start | bytes 1572872 | tf_op jit(solution)/shard_map/ppermute | solution.py:436
  135.7 19.4 %collective-permute-start.32 = (bf16[2,128,1024]{2,1,0:T(8,128)(2,1)}, bf16[2,128,1024]{2,1,0:T(8,128)(2,1)}, u32[]{:S(2)}, u32[]{:S(2)}) collective-permute-start(bf16[2,128,1024]{2,1,0:T(8,128)(2,1)} %collective-permute-done.28.refs_3_), channel_id=1, source_target_pairs={{4,8},{5,9},{6,10},{7,11},{8,4},{9,5},{10,6},{11,7},{20,24},{21,25... | collective-permute-start | bytes 1572872 | tf_op jit(solution)/shard_map/ppermute | solution.py:436
  139.4 15.8 %collective-permute-start.31 = (bf16[2,128,1024]{2,1,0:T(8,128)(2,1)}, bf16[2,128,1024]{2,1,0:T(8,128)(2,1)}, u32[]{:S(2)}, u32[]{:S(2)}) collective-permute-start(bf16[2,128,1024]{2,1,0:T(8,128)(2,1)} %collective-permute-done.28.refs_3_), channel_id=1, source_target_pairs={{0,2},{1,3},{2,0},{3,1},{4,6},{5,7},{6,4},{7,5},{8,10},{9,11},{10,... | collective-permute-start | bytes 1572872 | tf_op jit(solution)/shard_map/ppermute | solution.py:432
  144.0 22.1 %collective-permute-start.25 = (bf16[2,128,1024]{2,1,0:T(8,128)(2,1)}, bf16[2,128,1024]{2,1,0:T(8,128)(2,1)S(1)}, u32[]{:S(2)}, u32[]{:S(2)}) collective-permute-start(bf16[2,128,1024]{2,1,0:T(8,128)(2,1)} %collective-permute-done.21), channel_id=1, source_target_pairs={{4,0},{5,1},{6,2},{7,3},{8,12},{9,13},{10,14},{11,15},{20,16},{21,... | collective-permute-start | bytes 1572872 | tf_op jit(solution)/shard_map/ppermute | solution.py:436
  145.3 20.8 %collective-permute-start.24 = (bf16[2,128,1024]{2,1,0:T(8,128)(2,1)}, bf16[2,128,1024]{2,1,0:T(8,128)(2,1)S(1)}, u32[]{:S(2)}, u32[]{:S(2)}) collective-permute-start(bf16[2,128,1024]{2,1,0:T(8,128)(2,1)} %collective-permute-done.22.refs_2_), channel_id=1, source_target_pairs={{4,8},{5,9},{6,10},{7,11},{8,4},{9,5},{10,6},{11,7},{20,24},{21,25... | collective-permute-start | bytes 1572872 | tf_op jit(solution)/shard_map/ppermute | solution.py:436
  148.4 1.0 copy-start.6
  149.5 1.0 copy-start.8
  154.7 11.4 %collective-permute-start.23 = (bf16[2,128,1024]{2,1,0:T(8,128)(2,1)}, bf16[2,128,1024]{2,1,0:T(8,128)(2,1)S(1)}, u32[]{:S(2)}, u32[]{:S(2)}) collective-permute-start(bf16[2,128,1024]{2,1,0:T(8,128)(2,1)} %collective-permute-done.22.refs_2_), channel_id=1, source_target_pairs={{0,2},{1,3},{2,0},{3,1},{4,6},{5,7},{6,4},{7,5},{8,10},{9,11},{10,... | collective-permute-start | bytes 1572872 | tf_op jit(solution)/shard_map/ppermute | solution.py:432
  156.3 19.9 %collective-permute-start.35 = (bf16[2,128,1024]{2,1,0:T(8,128)(2,1)S(1)}, bf16[2,128,1024]{2,1,0:T(8,128)(2,1)S(1)}, u32[]{:S(2)}, u32[]{:S(2)}) collective-permute-start(bf16[2,128,1024]{2,1,0:T(8,128)(2,1)S(1)} %broadcast_select_fusion.2.refs_2_.refs_3_), channel_id=1, source_target_pairs={{0,2},{1,3},{2,0},{3,1},{4,6},{5,7},{6,4},{7,5},{8,10},{9,11},{10,... | collective-permute-start | bytes 1572872 | tf_op jit(solution)/shard_map/ppermute | solution.py:432
  157.4 18.9 %collective-permute-start.36 = (bf16[2,128,1024]{2,1,0:T(8,128)(2,1)}, bf16[2,128,1024]{2,1,0:T(8,128)(2,1)S(1)}, u32[]{:S(2)}, u32[]{:S(2)}) collective-permute-start(bf16[2,128,1024]{2,1,0:T(8,128)(2,1)} %collective-permute-done.32), channel_id=1, source_target_pairs={{4,0},{5,1},{6,2},{7,3},{8,12},{9,13},{10,14},{11,15},{20,16},{21,... | collective-permute-start | bytes 1572872 | tf_op jit(solution)/shard_map/ppermute | solution.py:436
  162.7 3.4 %copy-start.3 = (f32[2,128,8192]{2,1,0:T(8,128)}, f32[2,128,8192]{2,1,0:T(8,128)S(1)}, u32[]{:S(2)}) copy-start(f32[2,128,8192]{2,1,0:T(8,128)S(1)} %backward.6.refs_1_) | copy-start | bytes 25165828
  167.2 20.3 %collective-permute-start.29 = (bf16[2,128,1024]{2,1,0:T(8,128)(2,1)S(1)}, bf16[2,128,1024]{2,1,0:T(8,128)(2,1)S(1)}, u32[]{:S(2)}, u32[]{:S(2)}) collective-permute-start(bf16[2,128,1024]{2,1,0:T(8,128)(2,1)S(1)} %broadcast_select_fusion.3.refs_1_.refs_2_), channel_id=1, source_target_pairs={{0,2},{1,3},{2,0},{3,1},{4,6},{5,7},{6,4},{7,5},{8,10},{9,11},{10,... | collective-permute-start | bytes 1572872 | tf_op jit(solution)/shard_map/ppermute | solution.py:432
  168.6 18.9 %collective-permute-start.30 = (bf16[2,128,1024]{2,1,0:T(8,128)(2,1)S(1)}, bf16[2,128,1024]{2,1,0:T(8,128)(2,1)S(1)}, u32[]{:S(2)}, u32[]{:S(2)}) collective-permute-start(bf16[2,128,1024]{2,1,0:T(8,128)(2,1)S(1)} %collective-permute-done.24), channel_id=1, source_target_pairs={{4,0},{5,1},{6,2},{7,3},{8,12},{9,13},{10,14},{11,15},{20,16},{21,... | collective-permute-start | bytes 1572872 | tf_op jit(solution)/shard_map/ppermute | solution.py:436
  176.3 32.2 %slice-start = ((s8[8388608]{0:T(1024)(128)(4,1)}), s8[4194304]{0:T(1024)(128)(4,1)S(1)}, s32[]{:S(2)}) async-start(s8[8388608]{0:T(1024)(128)(4,1)} %bitcast.8), calls=%async_computation | async-start | bytes 8388608
  177.5 30.9 %slice-start.1 = ((s8[8388608]{0:T(1024)(128)(4,1)}), s8[4194304]{0:T(1024)(128)(4,1)S(1)}, s32[]{:S(2)}) async-start(s8[8388608]{0:T(1024)(128)(4,1)} %bitcast.8), calls=%async_computation.1 | async-start | bytes 8388608
  177.5 21.2 %collective-permute-start.37 = (bf16[2,128,1024]{2,1,0:T(8,128)(2,1)S(1)}, bf16[2,128,1024]{2,1,0:T(8,128)(2,1)S(1)}, u32[]{:S(2)}, u32[]{:S(2)}) collective-permute-start(bf16[2,128,1024]{2,1,0:T(8,128)(2,1)S(1)} %broadcast_select_fusion.refs_2_.refs_7_), channel_id=1, source_target_pairs={{0,2},{1,3},{2,0},{3,1},{4,6},{5,7},{6,4},{7,5},{8,10},{9,11},{10,... | collective-permute-start | bytes 1572872 | tf_op jit(solution)/shard_map/ppermute | solution.py:432
  198.7 9.7 %collective-permute-start.38 = (bf16[2,128,1024]{2,1,0:T(8,128)(2,1)S(1)}, bf16[2,128,1024]{2,1,0:T(8,128)(2,1)S(1)}, u32[]{:S(2)}, u32[]{:S(2)}) collective-permute-start(bf16[2,128,1024]{2,1,0:T(8,128)(2,1)S(1)} %collective-permute-done.37.refs_6_), channel_id=1, source_target_pairs={{0,1},{1,0},{2,3},{3,2},{4,5},{5,4},{6,7},{7,6},{8,9},{9,8},{10,11... | collective-permute-start | bytes 1572872 | tf_op jit(solution)/shard_map/ppermute | solution.py:429
  203.1 13.6 %collective-permute-start.34 = (bf16[2,128,1024]{2,1,0:T(8,128)(2,1)S(1)}, bf16[2,128,1024]{2,1,0:T(8,128)(2,1)S(1)}, u32[]{:S(2)}, u32[]{:S(2)}) collective-permute-start(bf16[2,128,1024]{2,1,0:T(8,128)(2,1)S(1)} %broadcast_select_fusion.1.refs_1_.refs_6_), channel_id=1, source_target_pairs={{0,2},{1,3},{2,0},{3,1},{4,6},{5,7},{6,4},{7,5},{8,10},{9,11},{10,... | collective-permute-start | bytes 1572872 | tf_op jit(solution)/shard_map/ppermute | solution.py:432
  206.8 13.3 %collective-permute-start.39 = (bf16[2,128,2048]{2,1,0:T(8,128)(2,1)}, bf16[2,128,2048]{2,1,0:T(8,128)(2,1)S(1)}, u32[]{:S(2)}, u32[]{:S(2)}) collective-permute-start(bf16[2,128,2048]{2,1,0:T(8,128)(2,1)} %get-tuple-element.141), channel_id=1, source_target_pairs={{0,1},{1,0},{2,3},{3,2},{4,5},{5,4},{6,7},{7,6},{8,9},{9,8},{10,11... | collective-permute-start | bytes 3145736 | tf_op jit(solution)/shard_map/ppermute | solution.py:429
  207.9 12.2 %collective-permute-start.40 = (bf16[2,128,2048]{2,1,0:T(8,128)(2,1)S(1)}, bf16[2,128,2048]{2,1,0:T(8,128)(2,1)S(1)}, u32[]{:S(2)}, u32[]{:S(2)}) collective-permute-start(bf16[2,128,2048]{2,1,0:T(8,128)(2,1)S(1)} %get-tuple-element.142), channel_id=1, source_target_pairs={{0,1},{1,0},{2,3},{3,2},{4,5},{5,4},{6,7},{7,6},{8,9},{9,8},{10,11... | collective-permute-start | bytes 3145736 | tf_op jit(solution)/shard_map/ppermute | solution.py:429
  207.9 12.2 %collective-permute-start.41 = (bf16[2,128,2048]{2,1,0:T(8,128)(2,1)S(1)}, bf16[2,128,2048]{2,1,0:T(8,128)(2,1)S(1)}, u32[]{:S(2)}, u32[]{:S(2)}) collective-permute-start(bf16[2,128,2048]{2,1,0:T(8,128)(2,1)S(1)} %get-tuple-element.143), channel_id=1, source_target_pairs={{0,1},{1,0},{2,3},{3,2},{4,5},{5,4},{6,7},{7,6},{8,9},{9,8},{10,11... | collective-permute-start | bytes 3145736 | tf_op jit(solution)/shard_map/ppermute | solution.py:429
  208.4 3.4 %copy-start.4 = (f32[2,128,8192]{2,1,0:T(8,128)S(1)}, f32[2,128,8192]{2,1,0:T(8,128)}, u32[]{:S(2)}) copy-start(f32[2,128,8192]{2,1,0:T(8,128)} %copy-done.3) | copy-start | bytes 25165828
  216.6 3.5 %collective-permute-start.42 = (bf16[2,128,2048]{2,1,0:T(8,128)(2,1)S(1)}, bf16[2,128,2048]{2,1,0:T(8,128)(2,1)S(1)}, u32[]{:S(2)}, u32[]{:S(2)}) collective-permute-start(bf16[2,128,2048]{2,1,0:T(8,128)(2,1)S(1)} %get-tuple-element.144), channel_id=1, source_target_pairs={{0,1},{1,0},{2,3},{3,2},{4,5},{5,4},{6,7},{7,6},{8,9},{9,8},{10,11... | collective-permute-start | bytes 3145736 | tf_op jit(solution)/shard_map/ppermute | solution.py:429
  216.7 3.4 %collective-permute-start.43 = (bf16[2,128,1024]{2,1,0:T(8,128)(2,1)S(1)}, bf16[2,128,1024]{2,1,0:T(8,128)(2,1)S(1)}, u32[]{:S(2)}, u32[]{:S(2)}) collective-permute-start(bf16[2,128,1024]{2,1,0:T(8,128)(2,1)S(1)} %collective-permute-done.34.refs_5_), channel_id=1, source_target_pairs={{0,1},{1,0},{2,3},{3,2},{4,5},{5,4},{6,7},{7,6},{8,9},{9,8},{10,11... | collective-permute-start | bytes 1572872 | tf_op jit(solution)/shard_map/ppermute | solution.py:429
